TPU v7x, 512 devices: a whole 4x8x8 slice. The times are simulated.
512 devices in a mesh: wide: 64 (over z, x, core), narrow: 8 (over y).
Axes of the slice: x: 4, y: 8, z: 8, core: 2. Of those that a mesh axis runs over, the one named last changes fastest.
Arguments:
- right_side: float32 [256, 512, 128], P('wide', 'narrow'), may hold values from -24 to 24
- alpha_coef: float32 [256, 512, 128], P('wide', 'narrow'), may hold values from 0.1 to 2
- beta_x: float32 [256, 512, 128], P('wide', 'narrow'), may hold values from 0.25 to 4
- beta_y: float32 [256, 512, 128], P('wide', 'narrow'), may hold values from 0.25 to 4
- beta_z: float32 [256, 512, 128], P('wide', 'narrow'), may hold values from 0.25 to 4
Outputs:
- solution_field: float32 [256, 512, 128], P('wide', 'narrow')
All inputs are finite; a program needn't handle non-finite values.
Results may differ from a plain program's by a relative error of at most 0.00002.
Values sent between devices are 32-bit elements; how exact they have to be, the bound alone decides.
No kernel may reach another device: no remote copies, remote signals or barrier semaphores. Data moves between devices by JAX's collectives and lax.ppermute only.
A program may use at most 64 MiB of HBM per device.

v0:
```python
import jax
import jax.numpy as jnp
from jax import lax
from jax.sharding import PartitionSpec as P

spectrum_low = 0.25
spectrum_high = 2.0


def extended(cells, sides, width):
    for axis, dim in sides:
        count = lax.axis_size(axis)
        ends = count - 1
        head = lax.slice_in_dim(cells, 0, width, axis=dim)
        tail = lax.slice_in_dim(cells, cells.shape[dim] - width, cells.shape[dim], axis=dim)
        cells = jnp.concatenate(
            [
                lax.ppermute(tail, axis, [(i, (i + 1) % count) for i in range(ends)]),
                cells,
                lax.ppermute(head, axis, [((i + 1) % count, i) for i in range(ends)]),
            ],
            axis=dim,
        )
    return cells


def shifted(value, axis, steps):
    count = lax.axis_size(axis)
    initial, last = (max(0, -steps), min(count, count - steps))
    return lax.ppermute(value, axis, [(source, source + steps) for source in range(initial, last)])


def average_cells(values):
    a, b, c = values.shape
    return values.reshape(a // 2, 2, b // 2, 2, c // 2, 2).mean(axis=(1, 3, 5))


def average_yz(values):
    a, b, c = values.shape
    return values.reshape(a, b // 2, 2, c // 2, 2).mean(axis=(2, 4))


def average_xz(values):
    a, b, c = values.shape
    return values.reshape(a // 2, 2, b, c // 2, 2).mean(axis=(1, 4))


def average_xy(values):
    a, b, c = values.shape
    return values.reshape(a // 2, 2, b // 2, 2, c).mean(axis=(1, 3))


def coarsen(raw):
    alpha, bxl, bxt, byl, byt, bzl = raw
    return (
        average_cells(alpha),
        average_yz(bxl[0::2]),
        average_yz(bxt),
        average_xz(byl[:, 0::2]),
        average_xz(byt),
        average_xy(bzl[:, :, 0::2]),
    )


def make_coef(raw, scale):
    alpha, bxl, bxt, byl, byt, bzl = raw
    bxh = jnp.concatenate([bxl[1:], bxt], 0)
    byh = jnp.concatenate([byl[:, 1:], byt], 1)
    bzh = jnp.concatenate([bzl[:, :, 1:], jnp.zeros_like(bzl[:, :, :1])], 2)
    total = bxl + bxh + byl + byh + bzl + bzh
    inverse = 1.0 / (alpha + scale * total)
    return (alpha, bxl, bxh, byl, byh, bzl, bzh, scale, inverse)


def operate(field, near, coef):
    alpha, bxl, bxh, byl, byh, bzl, bzh, scale, inverse = coef
    below_x, above_x, below_y, above_y = near
    below_z = jnp.concatenate([jnp.zeros_like(field[:, :, :1]), field[:, :, :-1]], 2)
    above_z = jnp.concatenate([field[:, :, 1:], jnp.zeros_like(field[:, :, :1])], 2)
    flux = (
        bxl * (field - below_x)
        + bxh * (field - above_x)
        + byl * (field - below_y)
        + byh * (field - above_y)
        + bzl * (field - below_z)
        + bzh * (field - above_z)
    )
    return alpha * field + scale * flux


def chebyshev(start, rhs, coef, degree, near_fn, from_zero):
    inverse = coef[8]
    theta = (spectrum_high + spectrum_low) / 2.0
    delta = (spectrum_high - spectrum_low) / 2.0
    sigma = theta / delta
    if from_zero:
        resid = rhs
    else:
        resid = rhs - operate(start, near_fn(start), coef)
    previous = start
    current = start + 1.0 / theta * inverse * resid
    rho_prev = 1.0 / sigma
    for step in range(1, degree):
        resid = rhs - operate(current, near_fn(current), coef)
        rho_now = 1.0 / (2.0 * sigma - rho_prev)
        upcoming = (
            current
            + rho_now * rho_prev * (current - previous)
            + 2.0 * rho_now / delta * inverse * resid
        )
        previous, current = (current, upcoming)
        rho_prev = rho_now
    return current


def split_padded(padded):
    return (padded[:-2, 1:-1], padded[2:, 1:-1], padded[1:-1, :-2], padded[1:-1, 2:])


def fine_near(field):
    return split_padded(extended(field, (("wide", 0), ("narrow", 1)), 1))


def middle_near(field):
    return split_padded(extended(field, (("wide", 0), ("narrow", 1)), 1))


def coarse_near(field):
    return split_padded(extended(field, (("wide", 0), ("narrow", 1)), 1))


def expand(values):
    return jnp.repeat(jnp.repeat(jnp.repeat(values, 2, axis=0), 2, axis=1), 2, axis=2)


def shards(right_side, alpha_coef, beta_x, beta_y, beta_z):
    index_wide = lax.axis_index("wide")
    index_narrow = lax.axis_index("narrow")
    keep_x = (index_wide > 0).astype(jnp.float32)
    keep_y = (index_narrow > 0).astype(jnp.float32)
    bxl = jnp.concatenate([beta_x[:1] * keep_x, beta_x[1:]], 0)
    byl = jnp.concatenate([beta_y[:, :1] * keep_y, beta_y[:, 1:]], 1)
    bzl = jnp.concatenate([jnp.zeros_like(beta_z[:, :, :1]), beta_z[:, :, 1:]], 2)
    bxt = shifted(beta_x[:1], "wide", -1)
    byt = shifted(beta_y[:, :1], "narrow", -1)
    raw0 = (alpha_coef, bxl, bxt, byl, byt, bzl)
    coef0 = make_coef(raw0, 1.0)
    level0 = chebyshev(jnp.zeros_like(right_side), right_side, coef0, 3, fine_near, True)
    rhs1 = average_cells(right_side - operate(level0, fine_near(level0), coef0))
    raw1 = coarsen(raw0)
    coef1 = make_coef(raw1, 0.25)
    level1 = chebyshev(jnp.zeros_like(rhs1), rhs1, coef1, 3, middle_near, True)
    rhs2 = average_cells(rhs1 - operate(level1, middle_near(level1), coef1))
    raw2 = coarsen(raw1)
    coef2 = make_coef(raw2, 0.0625)
    coarse_error = chebyshev(jnp.zeros_like(rhs2), rhs2, coef2, 4, coarse_near, True)
    level1 = chebyshev(level1 + expand(coarse_error), rhs1, coef1, 2, middle_near, False)
    restart = level0 + expand(level1)
    level0 = chebyshev(restart, right_side, coef0, 2, fine_near, False)
    return level0


def solution(mesh):
    return jax.shard_map(
        shards,
        mesh=mesh,
        in_specs=(
            P("wide", "narrow", None),
            P("wide", "narrow", None),
            P("wide", "narrow", None),
            P("wide", "narrow", None),
            P("wide", "narrow", None),
        ),
        out_specs=P("wide", "narrow", None),
        check_vma=False,
    )
```

profile of v0, /device:TPU:199, one launch (start us, length us, event | category | flops | bytes accessed | tf_op | source)
XLA Modules:
  0.0 311.6 jit_solution(2979237870784111154)
XLA Ops:
  8.2 10.6 %reshape.232 = f32[2,2,32,2,64,2]{5,4,3,2,1,0:T(8,128)} reshape(f32[4,64,128]{2,1,0:T(8,128)} %param.6) | data formatting | bytes 262144 | tf_op jit(solution)/shard_map/reshape | solution.py:35
  18.8 4.0 %reduce_sum.137 = f32[2,32,64]{2,1,0:T(8,128)S(1)} reduce(f32[2,2,32,2,64,2]{5,4,3,2,1,0:T(8,128)} %reshape.232, f32[]{:T(128)} %constant.22.clone.1), dimensions={1,3,5}, to_apply=%region_0.0 | reduce | flops 28672 | bytes 147460 | tf_op jit(solution)/shard_map/reduce_sum | solution.py:35
  24.8 6.3 %collective-permute-start.2 = (f32[1,64,128]{2,1,0:T(8,128)S(1)}, f32[1,64,128]{2,1,0:T(8,128)S(1)}, u32[]{:S(2)}, u32[]{:S(2)}) collective-permute-start(f32[1,64,128]{2,1,0:T(8,128)S(1)} %get-tuple-element.37), channel_id=1, source_target_pairs={{0,8},{8,16},{16,24},{24,32},{32,40},{40,48},{48,56},{56,64},{64,7... | collective-permute-start | bytes 98312 | tf_op jit(solution)/shard_map/ppermute | solution.py:18
  35.8 5.5 %reshape.233 = f32[2,32,2,64,2]{4,3,2,1,0:T(8,128)} reshape(f32[2,64,128]{2,1,0:T(8,128)S(1)} %slice.476) | data formatting | bytes 131072 | tf_op jit(solution)/shard_map/reshape | solution.py:40
  44.2 4.0 %collective-permute-start.4 = (f32[6,1,128]{2,1,0:T(1,128)S(1)}, f32[6,1,128]{2,1,0:T(1,128)S(1)}, u32[]{:S(2)}, u32[]{:S(2)}) collective-permute-start(f32[6,1,128]{2,1,0:T(1,128)S(1)} %get-tuple-element.13), channel_id=1, source_target_pairs={{0,1},{1,2},{2,3},{3,4},{4,5},{5,6},{6,7},{8,9},{9,10},{10,11},{11... | collective-permute-start | bytes 9224 | tf_op jit(solution)/shard_map/ppermute | solution.py:18
  49.5 3.0 collective-permute-done.5
  52.8 8.4 %collective-permute-start.6 = (f32[1,64,128]{2,1,0:T(8,128)S(1)}, f32[1,64,128]{2,1,0:T(8,128)S(1)}, u32[]{:S(2)}, u32[]{:S(2)}) collective-permute-start(f32[1,64,128]{2,1,0:T(8,128)S(1)} %get-tuple-element.33), channel_id=1, source_target_pairs={{0,8},{8,16},{16,24},{24,32},{32,40},{40,48},{48,56},{56,64},{64,7... | collective-permute-start | bytes 98312 | tf_op jit(solution)/shard_map/ppermute | solution.py:18
  65.6 4.2 %collective-permute-done.7 = f32[1,64,128]{2,1,0:T(8,128)S(1)} collective-permute-done((f32[1,64,128]{2,1,0:T(8,128)S(1)}, f32[1,64,128]{2,1,0:T(8,128)S(1)}, u32[]{:S(2)}, u32[]{:S(2)}) %collective-permute-start.7) | collective-permute-done | bytes 32800 | tf_op jit(solution)/shard_map/ppermute | solution.py:20
  69.7 3.2 %collective-permute-start.8 = (f32[6,1,128]{2,1,0:T(1,128)S(1)}, f32[6,1,128]{2,1,0:T(1,128)S(1)}, u32[]{:S(2)}, u32[]{:S(2)}) collective-permute-start(f32[6,1,128]{2,1,0:T(1,128)S(1)} %get-tuple-element.11), channel_id=1, source_target_pairs={{0,1},{1,2},{2,3},{3,4},{4,5},{5,6},{6,7},{8,9},{9,10},{10,11},{11... | collective-permute-start | bytes 9224 | tf_op jit(solution)/shard_map/ppermute | solution.py:18
  74.3 3.6 %collective-permute-done.9 = f32[6,1,128]{2,1,0:T(1,128)S(1)} collective-permute-done((f32[6,1,128]{2,1,0:T(1,128)S(1)}, f32[6,1,128]{2,1,0:T(1,128)S(1)}, u32[]{:S(2)}, u32[]{:S(2)}) %collective-permute-start.9) | collective-permute-done | bytes 3104 | tf_op jit(solution)/shard_map/ppermute | solution.py:20
  78.1 4.0 %collective-permute-start.10 = (f32[1,64,128]{2,1,0:T(8,128)S(1)}, f32[1,64,128]{2,1,0:T(8,128)S(1)}, u32[]{:S(2)}, u32[]{:S(2)}) collective-permute-start(f32[1,64,128]{2,1,0:T(8,128)S(1)} %get-tuple-element.29), channel_id=1, source_target_pairs={{0,8},{8,16},{16,24},{24,32},{32,40},{40,48},{48,56},{56,64},{64,7... | collective-permute-start | bytes 98312 | tf_op jit(solution)/shard_map/ppermute | solution.py:18
  84.2 6.5 %collective-permute-done.11 = f32[1,64,128]{2,1,0:T(8,128)S(1)} collective-permute-done((f32[1,64,128]{2,1,0:T(8,128)S(1)}, f32[1,64,128]{2,1,0:T(8,128)S(1)}, u32[]{:S(2)}, u32[]{:S(2)}) %collective-permute-start.11) | collective-permute-done | bytes 32800 | tf_op jit(solution)/shard_map/ppermute | solution.py:20
  90.7 4.8 %collective-permute-start.12 = (f32[6,1,128]{2,1,0:T(1,128)S(1)}, f32[6,1,128]{2,1,0:T(1,128)S(1)}, u32[]{:S(2)}, u32[]{:S(2)}) collective-permute-start(f32[6,1,128]{2,1,0:T(1,128)S(1)} %get-tuple-element.9), channel_id=1, source_target_pairs={{0,1},{1,2},{2,3},{3,4},{4,5},{5,6},{6,7},{8,9},{9,10},{10,11},{11... | collective-permute-start | bytes 9224 | tf_op jit(solution)/shard_map/ppermute | solution.py:18
  97.0 3.2 %collective-permute-done.13 = f32[6,1,128]{2,1,0:T(1,128)S(1)} collective-permute-done((f32[6,1,128]{2,1,0:T(1,128)S(1)}, f32[6,1,128]{2,1,0:T(1,128)S(1)}, u32[]{:S(2)}, u32[]{:S(2)}) %collective-permute-start.13) | collective-permute-done | bytes 3104 | tf_op jit(solution)/shard_map/ppermute | solution.py:20
  100.3 9.8 %reshape.238 = f32[2,2,32,2,64,2]{5,4,3,2,1,0:T(8,128)} reshape(f32[4,64,128]{2,1,0:T(8,128)S(1)} %fusion.41) | data formatting | bytes 262144 | tf_op jit(solution)/shard_map/reshape | solution.py:35
  110.1 4.0 %reduce_sum.167 = f32[2,32,64]{2,1,0:T(8,128)S(1)} reduce(f32[2,2,32,2,64,2]{5,4,3,2,1,0:T(8,128)} %reshape.238, f32[]{:T(128)} %constant.22.clone.1), dimensions={1,3,5}, to_apply=%region_6.0 | reduce | flops 28672 | bytes 147460 | tf_op jit(solution)/shard_map/reduce_sum | solution.py:35
  114.2 3.1 collective-permute-start.14
  119.6 6.0 %collective-permute-done.15 = f32[1,32,64]{2,1,0:T(8,128)S(1)} collective-permute-done((f32[1,32,64]{2,1,0:T(8,128)S(1)}, f32[1,32,64]{2,1,0:T(8,128)S(1)}, u32[]{:S(2)}, u32[]{:S(2)}) %collective-permute-start.15) | collective-permute-done | bytes 8224 | tf_op jit(solution)/shard_map/ppermute | solution.py:20
  125.7 3.8 %collective-permute-start.16 = (f32[4,1,64]{2,1,0:T(1,128)S(1)}, f32[4,1,64]{2,1,0:T(1,128)S(1)}, u32[]{:S(2)}, u32[]{:S(2)}) collective-permute-start(f32[4,1,64]{2,1,0:T(1,128)S(1)} %get-tuple-element.51), channel_id=1, source_target_pairs={{0,1},{1,2},{2,3},{3,4},{4,5},{5,6},{6,7},{8,9},{9,10},{10,11},{11... | collective-permute-start | bytes 3080 | tf_op jit(solution)/shard_map/ppermute | solution.py:18
  130.9 3.0 collective-permute-done.17
  133.9 3.2 %collective-permute-start.18 = (f32[1,32,64]{2,1,0:T(8,128)S(1)}, f32[1,32,64]{2,1,0:T(8,128)S(1)}, u32[]{:S(2)}, u32[]{:S(2)}) collective-permute-start(f32[1,32,64]{2,1,0:T(8,128)S(1)} %get-tuple-element.71), channel_id=1, source_target_pairs={{0,8},{8,16},{16,24},{24,32},{32,40},{40,48},{48,56},{56,64},{64,7... | collective-permute-start | bytes 24584 | tf_op jit(solution)/shard_map/ppermute | solution.py:18
  139.3 6.2 %collective-permute-done.19 = f32[1,32,64]{2,1,0:T(8,128)S(1)} collective-permute-done((f32[1,32,64]{2,1,0:T(8,128)S(1)}, f32[1,32,64]{2,1,0:T(8,128)S(1)}, u32[]{:S(2)}, u32[]{:S(2)}) %collective-permute-start.19) | collective-permute-done | bytes 8224 | tf_op jit(solution)/shard_map/ppermute | solution.py:20
  145.5 3.2 %collective-permute-start.20 = (f32[4,1,64]{2,1,0:T(1,128)S(1)}, f32[4,1,64]{2,1,0:T(1,128)S(1)}, u32[]{:S(2)}, u32[]{:S(2)}) collective-permute-start(f32[4,1,64]{2,1,0:T(1,128)S(1)} %get-tuple-element.49), channel_id=1, source_target_pairs={{0,1},{1,2},{2,3},{3,4},{4,5},{5,6},{6,7},{8,9},{9,10},{10,11},{11... | collective-permute-start | bytes 3080 | tf_op jit(solution)/shard_map/ppermute | solution.py:18
  150.1 3.0 collective-permute-done.21
  153.1 3.4 %collective-permute-start.22 = (f32[1,32,64]{2,1,0:T(8,128)S(1)}, f32[1,32,64]{2,1,0:T(8,128)S(1)}, u32[]{:S(2)}, u32[]{:S(2)}) collective-permute-start(f32[1,32,64]{2,1,0:T(8,128)S(1)} %get-tuple-element.67), channel_id=1, source_target_pairs={{0,8},{8,16},{16,24},{24,32},{32,40},{40,48},{48,56},{56,64},{64,7... | collective-permute-start | bytes 24584 | tf_op jit(solution)/shard_map/ppermute | solution.py:18
  160.6 4.3 %collective-permute-done.23 = f32[1,32,64]{2,1,0:T(8,128)S(1)} collective-permute-done((f32[1,32,64]{2,1,0:T(8,128)S(1)}, f32[1,32,64]{2,1,0:T(8,128)S(1)}, u32[]{:S(2)}, u32[]{:S(2)}) %collective-permute-start.23) | collective-permute-done | bytes 8224 | tf_op jit(solution)/shard_map/ppermute | solution.py:20
  169.1 3.0 collective-permute-done.25
  174.8 7.0 %collective-permute-start.26 = (f32[1,16,32]{2,1,0:T(8,128)S(1)}, f32[1,16,32]{2,1,0:T(8,128)S(1)}, u32[]{:S(2)}, u32[]{:S(2)}) collective-permute-start(f32[1,16,32]{2,1,0:T(8,128)S(1)} %bitcast_multiply_fusion), channel_id=1, source_target_pairs={{0,8},{8,16},{16,24},{24,32},{32,40},{40,48},{48,56},{56,64},{64,7... | collective-permute-start | bytes 6152 | tf_op jit(solution)/shard_map/ppermute | solution.py:18
  186.8 2.9 collective-permute-done.29
  189.8 8.9 %collective-permute-start.30 = (f32[1,16,32]{2,1,0:T(8,128)S(1)}, f32[1,16,32]{2,1,0:T(8,128)S(1)}, u32[]{:S(2)}, u32[]{:S(2)}) collective-permute-start(f32[1,16,32]{2,1,0:T(8,128)S(1)} %fusion.172), channel_id=1, source_target_pairs={{0,8},{8,16},{16,24},{24,32},{32,40},{40,48},{48,56},{56,64},{64,7... | collective-permute-start | bytes 6152 | tf_op jit(solution)/shard_map/ppermute | solution.py:18
  200.7 6.4 %collective-permute-done.31 = f32[1,16,32]{2,1,0:T(8,128)S(1)} collective-permute-done((f32[1,16,32]{2,1,0:T(8,128)S(1)}, f32[1,16,32]{2,1,0:T(8,128)S(1)}, u32[]{:S(2)}, u32[]{:S(2)}) %collective-permute-start.31) | collective-permute-done | bytes 2080 | tf_op jit(solution)/shard_map/ppermute | solution.py:20
  211.3 2.9 collective-permute-done.33
  214.3 3.4 %collective-permute-start.34 = (f32[1,16,32]{2,1,0:T(8,128)S(1)}, f32[1,16,32]{2,1,0:T(8,128)S(1)}, u32[]{:S(2)}, u32[]{:S(2)}) collective-permute-start(f32[1,16,32]{2,1,0:T(8,128)S(1)} %fusion.196), channel_id=1, source_target_pairs={{0,8},{8,16},{16,24},{24,32},{32,40},{40,48},{48,56},{56,64},{64,7... | collective-permute-start | bytes 6152 | tf_op jit(solution)/shard_map/ppermute | solution.py:18
  219.6 6.4 %collective-permute-done.35 = f32[1,16,32]{2,1,0:T(8,128)S(1)} collective-permute-done((f32[1,16,32]{2,1,0:T(8,128)S(1)}, f32[1,16,32]{2,1,0:T(8,128)S(1)}, u32[]{:S(2)}, u32[]{:S(2)}) %collective-permute-start.35) | collective-permute-done | bytes 2080 | tf_op jit(solution)/shard_map/ppermute | solution.py:20
  226.0 3.1 %collective-permute-start.36 = (f32[3,1,32]{2,1,0:T(1,128)S(1)}, f32[3,1,32]{2,1,0:T(1,128)S(1)}, u32[]{:S(2)}, u32[]{:S(2)}) collective-permute-start(f32[3,1,32]{2,1,0:T(1,128)S(1)} %get-tuple-element.77), channel_id=1, source_target_pairs={{0,1},{1,2},{2,3},{3,4},{4,5},{5,6},{6,7},{8,9},{9,10},{10,11},{11... | collective-permute-start | bytes 1160 | tf_op jit(solution)/shard_map/ppermute | solution.py:18
  230.5 2.9 collective-permute-done.37
  233.7 3.4 %collective-permute-start.38 = (f32[1,32,64]{2,1,0:T(8,128)S(1)}, f32[1,32,64]{2,1,0:T(8,128)S(1)}, u32[]{:S(2)}, u32[]{:S(2)}) collective-permute-start(f32[1,32,64]{2,1,0:T(8,128)S(1)} %get-tuple-element.59), channel_id=1, source_target_pairs={{0,8},{8,16},{16,24},{24,32},{32,40},{40,48},{48,56},{56,64},{64,7... | collective-permute-start | bytes 24584 | tf_op jit(solution)/shard_map/ppermute | solution.py:18
  239.0 6.4 %collective-permute-done.39 = f32[1,32,64]{2,1,0:T(8,128)S(1)} collective-permute-done((f32[1,32,64]{2,1,0:T(8,128)S(1)}, f32[1,32,64]{2,1,0:T(8,128)S(1)}, u32[]{:S(2)}, u32[]{:S(2)}) %collective-permute-start.39) | collective-permute-done | bytes 8224 | tf_op jit(solution)/shard_map/ppermute | solution.py:20
  249.7 3.0 collective-permute-done.41
  252.8 3.4 %collective-permute-start.42 = (f32[1,32,64]{2,1,0:T(8,128)S(1)}, f32[1,32,64]{2,1,0:T(8,128)S(1)}, u32[]{:S(2)}, u32[]{:S(2)}) collective-permute-start(f32[1,32,64]{2,1,0:T(8,128)S(1)} %get-tuple-element.55), channel_id=1, source_target_pairs={{0,8},{8,16},{16,24},{24,32},{32,40},{40,48},{48,56},{56,64},{64,7... | collective-permute-start | bytes 24584 | tf_op jit(solution)/shard_map/ppermute | solution.py:18
  258.1 6.4 %collective-permute-done.43 = f32[1,32,64]{2,1,0:T(8,128)S(1)} collective-permute-done((f32[1,32,64]{2,1,0:T(8,128)S(1)}, f32[1,32,64]{2,1,0:T(8,128)S(1)}, u32[]{:S(2)}, u32[]{:S(2)}) %collective-permute-start.43) | collective-permute-done | bytes 8224 | tf_op jit(solution)/shard_map/ppermute | solution.py:20
  268.8 3.0 collective-permute-done.45
  272.3 3.4 %collective-permute-start.46 = (f32[1,64,128]{2,1,0:T(8,128)S(1)}, f32[1,64,128]{2,1,0:T(8,128)S(1)}, u32[]{:S(2)}, u32[]{:S(2)}) collective-permute-start(f32[1,64,128]{2,1,0:T(8,128)S(1)} %get-tuple-element.25), channel_id=1, source_target_pairs={{0,8},{8,16},{16,24},{24,32},{32,40},{40,48},{48,56},{56,64},{64,7... | collective-permute-start | bytes 98312 | tf_op jit(solution)/shard_map/ppermute | solution.py:18
  277.6 6.6 %collective-permute-done.47 = f32[1,64,128]{2,1,0:T(8,128)S(1)} collective-permute-done((f32[1,64,128]{2,1,0:T(8,128)S(1)}, f32[1,64,128]{2,1,0:T(8,128)S(1)}, u32[]{:S(2)}, u32[]{:S(2)}) %collective-permute-start.47) | collective-permute-done | bytes 32800 | tf_op jit(solution)/shard_map/ppermute | solution.py:20
  288.4 2.9 collective-permute-done.49
  291.6 3.3 %collective-permute-start.50 = (f32[1,64,128]{2,1,0:T(8,128)S(1)}, f32[1,64,128]{2,1,0:T(8,128)S(1)}, u32[]{:S(2)}, u32[]{:S(2)}) collective-permute-start(f32[1,64,128]{2,1,0:T(8,128)S(1)} %get-tuple-element.21), channel_id=1, source_target_pairs={{0,8},{8,16},{16,24},{24,32},{32,40},{40,48},{48,56},{56,64},{64,7... | collective-permute-start | bytes 98312 | tf_op jit(solution)/shard_map/ppermute | solution.py:18
  296.9 6.6 %collective-permute-done.51 = f32[1,64,128]{2,1,0:T(8,128)S(1)} collective-permute-done((f32[1,64,128]{2,1,0:T(8,128)S(1)}, f32[1,64,128]{2,1,0:T(8,128)S(1)}, u32[]{:S(2)}, u32[]{:S(2)}) %collective-permute-start.51) | collective-permute-done | bytes 32800 | tf_op jit(solution)/shard_map/ppermute | solution.py:20
  307.8 2.9 collective-permute-done.53
  (182 shorter events, 88.1 us)
Async XLA Ops:
  0.7 22.1 %collective-permute-start.1 = (f32[4,1,128]{2,1,0:T(1,128)S(1)}, f32[4,1,128]{2,1,0:T(1,128)S(1)}, u32[]{:S(2)}, u32[]{:S(2)}) collective-permute-start(f32[4,1,128]{2,1,0:T(1,128)S(1)} %get-tuple-element.42), channel_id=1, source_target_pairs={{1,0},{2,1},{3,2},{4,3},{5,4},{6,5},{7,6},{9,8},{10,9},{11,10},{12... | collective-permute-start | bytes 6152 | tf_op jit(solution)/shard_map/ppermute | solution.py:30
  2.8 21.7 %collective-permute-start = (f32[1,64,128]{2,1,0:T(8,128)S(1)}, f32[1,64,128]{2,1,0:T(8,128)S(1)}, u32[]{:S(2)}, u32[]{:S(2)}) collective-permute-start(f32[1,64,128]{2,1,0:T(8,128)S(1)} %get-tuple-element.40), channel_id=1, source_target_pairs={{8,0},{16,8},{24,16},{32,24},{40,32},{48,40},{56,48},{64,56},{72,6... | collective-permute-start | bytes 98312 | tf_op jit(solution)/shard_map/ppermute | solution.py:30
  24.8 19.4 %collective-permute-start.2 = (f32[1,64,128]{2,1,0:T(8,128)S(1)}, f32[1,64,128]{2,1,0:T(8,128)S(1)}, u32[]{:S(2)}, u32[]{:S(2)}) collective-permute-start(f32[1,64,128]{2,1,0:T(8,128)S(1)} %get-tuple-element.37), channel_id=1, source_target_pairs={{0,8},{8,16},{16,24},{24,32},{32,40},{40,48},{48,56},{56,64},{64,7... | collective-permute-start | bytes 98312 | tf_op jit(solution)/shard_map/ppermute | solution.py:18
  31.1 13.1 %collective-permute-start.3 = (f32[1,64,128]{2,1,0:T(8,128)S(1)}, f32[1,64,128]{2,1,0:T(8,128)S(1)}, u32[]{:S(2)}, u32[]{:S(2)}) collective-permute-start(f32[1,64,128]{2,1,0:T(8,128)S(1)} %get-tuple-element.38), channel_id=1, source_target_pairs={{8,0},{16,8},{24,16},{32,24},{40,32},{48,40},{56,48},{64,56},{72,6... | collective-permute-start | bytes 98312 | tf_op jit(solution)/shard_map/ppermute | solution.py:20
  44.2 5.3 %collective-permute-start.4 = (f32[6,1,128]{2,1,0:T(1,128)S(1)}, f32[6,1,128]{2,1,0:T(1,128)S(1)}, u32[]{:S(2)}, u32[]{:S(2)}) collective-permute-start(f32[6,1,128]{2,1,0:T(1,128)S(1)} %get-tuple-element.13), channel_id=1, source_target_pairs={{0,1},{1,2},{2,3},{3,4},{4,5},{5,6},{6,7},{8,9},{9,10},{10,11},{11... | collective-permute-start | bytes 9224 | tf_op jit(solution)/shard_map/ppermute | solution.py:18
  48.2 4.3 %collective-permute-start.5 = (f32[6,1,128]{2,1,0:T(1,128)S(1)}, f32[6,1,128]{2,1,0:T(1,128)S(1)}, u32[]{:S(2)}, u32[]{:S(2)}) collective-permute-start(f32[6,1,128]{2,1,0:T(1,128)S(1)} %get-tuple-element.14), channel_id=1, source_target_pairs={{1,0},{2,1},{3,2},{4,3},{5,4},{6,5},{7,6},{9,8},{10,9},{11,10},{12... | collective-permute-start | bytes 9224 | tf_op jit(solution)/shard_map/ppermute | solution.py:20
  52.8 12.8 %collective-permute-start.6 = (f32[1,64,128]{2,1,0:T(8,128)S(1)}, f32[1,64,128]{2,1,0:T(8,128)S(1)}, u32[]{:S(2)}, u32[]{:S(2)}) collective-permute-start(f32[1,64,128]{2,1,0:T(8,128)S(1)} %get-tuple-element.33), channel_id=1, source_target_pairs={{0,8},{8,16},{16,24},{24,32},{32,40},{40,48},{48,56},{56,64},{64,7... | collective-permute-start | bytes 98312 | tf_op jit(solution)/shard_map/ppermute | solution.py:18
  61.2 8.6 %collective-permute-start.7 = (f32[1,64,128]{2,1,0:T(8,128)S(1)}, f32[1,64,128]{2,1,0:T(8,128)S(1)}, u32[]{:S(2)}, u32[]{:S(2)}) collective-permute-start(f32[1,64,128]{2,1,0:T(8,128)S(1)} %get-tuple-element.34), channel_id=1, source_target_pairs={{8,0},{16,8},{24,16},{32,24},{40,32},{48,40},{56,48},{64,56},{72,6... | collective-permute-start | bytes 98312 | tf_op jit(solution)/shard_map/ppermute | solution.py:20
  69.7 4.6 %collective-permute-start.8 = (f32[6,1,128]{2,1,0:T(1,128)S(1)}, f32[6,1,128]{2,1,0:T(1,128)S(1)}, u32[]{:S(2)}, u32[]{:S(2)}) collective-permute-start(f32[6,1,128]{2,1,0:T(1,128)S(1)} %get-tuple-element.11), channel_id=1, source_target_pairs={{0,1},{1,2},{2,3},{3,4},{4,5},{5,6},{6,7},{8,9},{9,10},{10,11},{11... | collective-permute-start | bytes 9224 | tf_op jit(solution)/shard_map/ppermute | solution.py:18
  72.9 5.0 %collective-permute-start.9 = (f32[6,1,128]{2,1,0:T(1,128)S(1)}, f32[6,1,128]{2,1,0:T(1,128)S(1)}, u32[]{:S(2)}, u32[]{:S(2)}) collective-permute-start(f32[6,1,128]{2,1,0:T(1,128)S(1)} %get-tuple-element.12), channel_id=1, source_target_pairs={{1,0},{2,1},{3,2},{4,3},{5,4},{6,5},{7,6},{9,8},{10,9},{11,10},{12... | collective-permute-start | bytes 9224 | tf_op jit(solution)/shard_map/ppermute | solution.py:20
  78.1 6.0 %collective-permute-start.10 = (f32[1,64,128]{2,1,0:T(8,128)S(1)}, f32[1,64,128]{2,1,0:T(8,128)S(1)}, u32[]{:S(2)}, u32[]{:S(2)}) collective-permute-start(f32[1,64,128]{2,1,0:T(8,128)S(1)} %get-tuple-element.29), channel_id=1, source_target_pairs={{0,8},{8,16},{16,24},{24,32},{32,40},{40,48},{48,56},{56,64},{64,7... | collective-permute-start | bytes 98312 | tf_op jit(solution)/shard_map/ppermute | solution.py:18
  82.1 8.6 %collective-permute-start.11 = (f32[1,64,128]{2,1,0:T(8,128)S(1)}, f32[1,64,128]{2,1,0:T(8,128)S(1)}, u32[]{:S(2)}, u32[]{:S(2)}) collective-permute-start(f32[1,64,128]{2,1,0:T(8,128)S(1)} %get-tuple-element.30), channel_id=1, source_target_pairs={{8,0},{16,8},{24,16},{32,24},{40,32},{48,40},{56,48},{64,56},{72,6... | collective-permute-start | bytes 98312 | tf_op jit(solution)/shard_map/ppermute | solution.py:20
  90.7 6.2 %collective-permute-start.12 = (f32[6,1,128]{2,1,0:T(1,128)S(1)}, f32[6,1,128]{2,1,0:T(1,128)S(1)}, u32[]{:S(2)}, u32[]{:S(2)}) collective-permute-start(f32[6,1,128]{2,1,0:T(1,128)S(1)} %get-tuple-element.9), channel_id=1, source_target_pairs={{0,1},{1,2},{2,3},{3,4},{4,5},{5,6},{6,7},{8,9},{9,10},{10,11},{11... | collective-permute-start | bytes 9224 | tf_op jit(solution)/shard_map/ppermute | solution.py:18
  95.5 4.6 %collective-permute-start.13 = (f32[6,1,128]{2,1,0:T(1,128)S(1)}, f32[6,1,128]{2,1,0:T(1,128)S(1)}, u32[]{:S(2)}, u32[]{:S(2)}) collective-permute-start(f32[6,1,128]{2,1,0:T(1,128)S(1)} %get-tuple-element.10), channel_id=1, source_target_pairs={{1,0},{2,1},{3,2},{4,3},{5,4},{6,5},{7,6},{9,8},{10,9},{11,10},{12... | collective-permute-start | bytes 9224 | tf_op jit(solution)/shard_map/ppermute | solution.py:20
  114.2 5.4 %collective-permute-start.14 = (f32[1,32,64]{2,1,0:T(8,128)S(1)}, f32[1,32,64]{2,1,0:T(8,128)S(1)}, u32[]{:S(2)}, u32[]{:S(2)}) collective-permute-start(f32[1,32,64]{2,1,0:T(8,128)S(1)} %get-tuple-element.75), channel_id=1, source_target_pairs={{0,8},{8,16},{16,24},{24,32},{32,40},{40,48},{48,56},{56,64},{64,7... | collective-permute-start | bytes 24584 | tf_op jit(solution)/shard_map/ppermute | solution.py:18
  117.3 8.4 %collective-permute-start.15 = (f32[1,32,64]{2,1,0:T(8,128)S(1)}, f32[1,32,64]{2,1,0:T(8,128)S(1)}, u32[]{:S(2)}, u32[]{:S(2)}) collective-permute-start(f32[1,32,64]{2,1,0:T(8,128)S(1)} %get-tuple-element.76), channel_id=1, source_target_pairs={{8,0},{16,8},{24,16},{32,24},{40,32},{48,40},{56,48},{64,56},{72,6... | collective-permute-start | bytes 24584 | tf_op jit(solution)/shard_map/ppermute | solution.py:20
  125.7 5.2 %collective-permute-start.16 = (f32[4,1,64]{2,1,0:T(1,128)S(1)}, f32[4,1,64]{2,1,0:T(1,128)S(1)}, u32[]{:S(2)}, u32[]{:S(2)}) collective-permute-start(f32[4,1,64]{2,1,0:T(1,128)S(1)} %get-tuple-element.51), channel_id=1, source_target_pairs={{0,1},{1,2},{2,3},{3,4},{4,5},{5,6},{6,7},{8,9},{9,10},{10,11},{11... | collective-permute-start | bytes 3080 | tf_op jit(solution)/shard_map/ppermute | solution.py:18
  129.5 4.3 %collective-permute-start.17 = (f32[4,1,64]{2,1,0:T(1,128)S(1)}, f32[4,1,64]{2,1,0:T(1,128)S(1)}, u32[]{:S(2)}, u32[]{:S(2)}) collective-permute-start(f32[4,1,64]{2,1,0:T(1,128)S(1)} %get-tuple-element.52), channel_id=1, source_target_pairs={{1,0},{2,1},{3,2},{4,3},{5,4},{6,5},{7,6},{9,8},{10,9},{11,10},{12... | collective-permute-start | bytes 3080 | tf_op jit(solution)/shard_map/ppermute | solution.py:20
  133.9 5.4 %collective-permute-start.18 = (f32[1,32,64]{2,1,0:T(8,128)S(1)}, f32[1,32,64]{2,1,0:T(8,128)S(1)}, u32[]{:S(2)}, u32[]{:S(2)}) collective-permute-start(f32[1,32,64]{2,1,0:T(8,128)S(1)} %get-tuple-element.71), channel_id=1, source_target_pairs={{0,8},{8,16},{16,24},{24,32},{32,40},{40,48},{48,56},{56,64},{64,7... | collective-permute-start | bytes 24584 | tf_op jit(solution)/shard_map/ppermute | solution.py:18
  137.1 8.4 %collective-permute-start.19 = (f32[1,32,64]{2,1,0:T(8,128)S(1)}, f32[1,32,64]{2,1,0:T(8,128)S(1)}, u32[]{:S(2)}, u32[]{:S(2)}) collective-permute-start(f32[1,32,64]{2,1,0:T(8,128)S(1)} %get-tuple-element.72), channel_id=1, source_target_pairs={{8,0},{16,8},{24,16},{32,24},{40,32},{48,40},{56,48},{64,56},{72,6... | collective-permute-start | bytes 24584 | tf_op jit(solution)/shard_map/ppermute | solution.py:20
  145.5 4.6 %collective-permute-start.20 = (f32[4,1,64]{2,1,0:T(1,128)S(1)}, f32[4,1,64]{2,1,0:T(1,128)S(1)}, u32[]{:S(2)}, u32[]{:S(2)}) collective-permute-start(f32[4,1,64]{2,1,0:T(1,128)S(1)} %get-tuple-element.49), channel_id=1, source_target_pairs={{0,1},{1,2},{2,3},{3,4},{4,5},{5,6},{6,7},{8,9},{9,10},{10,11},{11... | collective-permute-start | bytes 3080 | tf_op jit(solution)/shard_map/ppermute | solution.py:18
  148.7 4.3 %collective-permute-start.21 = (f32[4,1,64]{2,1,0:T(1,128)S(1)}, f32[4,1,64]{2,1,0:T(1,128)S(1)}, u32[]{:S(2)}, u32[]{:S(2)}) collective-permute-start(f32[4,1,64]{2,1,0:T(1,128)S(1)} %get-tuple-element.50), channel_id=1, source_target_pairs={{1,0},{2,1},{3,2},{4,3},{5,4},{6,5},{7,6},{9,8},{10,9},{11,10},{12... | collective-permute-start | bytes 3080 | tf_op jit(solution)/shard_map/ppermute | solution.py:20
  153.1 7.5 %collective-permute-start.22 = (f32[1,32,64]{2,1,0:T(8,128)S(1)}, f32[1,32,64]{2,1,0:T(8,128)S(1)}, u32[]{:S(2)}, u32[]{:S(2)}) collective-permute-start(f32[1,32,64]{2,1,0:T(8,128)S(1)} %get-tuple-element.67), channel_id=1, source_target_pairs={{0,8},{8,16},{16,24},{24,32},{32,40},{40,48},{48,56},{56,64},{64,7... | collective-permute-start | bytes 24584 | tf_op jit(solution)/shard_map/ppermute | solution.py:18
  156.5 8.4 %collective-permute-start.23 = (f32[1,32,64]{2,1,0:T(8,128)S(1)}, f32[1,32,64]{2,1,0:T(8,128)S(1)}, u32[]{:S(2)}, u32[]{:S(2)}) collective-permute-start(f32[1,32,64]{2,1,0:T(8,128)S(1)} %get-tuple-element.68), channel_id=1, source_target_pairs={{8,0},{16,8},{24,16},{32,24},{40,32},{48,40},{56,48},{64,56},{72,6... | collective-permute-start | bytes 24584 | tf_op jit(solution)/shard_map/ppermute | solution.py:20
  167.7 4.3 %collective-permute-start.25 = (f32[4,1,64]{2,1,0:T(1,128)S(1)}, f32[4,1,64]{2,1,0:T(1,128)S(1)}, u32[]{:S(2)}, u32[]{:S(2)}) collective-permute-start(f32[4,1,64]{2,1,0:T(1,128)S(1)} %get-tuple-element.48), channel_id=1, source_target_pairs={{1,0},{2,1},{3,2},{4,3},{5,4},{6,5},{7,6},{9,8},{10,9},{11,10},{12... | collective-permute-start | bytes 3080 | tf_op jit(solution)/shard_map/ppermute | solution.py:20
  172.9 8.9 %collective-permute-start.27 = (f32[1,16,32]{2,1,0:T(8,128)S(1)}, f32[1,16,32]{2,1,0:T(8,128)S(1)}, u32[]{:S(2)}, u32[]{:S(2)}) collective-permute-start(f32[1,16,32]{2,1,0:T(8,128)S(1)} %bitcast_multiply_fusion), channel_id=1, source_target_pairs={{8,0},{16,8},{24,16},{32,24},{40,32},{48,40},{56,48},{64,56},{72,6... | collective-permute-start | bytes 6152 | tf_op jit(solution)/shard_map/ppermute | solution.py:20
  174.8 7.7 %collective-permute-start.26 = (f32[1,16,32]{2,1,0:T(8,128)S(1)}, f32[1,16,32]{2,1,0:T(8,128)S(1)}, u32[]{:S(2)}, u32[]{:S(2)}) collective-permute-start(f32[1,16,32]{2,1,0:T(8,128)S(1)} %bitcast_multiply_fusion), channel_id=1, source_target_pairs={{0,8},{8,16},{16,24},{24,32},{32,40},{40,48},{48,56},{56,64},{64,7... | collective-permute-start | bytes 6152 | tf_op jit(solution)/shard_map/ppermute | solution.py:18
  185.4 4.3 %collective-permute-start.29 = (f32[3,1,32]{2,1,0:T(1,128)S(1)}, f32[3,1,32]{2,1,0:T(1,128)S(1)}, u32[]{:S(2)}, u32[]{:S(2)}) collective-permute-start(f32[3,1,32]{2,1,0:T(1,128)S(1)} %get-tuple-element.82), channel_id=1, source_target_pairs={{1,0},{2,1},{3,2},{4,3},{5,4},{6,5},{7,6},{9,8},{10,9},{11,10},{12... | collective-permute-start | bytes 1160 | tf_op jit(solution)/shard_map/ppermute | solution.py:20
  189.8 10.9 %collective-permute-start.30 = (f32[1,16,32]{2,1,0:T(8,128)S(1)}, f32[1,16,32]{2,1,0:T(8,128)S(1)}, u32[]{:S(2)}, u32[]{:S(2)}) collective-permute-start(f32[1,16,32]{2,1,0:T(8,128)S(1)} %fusion.172), channel_id=1, source_target_pairs={{0,8},{8,16},{16,24},{24,32},{32,40},{40,48},{48,56},{56,64},{64,7... | collective-permute-start | bytes 6152 | tf_op jit(solution)/shard_map/ppermute | solution.py:18
  198.7 8.3 %collective-permute-start.31 = (f32[1,16,32]{2,1,0:T(8,128)S(1)}, f32[1,16,32]{2,1,0:T(8,128)S(1)}, u32[]{:S(2)}, u32[]{:S(2)}) collective-permute-start(f32[1,16,32]{2,1,0:T(8,128)S(1)} %fusion.172), channel_id=1, source_target_pairs={{8,0},{16,8},{24,16},{32,24},{40,32},{48,40},{56,48},{64,56},{72,6... | collective-permute-start | bytes 6152 | tf_op jit(solution)/shard_map/ppermute | solution.py:20
  209.9 4.3 %collective-permute-start.33 = (f32[3,1,32]{2,1,0:T(1,128)S(1)}, f32[3,1,32]{2,1,0:T(1,128)S(1)}, u32[]{:S(2)}, u32[]{:S(2)}) collective-permute-start(f32[3,1,32]{2,1,0:T(1,128)S(1)} %get-tuple-element.80), channel_id=1, source_target_pairs={{1,0},{2,1},{3,2},{4,3},{5,4},{6,5},{7,6},{9,8},{10,9},{11,10},{12... | collective-permute-start | bytes 1160 | tf_op jit(solution)/shard_map/ppermute | solution.py:20
  214.3 5.3 %collective-permute-start.34 = (f32[1,16,32]{2,1,0:T(8,128)S(1)}, f32[1,16,32]{2,1,0:T(8,128)S(1)}, u32[]{:S(2)}, u32[]{:S(2)}) collective-permute-start(f32[1,16,32]{2,1,0:T(8,128)S(1)} %fusion.196), channel_id=1, source_target_pairs={{0,8},{8,16},{16,24},{24,32},{32,40},{40,48},{48,56},{56,64},{64,7... | collective-permute-start | bytes 6152 | tf_op jit(solution)/shard_map/ppermute | solution.py:18
  217.7 8.3 %collective-permute-start.35 = (f32[1,16,32]{2,1,0:T(8,128)S(1)}, f32[1,16,32]{2,1,0:T(8,128)S(1)}, u32[]{:S(2)}, u32[]{:S(2)}) collective-permute-start(f32[1,16,32]{2,1,0:T(8,128)S(1)} %fusion.196), channel_id=1, source_target_pairs={{8,0},{16,8},{24,16},{32,24},{40,32},{48,40},{56,48},{64,56},{72,6... | collective-permute-start | bytes 6152 | tf_op jit(solution)/shard_map/ppermute | solution.py:20
  226.0 4.5 %collective-permute-start.36 = (f32[3,1,32]{2,1,0:T(1,128)S(1)}, f32[3,1,32]{2,1,0:T(1,128)S(1)}, u32[]{:S(2)}, u32[]{:S(2)}) collective-permute-start(f32[3,1,32]{2,1,0:T(1,128)S(1)} %get-tuple-element.77), channel_id=1, source_target_pairs={{0,1},{1,2},{2,3},{3,4},{4,5},{5,6},{6,7},{8,9},{9,10},{10,11},{11... | collective-permute-start | bytes 1160 | tf_op jit(solution)/shard_map/ppermute | solution.py:18
  229.1 4.3 %collective-permute-start.37 = (f32[3,1,32]{2,1,0:T(1,128)S(1)}, f32[3,1,32]{2,1,0:T(1,128)S(1)}, u32[]{:S(2)}, u32[]{:S(2)}) collective-permute-start(f32[3,1,32]{2,1,0:T(1,128)S(1)} %get-tuple-element.78), channel_id=1, source_target_pairs={{1,0},{2,1},{3,2},{4,3},{5,4},{6,5},{7,6},{9,8},{10,9},{11,10},{12... | collective-permute-start | bytes 1160 | tf_op jit(solution)/shard_map/ppermute | solution.py:20
  233.7 5.3 %collective-permute-start.38 = (f32[1,32,64]{2,1,0:T(8,128)S(1)}, f32[1,32,64]{2,1,0:T(8,128)S(1)}, u32[]{:S(2)}, u32[]{:S(2)}) collective-permute-start(f32[1,32,64]{2,1,0:T(8,128)S(1)} %get-tuple-element.59), channel_id=1, source_target_pairs={{0,8},{8,16},{16,24},{24,32},{32,40},{40,48},{48,56},{56,64},{64,7... | collective-permute-start | bytes 24584 | tf_op jit(solution)/shard_map/ppermute | solution.py:18
  237.1 8.4 %collective-permute-start.39 = (f32[1,32,64]{2,1,0:T(8,128)S(1)}, f32[1,32,64]{2,1,0:T(8,128)S(1)}, u32[]{:S(2)}, u32[]{:S(2)}) collective-permute-start(f32[1,32,64]{2,1,0:T(8,128)S(1)} %get-tuple-element.60), channel_id=1, source_target_pairs={{8,0},{16,8},{24,16},{32,24},{40,32},{48,40},{56,48},{64,56},{72,6... | collective-permute-start | bytes 24584 | tf_op jit(solution)/shard_map/ppermute | solution.py:20
  245.5 4.3 %collective-permute-start.40 = (f32[4,1,64]{2,1,0:T(1,128)S(1)}, f32[4,1,64]{2,1,0:T(1,128)S(1)}, u32[]{:S(2)}, u32[]{:S(2)}) collective-permute-start(f32[4,1,64]{2,1,0:T(1,128)S(1)} %get-tuple-element.45), channel_id=1, source_target_pairs={{0,1},{1,2},{2,3},{3,4},{4,5},{5,6},{6,7},{8,9},{9,10},{10,11},{11... | collective-permute-start | bytes 3080 | tf_op jit(solution)/shard_map/ppermute | solution.py:18
  248.4 4.3 %collective-permute-start.41 = (f32[4,1,64]{2,1,0:T(1,128)S(1)}, f32[4,1,64]{2,1,0:T(1,128)S(1)}, u32[]{:S(2)}, u32[]{:S(2)}) collective-permute-start(f32[4,1,64]{2,1,0:T(1,128)S(1)} %get-tuple-element.46), channel_id=1, source_target_pairs={{1,0},{2,1},{3,2},{4,3},{5,4},{6,5},{7,6},{9,8},{10,9},{11,10},{12... | collective-permute-start | bytes 3080 | tf_op jit(solution)/shard_map/ppermute | solution.py:20
  252.8 5.3 %collective-permute-start.42 = (f32[1,32,64]{2,1,0:T(8,128)S(1)}, f32[1,32,64]{2,1,0:T(8,128)S(1)}, u32[]{:S(2)}, u32[]{:S(2)}) collective-permute-start(f32[1,32,64]{2,1,0:T(8,128)S(1)} %get-tuple-element.55), channel_id=1, source_target_pairs={{0,8},{8,16},{16,24},{24,32},{32,40},{40,48},{48,56},{56,64},{64,7... | collective-permute-start | bytes 24584 | tf_op jit(solution)/shard_map/ppermute | solution.py:18
  256.2 8.4 %collective-permute-start.43 = (f32[1,32,64]{2,1,0:T(8,128)S(1)}, f32[1,32,64]{2,1,0:T(8,128)S(1)}, u32[]{:S(2)}, u32[]{:S(2)}) collective-permute-start(f32[1,32,64]{2,1,0:T(8,128)S(1)} %get-tuple-element.56), channel_id=1, source_target_pairs={{8,0},{16,8},{24,16},{32,24},{40,32},{48,40},{56,48},{64,56},{72,6... | collective-permute-start | bytes 24584 | tf_op jit(solution)/shard_map/ppermute | solution.py:20
  267.4 4.3 %collective-permute-start.45 = (f32[4,1,64]{2,1,0:T(1,128)S(1)}, f32[4,1,64]{2,1,0:T(1,128)S(1)}, u32[]{:S(2)}, u32[]{:S(2)}) collective-permute-start(f32[4,1,64]{2,1,0:T(1,128)S(1)} %get-tuple-element.44), channel_id=1, source_target_pairs={{1,0},{2,1},{3,2},{4,3},{5,4},{6,5},{7,6},{9,8},{10,9},{11,10},{12... | collective-permute-start | bytes 3080 | tf_op jit(solution)/shard_map/ppermute | solution.py:20
  272.3 5.3 %collective-permute-start.46 = (f32[1,64,128]{2,1,0:T(8,128)S(1)}, f32[1,64,128]{2,1,0:T(8,128)S(1)}, u32[]{:S(2)}, u32[]{:S(2)}) collective-permute-start(f32[1,64,128]{2,1,0:T(8,128)S(1)} %get-tuple-element.25), channel_id=1, source_target_pairs={{0,8},{8,16},{16,24},{24,32},{32,40},{40,48},{48,56},{56,64},{64,7... | collective-permute-start | bytes 98312 | tf_op jit(solution)/shard_map/ppermute | solution.py:18
  275.6 8.6 %collective-permute-start.47 = (f32[1,64,128]{2,1,0:T(8,128)S(1)}, f32[1,64,128]{2,1,0:T(8,128)S(1)}, u32[]{:S(2)}, u32[]{:S(2)}) collective-permute-start(f32[1,64,128]{2,1,0:T(8,128)S(1)} %get-tuple-element.26), channel_id=1, source_target_pairs={{8,0},{16,8},{24,16},{32,24},{40,32},{48,40},{56,48},{64,56},{72,6... | collective-permute-start | bytes 98312 | tf_op jit(solution)/shard_map/ppermute | solution.py:20
  287.0 4.3 %collective-permute-start.49 = (f32[6,1,128]{2,1,0:T(1,128)S(1)}, f32[6,1,128]{2,1,0:T(1,128)S(1)}, u32[]{:S(2)}, u32[]{:S(2)}) collective-permute-start(f32[6,1,128]{2,1,0:T(1,128)S(1)} %get-tuple-element.8), channel_id=1, source_target_pairs={{1,0},{2,1},{3,2},{4,3},{5,4},{6,5},{7,6},{9,8},{10,9},{11,10},{12... | collective-permute-start | bytes 9224 | tf_op jit(solution)/shard_map/ppermute | solution.py:20
  291.6 5.3 %collective-permute-start.50 = (f32[1,64,128]{2,1,0:T(8,128)S(1)}, f32[1,64,128]{2,1,0:T(8,128)S(1)}, u32[]{:S(2)}, u32[]{:S(2)}) collective-permute-start(f32[1,64,128]{2,1,0:T(8,128)S(1)} %get-tuple-element.21), channel_id=1, source_target_pairs={{0,8},{8,16},{16,24},{24,32},{32,40},{40,48},{48,56},{56,64},{64,7... | collective-permute-start | bytes 98312 | tf_op jit(solution)/shard_map/ppermute | solution.py:18
  294.9 8.6 %collective-permute-start.51 = (f32[1,64,128]{2,1,0:T(8,128)S(1)}, f32[1,64,128]{2,1,0:T(8,128)S(1)}, u32[]{:S(2)}, u32[]{:S(2)}) collective-permute-start(f32[1,64,128]{2,1,0:T(8,128)S(1)} %get-tuple-element.22), channel_id=1, source_target_pairs={{8,0},{16,8},{24,16},{32,24},{40,32},{48,40},{56,48},{64,56},{72,6... | collective-permute-start | bytes 98312 | tf_op jit(solution)/shard_map/ppermute | solution.py:20
  306.4 4.3 %collective-permute-start.53 = (f32[6,1,128]{2,1,0:T(1,128)S(1)}, f32[6,1,128]{2,1,0:T(1,128)S(1)}, u32[]{:S(2)}, u32[]{:S(2)}) collective-permute-start(f32[6,1,128]{2,1,0:T(1,128)S(1)} %get-tuple-element.6), channel_id=1, source_target_pairs={{1,0},{2,1},{3,2},{4,3},{5,4},{6,5},{7,6},{9,8},{10,9},{11,10},{12... | collective-permute-start | bytes 9224 | tf_op jit(solution)/shard_map/ppermute | solution.py:20
  (8 other events, 58.1 us)
where the time goes:
time: 313 us; the launch traced here: 312 us
  starting transfers between devices  149 us (48%)
  waiting for transfers between devices  106 us (34%)
  local copies, waits for them, and re-layouts  38.4 us (12%)
  other arithmetic  17.3 us (6%)
    ppermute x26, waiting for transfers between devices, extended(): lax.ppermute(head, axis, [((i + 1) % count, i) for i in range(ends)])  105 us
    ppermute x26, starting transfers between devices, extended(): lax.ppermute(tail, axis, [(i, (i + 1) % count) for i in range(ends)])  103 us
    ppermute x26, starting transfers between devices, extended(): lax.ppermute(head, axis, [((i + 1) % count, i) for i in range(ends)])  41.8 us
    reshape x2, local copies, waits for them, and re-layouts, average_cells(): return values.reshape(a // 2, 2, b // 2, 2, c // 2, 2).mean(axis=(1, 3, 5))  20.4 us
    reduce_sum x6, other arithmetic, average_cells(): return values.reshape(a // 2, 2, b // 2, 2, c // 2, 2).mean(axis=(1, 3, 5))  8.44 us
    reshape x3, local copies, waits for them, and re-layouts, average_yz(): return values.reshape(a, b // 2, 2, c // 2, 2).mean(axis=(2, 4))  8.15 us
  transfers between devices with their start and end apart: 54, of which 25 were waited for; matrix products, arithmetic and copies ran while one was open for 12% of the time, Pallas kernels for 0%

commit v1 on v0

v1 whole, which is shorter than its diff:
```python
import functools

import jax
import jax.numpy as jnp
from jax import lax
from jax.experimental import pallas as pl
from jax.experimental.pallas import tpu as pltpu
from jax.sharding import PartitionSpec as P

F32 = jnp.float32
THETA = (2.0 + 0.25) / 2.0
DELTA = (2.0 - 0.25) / 2.0
SIGMA = THETA / DELTA
RHO = [1.0 / SIGMA]
for _step in range(3):
    RHO.append(1.0 / (2.0 * SIGMA - RHO[-1]))
MOMENTUM = [0.0] + [RHO[k] * RHO[k - 1] for k in range(1, 4)]
GAIN = [1.0 / THETA] + [2.0 * RHO[k] / DELTA for k in range(1, 4)]

PX, PY, PZ = 4, 64, 128
HY = 32
EY = PY + 2 * HY
PAD = 8
B, ALPHA, BX, BY, BZ = range(5)
ANY = pl.BlockSpec(memory_space=pl.ANY)
VMEM = pl.BlockSpec(memory_space=pltpu.VMEM)


def shape(*dims):
    return jax.ShapeDtypeStruct(dims, F32)


def params(mib=40):
    return pltpu.CompilerParams(vmem_limit_bytes=mib * 1024 * 1024)


def parity():
    return lax.rem(lax.axis_index("wide"), 2)


def lanes(rows):
    return lax.broadcasted_iota(jnp.int32, (rows, PZ), 1)


def moved(v, shift):
    return pltpu.roll(v, shift % PZ, 1)


def defect(x_ref, w_ref, q, wq, r0, n, reach):
    rows = pl.ds(PAD + r0, n)
    here = pl.ds(r0, n)
    x = x_ref[q, rows, :]
    total = w_ref[6, wq, here, :] - x
    total += w_ref[0, wq, here, :] * x_ref[q - 1, rows, :]
    total += w_ref[1, wq, here, :] * x_ref[q + 1, rows, :]
    total += w_ref[2, wq, here, :] * x_ref[q, pl.ds(PAD + r0 - 1, n), :]
    total += w_ref[3, wq, here, :] * x_ref[q, pl.ds(PAD + r0 + 1, n), :]
    total += w_ref[4, wq, here, :] * moved(x, reach)
    total += w_ref[5, wq, here, :] * moved(x, -reach)
    return x, total


def sweep(x_ref, prev_ref, w_ref, lo, hi, rows, reach, k, store, chunk, woff=0):
    def body(q, carry):
        for r0 in range(rows[0], rows[1], chunk):
            n = min(chunk, rows[1] - r0)
            x, z = defect(x_ref, w_ref, q, q + woff, r0, n, reach)
            new = x + GAIN[k] * z
            if k > 0:
                gap = x if prev_ref is None else x - prev_ref[q, pl.ds(PAD + r0, n), :]
                new += MOMENTUM[k] * gap
            store(q, r0, n, new)
        return carry

    lax.fori_loop(lo, hi, body, 0)


def into(ref):
    def store(q, r0, n, v):
        ref[q, pl.ds(PAD + r0, n), :] = v

    return store


def scaled(raw, b, x_ref, w_ref, lo, hi, rows, reach, scale, chunk, woff=0, d_ref=None, doff=0):
    alpha, bxl, byl, bzl = raw

    def body(q, carry):
        for r0 in range(0, rows, chunk):
            n = min(chunk, rows - r0)
            here = pl.ds(r0, n)
            x0, x1 = bxl(q, r0, n), bxl(q + 1, r0, n)
            y0, y1 = byl(q, r0, n), byl(q, r0 + 1, n)
            z0 = bzl(q, r0, n)
            z1 = moved(z0, -reach)
            d = alpha(q, r0, n) + scale * (x0 + x1 + y0 + y1 + z0 + z1)
            inside = d > 0.0
            inv = jnp.where(inside, 1.0 / jnp.where(inside, d, 1.0), 0.0)
            si = scale * inv
            wq = q + woff
            for a, f in enumerate((x0, x1, y0, y1, z0, z1)):
                w_ref[a, wq, here, :] = si * f
            c0 = inv * b(q, r0, n)
            w_ref[6, wq, here, :] = c0
            x_ref[q, pl.ds(PAD + r0, n), :] = c0 * (1.0 / THETA)
            if d_ref is not None:
                d_ref[q + doff, here, :] = d
        return carry

    lax.fori_loop(lo, hi, body, 0)


def clear_pads(ref, rows):
    ref[:, :PAD, :] = jnp.zeros((ref.shape[0], PAD, PZ), F32)
    ref[:, PAD + rows :, :] = jnp.zeros((ref.shape[0], PAD, PZ), F32)


def pair_lanes(v, reach):
    low = (lanes(v.shape[0]) & reach) == 0
    return v + jnp.where(low, moved(v, -reach), moved(v, reach))


def low_lanes(v, reach):
    low = (lanes(v.shape[0]) & reach) == 0
    return jnp.where(low, v, moved(v, reach))


def pair_rows(t_ref, rows):
    return t_ref[pl.ds(0, rows, 2), :] + t_ref[pl.ds(1, rows, 2), :]


def pack2(v0, v1):
    return jnp.where((lanes(v0.shape[0]) & 1) == 0, v0, v1)


def unpack2(v):
    even = (lanes(v.shape[0]) & 1) == 0
    return jnp.where(even, v, moved(v, 1)), jnp.where(even, moved(v, -1), v)


def pack4(items):
    place = lanes(items[0].shape[0]) & 3
    out = items[0]
    for i, item in enumerate(items[1:], 1):
        out = jnp.where(place == i, item, out)
    return out


def unpack4(v, i):
    place = lanes(v.shape[0]) & 3
    out = v
    for m in range(4):
        if m != i:
            out = jnp.where(place == m, moved(v, m - i), out)
    return out


def pack_kernel(b, al, bx, by, bz, a_out, lo_out, hi_out, xs_out):
    wide, narrow = lax.axis_index("wide"), lax.axis_index("narrow")
    par = lax.rem(wide, 2)
    row = lax.broadcasted_iota(jnp.int32, (PY, PZ), 0)
    first_row = jnp.logical_and(row == 0, jnp.broadcast_to(narrow, (PY, PZ)) == 0)
    first_x = jnp.broadcast_to(wide, (PY, PZ)) == 0
    first_z = lanes(PY) == 0
    for p in range(PX):
        vx = bx[p]
        if p == 0:
            vx = jnp.where(first_x, 0.0, vx)
        vy = jnp.where(first_row, 0.0, by[p])
        vz = jnp.where(first_z, 0.0, bz[p])
        for i, v in enumerate((b[p], al[p], vx, vy, vz)):
            a_out[i, p] = v
            lo_out[i, p] = v[:HY]
            hi_out[i, p] = v[PY - HY :]
            if p < 3:

                @pl.when(par == 0)
                def _():
                    xs_out[3 * i + p] = v

            if p > 0:

                @pl.when(par == 1)
                def _():
                    xs_out[3 * i + p - 1] = v

        if p == 3:
            xs_out[15] = vx


def corner_kernel(lo, hi, sw_out, xs_out):
    par = parity()
    for i in range(5):
        for p in range(PX):
            sw_out[i, p, :HY] = lo[i, p]
            sw_out[i, p, HY:] = hi[i, p]
            if p < 3:
                xs_out[3 * i + p, :HY] = lo[i, par + p]
                xs_out[3 * i + p, HY:] = hi[i, par + p]
    xs_out[15, :HY] = lo[BX, 3]
    xs_out[15, HY:] = hi[BX, 3]


def coarse_kernel(a, lo, hi, out, t):
    def line(i, planes):
        for ref, r0, n in ((lo, 0, HY), (a, HY, PY), (hi, HY + PY, HY)):
            v = ref[i, planes[0]]
            if len(planes) > 1:
                v = v + ref[i, planes[1]]
            t[pl.ds(r0, n), :] = v

    half = EY // 2
    got = []
    for c in range(2):
        both = (2 * c, 2 * c + 1)
        line(ALPHA, both)
        al = pair_lanes(pair_rows(t, half), 1) * 0.125
        line(BX, both[:1])
        bx = pair_lanes(pair_rows(t, half), 1) * 0.25
        line(BY, both)
        by = pair_lanes(t[pl.ds(0, half, 2), :], 1) * 0.25
        line(BZ, both)
        bz = low_lanes(pair_rows(t, half), 1) * 0.25
        got.append((al, bx, by, bz))
    for i in range(4):
        out[i] = pack2(got[0][i], got[1][i])


Q0 = 3


def fine_kernel(a, lo, hi, sw, xs, csw, cxs, send, xsend, pre, w_out, s, w, d, x, y, t, sems, out_sem):
    par = parity()
    copies = []

    def copy(src, dst):
        c = pltpu.make_async_copy(src, dst, sems.at[len(copies)])
        c.start()
        copies.append(c)

    own = pl.ds(PAD + HY, PY)
    low = pl.ds(PAD, HY)
    high = pl.ds(PAD + HY + PY, HY)
    block = pl.ds(Q0, PX)
    near = 7 * (1 - par)
    far = 7 * par
    extra = pl.ds(10 + par, 1)
    other = pl.ds(11 - par, 1)
    copy(a, s.at[:, block, own])
    copy(lo, s.at[:, block, low])
    copy(hi, s.at[:, block, high])
    copy(sw.at[:, pl.ds(par, 3)], s.at[:, pl.ds(near, 3), own])
    copy(sw.at[BX, pl.ds(3, 1)], s.at[BX, extra, own])
    copy(csw.at[:, pl.ds(par, 3), pl.ds(0, HY)], s.at[:, pl.ds(near, 3), low])
    copy(csw.at[:, pl.ds(par, 3), pl.ds(HY, HY)], s.at[:, pl.ds(near, 3), high])
    copy(csw.at[BX, pl.ds(3, 1), pl.ds(0, HY)], s.at[BX, extra, low])
    copy(csw.at[BX, pl.ds(3, 1), pl.ds(HY, HY)], s.at[BX, extra, high])
    for i in range(5):
        three = pl.ds(3 * i, 3)
        copy(xs.at[three], s.at[i, pl.ds(far, 3), own])
        copy(cxs.at[three, pl.ds(0, HY)], s.at[i, pl.ds(far, 3), low])
        copy(cxs.at[three, pl.ds(HY, HY)], s.at[i, pl.ds(far, 3), high])
    last = pl.ds(15, 1)
    copy(xs.at[last], s.at[BX, other, own])
    copy(cxs.at[last, pl.ds(0, HY)], s.at[BX, other, low])
    copy(cxs.at[last, pl.ds(HY, HY)], s.at[BX, other, high])
    for i in range(5):
        s[i, :, :PAD, :] = jnp.zeros((12, PAD, PZ), F32)
        s[i, :, PAD + EY :, :] = jnp.zeros((12, PAD, PZ), F32)
    clear_pads(x, EY)
    clear_pads(y, EY)
    for c in copies:
        c.wait()

    def raw(i):
        return lambda q, r0, n: s[i, q, pl.ds(PAD + r0, n), :]

    chunk = 32
    scaled((raw(ALPHA), raw(BX), raw(BY), raw(BZ)), raw(B), x, w, 0, 10, EY, 1, 1.0, chunk, d_ref=d)
    keep = pltpu.make_async_copy(w.at[:, pl.ds(2, 6), pl.ds(HY - 8, PY + 16)], w_out, out_sem)
    keep.start()
    rows = (0, EY)
    sweep(x, None, w, 1, 9, rows, 1, 1, into(y), chunk)
    sweep(y, x, w, 2, 8, rows, 1, 2, into(x), chunk)
    half = EY // 2
    got = []
    for c in range(2):
        for r0 in range(0, EY, chunk):
            v = 0.0
            for q in (Q0 + 2 * c, Q0 + 2 * c + 1):
                _, z = defect(x, w, q, q, r0, chunk, 1)
                v = v + d[q, pl.ds(r0, chunk), :] * z
            t[pl.ds(r0, chunk), :] = v
        got.append(pair_lanes(pair_rows(t, half), 1) * 0.125)
    mid = pl.ds(PAD + HY - 8, PY + 16)
    send[pl.ds(0, half), :] = pack2(got[0], got[1])
    send[pl.ds(half, PY + 16), :] = x[Q0 + 2 - par, mid, :]
    xsend[...] = x[Q0 + 1 + par, mid, :]
    for p in range(6):
        pre[p] = x[Q0 - 1 + p, mid, :]
    keep.wait()


R1 = EY // 2
R2 = EY // 4
C0 = 8


def middle_kernel(own, other, mine, its, rown, rother, rmine, rits, up, down, pre, w_out, coarse_out, rhs_out,
                  s, w, d, x, y, t, u, out_sem):
    par = parity()

    def place(i, e, v):
        v0, v1 = unpack2(v)
        s[i, 2 * e, pl.ds(PAD, R1), :] = v0
        s[i, 2 * e + 1, pl.ds(PAD, R1), :] = v1

    for i in range(5):
        s[i, :, :PAD, :] = jnp.zeros((21, PAD, PZ), F32)
        s[i, :, PAD + R1 :, :] = jnp.zeros((21, PAD, PZ), F32)
        s[i, 20, :, :] = jnp.zeros((R1 + 2 * PAD, PZ), F32)
    clear_pads(x, R1)
    clear_pads(y, R1)
    place(0, 4 + par, own[pl.ds(0, R1), :])
    place(0, 5 - par, other[pl.ds(0, R1), :])
    for i in range(4):
        place(i + 1, 4 + par, rown[i])
        place(i + 1, 5 - par, rother[i])
    for k in range(4):
        lower, upper = 3 - k, 6 + k
        e = jnp.where(par == 0, lower, upper)
        f = jnp.where(par == 0, upper, lower)
        place(0, e, mine[pl.ds(k * R1, R1), :])
        place(0, f, its[pl.ds(k * R1, R1), :])
        for i in range(4):
            place(i + 1, e, rmine[4 * k + i])
            place(i + 1, f, rits[4 * k + i])

    def raw(i):
        return lambda q, r0, n: s[i, q, pl.ds(PAD + r0, n), :]

    chunk = 32
    scaled((raw(1), raw(2), raw(3), raw(4)), raw(0), x, w, 0, 20, R1, 2, 0.25, chunk, d_ref=d)
    keep = pltpu.make_async_copy(w.at[:, pl.ds(C0 - 2, 8)], w_out, out_sem)
    keep.start()
    rows = (0, R1)
    sweep(x, None, w, 2, 18, rows, 2, 1, into(y), chunk)
    sweep(y, x, w, 3, 17, rows, 2, 2, into(x), chunk)
    for p in range(10):
        pre[p] = x[C0 - 3 + p, pl.ds(PAD, R1), :]

    def residual(c, carry):
        for r0 in range(0, R1, chunk):
            v = 0.0
            for k in range(2):
                q = 4 + 2 * c + k
                _, z = defect(x, w, q, q, r0, chunk, 2)
                v = v + d[q, pl.ds(r0, chunk), :] * z
            t[pl.ds(r0, chunk), :] = v
        rhs_out[c] = pair_lanes(pair_rows(t, R2), 2) * 0.125
        return carry

    lax.fori_loop(0, 6, residual, 0)

    def coarsen(c, carry):
        body = pl.ds(PAD, R1)

        def line(i, both):
            v = s[i, 2 * c, body, :]
            if both:
                v = v + s[i, 2 * c + 1, body, :]
            t[...] = v

        line(1, True)
        coarse_out[0, c] = pair_lanes(pair_rows(t, R2), 2) * 0.125
        line(2, False)
        coarse_out[1, c] = pair_lanes(pair_rows(t, R2), 2) * 0.25
        line(3, True)
        coarse_out[2, c] = pair_lanes(t[pl.ds(0, R2, 2), :], 2) * 0.25
        line(4, True)
        coarse_out[3, c] = low_lanes(pair_rows(t, R2), 2) * 0.25
        return carry

    lax.fori_loop(0, 10, coarsen, 0)

    def first(plane):
        c = plane + 4
        byl = coarse_out[2, c]
        u[...] = jnp.zeros(u.shape, F32)
        u[pl.ds(0, R2), :] = byl
        bzl = coarse_out[3, c]
        total = coarse_out[1, c] + coarse_out[1, c + 1] + byl + u[pl.ds(1, R2), :] + bzl + moved(bzl, -4)
        dd = coarse_out[0, c] + 0.0625 * total
        inside = dd > 0.0
        inv = jnp.where(inside, 1.0 / jnp.where(inside, dd, 1.0), 0.0)
        return inv * rhs_out[plane + 2] * (1.0 / THETA)

    up[...] = pack4([rhs_out[1 + 2], rhs_out[0 + 2], first(-1)])
    down[...] = pack4([rhs_out[0 + 2], rhs_out[1 + 2], first(2), coarse_out[1, 2 + 4]])
    keep.wait()


M0 = 5


def last_kernel(below, above, coarse, rhs, pre1_in, w1_in, pre0_in, sw, xs, w0_in, out,
                s, w2, x2, y2, pre1, w1, x1, y1, pre0, w0, x0, y0, t, sems):
    par = parity()
    copies = {}

    def copy(name, src, dst):
        c = pltpu.make_async_copy(src, dst, sems.at[len(copies)])
        c.start()
        copies[name] = c

    copy("pre1", pre1_in, pre1)
    copy("w1", w1_in, w1)
    copy("pre0", pre0_in, pre0.at[pl.ds(1, 6)])
    mid = PY + 16
    copy("sw", sw.at[pl.ds(R1, mid)], pre0.at[7 - 7 * par])
    copy("xs", xs.at[pl.ds(2 * R1, mid)], pre0.at[7 * par])
    copy("w0", w0_in, w0)

    body = pl.ds(PAD, R2)
    for i in range(5):
        clear_pads(s.at[i], R2)
    clear_pads(x2, R2)
    clear_pads(y2, R2)
    for c in range(10):
        for i in range(4):
            s[i + 1, c + 1, body, :] = coarse[i, c]
    lo, hi = below[...], above[...]
    s[0, 2, body, :] = unpack4(lo, 0)
    s[0, 1, body, :] = unpack4(lo, 1)
    for c in range(6):
        s[0, c + 3, body, :] = rhs[c]
    s[0, 9, body, :] = unpack4(hi, 0)
    s[0, 10, body, :] = unpack4(hi, 1)
    s[2, 11, body, :] = unpack4(hi, 3)

    def raw(i):
        return lambda q, r0, n: s[i, q, pl.ds(PAD + r0, n), :]

    scaled((raw(1), raw(2), raw(3), raw(4)), raw(0), x2, w2, 1, 11, R2, 4, 0.0625, R2)
    x2[0, body, :] = unpack4(lo, 2)
    x2[11, body, :] = unpack4(hi, 2)
    rows = (0, R2)
    sweep(x2, None, w2, 1, 11, rows, 4, 1, into(y2), R2)
    sweep(y2, x2, w2, 2, 10, rows, 4, 2, into(x2), R2)
    sweep(x2, y2, w2, 3, 9, rows, 4, 3, into(y2), R2)

    copies["pre1"].wait()
    clear_pads(x1, R1)
    clear_pads(y1, R1)
    for q in range(10):
        c = (q - 3) // 2 + M0
        v = y2[c, body, :]
        t[pl.ds(0, R2, 2), :] = v
        t[pl.ds(1, R2, 2), :] = v
        x1[q, pl.ds(PAD, R1), :] = pre1[q] + t[...]
    copies["w1"].wait()
    rows = (0, R1)
    sweep(x1, None, w1, 1, 9, rows, 2, 0, into(y1), 32, woff=-1)
    sweep(y1, x1, w1, 2, 8, rows, 2, 1, into(x1), 32, woff=-1)

    copies["pre0"].wait()
    copies["sw"].wait()
    copies["xs"].wait()
    clear_pads(x0, mid)
    clear_pads(y0, mid)
    for q in range(8):
        c = (q - 2) // 2 + 3 + 2 * par
        v = x1[c, pl.ds(PAD + 12, mid // 2), :]
        t0 = x0.at[q]
        t0[pl.ds(PAD, mid // 2, 2), :] = v
        t0[pl.ds(PAD + 1, mid // 2, 2), :] = v
        x0[q, pl.ds(PAD, mid), :] += pre0[q]
    copies["w0"].wait()
    sweep(x0, None, w0, 1, 7, (0, mid), 1, 0, into(y0), 40, woff=-1)

    def finish(q, r0, n, v):
        out[q - 2, pl.ds(r0 - 8, n), :] = v

    sweep(y0, x0, w0, 2, 6, (8, 8 + PY), 1, 1, finish, 32, woff=-1)


def swap(v, axis="wide"):
    count = lax.axis_size(axis)
    return lax.ppermute(v, axis, [(i, i ^ 1) for i in range(count)])


def across(v, chips):
    count = lax.axis_size("wide")
    step = 2 * chips - 1
    pairs = [(i, i + step) for i in range(1, count, 2) if i + step < count]
    pairs += [(i, i - step) for i in range(0, count, 2) if i - step >= 0]
    return lax.ppermute(v, "wide", pairs)


def shifted(v, axis, step):
    count = lax.axis_size(axis)
    return lax.ppermute(v, axis, [(i, i + step) for i in range(count) if 0 <= i + step < count])


def shards(right_side, alpha_coef, beta_x, beta_y, beta_z):
    a, ylo, yhi, xs = pl.pallas_call(
        pack_kernel,
        out_shape=(shape(5, PX, PY, PZ), shape(5, PX, HY, PZ), shape(5, PX, HY, PZ), shape(16, PY, PZ)),
        in_specs=[VMEM] * 5,
        out_specs=(VMEM,) * 4,
        compiler_params=params(),
        name="pack",
    )(right_side, alpha_coef, beta_x, beta_y, beta_z)
    lo = shifted(yhi, "narrow", 1)
    hi = shifted(ylo, "narrow", -1)
    xs = across(xs, 1)
    sw = swap(a)
    csw, cxs = pl.pallas_call(
        corner_kernel,
        out_shape=(shape(5, PX, 2 * HY, PZ), shape(16, 2 * HY, PZ)),
        in_specs=[VMEM] * 2,
        out_specs=(VMEM,) * 2,
        compiler_params=params(),
        name="corners",
    )(lo, hi)
    cxs = across(cxs, 1)
    csw = swap(csw)
    raw1 = pl.pallas_call(
        coarse_kernel,
        out_shape=shape(4, R1, PZ),
        in_specs=[VMEM] * 3,
        out_specs=VMEM,
        scratch_shapes=[pltpu.VMEM((EY, PZ), F32)],
        compiler_params=params(),
        name="coarse_coefficients",
    )(a, lo, hi)
    raw1_other = swap(raw1)
    pair = jnp.concatenate([raw1, raw1_other], 0)
    raw1_mine = jnp.concatenate([across(pair, 1), across(pair, 2)], 0)
    raw1_its = swap(raw1_mine)

    mid = PY + 16
    send, xsend, pre0, w0 = pl.pallas_call(
        fine_kernel,
        out_shape=(shape(R1 + mid, PZ), shape(mid, PZ), shape(6, mid, PZ), shape(7, 6, mid, PZ)),
        in_specs=[ANY] * 7,
        out_specs=(VMEM, VMEM, VMEM, ANY),
        scratch_shapes=[
            pltpu.VMEM((5, 12, EY + 2 * PAD, PZ), F32),
            pltpu.VMEM((7, 10, EY, PZ), F32),
            pltpu.VMEM((10, EY, PZ), F32),
            pltpu.VMEM((10, EY + 2 * PAD, PZ), F32),
            pltpu.VMEM((10, EY + 2 * PAD, PZ), F32),
            pltpu.VMEM((EY, PZ), F32),
            pltpu.SemaphoreType.DMA((27,)),
            pltpu.SemaphoreType.DMA,
        ],
        compiler_params=params(),
        name="level0_pre",
    )(a, lo, hi, sw, xs, csw, cxs)

    other = swap(send)
    pair = jnp.concatenate([send[:R1], other[:R1], xsend], 0)
    one = across(pair, 1)
    two = across(pair[: 2 * R1], 2)
    mine = jnp.concatenate([one[: 2 * R1], two], 0)
    its = swap(mine)

    up, down, pre1, w1, coarse, rhs = pl.pallas_call(
        middle_kernel,
        out_shape=(
            shape(R2, PZ), shape(R2, PZ), shape(10, R1, PZ), shape(7, 8, R1, PZ), shape(4, 10, R2, PZ),
            shape(6, R2, PZ),
        ),
        in_specs=[VMEM] * 8,
        out_specs=(VMEM, VMEM, VMEM, ANY, VMEM, VMEM),
        scratch_shapes=[
            pltpu.VMEM((5, 21, R1 + 2 * PAD, PZ), F32),
            pltpu.VMEM((7, 20, R1, PZ), F32),
            pltpu.VMEM((20, R1, PZ), F32),
            pltpu.VMEM((20, R1 + 2 * PAD, PZ), F32),
            pltpu.VMEM((20, R1 + 2 * PAD, PZ), F32),
            pltpu.VMEM((R1, PZ), F32),
            pltpu.VMEM((R2 + PAD, PZ), F32),
            pltpu.SemaphoreType.DMA,
        ],
        compiler_params=params(),
        name="level1_pre",
    )(send, other, mine, its, raw1, raw1_other, raw1_mine, raw1_its)

    below = shifted(up, "wide", 4)
    above = shifted(down, "wide", -4)
    return pl.pallas_call(
        last_kernel,
        out_shape=shape(PX, PY, PZ),
        in_specs=[VMEM] * 4 + [ANY] * 6,
        out_specs=VMEM,
        scratch_shapes=[
            pltpu.VMEM((5, 12, R2 + 2 * PAD, PZ), F32),
            pltpu.VMEM((7, 12, R2, PZ), F32),
            pltpu.VMEM((12, R2 + 2 * PAD, PZ), F32),
            pltpu.VMEM((12, R2 + 2 * PAD, PZ), F32),
            pltpu.VMEM((10, R1, PZ), F32),
            pltpu.VMEM((7, 8, R1, PZ), F32),
            pltpu.VMEM((10, R1 + 2 * PAD, PZ), F32),
            pltpu.VMEM((10, R1 + 2 * PAD, PZ), F32),
            pltpu.VMEM((8, mid, PZ), F32),
            pltpu.VMEM((7, 6, mid, PZ), F32),
            pltpu.VMEM((8, mid + 2 * PAD, PZ), F32),
            pltpu.VMEM((8, mid + 2 * PAD, PZ), F32),
            pltpu.VMEM((R1, PZ), F32),
            pltpu.SemaphoreType.DMA((6,)),
        ],
        compiler_params=params(),
        name="coarse_and_post",
    )(below, above, coarse, rhs, pre1, w1, pre0, other, one, w0)


def solution(mesh):
    spec = P("wide", "narrow", None)
    return jax.shard_map(shards, mesh=mesh, in_specs=(spec,) * 5, out_specs=spec, check_vma=False)
```

time: 313 us -> 111 us (0.35)
  the two profiles are of different devices: /device:TPU:199 before, /device:TPU:220 now
where the time goes in v1:
time: 111 us; the launch traced here: 110 us
  starting transfers between devices  50.4 us (45%)
  waiting for transfers between devices  34.5 us (31%)
  Pallas kernels  20.5 us (18%)
  local copies, waits for them, and re-layouts  4.57 us (4%)
    ppermute x6, starting transfers between devices, swap(): return lax.ppermute(v, axis, [(i, i ^ 1) for i in range(count)])  21.1 us
    ppermute x4, waiting for transfers between devices, shifted(): lax.ppermute(v, axis, [(i, i + step) for i in range(count) if 0 <= i + st...  17.6 us
    ppermute x6, waiting for transfers between devices, across(): return lax.ppermute(v, 'wide', pairs)  15.9 us
    ppermute x6, starting transfers between devices, across(): return lax.ppermute(v, 'wide', pairs)  14.7 us
    ppermute x4, starting transfers between devices, shifted(): lax.ppermute(v, axis, [(i, i + step) for i in range(count) if 0 <= i + st...  14.5 us
    pallas_call x1, Pallas kernels, shards(): pl.pallas_call(middle_kernel, out_shape=(shape(R2, PZ), shape(R2, PZ), sh...  8.33 us
    pallas_call x1, Pallas kernels, shards(): pl.pallas_call(last_kernel, out_shape=shape(PX, PY, PZ), in_specs=[VMEM]...  7.15 us
    unnamed x11, local copies, waits for them, and re-layouts  4.54 us
  transfers between devices with their start and end apart: 16, of which 7 were waited for; matrix products, arithmetic and copies ran while one was open for 0% of the time, Pallas kernels for 4%

profile of v1, /device:TPU:220, one launch (start us, length us, event | category | flops | bytes accessed | tf_op | source)
XLA Modules:
  0.0 110.3 jit_solution(11203305389047472669)
XLA Ops:
  0.0 0.0 copy-start
  0.0 0.9 copy-done
  0.9 0.0 copy-start.1
  0.9 0.9 copy-done.1
  1.8 0.0 copy-start.2
  1.8 0.9 copy-done.2
  2.7 0.0 copy-start.3
  2.7 0.9 copy-done.3
  3.6 0.0 copy-start.4
  3.6 0.9 copy-done.4
  4.5 0.2 pack.1
  4.7 4.7 %collective-permute-start = (f32[5,4,32,128]{3,2,1,0:T(8,128)S(1)}, f32[5,4,32,128]{3,2,1,0:T(8,128)S(1)}, u32[]{:S(2)}, u32[]{:S(2)}) collective-permute-start(f32[5,4,32,128]{3,2,1,0:T(8,128)S(1)} %get-tuple-element.22), channel_id=1, source_target_pairs={{0,1},{1,2},{2,3},{3,4},{4,5},{5,6},{6,7},{8,9},{9,10},{10,11},{11... | collective-permute-start | bytes 983048 | tf_op jit(solution)/shard_map/ppermute | solution.py:502
  9.4 1.9 %collective-permute-start.1 = (f32[5,4,32,128]{3,2,1,0:T(8,128)S(1)}, f32[5,4,32,128]{3,2,1,0:T(8,128)S(1)}, u32[]{:S(2)}, u32[]{:S(2)}) collective-permute-start(f32[5,4,32,128]{3,2,1,0:T(8,128)S(1)} %get-tuple-element.23), channel_id=1, source_target_pairs={{1,0},{2,1},{3,2},{4,3},{5,4},{6,5},{7,6},{9,8},{10,9},{11,10},{12... | collective-permute-start | bytes 983048 | tf_op jit(solution)/shard_map/ppermute | solution.py:502
  11.3 5.0 %collective-permute-done.lo = f32[5,4,32,128]{3,2,1,0:T(8,128)S(1)} collective-permute-done((f32[5,4,32,128]{3,2,1,0:T(8,128)S(1)}, f32[5,4,32,128]{3,2,1,0:T(8,128)S(1)}, u32[]{:S(2)}, u32[]{:S(2)}) %collective-permute-start) | collective-permute-done | bytes 327712 | tf_op jit(solution)/shard_map/ppermute | solution.py:502
  16.3 5.3 %collective-permute-done.1.hi = f32[5,4,32,128]{3,2,1,0:T(8,128)S(1)} collective-permute-done((f32[5,4,32,128]{3,2,1,0:T(8,128)S(1)}, f32[5,4,32,128]{3,2,1,0:T(8,128)S(1)}, u32[]{:S(2)}, u32[]{:S(2)}) %collective-permute-start.1) | collective-permute-done | bytes 327712 | tf_op jit(solution)/shard_map/ppermute | solution.py:502
  21.7 0.2 coarse_coefficients.1.rown
  21.9 1.9 %collective-permute-start.10 = (f32[4,64,128]{2,1,0:T(8,128)S(1)}, f32[4,64,128]{2,1,0:T(8,128)S(1)}, u32[]{:S(2)}, u32[]{:S(2)}) collective-permute-start(f32[4,64,128]{2,1,0:T(8,128)S(1)} %coarse_coefficients.1.rown), channel_id=1, source_target_pairs={{0,8},{8,0},{16,24},{24,16},{32,40},{40,32},{48,56},{56,48},{64,72... | collective-permute-start | bytes 393224 | tf_op jit(solution)/shard_map/ppermute | solution.py:489
  23.8 2.4 %collective-permute-start.2 = (f32[5,4,64,128]{3,2,1,0:T(8,128)S(1)}, f32[5,4,64,128]{3,2,1,0:T(8,128)S(1)}, u32[]{:S(2)}, u32[]{:S(2)}) collective-permute-start(f32[5,4,64,128]{3,2,1,0:T(8,128)S(1)} %get-tuple-element.21.a), channel_id=1, source_target_pairs={{0,8},{8,0},{16,24},{24,16},{32,40},{40,32},{48,56},{56,48},{64,72... | collective-permute-start | bytes 1966088 | tf_op jit(solution)/shard_map/ppermute | solution.py:489
  26.2 0.1 corners.1
  26.3 1.9 %collective-permute-start.4 = (f32[5,4,64,128]{3,2,1,0:T(8,128)S(1)}, f32[5,4,64,128]{3,2,1,0:T(8,128)S(1)}, u32[]{:S(2)}, u32[]{:S(2)}) collective-permute-start(f32[5,4,64,128]{3,2,1,0:T(8,128)S(1)} %get-tuple-element.25), channel_id=1, source_target_pairs={{0,8},{8,0},{16,24},{24,16},{32,40},{40,32},{48,56},{56,48},{64,72... | collective-permute-start | bytes 1966088 | tf_op jit(solution)/shard_map/ppermute | solution.py:489
  28.2 2.5 %collective-permute-start.3 = (f32[16,64,128]{2,1,0:T(8,128)S(1)}, f32[16,64,128]{2,1,0:T(8,128)S(1)}, u32[]{:S(2)}, u32[]{:S(2)}) collective-permute-start(f32[16,64,128]{2,1,0:T(8,128)S(1)} %get-tuple-element.24), channel_id=1, source_target_pairs={{8,16},{24,32},{40,48},{56,64},{72,80},{88,96},{104,112},{120,128}... | collective-permute-start | bytes 1572872 | tf_op jit(solution)/shard_map/ppermute | solution.py:497
  30.8 3.0 %collective-permute-start.5 = (f32[16,64,128]{2,1,0:T(8,128)S(1)}, f32[16,64,128]{2,1,0:T(8,128)S(1)}, u32[]{:S(2)}, u32[]{:S(2)}) collective-permute-start(f32[16,64,128]{2,1,0:T(8,128)S(1)} %get-tuple-element.26), channel_id=1, source_target_pairs={{8,16},{24,32},{40,48},{56,64},{72,80},{88,96},{104,112},{120,128}... | collective-permute-start | bytes 1572872 | tf_op jit(solution)/shard_map/ppermute | solution.py:497
  33.8 0.0 collective-permute-done.10.rother
  33.9 2.5 %collective-permute-start.11 = (f32[8,64,128]{2,1,0:T(8,128)S(1)}, f32[8,64,128]{2,1,0:T(8,128)S(1)}, u32[]{:S(2)}, u32[]{:S(2)}) collective-permute-start(f32[8,64,128]{2,1,0:T(8,128)S(1)} %pad_maximum_fusion), channel_id=1, source_target_pairs={{8,16},{24,32},{40,48},{56,64},{72,80},{88,96},{104,112},{120,128}... | collective-permute-start | bytes 786440 | tf_op jit(solution)/shard_map/ppermute | solution.py:497
  36.4 10.8 %collective-permute-done.11 = f32[8,64,128]{2,1,0:T(8,128)S(1)} collective-permute-done((f32[8,64,128]{2,1,0:T(8,128)S(1)}, f32[8,64,128]{2,1,0:T(8,128)S(1)}, u32[]{:S(2)}, u32[]{:S(2)}) %collective-permute-start.11) | collective-permute-done | bytes 262176 | tf_op jit(solution)/shard_map/ppermute | solution.py:497
  47.2 2.8 %collective-permute-start.12 = (f32[8,64,128]{2,1,0:T(8,128)S(1)}, f32[8,64,128]{2,1,0:T(8,128)S(1)}, u32[]{:S(2)}, u32[]{:S(2)}) collective-permute-start(f32[8,64,128]{2,1,0:T(8,128)S(1)} %pad_maximum_fusion), channel_id=1, source_target_pairs={{8,32},{24,48},{40,64},{56,80},{72,96},{88,112},{104,128},{120,144... | collective-permute-start | bytes 786440 | tf_op jit(solution)/shard_map/ppermute | solution.py:497
  50.0 0.0 collective-permute-done.3.xs
  50.0 0.0 collective-permute-done.2.sw
  50.0 0.0 collective-permute-done.5.cxs
  50.0 0.0 collective-permute-done.4.csw
  50.0 4.5 %level0_pre.1 = (f32[144,128]{1,0:T(8,128)S(1)}, f32[80,128]{1,0:T(8,128)S(1)}, f32[6,80,128]{2,1,0:T(8,128)S(1)}, f32[7,6,80,128]{3,2,1,0:T(8,128)S(1)}) custom-call(f32[5,4,64,128]{3,2,1,0:T(8,128)S(1)} %get-tuple-element.21.a, f32[5,4,32,128]{3,2,1,0:T(8,128)S(1)} %collective-permute-done.lo, f32[5,4,32,128]{3,2,1,0:T(8,128)S(1)} %collective-permute-done.1.hi, ...), custom_call_target="tpu_custom_call" | custom-call | tf_op jit(solution)/shard_map/level0_pre/pallas_call | solution.py:543
  54.6 8.0 %collective-permute-start.6 = (f32[144,128]{1,0:T(8,128)S(1)}, f32[144,128]{1,0:T(8,128)S(1)}, u32[]{:S(2)}, u32[]{:S(2)}) collective-permute-start(f32[144,128]{1,0:T(8,128)S(1)} %get-tuple-element.27.own), channel_id=1, source_target_pairs={{0,8},{8,0},{16,24},{24,16},{32,40},{40,32},{48,56},{56,48},{64,72... | collective-permute-start | bytes 221192 | tf_op jit(solution)/shard_map/ppermute | solution.py:489
  62.6 0.0 collective-permute-done.12
  62.6 1.9 %collective-permute-start.13 = (f32[16,64,128]{2,1,0:T(8,128)S(1)}, f32[16,64,128]{2,1,0:T(8,128)S(1)}, u32[]{:S(2)}, u32[]{:S(2)}) collective-permute-start(f32[16,64,128]{2,1,0:T(8,128)S(1)} %constant_dynamic-update-slice_fusion.rmine), channel_id=1, source_target_pairs={{0,8},{8,0},{16,24},{24,16},{32,40},{40,32},{48,56},{56,48},{64,72... | collective-permute-start | bytes 1572872 | tf_op jit(solution)/shard_map/ppermute | solution.py:489
  64.5 0.0 collective-permute-done.6.other.sw
  64.6 1.9 %collective-permute-start.7 = (f32[208,128]{1,0:T(8,128)S(1)}, f32[208,128]{1,0:T(8,128)S(1)}, u32[]{:S(2)}, u32[]{:S(2)}) collective-permute-start(f32[208,128]{1,0:T(8,128)S(1)} %pad_maximum_fusion.2), channel_id=1, source_target_pairs={{8,16},{24,32},{40,48},{56,64},{72,80},{88,96},{104,112},{120,128}... | collective-permute-start | bytes 319496 | tf_op jit(solution)/shard_map/ppermute | solution.py:497
  66.5 1.9 %collective-permute-start.8 = (f32[128,128]{1,0:T(8,128)S(1)}, f32[128,128]{1,0:T(8,128)S(1)}, u32[]{:S(2)}, u32[]{:S(2)}) collective-permute-start(f32[128,128]{1,0:T(8,128)S(1)} %pad_maximum_fusion.3), channel_id=1, source_target_pairs={{8,32},{24,48},{40,64},{56,80},{72,96},{88,112},{104,128},{120,144... | collective-permute-start | bytes 196616 | tf_op jit(solution)/shard_map/ppermute | solution.py:497
  68.5 2.2 %collective-permute-done.7.xs = f32[208,128]{1,0:T(8,128)S(1)} collective-permute-done((f32[208,128]{1,0:T(8,128)S(1)}, f32[208,128]{1,0:T(8,128)S(1)}, u32[]{:S(2)}, u32[]{:S(2)}) %collective-permute-start.7) | collective-permute-done | bytes 106528 | tf_op jit(solution)/shard_map/ppermute | solution.py:497
  70.6 3.0 %collective-permute-done.8 = f32[128,128]{1,0:T(8,128)S(1)} collective-permute-done((f32[128,128]{1,0:T(8,128)S(1)}, f32[128,128]{1,0:T(8,128)S(1)}, u32[]{:S(2)}, u32[]{:S(2)}) %collective-permute-start.8) | collective-permute-done | bytes 65568 | tf_op jit(solution)/shard_map/ppermute | solution.py:497
  73.6 5.0 %collective-permute-start.9 = (f32[256,128]{1,0:T(8,128)S(1)}, f32[256,128]{1,0:T(8,128)S(1)}, u32[]{:S(2)}, u32[]{:S(2)}) collective-permute-start(f32[256,128]{1,0:T(8,128)S(1)} %pad_maximum_fusion.1.mine), channel_id=1, source_target_pairs={{0,8},{8,0},{16,24},{24,16},{32,40},{40,32},{48,56},{56,48},{64,72... | collective-permute-start | bytes 393224 | tf_op jit(solution)/shard_map/ppermute | solution.py:489
  78.6 0.0 collective-permute-done.13.rits
  78.6 1.0 collective-permute-done.9.its
  79.6 8.3 %level1_pre.1 = (f32[32,128]{1,0:T(8,128)S(1)}, f32[32,128]{1,0:T(8,128)S(1)}, f32[10,64,128]{2,1,0:T(8,128)S(1)}, f32[7,8,64,128]{3,2,1,0:T(8,128)S(1)}, f32[4,...) custom-call(f32[144,128]{1,0:T(8,128)S(1)} %get-tuple-element.27.own, ...), custom_call_target="tpu_custom_call" | custom-call | tf_op jit(solution)/shard_map/level1_pre/pallas_call | solution.py:569
  87.9 5.9 %collective-permute-start.14 = (f32[32,128]{1,0:T(8,128)S(1)}, f32[32,128]{1,0:T(8,128)S(1)}, u32[]{:S(2)}, u32[]{:S(2)}) collective-permute-start(f32[32,128]{1,0:T(8,128)S(1)} %get-tuple-element.29), channel_id=1, source_target_pairs={{0,32},{8,40},{16,48},{24,56},{32,64},{40,72},{48,80},{56,88},{64,... | collective-permute-start | bytes 49160 | tf_op jit(solution)/shard_map/ppermute | solution.py:502
  93.9 1.9 %collective-permute-start.15 = (f32[32,128]{1,0:T(8,128)S(1)}, f32[32,128]{1,0:T(8,128)S(1)}, u32[]{:S(2)}, u32[]{:S(2)}) collective-permute-start(f32[32,128]{1,0:T(8,128)S(1)} %get-tuple-element.30), channel_id=1, source_target_pairs={{32,0},{40,8},{48,16},{56,24},{64,32},{72,40},{80,48},{88,56},{96,... | collective-permute-start | bytes 49160 | tf_op jit(solution)/shard_map/ppermute | solution.py:502
  95.8 0.0 collective-permute-done.14.below
  95.8 7.3 %collective-permute-done.15.above = f32[32,128]{1,0:T(8,128)S(1)} collective-permute-done((f32[32,128]{1,0:T(8,128)S(1)}, f32[32,128]{1,0:T(8,128)S(1)}, u32[]{:S(2)}, u32[]{:S(2)}) %collective-permute-start.15) | collective-permute-done | bytes 16416 | tf_op jit(solution)/shard_map/ppermute | solution.py:502
  103.1 7.1 %coarse_and_post.1 = f32[4,64,128]{2,1,0:T(8,128)} custom-call(f32[32,128]{1,0:T(8,128)S(1)} %collective-permute-done.14.below, f32[32,128]{1,0:T(8,128)S(1)} %collective-permute-done.15.above, f32[4,10,32,128]{3,2,1,0:T(8,128)S(1)} %get-tuple-element.31.coarse, f32[6,32,128]{2,1,0:T(8,128)S(1)} %get-tuple-element.32.rhs, ...), custom_call_target="tpu_custom_call" | custom-call | tf_op jit(solution)/shard_map/coarse_and_post/pallas_call | solution.py:593
  (9 shorter events, 0.1 us)
Async XLA Ops:
  0.0 0.9 copy-start
  0.9 0.9 copy-start.1
  1.8 0.9 copy-start.2
  2.7 0.9 copy-start.3
  3.6 0.9 copy-start.4
  4.7 11.6 %collective-permute-start = (f32[5,4,32,128]{3,2,1,0:T(8,128)S(1)}, f32[5,4,32,128]{3,2,1,0:T(8,128)S(1)}, u32[]{:S(2)}, u32[]{:S(2)}) collective-permute-start(f32[5,4,32,128]{3,2,1,0:T(8,128)S(1)} %get-tuple-element.22), channel_id=1, source_target_pairs={{0,1},{1,2},{2,3},{3,4},{4,5},{5,6},{6,7},{8,9},{9,10},{10,11},{11... | collective-permute-start | bytes 983048 | tf_op jit(solution)/shard_map/ppermute | solution.py:502
  9.4 12.2 %collective-permute-start.1 = (f32[5,4,32,128]{3,2,1,0:T(8,128)S(1)}, f32[5,4,32,128]{3,2,1,0:T(8,128)S(1)}, u32[]{:S(2)}, u32[]{:S(2)}) collective-permute-start(f32[5,4,32,128]{3,2,1,0:T(8,128)S(1)} %get-tuple-element.23), channel_id=1, source_target_pairs={{1,0},{2,1},{3,2},{4,3},{5,4},{6,5},{7,6},{9,8},{10,9},{11,10},{12... | collective-permute-start | bytes 983048 | tf_op jit(solution)/shard_map/ppermute | solution.py:502
  21.9 11.9 %collective-permute-start.10 = (f32[4,64,128]{2,1,0:T(8,128)S(1)}, f32[4,64,128]{2,1,0:T(8,128)S(1)}, u32[]{:S(2)}, u32[]{:S(2)}) collective-permute-start(f32[4,64,128]{2,1,0:T(8,128)S(1)} %coarse_coefficients.1.rown), channel_id=1, source_target_pairs={{0,8},{8,0},{16,24},{24,16},{32,40},{40,32},{48,56},{56,48},{64,72... | collective-permute-start | bytes 393224 | tf_op jit(solution)/shard_map/ppermute | solution.py:489
  23.8 26.2 %collective-permute-start.2 = (f32[5,4,64,128]{3,2,1,0:T(8,128)S(1)}, f32[5,4,64,128]{3,2,1,0:T(8,128)S(1)}, u32[]{:S(2)}, u32[]{:S(2)}) collective-permute-start(f32[5,4,64,128]{3,2,1,0:T(8,128)S(1)} %get-tuple-element.21.a), channel_id=1, source_target_pairs={{0,8},{8,0},{16,24},{24,16},{32,40},{40,32},{48,56},{56,48},{64,72... | collective-permute-start | bytes 1966088 | tf_op jit(solution)/shard_map/ppermute | solution.py:489
  26.3 23.7 %collective-permute-start.4 = (f32[5,4,64,128]{3,2,1,0:T(8,128)S(1)}, f32[5,4,64,128]{3,2,1,0:T(8,128)S(1)}, u32[]{:S(2)}, u32[]{:S(2)}) collective-permute-start(f32[5,4,64,128]{3,2,1,0:T(8,128)S(1)} %get-tuple-element.25), channel_id=1, source_target_pairs={{0,8},{8,0},{16,24},{24,16},{32,40},{40,32},{48,56},{56,48},{64,72... | collective-permute-start | bytes 1966088 | tf_op jit(solution)/shard_map/ppermute | solution.py:489
  28.2 21.8 %collective-permute-start.3 = (f32[16,64,128]{2,1,0:T(8,128)S(1)}, f32[16,64,128]{2,1,0:T(8,128)S(1)}, u32[]{:S(2)}, u32[]{:S(2)}) collective-permute-start(f32[16,64,128]{2,1,0:T(8,128)S(1)} %get-tuple-element.24), channel_id=1, source_target_pairs={{8,16},{24,32},{40,48},{56,64},{72,80},{88,96},{104,112},{120,128}... | collective-permute-start | bytes 1572872 | tf_op jit(solution)/shard_map/ppermute | solution.py:497
  30.8 19.2 %collective-permute-start.5 = (f32[16,64,128]{2,1,0:T(8,128)S(1)}, f32[16,64,128]{2,1,0:T(8,128)S(1)}, u32[]{:S(2)}, u32[]{:S(2)}) collective-permute-start(f32[16,64,128]{2,1,0:T(8,128)S(1)} %get-tuple-element.26), channel_id=1, source_target_pairs={{8,16},{24,32},{40,48},{56,64},{72,80},{88,96},{104,112},{120,128}... | collective-permute-start | bytes 1572872 | tf_op jit(solution)/shard_map/ppermute | solution.py:497
  33.9 13.3 %collective-permute-start.11 = (f32[8,64,128]{2,1,0:T(8,128)S(1)}, f32[8,64,128]{2,1,0:T(8,128)S(1)}, u32[]{:S(2)}, u32[]{:S(2)}) collective-permute-start(f32[8,64,128]{2,1,0:T(8,128)S(1)} %pad_maximum_fusion), channel_id=1, source_target_pairs={{8,16},{24,32},{40,48},{56,64},{72,80},{88,96},{104,112},{120,128}... | collective-permute-start | bytes 786440 | tf_op jit(solution)/shard_map/ppermute | solution.py:497
  47.2 15.4 %collective-permute-start.12 = (f32[8,64,128]{2,1,0:T(8,128)S(1)}, f32[8,64,128]{2,1,0:T(8,128)S(1)}, u32[]{:S(2)}, u32[]{:S(2)}) collective-permute-start(f32[8,64,128]{2,1,0:T(8,128)S(1)} %pad_maximum_fusion), channel_id=1, source_target_pairs={{8,32},{24,48},{40,64},{56,80},{72,96},{88,112},{104,128},{120,144... | collective-permute-start | bytes 786440 | tf_op jit(solution)/shard_map/ppermute | solution.py:497
  54.6 10.0 %collective-permute-start.6 = (f32[144,128]{1,0:T(8,128)S(1)}, f32[144,128]{1,0:T(8,128)S(1)}, u32[]{:S(2)}, u32[]{:S(2)}) collective-permute-start(f32[144,128]{1,0:T(8,128)S(1)} %get-tuple-element.27.own), channel_id=1, source_target_pairs={{0,8},{8,0},{16,24},{24,16},{32,40},{40,32},{48,56},{56,48},{64,72... | collective-permute-start | bytes 221192 | tf_op jit(solution)/shard_map/ppermute | solution.py:489
  62.6 16.0 %collective-permute-start.13 = (f32[16,64,128]{2,1,0:T(8,128)S(1)}, f32[16,64,128]{2,1,0:T(8,128)S(1)}, u32[]{:S(2)}, u32[]{:S(2)}) collective-permute-start(f32[16,64,128]{2,1,0:T(8,128)S(1)} %constant_dynamic-update-slice_fusion.rmine), channel_id=1, source_target_pairs={{0,8},{8,0},{16,24},{24,16},{32,40},{40,32},{48,56},{56,48},{64,72... | collective-permute-start | bytes 1572872 | tf_op jit(solution)/shard_map/ppermute | solution.py:489
  64.6 6.0 %collective-permute-start.7 = (f32[208,128]{1,0:T(8,128)S(1)}, f32[208,128]{1,0:T(8,128)S(1)}, u32[]{:S(2)}, u32[]{:S(2)}) collective-permute-start(f32[208,128]{1,0:T(8,128)S(1)} %pad_maximum_fusion.2), channel_id=1, source_target_pairs={{8,16},{24,32},{40,48},{56,64},{72,80},{88,96},{104,112},{120,128}... | collective-permute-start | bytes 319496 | tf_op jit(solution)/shard_map/ppermute | solution.py:497
  66.5 7.1 %collective-permute-start.8 = (f32[128,128]{1,0:T(8,128)S(1)}, f32[128,128]{1,0:T(8,128)S(1)}, u32[]{:S(2)}, u32[]{:S(2)}) collective-permute-start(f32[128,128]{1,0:T(8,128)S(1)} %pad_maximum_fusion.3), channel_id=1, source_target_pairs={{8,32},{24,48},{40,64},{56,80},{72,96},{88,112},{104,128},{120,144... | collective-permute-start | bytes 196616 | tf_op jit(solution)/shard_map/ppermute | solution.py:497
  73.6 6.0 %collective-permute-start.9 = (f32[256,128]{1,0:T(8,128)S(1)}, f32[256,128]{1,0:T(8,128)S(1)}, u32[]{:S(2)}, u32[]{:S(2)}) collective-permute-start(f32[256,128]{1,0:T(8,128)S(1)} %pad_maximum_fusion.1.mine), channel_id=1, source_target_pairs={{0,8},{8,0},{16,24},{24,16},{32,40},{40,32},{48,56},{56,48},{64,72... | collective-permute-start | bytes 393224 | tf_op jit(solution)/shard_map/ppermute | solution.py:489
  87.9 7.9 %collective-permute-start.14 = (f32[32,128]{1,0:T(8,128)S(1)}, f32[32,128]{1,0:T(8,128)S(1)}, u32[]{:S(2)}, u32[]{:S(2)}) collective-permute-start(f32[32,128]{1,0:T(8,128)S(1)} %get-tuple-element.29), channel_id=1, source_target_pairs={{0,32},{8,40},{16,48},{24,56},{32,64},{40,72},{48,80},{56,88},{64,... | collective-permute-start | bytes 49160 | tf_op jit(solution)/shard_map/ppermute | solution.py:502
  93.9 9.2 %collective-permute-start.15 = (f32[32,128]{1,0:T(8,128)S(1)}, f32[32,128]{1,0:T(8,128)S(1)}, u32[]{:S(2)}, u32[]{:S(2)}) collective-permute-start(f32[32,128]{1,0:T(8,128)S(1)} %get-tuple-element.30), channel_id=1, source_target_pairs={{32,0},{40,8},{48,16},{56,24},{64,32},{72,40},{80,48},{88,56},{96,... | collective-permute-start | bytes 49160 | tf_op jit(solution)/shard_map/ppermute | solution.py:502

commit v2 on v0

v2 whole, which is shorter than its diff:
```python
import jax
import jax.numpy as jnp
from jax import lax
from jax.experimental import pallas as pl
from jax.experimental.pallas import tpu as pltpu
from jax.sharding import PartitionSpec as P

F32 = jnp.float32
THETA = (2.0 + 0.25) / 2.0
DELTA = (2.0 - 0.25) / 2.0
SIGMA = THETA / DELTA
RHO = [1.0 / SIGMA]
for _step in range(3):
    RHO.append(1.0 / (2.0 * SIGMA - RHO[-1]))
MOMENTUM = [0.0] + [RHO[k] * RHO[k - 1] for k in range(1, 4)]
GAIN = [1.0 / THETA] + [2.0 * RHO[k] / DELTA for k in range(1, 4)]

PX, PY, PZ = 4, 64, 128
HY = 8
EY = PY + 2 * HY
H1 = PY // 2
G1 = 16
R1 = H1 + 2 * G1
R2 = R1 // 2
RAW = 5 * PX * EY
SIDE = 5 * PX * HY
PAD = 8
B, ALPHA, BX, BY, BZ = range(5)
ANY = pl.BlockSpec(memory_space=pl.ANY)
VMEM = pl.BlockSpec(memory_space=pltpu.VMEM)
HBM = pl.BlockSpec(memory_space=pltpu.HBM)


def shape(*dims):
    return jax.ShapeDtypeStruct(dims, F32)


def scratch(*dims):
    return pltpu.VMEM(dims, F32)


def call(kernel, name, out_shape, out_specs, in_specs, scratch_shapes, flops, mib=24, aliases=None):
    return pl.pallas_call(
        kernel,
        out_shape=out_shape,
        in_specs=in_specs,
        out_specs=out_specs,
        scratch_shapes=scratch_shapes,
        compiler_params=pltpu.CompilerParams(vmem_limit_bytes=mib * 1024 * 1024),
        cost_estimate=pl.CostEstimate(flops=flops, bytes_accessed=0, transcendentals=0),
        input_output_aliases=aliases or {},
        name=name,
    )


def parity():
    return lax.rem(lax.axis_index("wide"), 2)


def lanes(rows):
    return lax.broadcasted_iota(jnp.int32, (rows, PZ), 1)


def moved(v, shift):
    return pltpu.roll(v, shift % PZ, 1)


def planes(lo, hi, each, unroll):
    steps = (hi - lo) // unroll

    def body(i, carry):
        for k in range(unroll):
            each(lo + i * unroll + k)
        return carry

    if steps > 1:
        lax.fori_loop(0, steps, body, 0)
    else:
        steps = 0
    for q in range(lo + steps * unroll, hi):
        each(q)


def defect(x_ref, c_ref, w_ref, q, r0, n, reach, cq, cr, wq, wr):
    rows = pl.ds(PAD + r0, n)
    here = pl.ds(wr + r0, n)
    x = x_ref[q, rows, :]
    total = c_ref[cq, pl.ds(cr + r0, n), :] - x
    total += w_ref[0, wq, here, :] * x_ref[q - 1, rows, :]
    total += w_ref[1, wq, here, :] * x_ref[q + 1, rows, :]
    total += w_ref[2, wq, here, :] * x_ref[q, pl.ds(PAD + r0 - 1, n), :]
    total += w_ref[3, wq, here, :] * x_ref[q, pl.ds(PAD + r0 + 1, n), :]
    total += w_ref[4, wq, here, :] * moved(x, reach)
    total += w_ref[5, wq, here, :] * moved(x, -reach)
    return x, total


def sweep(x_ref, prev_ref, c_ref, w_ref, lo, hi, rows, reach, k, store, chunk, woff=0, coff=0, wr=0, cr=0, unroll=8):
    def each(q):
        for r0 in range(rows[0], rows[1], chunk):
            n = min(chunk, rows[1] - r0)
            x, z = defect(x_ref, c_ref, w_ref, q, r0, n, reach, q + coff, cr, q + woff, wr)
            new = x + GAIN[k] * z
            if k > 0:
                gap = x if prev_ref is None else x - prev_ref[q, pl.ds(PAD + r0, n), :]
                new += MOMENTUM[k] * gap
            store(q, r0, n, new)

    planes(lo, hi, each, unroll)


def into(ref):
    def store(q, r0, n, v):
        ref[q, pl.ds(PAD + r0, n), :] = v

    return store


def inverse(d):
    inside = d > 0.0
    return jnp.where(inside, 1.0 / jnp.where(inside, d, 1.0), 0.0)


def faces(alpha, x0, x1, y0, y1, z0, reach, scale):
    z1 = moved(z0, -reach)
    d = alpha + scale * (x0 + x1 + y0 + y1 + z0 + z1)
    inv = inverse(d)
    si = scale * inv
    return d, inv, [si * f for f in (x0, x1, y0, y1, z0, z1)]


def next_rows(load, r0, n, rows):
    if r0 + n < rows:
        return load(r0 + 1, n)
    return pltpu.roll(load(r0, n), n - 1, 0)


def clear_pads(ref, rows):
    ref[:, :PAD, :] = jnp.zeros((ref.shape[0], PAD, PZ), F32)
    ref[:, PAD + rows :, :] = jnp.zeros((ref.shape[0], PAD, PZ), F32)


def pair_lanes(v, reach):
    low = (lanes(v.shape[0]) & reach) == 0
    return v + jnp.where(low, moved(v, -reach), moved(v, reach))


def low_lanes(v, reach):
    low = (lanes(v.shape[0]) & reach) == 0
    return jnp.where(low, v, moved(v, reach))


def pack2(v0, v1):
    return jnp.where((lanes(v0.shape[0]) & 1) == 0, v0, v1)


def unpack2(v):
    even = (lanes(v.shape[0]) & 1) == 0
    return jnp.where(even, v, moved(v, 1)), jnp.where(even, moved(v, -1), v)


def pack4(items):
    place = lanes(items[0].shape[0]) & 3
    out = items[0]
    for i, item in enumerate(items[1:], 1):
        out = jnp.where(place == i, item, out)
    return out


def unpack4(v, i):
    place = lanes(v.shape[0]) & 3
    out = v
    for m in range(4):
        if m != i:
            out = jnp.where(place == m, moved(v, m - i), out)
    return out


def coarser(load, rows, reach):
    def cell(i):
        return load(i, 0, 0) + load(i, 0, 1) + load(i, 1, 0) + load(i, 1, 1)

    al = pair_lanes(cell(0), reach) * 0.125
    bx = pair_lanes(load(1, 0, 0) + load(1, 0, 1), reach) * 0.25
    by = pair_lanes(load(2, 0, 0) + load(2, 1, 0), reach) * 0.25
    bz = low_lanes(cell(3), reach) * 0.25
    return al, bx, by, bz


def pack_kernel(b, al, bx, by, bz, a, lo_out, hi_out, xs_out, raw, sems):
    wide, narrow = lax.axis_index("wide"), lax.axis_index("narrow")
    par = lax.rem(wide, 2)
    copies = [pltpu.make_async_copy(ref, a.at[i], sems.at[i]) for i, ref in enumerate((b, al, bx, by, bz))]
    for c in copies:
        c.start()
    for c in copies:
        c.wait()
    row = lax.broadcasted_iota(jnp.int32, (PAD, PZ), 0)
    first_row = jnp.logical_and(row == 0, jnp.broadcast_to(narrow, (PAD, PZ)) == 0)
    a[BX, 0] = jnp.where(jnp.broadcast_to(wide, (PY, PZ)) == 0, 0.0, a[BX, 0])
    first_z = lanes(PY) == 0
    for p in range(PX):
        a[BY, p, :PAD] = jnp.where(first_row, 0.0, a[BY, p, :PAD])
        a[BZ, p] = jnp.where(first_z, 0.0, a[BZ, p])
    got = []
    for c in range(2):

        def load(i, k, row):
            return a[i + 1, 2 * c + k, pl.ds(row, H1, 2), :]

        got.append(coarser(load, H1, 1))
    for i in range(4):
        v = pack2(got[0][i], got[1][i])
        raw[i] = v
        lo_out[pl.ds(SIDE + G1 * i, G1), :] = v[:G1]
        hi_out[pl.ds(SIDE + G1 * i, G1), :] = v[H1 - G1 :]
    for i in range(5):
        for p in range(PX):
            here = pl.ds((PX * i + p) * HY, HY)
            lo_out[here, :] = a[i, p, :HY]
            hi_out[here, :] = a[i, p, PY - HY :]
        for p in range(3):
            xs_out[3 * i + p] = a[i, par + p]
    xs_out[15] = a[BX, 3]


def corner_kernel(a, raw, lo, hi, _, sw, xs):
    par = parity()
    for i in range(5):
        for p in range(PX):
            k = PX * i + p
            sw[pl.ds(k * EY, HY), :] = lo[pl.ds(k * HY, HY), :]
            sw[pl.ds(k * EY + HY, PY), :] = a[i, p]
            sw[pl.ds(k * EY + HY + PY, HY), :] = hi[pl.ds(k * HY, HY), :]
        for p in range(3):
            here = pl.ds(pl.multiple_of((PX * i + p + par) * HY, HY), HY)
            xs[3 * i + p, :HY] = lo[here, :]
            xs[3 * i + p, HY:] = hi[here, :]
    here = pl.ds((PX * BX + 3) * HY, HY)
    xs[15, :HY] = lo[here, :]
    xs[15, HY:] = hi[here, :]
    for i in range(4):
        here = pl.ds(SIDE + G1 * i, G1)
        base = RAW + R1 * i
        sw[pl.ds(base, G1), :] = lo[here, :]
        sw[pl.ds(base + G1, H1), :] = raw[i]
        sw[pl.ds(base + G1 + H1, G1), :] = hi[here, :]


Q0 = 3


def fine_kernel(own, sw, xs, cxs, rhs, rhs_lo, rhs_hi, edge, xedge, pre, w, cc, sx, sf, d, x, y, z, t):
    par = parity()
    near = 7 * (1 - par)
    far = 7 * par

    def plane(ref, k, r0=0, n=EY):
        return ref[pl.ds(pl.multiple_of(k * EY + r0, 8) if (r0 % 8 == 0) else k * EY + r0, n), :]

    for p in range(PX):
        sx[Q0 + p] = plane(own, PX * BX + p)
    for k in range(3):
        sx[near + k] = plane(sw, PX * BX + par + k)
    sx[10 + par] = plane(sw, PX * BX + 3)

    def joined(dst, i):
        dst[:HY] = cxs[i, :HY]
        dst[HY : HY + PY] = xs[i]
        dst[HY + PY :] = cxs[i, HY:]

    for k in range(3):
        joined(sx.at[far + k], 3 * BX + k)
    joined(sx.at[11 - par], 15)
    for j, i in enumerate((B, ALPHA, BY, BZ)):
        for k in range(3):
            joined(sf.at[3 * j + k], 3 * i + k)
    clear_pads(x, EY)
    clear_pads(y, EY)
    chunk = 40

    def prepare(q, get):
        for r0 in range(0, EY, chunk):
            here = pl.ds(r0, chunk)

            def load(i):
                return lambda r, n: get(i, r, n)

            dd, inv, w6 = faces(
                load(ALPHA)(r0, chunk), sx[q, here, :], sx[q + 1, here, :], load(BY)(r0, chunk),
                next_rows(load(BY), r0, chunk, EY), load(BZ)(r0, chunk), 1, 1.0,
            )
            for a, f in enumerate(w6):
                w[a, q, here, :] = f
            c0 = inv * load(B)(r0, chunk)
            cc[q, here, :] = c0
            x[q, pl.ds(PAD + r0, chunk), :] = c0 * (1.0 / THETA)
            d[q, here, :] = dd

    for p in range(PX):
        prepare(Q0 + p, lambda i, r, n: plane(own, PX * i + p, r, n))
    for k in range(3):
        prepare(near + k, lambda i, r, n: plane(sw, PX * i + par + k, r, n))
    slot = {B: 0, ALPHA: 1, BY: 2, BZ: 3}
    for k in range(3):
        prepare(far + k, lambda i, r, n: sf[3 * slot[i] + k, pl.ds(r, n), :])

    rows = (0, EY)
    sweep(x, None, cc, w, 1, 9, rows, 1, 1, into(y), chunk)
    sweep(y, x, cc, w, 2, 8, rows, 1, 2, into(z), chunk)
    got = []
    for c in range(2):
        for r0 in range(0, EY, chunk):
            v = 0.0
            for q in (Q0 + 2 * c, Q0 + 2 * c + 1):
                _, zz = defect(z, cc, w, q, r0, chunk, 1, q, 0, q, 0)
                v = v + d[q, pl.ds(r0, chunk), :] * zz
            t[c, pl.ds(r0, chunk), :] = v
        got.append(pair_lanes(t[c, pl.ds(HY, H1, 2), :] + t[c, pl.ds(HY + 1, H1, 2), :], 1) * 0.125)
    v = pack2(got[0], got[1])
    rhs[...] = v
    rhs_lo[...] = v[:G1]
    rhs_hi[...] = v[H1 - G1 :]
    mid = pl.ds(PAD, EY)
    edge[...] = z[Q0 + 2 - par, mid, :]
    xedge[...] = z[Q0 + 1 + par, mid, :]
    for p in range(6):
        pre[p] = z[Q0 - 1 + p, mid, :]


def extend_kernel(lo, rhs, hi, edge, _, send):
    send[:G1] = lo[...]
    send[pl.ds(G1, H1), :] = rhs[...]
    send[pl.ds(G1 + H1, G1), :] = hi[...]
    send[pl.ds(R1, EY), :] = edge[...]


C0 = 8
M0 = 5


def place_coefficients(s, i, e, v):
    v0, v1 = unpack2(v)
    s[i, 2 * e, pl.ds(PAD, R1), :] = v0
    s[i, 2 * e + 1, pl.ds(PAD, R1), :] = v1


def middle_faces(s, w1, inv1, d1, q):
    for r0 in range(0, R1, 32):
        here, up, out = pl.ds(PAD + r0, 32), pl.ds(PAD + r0 + 1, 32), pl.ds(r0, 32)
        dd, inv, w6 = faces(
            s[0, q, here, :], s[1, q, here, :], s[1, q + 1, here, :], s[2, q, here, :], s[2, q, up, :],
            s[3, q, here, :], 2, 0.25,
        )
        for a, f in enumerate(w6):
            w1[a, q, out, :] = f
        inv1[q, out, :] = inv
        d1[q, out, :] = dd


def sides(par, k):
    lower, upper = 3 - k, 6 + k
    return jnp.where(par == 0, lower, upper), jnp.where(par == 0, upper, lower)


def near_coefficients_kernel(own, other, one, two, s, w1, inv1, d1):
    par = parity()
    for i in range(4):
        s[i, 20, :, :] = jnp.zeros((R1 + 2 * PAD, PZ), F32)
        s[i, :, PAD + R1 :, :] = jnp.zeros((21, PAD, PZ), F32)
        place_coefficients(s, i, 4 + par, own[i])
        place_coefficients(s, i, 5 - par, other[i])
        for k in range(4):
            ref = one if k < 2 else two
            place_coefficients(s, i, sides(par, k)[0], ref[4 * (k % 2) + i])
    for k in range(11):
        middle_faces(s, w1, inv1, d1, 8 * par + k)


def level2_load(s, c):
    def load(i, k, row):
        return s[i, 2 * c + k, pl.ds(PAD + row, R2, 2), :]

    return load


def coarse_coefficients_kernel(s, w2, inv2, last, s2):
    def coarsen(c):
        for i, v in enumerate(coarser(level2_load(s, c), R2, 2)):
            s2[i, c, pl.ds(0, R2), :] = v

    s2[2, :, R2:, :] = jnp.zeros((10, PAD, PZ), F32)
    planes(0, 10, coarsen, 10)
    body = pl.ds(0, R2)

    def scale(c):
        _, inv, w6 = faces(
            s2[0, c, body, :], s2[1, c, body, :], s2[1, c + 1, body, :], s2[2, c, body, :], s2[2, c, pl.ds(1, R2), :],
            s2[3, c, body, :], 4, 0.0625,
        )
        for a, f in enumerate(w6):
            w2[a, c + 1] = f
        inv2[c + 1] = inv

    planes(0, 9, scale, 9)
    for i in range(4):
        last[i] = s2[i, 9]


def join_kernel(one, two, raw_one, raw_two, out):
    out[pl.ds(0, 2 * R1), :] = one[pl.ds(0, 2 * R1), :]
    out[pl.ds(2 * R1, 2 * R1), :] = two[...]
    for k in range(8):
        out[pl.ds((4 + k) * R1, R1), :] = raw_one[k]
        out[pl.ds((12 + k) * R1, R1), :] = raw_two[k]


def middle_kernel(own, other, one, two, its, s_in, w_in, inv_in, d_in, edge, cc, pre, rhs, s, w, inv, d, x, y, z, t, u):
    par = parity()
    clear_pads(x, R1)
    clear_pads(y, R1)
    for k in range(4):
        e = sides(par, k)[1]
        for i in range(4):
            place_coefficients(s, i, e, its[pl.ds((4 + 4 * k + i) * R1, R1), :])
    for k in range(9):
        middle_faces(s, w, inv, d, 11 - 11 * par + k)

    def place(e, v):
        for k, b in enumerate(unpack2(v)):
            q = 2 * e + k
            c0 = inv[q] * b
            cc[q] = c0
            x[q, pl.ds(PAD, R1), :] = c0 * (1.0 / THETA)

    place(4 + par, own[pl.ds(0, R1), :])
    place(5 - par, other[pl.ds(0, R1), :])
    for k in range(4):
        e, f = sides(par, k)
        ref = one if k < 2 else two
        place(e, ref[pl.ds((k % 2) * R1, R1), :])
        place(f, its[pl.ds(k * R1, R1), :])

    rows = (0, R1)
    sweep(x, None, cc, w, 2, 18, rows, 2, 1, into(y), 32)
    sweep(y, x, cc, w, 3, 17, rows, 2, 2, into(z), 32)

    def residual(c):
        for r0 in range(0, R1, 32):
            v = 0.0
            for k in range(2):
                q = 4 + 2 * c + k
                _, zz = defect(z, cc, w, q, r0, 32, 2, q, 0, q, 0)
                v = v + d[q, pl.ds(r0, 32), :] * zz
            t[c, pl.ds(r0, 32), :] = v
        rhs[c] = pair_lanes(t[c, pl.ds(0, R2, 2), :] + t[c, pl.ds(1, R2, 2), :], 2) * 0.125

    planes(0, 6, residual, 6)

    def first(k, plane):
        load = level2_load(s, plane + 4)
        al, bx, by, bz = coarser(load, R2, 2)
        after = level2_load(s, plane + 5)
        bx1 = pair_lanes(after(1, 0, 0) + after(1, 0, 1), 2) * 0.25
        u[k, pl.ds(0, R2), :] = by
        u[k, pl.ds(R2, PAD), :] = jnp.zeros((PAD, PZ), F32)
        _, inv2, _ = faces(al, bx, bx1, by, u[k, pl.ds(1, R2), :], bz, 4, 0.0625)
        return inv2 * rhs[plane + 2] * (1.0 / THETA), bx

    up = pack4([rhs[1 + 2], rhs[0 + 2], first(0, -1)[0]])
    down = pack4([rhs[0 + 2], rhs[1 + 2], *first(1, 2)])
    edge[...] = jnp.where(jnp.broadcast_to(par, up.shape) == 0, down, up)
    for p in range(10):
        pre[p] = z[C0 - 3 + p, pl.ds(PAD, R1), :]


def last_kernel(mine, its, rhs, w2, inv2, last, pre1, w1, c1, pre0, sw, xs, w0, c0, out,
                wx, c2, x2, y2, z2, x1, y1, z1, x0, y0):
    par = parity()
    body = pl.ds(PAD, R2)
    upper = jnp.broadcast_to(par, mine.shape) == 1
    lo, hi = jnp.where(upper, its[...], mine[...]), jnp.where(upper, mine[...], its[...])
    clear_pads(x2, R2)
    clear_pads(y2, R2)
    clear_pads(z2, R2)
    _, inv, w6 = faces(
        last[0, :R2], last[1, :R2], unpack4(hi, 3), last[2, :R2], last[2, pl.ds(1, R2), :], last[3, :R2], 4, 0.0625
    )
    for a, f in enumerate(w6):
        wx[a, 0] = f

    def start(j, b, dinv):
        v = dinv * b
        c2[j] = v
        x2[j, body, :] = v * (1.0 / THETA)

    start(1, unpack4(lo, 1), inv2[1])
    start(2, unpack4(lo, 0), inv2[2])
    for c in range(6):
        start(c + 3, rhs[c], inv2[c + 3])
    start(9, unpack4(hi, 0), inv2[9])
    start(10, unpack4(hi, 1), inv)
    x2[0, body, :] = unpack4(lo, 2)
    x2[11, body, :] = unpack4(hi, 2)
    rows = (0, R2)
    sweep(x2, None, c2, w2, 1, 10, rows, 4, 1, into(y2), R2, unroll=9)
    sweep(x2, None, c2, wx, 10, 11, rows, 4, 1, into(y2), R2, woff=-10)
    sweep(y2, x2, c2, w2, 2, 10, rows, 4, 2, into(z2), R2, unroll=8)
    sweep(z2, y2, c2, w2, 3, 9, rows, 4, 3, into(x2), R2, unroll=6)

    clear_pads(x1, R1)
    clear_pads(y1, R1)
    for q in range(10):
        v = x2[(q - 3) // 2 + M0, body, :]
        z1[q, pl.ds(PAD, R2, 2), :] = v
        z1[q, pl.ds(PAD + 1, R2, 2), :] = v
        x1[q, pl.ds(PAD, R1), :] = pre1[q] + z1[q, pl.ds(PAD, R1), :]
    rows = (0, R1)
    off = C0 - 3
    sweep(x1, None, c1, w1, 1, 9, rows, 2, 0, into(y1), 32, woff=off, coff=off)
    sweep(y1, x1, c1, w1, 2, 8, rows, 2, 1, into(z1), 32, woff=off, coff=off, unroll=6)

    clear_pads(x0, EY)
    clear_pads(y0, EY)
    near, far = 7 - 7 * par, 7 * par
    body = pl.ds(PAD, EY)
    for q in range(8):
        v = z1[(q - 2) // 2 + 3 + 2 * par, pl.ds(PAD + 12, EY // 2), :]
        x0[q, pl.ds(PAD, EY // 2, 2), :] = v
        x0[q, pl.ds(PAD + 1, EY // 2, 2), :] = v
        if 0 < q < 7:
            x0[q, body, :] += pre0[q - 1]
    x0[near, body, :] += sw[pl.ds(R1, EY), :]
    x0[far, body, :] += xs[pl.ds(2 * R1, EY), :]
    off = Q0 - 2
    sweep(x0, None, c0, w0, 1, 7, (0, EY), 1, 0, into(y0), 40, woff=off, coff=off, unroll=6)

    def finish(q, r0, n, v):
        out[q - 2, pl.ds(r0 - 8, n), :] = v

    sweep(y0, x0, c0, w0, 2, 6, (8, 8 + PY), 1, 1, finish, 32, woff=off, coff=off, unroll=4)


def swap(v):
    return lax.ppermute(v, "wide", [(i, i ^ 1) for i in range(lax.axis_size("wide"))])


def across(v, chips):
    count = lax.axis_size("wide")
    step = 2 * chips - 1
    pairs = [(i, i + step) for i in range(1, count, 2) if i + step < count]
    pairs += [(i, i - step) for i in range(0, count, 2) if i - step >= 0]
    return lax.ppermute(v, "wide", pairs)


def shifted(v, axis, step):
    count = lax.axis_size(axis)
    return lax.ppermute(v, axis, [(i, i + step) for i in range(count) if 0 <= i + step < count])


def shards(right_side, alpha_coef, beta_x, beta_y, beta_z):
    a, ylo, yhi, xs, raw = call(
        pack_kernel, "pack",
        (shape(5, PX, PY, PZ), shape(SIDE + 4 * G1, PZ), shape(SIDE + 4 * G1, PZ), shape(16, PY, PZ),
         shape(4, H1, PZ)),
        (VMEM,) * 5, [ANY] * 5, [pltpu.SemaphoreType.DMA((5,))], 1000,
    )(*[pltpu.with_memory_space_constraint(v, pltpu.HBM) for v in (right_side, alpha_coef, beta_x, beta_y, beta_z)])
    lo = shifted(yhi, "narrow", 1)
    hi = shifted(ylo, "narrow", -1)
    xs = across(xs, 1)
    own, cxs = call(
        corner_kernel, "corners", (shape(RAW + 4 * R1, PZ), shape(16, 2 * HY, PZ)), (VMEM,) * 2,
        [VMEM] * 4 + [ANY], [], 1000,
    )(a, raw, lo, hi, xs)
    sw = swap(own)
    cxs = across(cxs, 1)

    raw_own, raw_other = own[RAW:].reshape(4, R1, PZ), sw[RAW:].reshape(4, R1, PZ)
    raw1 = jnp.concatenate([raw_own, raw_other], 0)
    raw1_one, raw1_two = across(raw1, 1), across(raw1, 2)

    rhs, rhs_lo, rhs_hi, edge0, xedge0, pre0, w0, c0 = call(
        fine_kernel, "level0_pre",
        (shape(H1, PZ), shape(G1, PZ), shape(G1, PZ), shape(EY, PZ), shape(EY, PZ), shape(6, EY, PZ),
         shape(6, 10, EY, PZ), shape(10, EY, PZ)),
        (VMEM,) * 8, [VMEM] * 4,
        [scratch(12, EY, PZ), scratch(12, EY, PZ), scratch(10, EY, PZ)] + [scratch(10, EY + 2 * PAD, PZ)] * 3
        + [scratch(2, EY, PZ)],
        20000000000,
    )(own, sw, xs, cxs)
    rhs_below = shifted(rhs_hi, "narrow", 1)
    rhs_above = shifted(rhs_lo, "narrow", -1)
    s1, w1, inv1, d1 = call(
        near_coefficients_kernel, "near_coefficients",
        (shape(4, 21, R1 + 2 * PAD, PZ), shape(6, 20, R1, PZ), shape(20, R1, PZ), shape(20, R1, PZ)),
        (VMEM,) * 4, [VMEM] * 4, [], 20000000000,
    )(raw_own, raw_other, raw1_one, raw1_two)
    send = call(extend_kernel, "extend", shape(R1 + EY, PZ), VMEM, [VMEM] * 4 + [ANY], [], 1000)(
        rhs_below, rhs, rhs_above, edge0, d1
    )

    other = swap(send)
    pair = jnp.concatenate([send[:R1], other[:R1], xedge0], 0)
    one = across(pair, 1)
    two = across(pair[: 2 * R1], 2)
    mine = call(join_kernel, "join", shape(20 * R1, PZ), VMEM, [VMEM] * 4, [], 1000)(
        one, two, raw1_one, raw1_two
    )
    its = swap(mine)

    edge, c1, pre1, rhs2, s1, w1, _, _ = call(
        middle_kernel, "level1_pre",
        (shape(R2, PZ), shape(20, R1, PZ), shape(10, R1, PZ), shape(6, R2, PZ),
         shape(4, 21, R1 + 2 * PAD, PZ), shape(6, 20, R1, PZ), shape(20, R1, PZ), shape(20, R1, PZ)),
        (VMEM,) * 8, [VMEM] * 9,
        [scratch(20, R1 + 2 * PAD, PZ)] * 3 + [scratch(6, R1, PZ), scratch(2, R2 + PAD, PZ)],
        4000000, aliases={5: 4, 6: 5, 7: 6, 8: 7},
    )(send, other, one, two, its, s1, w1, inv1, d1)

    w2, inv2, last2 = call(
        coarse_coefficients_kernel, "level2_coefficients",
        (shape(6, 12, R2, PZ), shape(12, R2, PZ), shape(4, R2 + PAD, PZ)),
        (VMEM,) * 3, [VMEM], [scratch(4, 10, R2 + PAD, PZ)], 4000000,
    )(s1)
    mine2 = across(edge, 2)
    its2 = swap(mine2)
    return call(
        last_kernel, "coarse_and_post", shape(PX, PY, PZ), VMEM, [VMEM] * 14,
        [scratch(6, 1, R2, PZ), scratch(12, R2, PZ)] + [scratch(12, R2 + 2 * PAD, PZ)] * 3
        + [scratch(10, R1 + 2 * PAD, PZ)] * 3 + [scratch(8, EY + 2 * PAD, PZ)] * 2,
        4000000,
    )(mine2, its2, rhs2, w2, inv2, last2, pre1, w1, c1, pre0, other, one, w0, c0)


def solution(mesh):
    spec = P("wide", "narrow", None)
    return jax.shard_map(shards, mesh=mesh, in_specs=(spec,) * 5, out_specs=spec, check_vma=False)
```

time: 313 us -> 81.7 us (0.26)
  the two profiles are of different devices: /device:TPU:199 before, /device:TPU:223 now
where the time goes in v2:
time: 81.7 us; the launch traced here: 81.2 us
  starting transfers between devices  50.3 us (62%)
  waiting for transfers between devices  21.6 us (26%)
  Pallas kernels  8.93 us (11%)
    ppermute x7, starting transfers between devices, across(): return lax.ppermute(v, 'wide', pairs)  30.7 us
    ppermute x7, waiting for transfers between devices, across(): return lax.ppermute(v, 'wide', pairs)  12 us
    ppermute x4, starting transfers between devices, shifted(): lax.ppermute(v, axis, [(i, i + step) for i in range(count) if 0 <= i + st...  11.6 us
    ppermute x4, starting transfers between devices, swap(): lax.ppermute(v, 'wide', [(i, i ^ 1) for i in range(lax.axis_size('wide'))])  8.04 us
    ppermute x4, waiting for transfers between devices, shifted(): lax.ppermute(v, axis, [(i, i + step) for i in range(count) if 0 <= i + st...  5.99 us
    ppermute x4, waiting for transfers between devices, swap(): lax.ppermute(v, 'wide', [(i, i ^ 1) for i in range(lax.axis_size('wide'))])  3.64 us
    pallas_call x1, Pallas kernels, shards(): call(middle_kernel, 'level1_pre', (shape(R2, PZ), shape(20, R1, PZ), shap...  2.86 us
    pallas_call x1, Pallas kernels, shards(): call(last_kernel, 'coarse_and_post', shape(PX, PY, PZ), VMEM, [VMEM] * 14...  1.94 us
  transfers between devices with their start and end apart: 15, of which 8 were waited for; matrix products, arithmetic and copies ran while one was open for 0% of the time, Pallas kernels for 3%

profile of v2, /device:TPU:223, one launch (start us, length us, event | category | flops | bytes accessed | tf_op | source)
XLA Modules:
  0.0 81.2 jit_solution(2566385358931086655)
XLA Ops:
  0.0 1.4 %pack.1 = (f32[5,4,64,128]{3,2,1,0:T(8,128)S(1)}, f32[224,128]{1,0:T(8,128)S(1)}, f32[224,128]{1,0:T(8,128)S(1)}, f32[16,64,128]{2,1,0:T(8,128)S(1)}, f32[4,32,128]{2,1,0:T(8,128)S(1)}) custom-call(f32[4,64,128]{2,1,0:T(8,128)} %b.1, f32[4,64,128]{2,1,0:T(8,128)} %al.1, f32[4,64,128]{2,1,0:T(8,128)} %bx.1, f32[4,64,128]{2,1,0:T(8,128)} %by.1, f32[4,64,128]{2,1,0:T(8,128)} %bz.1), custom_call_target="tpu_custom_call" | custom-call | flops 1000 | tf_op jit(solution)/shard_map/pack/pallas_call | solution.py:562
  1.4 5.7 %collective-permute-start.2 = (f32[16,64,128]{2,1,0:T(8,128)S(1)}, f32[16,64,128]{2,1,0:T(8,128)S(1)}, u32[]{:S(2)}, u32[]{:S(2)}) collective-permute-start(f32[16,64,128]{2,1,0:T(8,128)S(1)} %get-tuple-element.37), channel_id=1, source_target_pairs={{8,16},{24,32},{40,48},{56,64},{72,80},{88,96},{104,112},{120,128}... | collective-permute-start | bytes 1572872 | tf_op jit(solution)/shard_map/ppermute | solution.py:553
  7.1 4.4 %collective-permute-start = (f32[224,128]{1,0:T(8,128)S(1)}, f32[224,128]{1,0:T(8,128)S(1)}, u32[]{:S(2)}, u32[]{:S(2)}) collective-permute-start(f32[224,128]{1,0:T(8,128)S(1)} %get-tuple-element.35), channel_id=1, source_target_pairs={{0,1},{1,2},{2,3},{3,4},{4,5},{5,6},{6,7},{8,9},{9,10},{10,11},{11... | collective-permute-start | bytes 344072 | tf_op jit(solution)/shard_map/ppermute | solution.py:558
  11.5 1.9 %collective-permute-start.1 = (f32[224,128]{1,0:T(8,128)S(1)}, f32[224,128]{1,0:T(8,128)S(1)}, u32[]{:S(2)}, u32[]{:S(2)}) collective-permute-start(f32[224,128]{1,0:T(8,128)S(1)} %get-tuple-element.36), channel_id=1, source_target_pairs={{1,0},{2,1},{3,2},{4,3},{5,4},{6,5},{7,6},{9,8},{10,9},{11,10},{12... | collective-permute-start | bytes 344072 | tf_op jit(solution)/shard_map/ppermute | solution.py:558
  13.4 0.0 collective-permute-done.lo
  13.4 4.8 %collective-permute-done.1.hi = f32[224,128]{1,0:T(8,128)S(1)} collective-permute-done((f32[224,128]{1,0:T(8,128)S(1)}, f32[224,128]{1,0:T(8,128)S(1)}, u32[]{:S(2)}, u32[]{:S(2)}) %collective-permute-start.1) | collective-permute-done | bytes 114720 | tf_op jit(solution)/shard_map/ppermute | solution.py:558
  18.2 0.0 collective-permute-done.2._.xs
  18.3 0.1 corners.1
  18.3 1.9 %collective-permute-start.3 = (f32[1856,128]{1,0:T(8,128)S(1)}, f32[1856,128]{1,0:T(8,128)S(1)}, u32[]{:S(2)}, u32[]{:S(2)}) collective-permute-start(f32[1856,128]{1,0:T(8,128)S(1)} %get-tuple-element.38.own), channel_id=1, source_target_pairs={{0,8},{8,0},{16,24},{24,16},{32,40},{40,32},{48,56},{56,48},{64,72... | collective-permute-start | bytes 2850824 | tf_op jit(solution)/shard_map/ppermute | solution.py:545
  20.3 4.9 %collective-permute-start.4 = (f32[16,16,128]{2,1,0:T(8,128)S(1)}, f32[16,16,128]{2,1,0:T(8,128)S(1)}, u32[]{:S(2)}, u32[]{:S(2)}) collective-permute-start(f32[16,16,128]{2,1,0:T(8,128)S(1)} %get-tuple-element.39), channel_id=1, source_target_pairs={{8,16},{24,32},{40,48},{56,64},{72,80},{88,96},{104,112},{120,128}... | collective-permute-start | bytes 393224 | tf_op jit(solution)/shard_map/ppermute | solution.py:553
  25.2 0.0 collective-permute-done.3.sw
  25.3 3.5 %collective-permute-start.8 = (f32[8,64,128]{2,1,0:T(8,128)S(1)}, f32[8,64,128]{2,1,0:T(8,128)S(1)}, u32[]{:S(2)}, u32[]{:S(2)}) collective-permute-start(f32[8,64,128]{2,1,0:T(8,128)S(1)} %pad_maximum_fusion), channel_id=1, source_target_pairs={{8,32},{24,48},{40,64},{56,80},{72,96},{88,112},{104,128},{120,144... | collective-permute-start | bytes 786440 | tf_op jit(solution)/shard_map/ppermute | solution.py:553
  28.7 4.0 %collective-permute-start.7 = (f32[8,64,128]{2,1,0:T(8,128)S(1)}, f32[8,64,128]{2,1,0:T(8,128)S(1)}, u32[]{:S(2)}, u32[]{:S(2)}) collective-permute-start(f32[8,64,128]{2,1,0:T(8,128)S(1)} %pad_maximum_fusion), channel_id=1, source_target_pairs={{8,16},{24,32},{40,48},{56,64},{72,80},{88,96},{104,112},{120,128}... | collective-permute-start | bytes 786440 | tf_op jit(solution)/shard_map/ppermute | solution.py:553
  32.7 0.0 collective-permute-done.4.cxs
  32.7 1.4 %level0_pre.1 = (f32[32,128]{1,0:T(8,128)S(1)}, f32[16,128]{1,0:T(8,128)S(1)}, f32[16,128]{1,0:T(8,128)S(1)}, f32[80,128]{1,0:T(8,128)S(1)}, f32[80,128]{1,0:T(8...) custom-call(f32[1856,128]{1,0:T(8,128)S(1)} %get-tuple-element.38.own, ...), custom_call_target="tpu_custom_call" | custom-call | flops 20000000000 | tf_op jit(solution)/shard_map/level0_pre/pallas_call | solution.py:582
  34.1 1.9 %collective-permute-start.5 = (f32[16,128]{1,0:T(8,128)S(1)}, f32[16,128]{1,0:T(8,128)S(1)}, u32[]{:S(2)}, u32[]{:S(2)}) collective-permute-start(f32[16,128]{1,0:T(8,128)S(1)} %get-tuple-element.40), channel_id=1, source_target_pairs={{0,1},{1,2},{2,3},{3,4},{4,5},{5,6},{6,7},{8,9},{9,10},{10,11},{11... | collective-permute-start | bytes 24584 | tf_op jit(solution)/shard_map/ppermute | solution.py:558
  36.0 3.4 %collective-permute-start.6 = (f32[16,128]{1,0:T(8,128)S(1)}, f32[16,128]{1,0:T(8,128)S(1)}, u32[]{:S(2)}, u32[]{:S(2)}) collective-permute-start(f32[16,128]{1,0:T(8,128)S(1)} %get-tuple-element.42), channel_id=1, source_target_pairs={{1,0},{2,1},{3,2},{4,3},{5,4},{6,5},{7,6},{9,8},{10,9},{11,10},{12... | collective-permute-start | bytes 24584 | tf_op jit(solution)/shard_map/ppermute | solution.py:558
  39.4 0.0 collective-permute-done.8.two.raw_two
  39.4 0.4 collective-permute-done.7.one.raw_one
  39.8 0.8 %near_coefficients.1 = (f32[4,21,80,128]{3,2,1,0:T(8,128)S(1)}, f32[6,20,64,128]{3,2,1,0:T(8,128)S(1)}, f32[20,64,128]{2,1,0:T(8,128)S(1)}, f32[20,64,128]{2,1,0:T(8,128)S(1)}) custom-call(f32[4,64,128]{2,1,0:T(8,128)S(1)} %bitcast.3, f32[4,64,128]{2,1,0:T(8,128)S(1)} %bitcast.5, f32[8,64,128]{2,1,0:T(8,128)S(1)} %collective-permute-done.7.one.raw_one, ...), custom_call_target="tpu_custom_call" | custom-call | flops 20000000000 | tf_op jit(solution)/shard_map/near_coefficients/pallas_call | solution.py:593
  40.6 0.0 collective-permute-done.5.lo
  40.6 1.2 %collective-permute-done.6.hi = f32[16,128]{1,0:T(8,128)S(1)} collective-permute-done((f32[16,128]{1,0:T(8,128)S(1)}, f32[16,128]{1,0:T(8,128)S(1)}, u32[]{:S(2)}, u32[]{:S(2)}) %collective-permute-start.6) | collective-permute-done | bytes 8224 | tf_op jit(solution)/shard_map/ppermute | solution.py:558
  41.8 2.3 %collective-permute-start.9 = (f32[144,128]{1,0:T(8,128)S(1)}, f32[144,128]{1,0:T(8,128)S(1)}, u32[]{:S(2)}, u32[]{:S(2)}) collective-permute-start(f32[144,128]{1,0:T(8,128)S(1)} %extend.1.own), channel_id=1, source_target_pairs={{0,8},{8,0},{16,24},{24,16},{32,40},{40,32},{48,56},{56,48},{64,72... | collective-permute-start | bytes 221192 | tf_op jit(solution)/shard_map/ppermute | solution.py:545
  44.1 0.9 %collective-permute-done.9.other.sw = f32[144,128]{1,0:T(8,128)S(1)} collective-permute-done((f32[144,128]{1,0:T(8,128)S(1)}, f32[144,128]{1,0:T(8,128)S(1)}, u32[]{:S(2)}, u32[]{:S(2)}) %collective-permute-start.9) | collective-permute-done | bytes 73760 | tf_op jit(solution)/shard_map/ppermute | solution.py:545
  45.0 6.4 %collective-permute-start.10 = (f32[208,128]{1,0:T(8,128)S(1)}, f32[208,128]{1,0:T(8,128)S(1)}, u32[]{:S(2)}, u32[]{:S(2)}) collective-permute-start(f32[208,128]{1,0:T(8,128)S(1)} %pad_maximum_fusion.1), channel_id=1, source_target_pairs={{8,16},{24,32},{40,48},{56,64},{72,80},{88,96},{104,112},{120,128}... | collective-permute-start | bytes 319496 | tf_op jit(solution)/shard_map/ppermute | solution.py:553
  51.4 3.1 %collective-permute-start.11 = (f32[128,128]{1,0:T(8,128)S(1)}, f32[128,128]{1,0:T(8,128)S(1)}, u32[]{:S(2)}, u32[]{:S(2)}) collective-permute-start(f32[128,128]{1,0:T(8,128)S(1)} %pad_maximum_fusion.2), channel_id=1, source_target_pairs={{8,32},{24,48},{40,64},{56,80},{72,96},{88,112},{104,128},{120,144... | collective-permute-start | bytes 196616 | tf_op jit(solution)/shard_map/ppermute | solution.py:553
  54.5 6.1 %collective-permute-done.11.two = f32[128,128]{1,0:T(8,128)S(1)} collective-permute-done((f32[128,128]{1,0:T(8,128)S(1)}, f32[128,128]{1,0:T(8,128)S(1)}, u32[]{:S(2)}, u32[]{:S(2)}) %collective-permute-start.11) | collective-permute-done | bytes 65568 | tf_op jit(solution)/shard_map/ppermute | solution.py:553
  60.6 0.0 collective-permute-done.10.one.xs
  60.6 1.9 %collective-permute-start.12 = (f32[1280,128]{1,0:T(8,128)S(1)}, f32[1280,128]{1,0:T(8,128)S(1)}, u32[]{:S(2)}, u32[]{:S(2)}) collective-permute-start(f32[1280,128]{1,0:T(8,128)S(1)} %join.1), channel_id=1, source_target_pairs={{0,8},{8,0},{16,24},{24,16},{32,40},{40,32},{48,56},{56,48},{64,72... | collective-permute-start | bytes 1966088 | tf_op jit(solution)/shard_map/ppermute | solution.py:545
  62.5 2.1 %collective-permute-done.12.its = f32[1280,128]{1,0:T(8,128)S(1)} collective-permute-done((f32[1280,128]{1,0:T(8,128)S(1)}, f32[1280,128]{1,0:T(8,128)S(1)}, u32[]{:S(2)}, u32[]{:S(2)}) %collective-permute-start.12) | collective-permute-done | bytes 655392 | tf_op jit(solution)/shard_map/ppermute | solution.py:545
  64.6 2.9 %level1_pre.1 = (f32[32,128]{1,0:T(8,128)S(1)}, f32[20,64,128]{2,1,0:T(8,128)S(1)}, f32[10,64,128]{2,1,0:T(8,128)S(1)}, f32[6,32,128]{2,1,0:T(8,128)S(1)}, f32[4...) custom-call(f32[144,128]{1,0:T(8,128)S(1)} %extend.1.own, ...), custom_call_target="tpu_custom_call", output_to_operand_aliasing={{4}: (5, {}), {5}: (6, {}), {6}: (7, {}), {7}: (8, {})} | custom-call | flops 4000000 | tf_op jit(solution)/shard_map/level1_pre/pallas_call | solution.py:611
  67.5 3.1 %collective-permute-start.13 = (f32[32,128]{1,0:T(8,128)S(1)}, f32[32,128]{1,0:T(8,128)S(1)}, u32[]{:S(2)}, u32[]{:S(2)}) collective-permute-start(f32[32,128]{1,0:T(8,128)S(1)} %get-tuple-element.49), channel_id=1, source_target_pairs={{8,32},{24,48},{40,64},{56,80},{72,96},{88,112},{104,128},{120,144... | collective-permute-start | bytes 49160 | tf_op jit(solution)/shard_map/ppermute | solution.py:553
  70.6 5.5 %collective-permute-done.13.mine = f32[32,128]{1,0:T(8,128)S(1)} collective-permute-done((f32[32,128]{1,0:T(8,128)S(1)}, f32[32,128]{1,0:T(8,128)S(1)}, u32[]{:S(2)}, u32[]{:S(2)}) %collective-permute-start.13) | collective-permute-done | bytes 16416 | tf_op jit(solution)/shard_map/ppermute | solution.py:553
  76.1 1.9 %collective-permute-start.14 = (f32[32,128]{1,0:T(8,128)S(1)}, f32[32,128]{1,0:T(8,128)S(1)}, u32[]{:S(2)}, u32[]{:S(2)}) collective-permute-start(f32[32,128]{1,0:T(8,128)S(1)} %collective-permute-done.13.mine), channel_id=1, source_target_pairs={{0,8},{8,0},{16,24},{24,16},{32,40},{40,32},{48,56},{56,48},{64,72... | collective-permute-start | bytes 49160 | tf_op jit(solution)/shard_map/ppermute | solution.py:545
  78.1 0.4 level2_coefficients.1
  78.5 0.7 collective-permute-done.14.its
  79.2 1.9 %coarse_and_post.1 = f32[4,64,128]{2,1,0:T(8,128)} custom-call(f32[32,128]{1,0:T(8,128)S(1)} %collective-permute-done.13.mine, f32[32,128]{1,0:T(8,128)S(1)} %collective-permute-done.14.its, f32[6,32,128]{2,1,0:T(8,128)S(1)} %get-tuple-element.50.rhs, f32[6,12,32,128]{3,2,1,0:T(8,128)S(1)} %get-tuple-element.52.w2, ...), custom_call_target="tpu_custom_call" | custom-call | flops 4000000 | tf_op jit(solution)/shard_map/coarse_and_post/pallas_call | solution.py:627
  (9 shorter events, 0.1 us)
Async XLA Ops:
  1.4 16.9 %collective-permute-start.2 = (f32[16,64,128]{2,1,0:T(8,128)S(1)}, f32[16,64,128]{2,1,0:T(8,128)S(1)}, u32[]{:S(2)}, u32[]{:S(2)}) collective-permute-start(f32[16,64,128]{2,1,0:T(8,128)S(1)} %get-tuple-element.37), channel_id=1, source_target_pairs={{8,16},{24,32},{40,48},{56,64},{72,80},{88,96},{104,112},{120,128}... | collective-permute-start | bytes 1572872 | tf_op jit(solution)/shard_map/ppermute | solution.py:553
  7.1 6.4 %collective-permute-start = (f32[224,128]{1,0:T(8,128)S(1)}, f32[224,128]{1,0:T(8,128)S(1)}, u32[]{:S(2)}, u32[]{:S(2)}) collective-permute-start(f32[224,128]{1,0:T(8,128)S(1)} %get-tuple-element.35), channel_id=1, source_target_pairs={{0,1},{1,2},{2,3},{3,4},{4,5},{5,6},{6,7},{8,9},{9,10},{10,11},{11... | collective-permute-start | bytes 344072 | tf_op jit(solution)/shard_map/ppermute | solution.py:558
  11.5 6.7 %collective-permute-start.1 = (f32[224,128]{1,0:T(8,128)S(1)}, f32[224,128]{1,0:T(8,128)S(1)}, u32[]{:S(2)}, u32[]{:S(2)}) collective-permute-start(f32[224,128]{1,0:T(8,128)S(1)} %get-tuple-element.36), channel_id=1, source_target_pairs={{1,0},{2,1},{3,2},{4,3},{5,4},{6,5},{7,6},{9,8},{10,9},{11,10},{12... | collective-permute-start | bytes 344072 | tf_op jit(solution)/shard_map/ppermute | solution.py:558
  18.3 6.9 %collective-permute-start.3 = (f32[1856,128]{1,0:T(8,128)S(1)}, f32[1856,128]{1,0:T(8,128)S(1)}, u32[]{:S(2)}, u32[]{:S(2)}) collective-permute-start(f32[1856,128]{1,0:T(8,128)S(1)} %get-tuple-element.38.own), channel_id=1, source_target_pairs={{0,8},{8,0},{16,24},{24,16},{32,40},{40,32},{48,56},{56,48},{64,72... | collective-permute-start | bytes 2850824 | tf_op jit(solution)/shard_map/ppermute | solution.py:545
  20.3 12.5 %collective-permute-start.4 = (f32[16,16,128]{2,1,0:T(8,128)S(1)}, f32[16,16,128]{2,1,0:T(8,128)S(1)}, u32[]{:S(2)}, u32[]{:S(2)}) collective-permute-start(f32[16,16,128]{2,1,0:T(8,128)S(1)} %get-tuple-element.39), channel_id=1, source_target_pairs={{8,16},{24,32},{40,48},{56,64},{72,80},{88,96},{104,112},{120,128}... | collective-permute-start | bytes 393224 | tf_op jit(solution)/shard_map/ppermute | solution.py:553
  25.3 14.1 %collective-permute-start.8 = (f32[8,64,128]{2,1,0:T(8,128)S(1)}, f32[8,64,128]{2,1,0:T(8,128)S(1)}, u32[]{:S(2)}, u32[]{:S(2)}) collective-permute-start(f32[8,64,128]{2,1,0:T(8,128)S(1)} %pad_maximum_fusion), channel_id=1, source_target_pairs={{8,32},{24,48},{40,64},{56,80},{72,96},{88,112},{104,128},{120,144... | collective-permute-start | bytes 786440 | tf_op jit(solution)/shard_map/ppermute | solution.py:553
  28.7 11.0 %collective-permute-start.7 = (f32[8,64,128]{2,1,0:T(8,128)S(1)}, f32[8,64,128]{2,1,0:T(8,128)S(1)}, u32[]{:S(2)}, u32[]{:S(2)}) collective-permute-start(f32[8,64,128]{2,1,0:T(8,128)S(1)} %pad_maximum_fusion), channel_id=1, source_target_pairs={{8,16},{24,32},{40,48},{56,64},{72,80},{88,96},{104,112},{120,128}... | collective-permute-start | bytes 786440 | tf_op jit(solution)/shard_map/ppermute | solution.py:553
  34.1 6.5 %collective-permute-start.5 = (f32[16,128]{1,0:T(8,128)S(1)}, f32[16,128]{1,0:T(8,128)S(1)}, u32[]{:S(2)}, u32[]{:S(2)}) collective-permute-start(f32[16,128]{1,0:T(8,128)S(1)} %get-tuple-element.40), channel_id=1, source_target_pairs={{0,1},{1,2},{2,3},{3,4},{4,5},{5,6},{6,7},{8,9},{9,10},{10,11},{11... | collective-permute-start | bytes 24584 | tf_op jit(solution)/shard_map/ppermute | solution.py:558
  36.0 5.8 %collective-permute-start.6 = (f32[16,128]{1,0:T(8,128)S(1)}, f32[16,128]{1,0:T(8,128)S(1)}, u32[]{:S(2)}, u32[]{:S(2)}) collective-permute-start(f32[16,128]{1,0:T(8,128)S(1)} %get-tuple-element.42), channel_id=1, source_target_pairs={{1,0},{2,1},{3,2},{4,3},{5,4},{6,5},{7,6},{9,8},{10,9},{11,10},{12... | collective-permute-start | bytes 24584 | tf_op jit(solution)/shard_map/ppermute | solution.py:558
  41.8 3.2 %collective-permute-start.9 = (f32[144,128]{1,0:T(8,128)S(1)}, f32[144,128]{1,0:T(8,128)S(1)}, u32[]{:S(2)}, u32[]{:S(2)}) collective-permute-start(f32[144,128]{1,0:T(8,128)S(1)} %extend.1.own), channel_id=1, source_target_pairs={{0,8},{8,0},{16,24},{24,16},{32,40},{40,32},{48,56},{56,48},{64,72... | collective-permute-start | bytes 221192 | tf_op jit(solution)/shard_map/ppermute | solution.py:545
  45.0 15.6 %collective-permute-start.10 = (f32[208,128]{1,0:T(8,128)S(1)}, f32[208,128]{1,0:T(8,128)S(1)}, u32[]{:S(2)}, u32[]{:S(2)}) collective-permute-start(f32[208,128]{1,0:T(8,128)S(1)} %pad_maximum_fusion.1), channel_id=1, source_target_pairs={{8,16},{24,32},{40,48},{56,64},{72,80},{88,96},{104,112},{120,128}... | collective-permute-start | bytes 319496 | tf_op jit(solution)/shard_map/ppermute | solution.py:553
  51.4 9.2 %collective-permute-start.11 = (f32[128,128]{1,0:T(8,128)S(1)}, f32[128,128]{1,0:T(8,128)S(1)}, u32[]{:S(2)}, u32[]{:S(2)}) collective-permute-start(f32[128,128]{1,0:T(8,128)S(1)} %pad_maximum_fusion.2), channel_id=1, source_target_pairs={{8,32},{24,48},{40,64},{56,80},{72,96},{88,112},{104,128},{120,144... | collective-permute-start | bytes 196616 | tf_op jit(solution)/shard_map/ppermute | solution.py:553
  60.6 4.0 %collective-permute-start.12 = (f32[1280,128]{1,0:T(8,128)S(1)}, f32[1280,128]{1,0:T(8,128)S(1)}, u32[]{:S(2)}, u32[]{:S(2)}) collective-permute-start(f32[1280,128]{1,0:T(8,128)S(1)} %join.1), channel_id=1, source_target_pairs={{0,8},{8,0},{16,24},{24,16},{32,40},{40,32},{48,56},{56,48},{64,72... | collective-permute-start | bytes 1966088 | tf_op jit(solution)/shard_map/ppermute | solution.py:545
  67.5 8.7 %collective-permute-start.13 = (f32[32,128]{1,0:T(8,128)S(1)}, f32[32,128]{1,0:T(8,128)S(1)}, u32[]{:S(2)}, u32[]{:S(2)}) collective-permute-start(f32[32,128]{1,0:T(8,128)S(1)} %get-tuple-element.49), channel_id=1, source_target_pairs={{8,32},{24,48},{40,64},{56,80},{72,96},{88,112},{104,128},{120,144... | collective-permute-start | bytes 49160 | tf_op jit(solution)/shard_map/ppermute | solution.py:553
  76.1 3.1 %collective-permute-start.14 = (f32[32,128]{1,0:T(8,128)S(1)}, f32[32,128]{1,0:T(8,128)S(1)}, u32[]{:S(2)}, u32[]{:S(2)}) collective-permute-start(f32[32,128]{1,0:T(8,128)S(1)} %collective-permute-done.13.mine), channel_id=1, source_target_pairs={{0,8},{8,0},{16,24},{24,16},{32,40},{40,32},{48,56},{56,48},{64,72... | collective-permute-start | bytes 49160 | tf_op jit(solution)/shard_map/ppermute | solution.py:545

commit v3 on v2

v3 whole, which is shorter than its diff:
```python
import jax
import jax.numpy as jnp
from jax import lax
from jax.experimental import pallas as pl
from jax.experimental.pallas import tpu as pltpu
from jax.sharding import PartitionSpec as P

F32 = jnp.float32
THETA = (2.0 + 0.25) / 2.0
DELTA = (2.0 - 0.25) / 2.0
SIGMA = THETA / DELTA
RHO = [1.0 / SIGMA]
for _step in range(3):
    RHO.append(1.0 / (2.0 * SIGMA - RHO[-1]))
MOMENTUM = [0.0] + [RHO[k] * RHO[k - 1] for k in range(1, 4)]
GAIN = [1.0 / THETA] + [2.0 * RHO[k] / DELTA for k in range(1, 4)]

PX, PY, PZ = 4, 64, 128
HY = 8
EY = PY + 2 * HY
H1 = PY // 2
G1 = 16
R1 = H1 + 2 * G1
R2 = R1 // 2
RAW = 5 * PX * EY
SIDE = 5 * PX * HY
PAD = 8
SMALL, LARGE = 1000, 2 * 10**10
B, ALPHA, BX, BY, BZ = range(5)
ANY = pl.BlockSpec(memory_space=pl.ANY)
VMEM = pl.BlockSpec(memory_space=pltpu.VMEM)
HBM = pl.BlockSpec(memory_space=pltpu.HBM)


def shape(*dims):
    return jax.ShapeDtypeStruct(dims, F32)


def scratch(*dims):
    return pltpu.VMEM(dims, F32)


def call(kernel, name, out_shape, out_specs, in_specs, scratch_shapes, flops, mib=24, aliases=None):
    return pl.pallas_call(
        kernel,
        out_shape=out_shape,
        in_specs=in_specs,
        out_specs=out_specs,
        scratch_shapes=scratch_shapes,
        compiler_params=pltpu.CompilerParams(vmem_limit_bytes=mib * 1024 * 1024),
        cost_estimate=pl.CostEstimate(flops=flops, bytes_accessed=0, transcendentals=0),
        input_output_aliases=aliases or {},
        name=name,
    )


def parity():
    return lax.rem(lax.axis_index("wide"), 2)


def lanes(rows):
    return lax.broadcasted_iota(jnp.int32, (rows, PZ), 1)


def moved(v, shift):
    return pltpu.roll(v, shift % PZ, 1)


def planes(lo, hi, each, unroll):
    if not unroll:
        each(lo)
        return
    steps = (hi - lo) // unroll

    def body(i, carry):
        for k in range(unroll):
            each(lo + i * unroll + k)
        return carry

    if steps > 1:
        lax.fori_loop(0, steps, body, 0)
    else:
        steps = 0
    for q in range(lo + steps * unroll, hi):
        each(q)


def defect(x_ref, c_ref, w_ref, q, r0, n, reach, cq, cr, wq, wr):
    rows = pl.ds(PAD + r0, n)
    here = pl.ds(wr + r0, n)
    x = x_ref[q, rows, :]
    total = c_ref[cq, pl.ds(cr + r0, n), :] - x
    total += w_ref[0, wq, here, :] * x_ref[q - 1, rows, :]
    total += w_ref[1, wq, here, :] * x_ref[q + 1, rows, :]
    total += w_ref[2, wq, here, :] * x_ref[q, pl.ds(PAD + r0 - 1, n), :]
    total += w_ref[3, wq, here, :] * x_ref[q, pl.ds(PAD + r0 + 1, n), :]
    total += w_ref[4, wq, here, :] * moved(x, reach)
    total += w_ref[5, wq, here, :] * moved(x, -reach)
    return x, total


def sweep(x_ref, prev_ref, c_ref, w_ref, lo, hi, rows, reach, k, store, chunk, woff=0, coff=0, wr=0, cr=0, unroll=8):
    def each(q):
        for r0 in range(rows[0], rows[1], chunk):
            n = min(chunk, rows[1] - r0)
            x, z = defect(x_ref, c_ref, w_ref, q, r0, n, reach, q + coff, cr, q + woff, wr)
            new = x + GAIN[k] * z
            if k > 0:
                gap = x if prev_ref is None else x - prev_ref[q, pl.ds(PAD + r0, n), :]
                new += MOMENTUM[k] * gap
            store(q, r0, n, new)

    planes(lo, hi, each, unroll)


def into(ref):
    def store(q, r0, n, v):
        ref[q, pl.ds(PAD + r0, n), :] = v

    return store


def inverse(d):
    inside = d > 0.0
    return jnp.where(inside, 1.0 / jnp.where(inside, d, 1.0), 0.0)


def faces(alpha, x0, x1, y0, y1, z0, reach, scale):
    z1 = moved(z0, -reach)
    d = alpha + scale * (x0 + x1 + y0 + y1 + z0 + z1)
    inv = inverse(d)
    si = scale * inv
    return d, inv, [si * f for f in (x0, x1, y0, y1, z0, z1)]


def next_rows(load, r0, n, rows):
    if r0 + n < rows:
        return load(r0 + 1, n)
    return pltpu.roll(load(r0, n), n - 1, 0)


def clear_pads(ref, rows):
    ref[:, :PAD, :] = jnp.zeros((ref.shape[0], PAD, PZ), F32)
    ref[:, PAD + rows :, :] = jnp.zeros((ref.shape[0], PAD, PZ), F32)


def pair_lanes(v, reach):
    low = (lanes(v.shape[0]) & reach) == 0
    return v + jnp.where(low, moved(v, -reach), moved(v, reach))


def low_lanes(v, reach):
    low = (lanes(v.shape[0]) & reach) == 0
    return jnp.where(low, v, moved(v, reach))


def pack2(v0, v1):
    return jnp.where((lanes(v0.shape[0]) & 1) == 0, v0, v1)


def unpack2(v):
    even = (lanes(v.shape[0]) & 1) == 0
    return jnp.where(even, v, moved(v, 1)), jnp.where(even, moved(v, -1), v)


def pack4(items):
    place = lanes(items[0].shape[0]) & 3
    out = items[0]
    for i, item in enumerate(items[1:], 1):
        out = jnp.where(place == i, item, out)
    return out


def unpack4(v, i):
    place = lanes(v.shape[0]) & 3
    out = v
    for m in range(4):
        if m != i:
            out = jnp.where(place == m, moved(v, m - i), out)
    return out


def coarser(load, rows, reach):
    def cell(i):
        return load(i, 0, 0) + load(i, 0, 1) + load(i, 1, 0) + load(i, 1, 1)

    al = pair_lanes(cell(0), reach) * 0.125
    bx = pair_lanes(load(1, 0, 0) + load(1, 0, 1), reach) * 0.25
    by = pair_lanes(load(2, 0, 0) + load(2, 1, 0), reach) * 0.25
    bz = low_lanes(cell(3), reach) * 0.25
    return al, bx, by, bz


def pack_kernel(b, al, bx, by, bz, a, lo_out, hi_out, raw, sems):
    wide, narrow = lax.axis_index("wide"), lax.axis_index("narrow")
    copies = [pltpu.make_async_copy(ref, a.at[i], sems.at[i]) for i, ref in enumerate((b, al, bx, by, bz))]
    for c in copies:
        c.start()
    for c in copies:
        c.wait()
    row = lax.broadcasted_iota(jnp.int32, (PAD, PZ), 0)
    first_row = jnp.logical_and(row == 0, jnp.broadcast_to(narrow, (PAD, PZ)) == 0)
    a[BX, 0] = jnp.where(jnp.broadcast_to(wide, (PY, PZ)) == 0, 0.0, a[BX, 0])
    first_z = lanes(PY) == 0
    for p in range(PX):
        a[BY, p, :PAD] = jnp.where(first_row, 0.0, a[BY, p, :PAD])
        a[BZ, p] = jnp.where(first_z, 0.0, a[BZ, p])
    got = []
    for c in range(2):

        def load(i, k, row):
            return a[i + 1, 2 * c + k, pl.ds(row, H1, 2), :]

        got.append(coarser(load, H1, 1))
    for i in range(4):
        v = pack2(got[0][i], got[1][i])
        raw[i] = v
        lo_out[pl.ds(SIDE + G1 * i, G1), :] = v[:G1]
        hi_out[pl.ds(SIDE + G1 * i, G1), :] = v[H1 - G1 :]
    for i in range(5):
        for p in range(PX):
            here = pl.ds((PX * i + p) * HY, HY)
            lo_out[here, :] = a[i, p, :HY]
            hi_out[here, :] = a[i, p, PY - HY :]


def plane(ref, k, r0=0, n=EY):
    start = k * EY + r0
    return ref[pl.ds(pl.multiple_of(start, 8) if r0 % 8 == 0 else start, n), :]


def corner_kernel(a, raw, lo, hi, sw, xs, x):
    par = parity()
    for i in range(5):
        for p in range(PX):
            k = PX * i + p
            sw[pl.ds(k * EY, HY), :] = lo[pl.ds(k * HY, HY), :]
            sw[pl.ds(k * EY + HY, PY), :] = a[i, p]
            sw[pl.ds(k * EY + HY + PY, HY), :] = hi[pl.ds(k * HY, HY), :]
    for i in range(4):
        here = pl.ds(SIDE + G1 * i, G1)
        base = RAW + R1 * i
        sw[pl.ds(base, G1), :] = lo[here, :]
        sw[pl.ds(base + G1, H1), :] = raw[i]
        sw[pl.ds(base + G1 + H1, G1), :] = hi[here, :]
    for i in range(5):
        xs[pl.ds(i * EY, EY), :] = plane(sw, PX * i + 3 * par)
    clear_pads(x, EY)
    body = pl.ds(PAD, EY)

    def prepared(p):
        by = plane(sw, PX * BY + p)
        _, inv, w = faces(
            plane(sw, PX * ALPHA + p), plane(sw, PX * BX + p), plane(sw, PX * BX + p + 1), by,
            pltpu.roll(by, EY - 1, 0), plane(sw, PX * BZ + p), 1, 1.0,
        )
        return w, inv * plane(sw, PX * B + p)

    for p in range(3):
        x[p, body, :] = prepared(p)[1] * (1.0 / THETA)
    second = 1 + par
    w, c0 = prepared(second)
    lower = jnp.broadcast_to(par, c0.shape) == 0
    v = x[second, body, :]
    z = c0 - v + w[0] * x[second - 1, body, :] + jnp.where(lower, w[1] * x[2, body, :], 0.0)
    z += w[2] * x[second, pl.ds(PAD - 1, EY), :] + w[3] * x[second, pl.ds(PAD + 1, EY), :]
    z += w[4] * moved(v, 1) + w[5] * moved(v, -1)
    xs[pl.ds(5 * EY, EY), :] = v
    xs[pl.ds(6 * EY, EY), :] = v + GAIN[1] * z + MOMENTUM[1] * v
    xs[pl.ds(7 * EY, EY), :] = jnp.where(lower, plane(sw, PX * BX + second), w[1])


Q0 = 3


def fine_kernel(own, sw, xs, rhs, rhs_lo, rhs_hi, edge, xedge, pre, w, cc, sx, d, x, y, z, t):
    par = parity()
    near = 7 * (1 - par)
    far = 2 + 5 * par
    for p in range(PX):
        sx[Q0 + p] = plane(own, PX * BX + p)
    for k in range(3):
        sx[near + k] = plane(sw, PX * BX + par + k)
    sx[10 + par] = plane(sw, PX * BX + 3)
    sx[far] = plane(xs, BX)
    sx[11 - 3 * par] = plane(xs, 7)
    clear_pads(x, EY)
    clear_pads(y, EY)
    chunk = 40

    def prepare(q, get):
        for r0 in range(0, EY, chunk):
            here = pl.ds(r0, chunk)

            def load(i):
                return lambda r, n: get(i, r, n)

            dd, inv, w6 = faces(
                load(ALPHA)(r0, chunk), sx[q, here, :], sx[q + 1, here, :], load(BY)(r0, chunk),
                next_rows(load(BY), r0, chunk, EY), load(BZ)(r0, chunk), 1, 1.0,
            )
            for a, f in enumerate(w6):
                w[a, q, here, :] = f
            c0 = inv * load(B)(r0, chunk)
            cc[q, here, :] = c0
            x[q, pl.ds(PAD + r0, chunk), :] = c0 * (1.0 / THETA)
            d[q, here, :] = dd

    for p in range(PX):
        prepare(Q0 + p, lambda i, r, n: plane(own, PX * i + p, r, n))
    for k in range(3):
        prepare(near + k, lambda i, r, n: plane(sw, PX * i + par + k, r, n))
    prepare(far, lambda i, r, n: plane(xs, i, r, n))
    beyond = 1 + 7 * par
    body = pl.ds(PAD, EY)
    x[beyond, body, :] = plane(xs, 5)
    missing = GAIN[1] * plane(xs, 7) * x[2, body, :]
    y[beyond, body, :] = plane(xs, 6) + jnp.where(jnp.broadcast_to(par, missing.shape) == 0, missing, 0.0)

    rows = (0, EY)
    sweep(x, None, cc, w, 2, 8, rows, 1, 1, into(y), chunk)
    sweep(x, None, cc, w, 8 - 7 * par, 9 - 7 * par, rows, 1, 1, into(y), chunk, unroll=0)
    sweep(y, x, cc, w, 2, 8, rows, 1, 2, into(z), chunk)
    got = []
    for c in range(2):
        for r0 in range(0, EY, chunk):
            v = 0.0
            for q in (Q0 + 2 * c, Q0 + 2 * c + 1):
                _, zz = defect(z, cc, w, q, r0, chunk, 1, q, 0, q, 0)
                v = v + d[q, pl.ds(r0, chunk), :] * zz
            t[c, pl.ds(r0, chunk), :] = v
        got.append(pair_lanes(t[c, pl.ds(HY, H1, 2), :] + t[c, pl.ds(HY + 1, H1, 2), :], 1) * 0.125)
    v = pack2(got[0], got[1])
    rhs[...] = v
    rhs_lo[...] = v[:G1]
    rhs_hi[...] = v[H1 - G1 :]
    mid = pl.ds(PAD, EY)
    edge[...] = z[Q0 + 2 - par, mid, :]
    xedge[...] = z[Q0 + 1 + par, mid, :]
    for p in range(6):
        pre[p] = z[Q0 - 1 + p, mid, :]


C0 = 5
N1 = 14
M0 = 5
S_SHAPE = (4, N1, R1 + 2 * PAD, PZ)
O_EDGE = R1
O_ONE = O_EDGE + EY
O_BESIDE = O_ONE + R1
O_TWO = O_BESIDE + R1
O_RAW = O_TWO + 2 * R1
O_END = O_RAW + 8 * R1


def place_coefficients(s, i, e, v):
    v0, v1 = unpack2(v)
    s[i, 1 + 2 * e, pl.ds(PAD, R1), :] = v0
    s[i, 2 + 2 * e, pl.ds(PAD, R1), :] = v1


def middle_faces(s, w1, inv1, d1, q):
    for r0 in range(0, R1, 32):
        here, up, out = pl.ds(PAD + r0, 32), pl.ds(PAD + r0 + 1, 32), pl.ds(r0, 32)
        dd, inv, w6 = faces(
            s[0, q, here, :], s[1, q, here, :], s[1, q + 1, here, :], s[2, q, here, :], s[2, q, up, :],
            s[3, q, here, :], 2, 0.25,
        )
        for a, f in enumerate(w6):
            w1[a, q, out, :] = f
        inv1[q, out, :] = inv
        d1[q, out, :] = dd


def sides(par, k):
    lower, upper = 1 - k, 4 + k
    return jnp.where(par == 0, lower, upper), jnp.where(par == 0, upper, lower)


def level2_load(s, plane):
    def load(i, k, row):
        return s[i, 2 * plane + C0 + k, pl.ds(PAD + row, R2, 2), :]

    return load


def near_coefficients_kernel(own, other, beside, s, w1, inv1, d1, coarse):
    par = parity()
    for i in range(4):
        s[i, :, PAD + R1 :, :] = jnp.zeros((N1, PAD, PZ), F32)
        rows = pl.ds(R1 * i, R1)
        place_coefficients(s, i, 2 + par, own[rows, :])
        place_coefficients(s, i, 3 - par, other[rows, :])
        place_coefficients(s, i, sides(par, 0)[0], beside[pl.ds(R1 * (4 + i), R1), :])
        place_coefficients(s, i, sides(par, 1)[0], beside[rows, :])
    for k in range(7):
        middle_faces(s, w1, inv1, d1, 1 + 4 * par + k)
    for k in range(2):
        coarse[pl.ds(R2 * k, R2), :] = pack4(coarser(level2_load(s, k), R2, 2))


def extend_kernel(lo, rhs, hi, xedge, s, inv, coarse, send, send2):
    par = parity()
    send[:G1] = lo[...]
    send[pl.ds(G1, H1), :] = rhs[...]
    send[pl.ds(G1 + H1, G1), :] = hi[...]
    send[pl.ds(R1, EY), :] = xedge[...]
    v = send[:R1]
    odd = jnp.broadcast_to(par, v.shape)
    v0, v1 = unpack2(v)
    q = C0 + 3 * par
    x1 = inv[q] * jnp.where(odd == 0, v0, v1) * (1.0 / THETA)
    send2[:R1] = pack2(x1, s[1, q, pl.ds(PAD, R1), :])
    send2[R1:] = coarse[...]


def join_kernel(own, edge, one, beside, two, raw_beside, out):
    out[:R1] = own[:R1]
    out[pl.ds(O_EDGE, EY), :] = edge[...]
    out[pl.ds(O_ONE, R1), :] = one[:R1]
    out[pl.ds(O_BESIDE, R1), :] = beside[:R1]
    out[pl.ds(O_TWO, 2 * R1), :] = two[...]
    out[pl.ds(O_RAW, 4 * R1), :] = raw_beside[pl.ds(4 * R1, 4 * R1), :]
    out[pl.ds(O_RAW + 4 * R1, 4 * R1), :] = raw_beside[pl.ds(0, 4 * R1), :]


def both_sides(par, mine, its):
    upper = jnp.broadcast_to(par, mine.shape) == 1
    return jnp.where(upper, its, mine), jnp.where(upper, mine, its)


def middle_kernel(own, one, beside, two, its, s_in, w_in, inv_in, d_in, edge, cc, pre, rhs, s, w, inv, d,
                  x, y, z, t, u):
    par = parity()
    clear_pads(x, R1)
    clear_pads(y, R1)
    body = pl.ds(PAD, R1)
    lower, upper = both_sides(par, two[:R1], its[pl.ds(O_TWO, R1), :])
    x[0, body, :] = unpack2(lower)[0]
    x1, bx = unpack2(upper)
    x[N1 - 1, body, :] = x1
    s[1, N1 - 1, body, :] = bx
    for k in range(2):
        e = sides(par, k)[1]
        for i in range(4):
            place_coefficients(s, i, e, its[pl.ds(O_RAW + (4 * k + i) * R1, R1), :])
    for k in range(5):
        middle_faces(s, w, inv, d, jnp.where(par == 0, 8 + k, 1 + k if k < 4 else 12))

    def place(e, v):
        for k, b in enumerate(unpack2(v)):
            q = 1 + 2 * e + k
            c0 = inv[q] * b
            cc[q] = c0
            x[q, body, :] = c0 * (1.0 / THETA)

    place(2 + par, own[:R1])
    place(3 - par, its[:R1])
    for k, ref, row in ((0, one, O_ONE), (1, beside, O_BESIDE)):
        e, f = sides(par, k)
        place(e, ref[:R1])
        place(f, its[pl.ds(row, R1), :])

    rows = (0, R1)
    sweep(x, None, cc, w, 1, 13, rows, 2, 1, into(y), 32, unroll=12)
    sweep(y, x, cc, w, 2, 12, rows, 2, 2, into(z), 32, unroll=10)

    for c in range(4):
        for r0 in range(0, R1, 32):
            v = 0.0
            for k in range(2):
                q = C0 - 2 + 2 * c + k
                _, zz = defect(z, cc, w, q, r0, 32, 2, q, 0, q, 0)
                v = v + d[q, pl.ds(r0, 32), :] * zz
            t[c, pl.ds(r0, 32), :] = v
        rhs[c] = pair_lanes(t[c, pl.ds(0, R2, 2), :] + t[c, pl.ds(1, R2, 2), :], 2) * 0.125

    def first(k, plane):
        al, bx, by, bz = coarser(level2_load(s, plane), R2, 2)
        after = level2_load(s, plane + 1)
        bx1 = pair_lanes(after(1, 0, 0) + after(1, 0, 1), 2) * 0.25
        u[k, pl.ds(0, R2), :] = by
        u[k, pl.ds(R2, PAD), :] = jnp.zeros((PAD, PZ), F32)
        _, inv2, _ = faces(al, bx, bx1, by, u[k, pl.ds(1, R2), :], bz, 4, 0.0625)
        return inv2 * rhs[plane + 1] * (1.0 / THETA), bx

    below, above = first(0, -1), first(1, 2)
    up = pack4([rhs[3], rhs[2], rhs[1], below[0]])
    down = pack4([rhs[0], rhs[1], rhs[2], above[0]])
    wide = jnp.broadcast_to(lax.axis_index("wide"), up.shape)
    ends = (lanes(R2) & 3) == 0
    down = jnp.where(wide == 0, jnp.where(ends, rhs[1], 0.0), down)
    up = jnp.where(wide == lax.axis_size("wide") - 1, jnp.where(ends, rhs[2], 0.0), up)
    edge[:R2] = jnp.where(jnp.broadcast_to(par, up.shape) == 0, down, up)
    edge[R2:] = above[1]
    for p in range(10):
        pre[p] = z[C0 - 3 + p, body, :]


def coarse_coefficients_kernel(s, two, its, w2, inv2, last, s2):
    par = parity()
    for c in range(2, 8):
        for i, v in enumerate(coarser(level2_load(s, c - 4), R2, 2)):
            s2[i, c, pl.ds(0, R2), :] = v
    for k in range(2):
        rows = pl.ds(R1 + R2 * k, R2)
        lower, upper = both_sides(par, two[rows, :], its[pl.ds(O_TWO + R1 + R2 * k, R2), :])
        for i in range(4):
            s2[i, k, pl.ds(0, R2), :] = unpack4(lower, i)
            s2[i, 8 + k, pl.ds(0, R2), :] = unpack4(upper, i)
    s2[2, :, R2:, :] = jnp.zeros((10, PAD, PZ), F32)
    body = pl.ds(0, R2)
    for c in range(9):
        _, inv, w6 = faces(
            s2[0, c, body, :], s2[1, c, body, :], s2[1, c + 1, body, :], s2[2, c, body, :], s2[2, c, pl.ds(1, R2), :],
            s2[3, c, body, :], 4, 0.0625,
        )
        for a, f in enumerate(w6):
            w2[a, c + 1] = f
        inv2[c + 1] = inv
    for i in range(4):
        last[i] = s2[i, 9]


def last_kernel(two2, its2, rhs, w2, inv2, last, pre1, w1, c1, pre0, sw, xs, w0, c0, out,
                wx, c2, x2, y2, z2, x1, y1, z1, x0, y0):
    par = parity()
    body = pl.ds(PAD, R2)
    lo, hi = both_sides(par, two2[:R2], its2[:R2])
    _, beyond = both_sides(par, two2[R2:], its2[R2:])
    clear_pads(x2, R2)
    clear_pads(y2, R2)
    clear_pads(z2, R2)
    _, inv, w6 = faces(
        last[0, :R2], last[1, :R2], beyond, last[2, :R2], last[2, pl.ds(1, R2), :], last[3, :R2], 4, 0.0625
    )
    for a, f in enumerate(w6):
        wx[a, 0] = f

    def start(j, b, dinv):
        v = dinv * b
        c2[j] = v
        x2[j, body, :] = v * (1.0 / THETA)

    for k in range(3):
        start(3 - k, unpack4(lo, k), inv2[3 - k])
        start(8 + k, unpack4(hi, k), inv2[8 + k] if k < 2 else inv)
    for c in range(4):
        start(c + 4, rhs[c], inv2[c + 4])
    x2[0, body, :] = unpack4(lo, 3)
    x2[11, body, :] = unpack4(hi, 3)
    rows = (0, R2)
    sweep(x2, None, c2, w2, 1, 10, rows, 4, 1, into(y2), R2, unroll=9)
    sweep(x2, None, c2, wx, 10, 11, rows, 4, 1, into(y2), R2, woff=-10)
    sweep(y2, x2, c2, w2, 2, 10, rows, 4, 2, into(z2), R2, unroll=8)
    sweep(z2, y2, c2, w2, 3, 9, rows, 4, 3, into(x2), R2, unroll=6)

    clear_pads(x1, R1)
    clear_pads(y1, R1)
    for q in range(10):
        v = x2[(q - 3) // 2 + M0, body, :]
        z1[q, pl.ds(PAD, R2, 2), :] = v
        z1[q, pl.ds(PAD + 1, R2, 2), :] = v
        x1[q, pl.ds(PAD, R1), :] = pre1[q] + z1[q, pl.ds(PAD, R1), :]
    rows = (0, R1)
    off = C0 - 3
    sweep(x1, None, c1, w1, 1, 9, rows, 2, 0, into(y1), 32, woff=off, coff=off)
    sweep(y1, x1, c1, w1, 2, 8, rows, 2, 1, into(z1), 32, woff=off, coff=off, unroll=6)

    clear_pads(x0, EY)
    clear_pads(y0, EY)
    near, far = 7 - 7 * par, 7 * par
    body = pl.ds(PAD, EY)
    for q in range(8):
        v = z1[(q - 2) // 2 + 3 + 2 * par, pl.ds(PAD + 12, EY // 2), :]
        x0[q, pl.ds(PAD, EY // 2, 2), :] = v
        x0[q, pl.ds(PAD + 1, EY // 2, 2), :] = v
        if 0 < q < 7:
            x0[q, body, :] += pre0[q - 1]
    x0[near, body, :] += sw[pl.ds(O_EDGE, EY), :]
    x0[far, body, :] += xs[pl.ds(R1, EY), :]
    off = Q0 - 2
    sweep(x0, None, c0, w0, 1, 7, (0, EY), 1, 0, into(y0), 40, woff=off, coff=off, unroll=6)

    def finish(q, r0, n, v):
        out[q - 2, pl.ds(r0 - 8, n), :] = v

    sweep(y0, x0, c0, w0, 2, 6, (8, 8 + PY), 1, 1, finish, 32, woff=off, coff=off, unroll=4)


def swap(v):
    return lax.ppermute(v, "wide", [(i, i ^ 1) for i in range(lax.axis_size("wide"))])


def across(v, chips, ends=()):
    count = lax.axis_size("wide")
    step = 2 * chips - 1
    pairs = [(i, i + step) for i in range(1, count, 2) if i + step < count]
    pairs += [(i, i - step) for i in range(0, count, 2) if i - step >= 0]
    return lax.ppermute(v, "wide", pairs + list(ends))


def from_beside(v):
    count = lax.axis_size("wide")
    pairs = [(i, i + 2) for i in range(0, count - 2, 2)] + [(i, i - 2) for i in range(3, count, 2)]
    return lax.ppermute(v, "wide", pairs)


def shifted(v, axis, step):
    count = lax.axis_size(axis)
    return lax.ppermute(v, axis, [(i, i + step) for i in range(count) if 0 <= i + step < count])


def shards(right_side, alpha_coef, beta_x, beta_y, beta_z):
    a, ylo, yhi, raw = call(
        pack_kernel, "pack",
        (shape(5, PX, PY, PZ), shape(SIDE + 4 * G1, PZ), shape(SIDE + 4 * G1, PZ), shape(4, H1, PZ)),
        (VMEM,) * 4, [ANY] * 5, [pltpu.SemaphoreType.DMA((5,))], SMALL,
    )(*[pltpu.with_memory_space_constraint(v, pltpu.HBM) for v in (right_side, alpha_coef, beta_x, beta_y, beta_z)])
    lo = shifted(yhi, "narrow", 1)
    hi = shifted(ylo, "narrow", -1)
    own, xs = call(
        corner_kernel, "corners", (shape(RAW + 4 * R1, PZ), shape(8 * EY, PZ)), (VMEM,) * 2, [VMEM] * 4,
        [scratch(3, EY + 2 * PAD, PZ)], SMALL,
    )(a, raw, lo, hi)
    xs = across(xs, 1)
    sw = swap(own)
    raw_beside = from_beside(jnp.concatenate([own[RAW:], sw[RAW:]], 0))

    rhs, rhs_lo, rhs_hi, edge0, xedge0, pre0, w0, c0 = call(
        fine_kernel, "level0_pre",
        (shape(H1, PZ), shape(G1, PZ), shape(G1, PZ), shape(EY, PZ), shape(EY, PZ), shape(6, EY, PZ),
         shape(6, 10, EY, PZ), shape(10, EY, PZ)),
        (VMEM,) * 8, [VMEM] * 3,
        [scratch(12, EY, PZ), scratch(10, EY, PZ)] + [scratch(10, EY + 2 * PAD, PZ)] * 3 + [scratch(2, EY, PZ)],
        LARGE,
    )(own, sw, xs)
    rhs_below = shifted(rhs_hi, "narrow", 1)
    rhs_above = shifted(rhs_lo, "narrow", -1)
    w1_shapes = (shape(*S_SHAPE), shape(6, N1, R1, PZ), shape(N1, R1, PZ), shape(N1, R1, PZ))
    s1, w1, inv1, d1, coarse = call(
        near_coefficients_kernel, "near_coefficients", w1_shapes + (shape(R1, PZ),),
        (VMEM,) * 5, [VMEM] * 3, [], LARGE,
    )(own[RAW:], sw[RAW:], raw_beside)
    send, send2 = call(
        extend_kernel, "extend", (shape(R1 + EY, PZ), shape(2 * R1, PZ)), (VMEM,) * 2, [VMEM] * 7, [], SMALL
    )(rhs_below, rhs, rhs_above, xedge0, s1, inv1, coarse)

    one = across(send, 1)
    beside = from_beside(send[:R1])
    two = across(send2, 2)
    mine = call(join_kernel, "join", shape(O_END, PZ), VMEM, [VMEM] * 6, [], SMALL)(
        send, edge0, one, beside, two, raw_beside
    )
    its = swap(mine)

    edge, c1, pre1, rhs2, s1, w1, _, _ = call(
        middle_kernel, "level1_pre",
        (shape(2 * R2, PZ), shape(N1, R1, PZ), shape(10, R1, PZ), shape(4, R2, PZ)) + w1_shapes,
        (VMEM,) * 8, [VMEM] * 9,
        [scratch(N1, R1 + 2 * PAD, PZ)] * 3 + [scratch(4, R1, PZ), scratch(2, R2 + PAD, PZ)],
        LARGE, aliases={5: 4, 6: 5, 7: 6, 8: 7},
    )(send, one, beside, two, its, s1, w1, inv1, d1)

    w2, inv2, last2 = call(
        coarse_coefficients_kernel, "level2_coefficients",
        (shape(6, 12, R2, PZ), shape(12, R2, PZ), shape(4, R2 + PAD, PZ)),
        (VMEM,) * 3, [VMEM] * 3, [scratch(4, 10, R2 + PAD, PZ)], LARGE,
    )(s1, two, its)
    count = lax.axis_size("wide")
    two2 = across(edge, 2, ((0, 2), (count - 1, count - 3)))
    its2 = swap(two2)
    return call(
        last_kernel, "coarse_and_post", shape(PX, PY, PZ), VMEM, [VMEM] * 14,
        [scratch(6, 1, R2, PZ), scratch(12, R2, PZ)] + [scratch(12, R2 + 2 * PAD, PZ)] * 3
        + [scratch(10, R1 + 2 * PAD, PZ)] * 3 + [scratch(8, EY + 2 * PAD, PZ)] * 2,
        LARGE,
    )(two2, its2, rhs2, w2, inv2, last2, pre1, w1, c1, pre0, its, one, w0, c0)


def solution(mesh):
    spec = P("wide", "narrow", None)
    return jax.shard_map(shards, mesh=mesh, in_specs=(spec,) * 5, out_specs=spec, check_vma=False)
```

time: 81.7 us -> 74.1 us (0.907)
  the two profiles are of different devices: /device:TPU:223 before, /device:TPU:215 now
where the time goes in v3:
time: 74.1 us; the launch traced here: 73.6 us
  starting transfers between devices  42.6 us (57%)
  waiting for transfers between devices  22.6 us (30%)
  Pallas kernels  8.08 us (11%)
    ppermute x4, starting transfers between devices, across(): return lax.ppermute(v, 'wide', pairs + list(ends))  18.5 us
    ppermute x4, starting transfers between devices, shifted(): lax.ppermute(v, axis, [(i, i + step) for i in range(count) if 0 <= i + st...  12 us
    ppermute x4, waiting for transfers between devices, across(): return lax.ppermute(v, 'wide', pairs + list(ends))  8.44 us
    ppermute x3, starting transfers between devices, swap(): lax.ppermute(v, 'wide', [(i, i ^ 1) for i in range(lax.axis_size('wide'))])  7.27 us
    ppermute x4, waiting for transfers between devices, shifted(): lax.ppermute(v, axis, [(i, i + step) for i in range(count) if 0 <= i + st...  6.71 us
    ppermute x2, waiting for transfers between devices, from_beside(): return lax.ppermute(v, 'wide', pairs)  4.98 us
    ppermute x2, starting transfers between devices, from_beside(): return lax.ppermute(v, 'wide', pairs)  4.92 us
    ppermute x3, waiting for transfers between devices, swap(): lax.ppermute(v, 'wide', [(i, i ^ 1) for i in range(lax.axis_size('wide'))])  2.51 us
  transfers between devices with their start and end apart: 13, of which 8 were waited for; matrix products, arithmetic and copies ran while one was open for 0% of the time, Pallas kernels for 3%

profile of v3, /device:TPU:215, one launch (start us, length us, event | category | flops | bytes accessed | tf_op | source)
XLA Modules:
  0.0 73.6 jit_solution(11968387585457601358)
XLA Ops:
  0.0 1.3 %pack.1 = (f32[5,4,64,128]{3,2,1,0:T(8,128)S(1)}, f32[224,128]{1,0:T(8,128)S(1)}, f32[224,128]{1,0:T(8,128)S(1)}, f32[4,32,128]{2,1,0:T(8,128)S(1)}) custom-call(f32[4,64,128]{2,1,0:T(8,128)} %b.1, f32[4,64,128]{2,1,0:T(8,128)} %al.1, f32[4,64,128]{2,1,0:T(8,128)} %bx.1, f32[4,64,128]{2,1,0:T(8,128)} %by.1, f32[4,64,128]{2,1,0:T(8,128)} %bz.1), custom_call_target="tpu_custom_call" | custom-call | flops 1000 | tf_op jit(solution)/shard_map/pack/pallas_call | solution.py:615
  1.4 3.2 %collective-permute-start = (f32[224,128]{1,0:T(8,128)S(1)}, f32[224,128]{1,0:T(8,128)S(1)}, u32[]{:S(2)}, u32[]{:S(2)}) collective-permute-start(f32[224,128]{1,0:T(8,128)S(1)} %get-tuple-element.37), channel_id=1, source_target_pairs={{0,1},{1,2},{2,3},{3,4},{4,5},{5,6},{6,7},{8,9},{9,10},{10,11},{11... | collective-permute-start | bytes 344072 | tf_op jit(solution)/shard_map/ppermute | solution.py:611
  4.6 2.1 %collective-permute-start.1 = (f32[224,128]{1,0:T(8,128)S(1)}, f32[224,128]{1,0:T(8,128)S(1)}, u32[]{:S(2)}, u32[]{:S(2)}) collective-permute-start(f32[224,128]{1,0:T(8,128)S(1)} %get-tuple-element.38), channel_id=1, source_target_pairs={{1,0},{2,1},{3,2},{4,3},{5,4},{6,5},{7,6},{9,8},{10,9},{11,10},{12... | collective-permute-start | bytes 344072 | tf_op jit(solution)/shard_map/ppermute | solution.py:611
  6.7 0.6 collective-permute-done.lo
  7.3 4.3 %collective-permute-done.1.hi = f32[224,128]{1,0:T(8,128)S(1)} collective-permute-done((f32[224,128]{1,0:T(8,128)S(1)}, f32[224,128]{1,0:T(8,128)S(1)}, u32[]{:S(2)}, u32[]{:S(2)}) %collective-permute-start.1) | collective-permute-done | bytes 114720 | tf_op jit(solution)/shard_map/ppermute | solution.py:611
  11.5 0.3 corners.1
  11.8 3.4 %collective-permute-start.2 = (f32[1856,128]{1,0:T(8,128)S(1)}, f32[1856,128]{1,0:T(8,128)S(1)}, u32[]{:S(2)}, u32[]{:S(2)}) collective-permute-start(f32[1856,128]{1,0:T(8,128)S(1)} %get-tuple-element.39.own), channel_id=1, source_target_pairs={{0,8},{8,0},{16,24},{24,16},{32,40},{40,32},{48,56},{56,48},{64,72... | collective-permute-start | bytes 2850824 | tf_op jit(solution)/shard_map/ppermute | solution.py:592
  15.3 5.0 %collective-permute-start.3 = (f32[640,128]{1,0:T(8,128)S(1)}, f32[640,128]{1,0:T(8,128)S(1)}, u32[]{:S(2)}, u32[]{:S(2)}) collective-permute-start(f32[640,128]{1,0:T(8,128)S(1)} %get-tuple-element.40), channel_id=1, source_target_pairs={{8,16},{24,32},{40,48},{56,64},{72,80},{88,96},{104,112},{120,128}... | collective-permute-start | bytes 983048 | tf_op jit(solution)/shard_map/ppermute | solution.py:600
  20.3 0.0 collective-permute-done.2.sw
  20.4 1.9 %collective-permute-start.6 = (f32[512,128]{1,0:T(8,128)S(1)}, f32[512,128]{1,0:T(8,128)S(1)}, u32[]{:S(2)}, u32[]{:S(2)}) collective-permute-start(f32[512,128]{1,0:T(8,128)S(1)} %pad_maximum_fusion), channel_id=1, source_target_pairs={{0,16},{16,32},{32,48},{48,64},{64,80},{80,96},{96,112},{112,128},... | collective-permute-start | bytes 786440 | tf_op jit(solution)/shard_map/ppermute | solution.py:606
  22.3 4.7 %collective-permute-done.3.xs = f32[640,128]{1,0:T(8,128)S(1)} collective-permute-done((f32[640,128]{1,0:T(8,128)S(1)}, f32[640,128]{1,0:T(8,128)S(1)}, u32[]{:S(2)}, u32[]{:S(2)}) %collective-permute-start.3) | collective-permute-done | bytes 327712 | tf_op jit(solution)/shard_map/ppermute | solution.py:600
  27.0 1.2 %level0_pre.1 = (f32[32,128]{1,0:T(8,128)S(1)}, f32[16,128]{1,0:T(8,128)S(1)}, f32[16,128]{1,0:T(8,128)S(1)}, f32[80,128]{1,0:T(8,128)S(1)}, f32[80,128]{1,0:T(8...) custom-call(f32[1856,128]{1,0:T(8,128)S(1)} %get-tuple-element.39.own, ...), custom_call_target="tpu_custom_call" | custom-call | flops 20000000000 | tf_op jit(solution)/shard_map/level0_pre/pallas_call | solution.py:630
  28.1 4.8 %collective-permute-start.4 = (f32[16,128]{1,0:T(8,128)S(1)}, f32[16,128]{1,0:T(8,128)S(1)}, u32[]{:S(2)}, u32[]{:S(2)}) collective-permute-start(f32[16,128]{1,0:T(8,128)S(1)} %get-tuple-element.41), channel_id=1, source_target_pairs={{0,1},{1,2},{2,3},{3,4},{4,5},{5,6},{6,7},{8,9},{9,10},{10,11},{11... | collective-permute-start | bytes 24584 | tf_op jit(solution)/shard_map/ppermute | solution.py:611
  32.9 1.9 %collective-permute-start.5 = (f32[16,128]{1,0:T(8,128)S(1)}, f32[16,128]{1,0:T(8,128)S(1)}, u32[]{:S(2)}, u32[]{:S(2)}) collective-permute-start(f32[16,128]{1,0:T(8,128)S(1)} %get-tuple-element.43), channel_id=1, source_target_pairs={{1,0},{2,1},{3,2},{4,3},{5,4},{6,5},{7,6},{9,8},{10,9},{11,10},{12... | collective-permute-start | bytes 24584 | tf_op jit(solution)/shard_map/ppermute | solution.py:611
  34.8 0.0 collective-permute-done.6.beside.raw_beside
  34.9 0.6 near_coefficients.1
  35.5 0.0 collective-permute-done.4.lo
  35.5 1.8 %collective-permute-done.5.hi = f32[16,128]{1,0:T(8,128)S(1)} collective-permute-done((f32[16,128]{1,0:T(8,128)S(1)}, f32[16,128]{1,0:T(8,128)S(1)}, u32[]{:S(2)}, u32[]{:S(2)}) %collective-permute-start.5) | collective-permute-done | bytes 8224 | tf_op jit(solution)/shard_map/ppermute | solution.py:611
  37.3 0.1 extend.1
  37.4 6.5 %collective-permute-start.7 = (f32[144,128]{1,0:T(8,128)S(1)}, f32[144,128]{1,0:T(8,128)S(1)}, u32[]{:S(2)}, u32[]{:S(2)}) collective-permute-start(f32[144,128]{1,0:T(8,128)S(1)} %get-tuple-element.48.own), channel_id=1, source_target_pairs={{8,16},{24,32},{40,48},{56,64},{72,80},{88,96},{104,112},{120,128}... | collective-permute-start | bytes 221192 | tf_op jit(solution)/shard_map/ppermute | solution.py:600
  43.9 1.9 %collective-permute-start.9 = (f32[128,128]{1,0:T(8,128)S(1)}, f32[128,128]{1,0:T(8,128)S(1)}, u32[]{:S(2)}, u32[]{:S(2)}) collective-permute-start(f32[128,128]{1,0:T(8,128)S(1)} %get-tuple-element.49), channel_id=1, source_target_pairs={{8,32},{24,48},{40,64},{56,80},{72,96},{88,112},{104,128},{120,144... | collective-permute-start | bytes 196616 | tf_op jit(solution)/shard_map/ppermute | solution.py:600
  45.8 3.0 %collective-permute-start.8 = (f32[64,128]{1,0:T(8,128)S(1)}, f32[64,128]{1,0:T(8,128)S(1)}, u32[]{:S(2)}, u32[]{:S(2)}) collective-permute-start(f32[64,128]{1,0:T(8,128)S(1)} %slice.13), channel_id=1, source_target_pairs={{0,16},{16,32},{32,48},{48,64},{64,80},{80,96},{96,112},{112,128},... | collective-permute-start | bytes 98312 | tf_op jit(solution)/shard_map/ppermute | solution.py:606
  48.8 5.0 %collective-permute-done.8.beside = f32[64,128]{1,0:T(8,128)S(1)} collective-permute-done((f32[64,128]{1,0:T(8,128)S(1)}, f32[64,128]{1,0:T(8,128)S(1)}, u32[]{:S(2)}, u32[]{:S(2)}) %collective-permute-start.8) | collective-permute-done | bytes 32800 | tf_op jit(solution)/shard_map/ppermute | solution.py:606
  53.8 0.0 collective-permute-done.9.two
  53.8 0.0 collective-permute-done.7.one.xs
  53.8 1.9 %collective-permute-start.10 = (f32[912,128]{1,0:T(8,128)S(1)}, f32[912,128]{1,0:T(8,128)S(1)}, u32[]{:S(2)}, u32[]{:S(2)}) collective-permute-start(f32[912,128]{1,0:T(8,128)S(1)} %join.1), channel_id=1, source_target_pairs={{0,8},{8,0},{16,24},{24,16},{32,40},{40,32},{48,56},{56,48},{64,72... | collective-permute-start | bytes 1400840 | tf_op jit(solution)/shard_map/ppermute | solution.py:592
  55.8 1.8 %collective-permute-done.10.its.sw = f32[912,128]{1,0:T(8,128)S(1)} collective-permute-done((f32[912,128]{1,0:T(8,128)S(1)}, f32[912,128]{1,0:T(8,128)S(1)}, u32[]{:S(2)}, u32[]{:S(2)}) %collective-permute-start.10) | collective-permute-done | bytes 466976 | tf_op jit(solution)/shard_map/ppermute | solution.py:592
  57.6 2.0 %level1_pre.1 = (f32[64,128]{1,0:T(8,128)S(1)}, f32[14,64,128]{2,1,0:T(8,128)S(1)}, f32[10,64,128]{2,1,0:T(8,128)S(1)}, f32[4,32,128]{2,1,0:T(8,128)S(1)}, f32[4...) custom-call(f32[144,128]{1,0:T(8,128)S(1)} %get-tuple-element.48.own, ...), custom_call_target="tpu_custom_call", output_to_operand_aliasing={{4}: (5, {}), {5}: (6, {}), {6}: (7, {}), {7}: (8, {})} | custom-call | flops 20000000000 | tf_op jit(solution)/shard_map/level1_pre/pallas_call | solution.py:657
  59.6 5.1 %collective-permute-start.11 = (f32[64,128]{1,0:T(8,128)S(1)}, f32[64,128]{1,0:T(8,128)S(1)}, u32[]{:S(2)}, u32[]{:S(2)}) collective-permute-start(f32[64,128]{1,0:T(8,128)S(1)} %get-tuple-element.53), channel_id=1, source_target_pairs={{8,32},{24,48},{40,64},{56,80},{72,96},{88,112},{104,128},{120,144... | collective-permute-start | bytes 98312 | tf_op jit(solution)/shard_map/ppermute | solution.py:600
  64.7 3.8 %collective-permute-done.11.two2 = f32[64,128]{1,0:T(8,128)S(1)} collective-permute-done((f32[64,128]{1,0:T(8,128)S(1)}, f32[64,128]{1,0:T(8,128)S(1)}, u32[]{:S(2)}, u32[]{:S(2)}) %collective-permute-start.11) | collective-permute-done | bytes 32800 | tf_op jit(solution)/shard_map/ppermute | solution.py:600
  68.4 1.9 %collective-permute-start.12 = (f32[64,128]{1,0:T(8,128)S(1)}, f32[64,128]{1,0:T(8,128)S(1)}, u32[]{:S(2)}, u32[]{:S(2)}) collective-permute-start(f32[64,128]{1,0:T(8,128)S(1)} %collective-permute-done.11.two2), channel_id=1, source_target_pairs={{0,8},{8,0},{16,24},{24,16},{32,40},{40,32},{48,56},{56,48},{64,72... | collective-permute-start | bytes 98312 | tf_op jit(solution)/shard_map/ppermute | solution.py:592
  70.3 0.5 level2_coefficients.1
  70.8 0.7 collective-permute-done.12.its2
  71.5 2.1 %coarse_and_post.1 = f32[4,64,128]{2,1,0:T(8,128)} custom-call(f32[64,128]{1,0:T(8,128)S(1)} %collective-permute-done.11.two2, f32[64,128]{1,0:T(8,128)S(1)} %collective-permute-done.12.its2, f32[4,32,128]{2,1,0:T(8,128)S(1)} %get-tuple-element.54.rhs, f32[6,12,32,128]{3,2,1,0:T(8,128)S(1)} %get-tuple-element.56.w2, ...), custom_call_target="tpu_custom_call" | custom-call | flops 20000000000 | tf_op jit(solution)/shard_map/coarse_and_post/pallas_call | solution.py:673
  (5 shorter events, 0.1 us)
Async XLA Ops:
  1.4 5.9 %collective-permute-start = (f32[224,128]{1,0:T(8,128)S(1)}, f32[224,128]{1,0:T(8,128)S(1)}, u32[]{:S(2)}, u32[]{:S(2)}) collective-permute-start(f32[224,128]{1,0:T(8,128)S(1)} %get-tuple-element.37), channel_id=1, source_target_pairs={{0,1},{1,2},{2,3},{3,4},{4,5},{5,6},{6,7},{8,9},{9,10},{10,11},{11... | collective-permute-start | bytes 344072 | tf_op jit(solution)/shard_map/ppermute | solution.py:611
  4.6 7.0 %collective-permute-start.1 = (f32[224,128]{1,0:T(8,128)S(1)}, f32[224,128]{1,0:T(8,128)S(1)}, u32[]{:S(2)}, u32[]{:S(2)}) collective-permute-start(f32[224,128]{1,0:T(8,128)S(1)} %get-tuple-element.38), channel_id=1, source_target_pairs={{1,0},{2,1},{3,2},{4,3},{5,4},{6,5},{7,6},{9,8},{10,9},{11,10},{12... | collective-permute-start | bytes 344072 | tf_op jit(solution)/shard_map/ppermute | solution.py:611
  11.8 8.5 %collective-permute-start.2 = (f32[1856,128]{1,0:T(8,128)S(1)}, f32[1856,128]{1,0:T(8,128)S(1)}, u32[]{:S(2)}, u32[]{:S(2)}) collective-permute-start(f32[1856,128]{1,0:T(8,128)S(1)} %get-tuple-element.39.own), channel_id=1, source_target_pairs={{0,8},{8,0},{16,24},{24,16},{32,40},{40,32},{48,56},{56,48},{64,72... | collective-permute-start | bytes 2850824 | tf_op jit(solution)/shard_map/ppermute | solution.py:592
  15.3 11.7 %collective-permute-start.3 = (f32[640,128]{1,0:T(8,128)S(1)}, f32[640,128]{1,0:T(8,128)S(1)}, u32[]{:S(2)}, u32[]{:S(2)}) collective-permute-start(f32[640,128]{1,0:T(8,128)S(1)} %get-tuple-element.40), channel_id=1, source_target_pairs={{8,16},{24,32},{40,48},{56,64},{72,80},{88,96},{104,112},{120,128}... | collective-permute-start | bytes 983048 | tf_op jit(solution)/shard_map/ppermute | solution.py:600
  20.4 14.5 %collective-permute-start.6 = (f32[512,128]{1,0:T(8,128)S(1)}, f32[512,128]{1,0:T(8,128)S(1)}, u32[]{:S(2)}, u32[]{:S(2)}) collective-permute-start(f32[512,128]{1,0:T(8,128)S(1)} %pad_maximum_fusion), channel_id=1, source_target_pairs={{0,16},{16,32},{32,48},{48,64},{64,80},{80,96},{96,112},{112,128},... | collective-permute-start | bytes 786440 | tf_op jit(solution)/shard_map/ppermute | solution.py:606
  28.1 7.3 %collective-permute-start.4 = (f32[16,128]{1,0:T(8,128)S(1)}, f32[16,128]{1,0:T(8,128)S(1)}, u32[]{:S(2)}, u32[]{:S(2)}) collective-permute-start(f32[16,128]{1,0:T(8,128)S(1)} %get-tuple-element.41), channel_id=1, source_target_pairs={{0,1},{1,2},{2,3},{3,4},{4,5},{5,6},{6,7},{8,9},{9,10},{10,11},{11... | collective-permute-start | bytes 24584 | tf_op jit(solution)/shard_map/ppermute | solution.py:611
  32.9 4.4 %collective-permute-start.5 = (f32[16,128]{1,0:T(8,128)S(1)}, f32[16,128]{1,0:T(8,128)S(1)}, u32[]{:S(2)}, u32[]{:S(2)}) collective-permute-start(f32[16,128]{1,0:T(8,128)S(1)} %get-tuple-element.43), channel_id=1, source_target_pairs={{1,0},{2,1},{3,2},{4,3},{5,4},{6,5},{7,6},{9,8},{10,9},{11,10},{12... | collective-permute-start | bytes 24584 | tf_op jit(solution)/shard_map/ppermute | solution.py:611
  37.4 16.4 %collective-permute-start.7 = (f32[144,128]{1,0:T(8,128)S(1)}, f32[144,128]{1,0:T(8,128)S(1)}, u32[]{:S(2)}, u32[]{:S(2)}) collective-permute-start(f32[144,128]{1,0:T(8,128)S(1)} %get-tuple-element.48.own), channel_id=1, source_target_pairs={{8,16},{24,32},{40,48},{56,64},{72,80},{88,96},{104,112},{120,128}... | collective-permute-start | bytes 221192 | tf_op jit(solution)/shard_map/ppermute | solution.py:600
  43.9 9.9 %collective-permute-start.9 = (f32[128,128]{1,0:T(8,128)S(1)}, f32[128,128]{1,0:T(8,128)S(1)}, u32[]{:S(2)}, u32[]{:S(2)}) collective-permute-start(f32[128,128]{1,0:T(8,128)S(1)} %get-tuple-element.49), channel_id=1, source_target_pairs={{8,32},{24,48},{40,64},{56,80},{72,96},{88,112},{104,128},{120,144... | collective-permute-start | bytes 196616 | tf_op jit(solution)/shard_map/ppermute | solution.py:600
  45.8 8.0 %collective-permute-start.8 = (f32[64,128]{1,0:T(8,128)S(1)}, f32[64,128]{1,0:T(8,128)S(1)}, u32[]{:S(2)}, u32[]{:S(2)}) collective-permute-start(f32[64,128]{1,0:T(8,128)S(1)} %slice.13), channel_id=1, source_target_pairs={{0,16},{16,32},{32,48},{48,64},{64,80},{80,96},{96,112},{112,128},... | collective-permute-start | bytes 98312 | tf_op jit(solution)/shard_map/ppermute | solution.py:606
  53.8 3.7 %collective-permute-start.10 = (f32[912,128]{1,0:T(8,128)S(1)}, f32[912,128]{1,0:T(8,128)S(1)}, u32[]{:S(2)}, u32[]{:S(2)}) collective-permute-start(f32[912,128]{1,0:T(8,128)S(1)} %join.1), channel_id=1, source_target_pairs={{0,8},{8,0},{16,24},{24,16},{32,40},{40,32},{48,56},{56,48},{64,72... | collective-permute-start | bytes 1400840 | tf_op jit(solution)/shard_map/ppermute | solution.py:592
  59.6 8.8 %collective-permute-start.11 = (f32[64,128]{1,0:T(8,128)S(1)}, f32[64,128]{1,0:T(8,128)S(1)}, u32[]{:S(2)}, u32[]{:S(2)}) collective-permute-start(f32[64,128]{1,0:T(8,128)S(1)} %get-tuple-element.53), channel_id=1, source_target_pairs={{8,32},{24,48},{40,64},{56,80},{72,96},{88,112},{104,128},{120,144... | collective-permute-start | bytes 98312 | tf_op jit(solution)/shard_map/ppermute | solution.py:600
  68.4 3.1 %collective-permute-start.12 = (f32[64,128]{1,0:T(8,128)S(1)}, f32[64,128]{1,0:T(8,128)S(1)}, u32[]{:S(2)}, u32[]{:S(2)}) collective-permute-start(f32[64,128]{1,0:T(8,128)S(1)} %collective-permute-done.11.two2), channel_id=1, source_target_pairs={{0,8},{8,0},{16,24},{24,16},{32,40},{40,32},{48,56},{56,48},{64,72... | collective-permute-start | bytes 98312 | tf_op jit(solution)/shard_map/ppermute | solution.py:592

commit v4 on v3

--- a/solution.py
+++ b/solution.py
@@ -23,6 +23,7 @@
 R1 = H1 + 2 * G1
 R2 = R1 // 2
 RAW = 5 * PX * EY
+SRAW = 8 * EY
 SIDE = 5 * PX * HY
 PAD = 8
 SMALL, LARGE = 1000, 2 * 10**10
@@ -229,61 +230,64 @@
     return ref[pl.ds(pl.multiple_of(start, 8) if r0 % 8 == 0 else start, n), :]
 
 
-def corner_kernel(a, raw, lo, hi, sw, xs, x):
+def corner_kernel(a, raw, lo, hi, own, sw, xs, x, v):
     par = parity()
     for i in range(5):
         for p in range(PX):
             k = PX * i + p
-            sw[pl.ds(k * EY, HY), :] = lo[pl.ds(k * HY, HY), :]
-            sw[pl.ds(k * EY + HY, PY), :] = a[i, p]
-            sw[pl.ds(k * EY + HY + PY, HY), :] = hi[pl.ds(k * HY, HY), :]
+            own[pl.ds(k * EY, HY), :] = lo[pl.ds(k * HY, HY), :]
+            own[pl.ds(k * EY + HY, PY), :] = a[i, p]
+            own[pl.ds(k * EY + HY + PY, HY), :] = hi[pl.ds(k * HY, HY), :]
     for i in range(4):
         here = pl.ds(SIDE + G1 * i, G1)
-        base = RAW + R1 * i
-        sw[pl.ds(base, G1), :] = lo[here, :]
-        sw[pl.ds(base + G1, H1), :] = raw[i]
-        sw[pl.ds(base + G1 + H1, G1), :] = hi[here, :]
+        for ref, base in ((own, RAW + R1 * i), (sw, SRAW + R1 * i)):
+            ref[pl.ds(base, G1), :] = lo[here, :]
+            ref[pl.ds(base + G1, H1), :] = raw[i]
+            ref[pl.ds(base + G1 + H1, G1), :] = hi[here, :]
+    xs[pl.ds(SRAW, R1), :] = own[pl.ds(RAW + R1, R1), :]
     for i in range(5):
-        xs[pl.ds(i * EY, EY), :] = plane(sw, PX * i + 3 * par)
+        here = pl.ds(i * EY, EY)
+        xs[here, :] = plane(own, PX * i + 3 * par)
+        sw[here, :] = plane(own, PX * i + 3 - 3 * par)
     clear_pads(x, EY)
     body = pl.ds(PAD, EY)
-
-    def prepared(p):
-        by = plane(sw, PX * BY + p)
+    kept = []
+    for p in range(3):
+        by = plane(own, PX * BY + p)
         _, inv, w = faces(
-            plane(sw, PX * ALPHA + p), plane(sw, PX * BX + p), plane(sw, PX * BX + p + 1), by,
-            pltpu.roll(by, EY - 1, 0), plane(sw, PX * BZ + p), 1, 1.0,
+            plane(own, PX * ALPHA + p), plane(own, PX * BX + p), plane(own, PX * BX + p + 1), by,
+            pltpu.roll(by, EY - 1, 0), plane(own, PX * BZ + p), 1, 1.0,
         )
-        return w, inv * plane(sw, PX * B + p)
-
-    for p in range(3):
-        x[p, body, :] = prepared(p)[1] * (1.0 / THETA)
-    second = 1 + par
-    w, c0 = prepared(second)
-    lower = jnp.broadcast_to(par, c0.shape) == 0
-    v = x[second, body, :]
-    z = c0 - v + w[0] * x[second - 1, body, :] + jnp.where(lower, w[1] * x[2, body, :], 0.0)
-    z += w[2] * x[second, pl.ds(PAD - 1, EY), :] + w[3] * x[second, pl.ds(PAD + 1, EY), :]
-    z += w[4] * moved(v, 1) + w[5] * moved(v, -1)
-    xs[pl.ds(5 * EY, EY), :] = v
-    xs[pl.ds(6 * EY, EY), :] = v + GAIN[1] * z + MOMENTUM[1] * v
-    xs[pl.ds(7 * EY, EY), :] = jnp.where(lower, plane(sw, PX * BX + second), w[1])
+        c0 = inv * plane(own, PX * B + p)
+        x[p, body, :] = c0 * (1.0 / THETA)
+        kept.append((w, c0))
+    for up in range(2):
+        second = 1 + up
+        w, c0 = kept[second]
+        here = x[second, body, :]
+        z = c0 - here + w[0] * x[second - 1, body, :]
+        if not up:
+            z += w[1] * x[2, body, :]
+        z += w[2] * x[second, pl.ds(PAD - 1, EY), :] + w[3] * x[second, pl.ds(PAD + 1, EY), :]
+        z += w[4] * moved(here, 1) + w[5] * moved(here, -1)
+        v[up, pl.ds(0, EY), :] = here
+        v[up, pl.ds(EY, EY), :] = here + GAIN[1] * z + MOMENTUM[1] * here
+        v[up, pl.ds(2 * EY, EY), :] = w[1] if up else plane(own, PX * BX + second)
+    xs[pl.ds(5 * EY, 3 * EY), :] = v[par]
+    sw[pl.ds(5 * EY, 3 * EY), :] = v[1 - par]
 
 
 Q0 = 3
 
 
-def fine_kernel(own, sw, xs, rhs, rhs_lo, rhs_hi, edge, xedge, pre, w, cc, sx, d, x, y, z, t):
+def fine_kernel(own, sw, xs, _, rhs, rhs_lo, rhs_hi, edge, xedge, pre, w, cc, sx, d, x, y, z, t):
     par = parity()
-    near = 7 * (1 - par)
-    far = 2 + 5 * par
+    sides2 = ((xs, par), (sw, 1 - par))
     for p in range(PX):
         sx[Q0 + p] = plane(own, PX * BX + p)
-    for k in range(3):
-        sx[near + k] = plane(sw, PX * BX + par + k)
-    sx[10 + par] = plane(sw, PX * BX + 3)
-    sx[far] = plane(xs, BX)
-    sx[11 - 3 * par] = plane(xs, 7)
+    for ref, above in sides2:
+        sx[2 + 5 * above] = plane(ref, BX)
+        sx[9 - above] = plane(ref, 7)
     clear_pads(x, EY)
     clear_pads(y, EY)
     chunk = 40
@@ -308,18 +312,17 @@
 
     for p in range(PX):
         prepare(Q0 + p, lambda i, r, n: plane(own, PX * i + p, r, n))
-    for k in range(3):
-        prepare(near + k, lambda i, r, n: plane(sw, PX * i + par + k, r, n))
-    prepare(far, lambda i, r, n: plane(xs, i, r, n))
-    beyond = 1 + 7 * par
     body = pl.ds(PAD, EY)
-    x[beyond, body, :] = plane(xs, 5)
-    missing = GAIN[1] * plane(xs, 7) * x[2, body, :]
-    y[beyond, body, :] = plane(xs, 6) + jnp.where(jnp.broadcast_to(par, missing.shape) == 0, missing, 0.0)
+    for ref, above in sides2:
+        q = 2 + 5 * above
+        prepare(q, lambda i, r, n: plane(ref, i, r, n))
+        x[1 + 7 * above, body, :] = plane(ref, 5)
+        missing = GAIN[1] * plane(ref, 7) * x[q, body, :]
+        below = jnp.broadcast_to(above, missing.shape) == 0
+        y[1 + 7 * above, body, :] = plane(ref, 6) + jnp.where(below, missing, 0.0)
 
     rows = (0, EY)
     sweep(x, None, cc, w, 2, 8, rows, 1, 1, into(y), chunk)
-    sweep(x, None, cc, w, 8 - 7 * par, 9 - 7 * par, rows, 1, 1, into(y), chunk, unroll=0)
     sweep(y, x, cc, w, 2, 8, rows, 1, 2, into(z), chunk)
     got = []
     for c in range(2):
@@ -384,44 +387,74 @@
     return load
 
 
-def near_coefficients_kernel(own, other, beside, s, w1, inv1, d1, coarse):
+def near_coefficients_kernel(own, other, one, beside, s, w1, inv1, d1):
     par = parity()
     for i in range(4):
         s[i, :, PAD + R1 :, :] = jnp.zeros((N1, PAD, PZ), F32)
         rows = pl.ds(R1 * i, R1)
+        sent = pl.ds(R1 * (1 + i), R1)
         place_coefficients(s, i, 2 + par, own[rows, :])
         place_coefficients(s, i, 3 - par, other[rows, :])
-        place_coefficients(s, i, sides(par, 0)[0], beside[pl.ds(R1 * (4 + i), R1), :])
-        place_coefficients(s, i, sides(par, 1)[0], beside[rows, :])
+        place_coefficients(s, i, sides(par, 0)[0], one[sent, :])
+        place_coefficients(s, i, sides(par, 1)[0], beside[sent, :])
     for k in range(7):
         middle_faces(s, w1, inv1, d1, 1 + 4 * par + k)
-    for k in range(2):
-        coarse[pl.ds(R2 * k, R2), :] = pack4(coarser(level2_load(s, k), R2, 2))
-
-
-def extend_kernel(lo, rhs, hi, xedge, s, inv, coarse, send, send2):
+
+
+def chip_coefficients_kernel(own, other, xs, out, s, u):
     par = parity()
-    send[:G1] = lo[...]
-    send[pl.ds(G1, H1), :] = rhs[...]
-    send[pl.ds(G1 + H1, G1), :] = hi[...]
-    send[pl.ds(R1, EY), :] = xedge[...]
+    for i in range(4):
+        rows = pl.ds(R1 * i, R1)
+        for p, ref in ((par, own), (1 - par, other)):
+            v0, v1 = unpack2(ref[rows, :])
+            s[i, 2 * p] = v0
+            s[i, 2 * p + 1] = v1
+    s[1, 4] = unpack2(xs[pl.ds(SRAW, R1), :])[0]
+    q = 3 * par
+    u[:R1] = s[2, q]
+    u[R1:] = jnp.zeros((PAD, PZ), F32)
+    _, inv, _ = faces(s[0, q], s[1, q], s[1, q + 1], u[:R1], u[pl.ds(1, R1), :], s[3, q], 2, 0.25)
+    out[:R1] = inv * (1.0 / THETA)
+    out[pl.ds(R1, R1), :] = s[1, q]
+    for c in range(2):
+
+        def load(i, k, row):
+            return s[i, 2 * c + k, pl.ds(row, R2, 2), :]
+
+        out[pl.ds(2 * R1 + R2 * c, R2), :] = pack4(coarser(load, R2, 2))
+
+
+def extend_kernel(lo, rhs, hi, xedge, raw, chip, send, send1, send2):
+    par = parity()
+    for out in (send, send1):
+        out[:G1] = lo[...]
+        out[pl.ds(G1, H1), :] = rhs[...]
+        out[pl.ds(G1 + H1, G1), :] = hi[...]
+        out[pl.ds(R1, 4 * R1), :] = raw[...]
+    send[pl.ds(5 * R1, EY), :] = xedge[...]
     v = send[:R1]
     odd = jnp.broadcast_to(par, v.shape)
     v0, v1 = unpack2(v)
-    q = C0 + 3 * par
-    x1 = inv[q] * jnp.where(odd == 0, v0, v1) * (1.0 / THETA)
-    send2[:R1] = pack2(x1, s[1, q, pl.ds(PAD, R1), :])
-    send2[R1:] = coarse[...]
-
-
-def join_kernel(own, edge, one, beside, two, raw_beside, out):
+    send2[:R1] = pack2(chip[:R1] * jnp.where(odd == 0, v0, v1), chip[pl.ds(R1, R1), :])
+    send2[R1:] = chip[pl.ds(2 * R1, R1), :]
+
+
+def join_kernel(own, edge, one, beside, two, out):
     out[:R1] = own[:R1]
     out[pl.ds(O_EDGE, EY), :] = edge[...]
     out[pl.ds(O_ONE, R1), :] = one[:R1]
     out[pl.ds(O_BESIDE, R1), :] = beside[:R1]
     out[pl.ds(O_TWO, 2 * R1), :] = two[...]
-    out[pl.ds(O_RAW, 4 * R1), :] = raw_beside[pl.ds(4 * R1, 4 * R1), :]
-    out[pl.ds(O_RAW + 4 * R1, 4 * R1), :] = raw_beside[pl.ds(0, 4 * R1), :]
+    out[pl.ds(O_RAW, 4 * R1), :] = one[pl.ds(R1, 4 * R1), :]
+    out[pl.ds(O_RAW + 4 * R1, 4 * R1), :] = beside[pl.ds(R1, 4 * R1), :]
+
+
+def tick_kernel(_, out):
+    out[...] = jnp.zeros(out.shape, F32)
+
+
+def first_to_arrive(v):
+    return call(tick_kernel, "tick", shape(PAD, PZ), VMEM, [ANY], [], LARGE)(v)
 
 
 def both_sides(par, mine, its):
@@ -578,7 +611,7 @@
         if 0 < q < 7:
             x0[q, body, :] += pre0[q - 1]
     x0[near, body, :] += sw[pl.ds(O_EDGE, EY), :]
-    x0[far, body, :] += xs[pl.ds(R1, EY), :]
+    x0[far, body, :] += xs[pl.ds(5 * R1, EY), :]
     off = Q0 - 2
     sweep(x0, None, c0, w0, 1, 7, (0, EY), 1, 0, into(y0), 40, woff=off, coff=off, unroll=6)
 
@@ -619,40 +652,41 @@
     )(*[pltpu.with_memory_space_constraint(v, pltpu.HBM) for v in (right_side, alpha_coef, beta_x, beta_y, beta_z)])
     lo = shifted(yhi, "narrow", 1)
     hi = shifted(ylo, "narrow", -1)
-    own, xs = call(
-        corner_kernel, "corners", (shape(RAW + 4 * R1, PZ), shape(8 * EY, PZ)), (VMEM,) * 2, [VMEM] * 4,
-        [scratch(3, EY + 2 * PAD, PZ)], SMALL,
+    own, sw, xs = call(
+        corner_kernel, "corners", (shape(RAW + 4 * R1, PZ), shape(SRAW + 4 * R1, PZ), shape(SRAW + R1, PZ)),
+        (VMEM,) * 3, [VMEM] * 4, [scratch(3, EY + 2 * PAD, PZ), scratch(2, 3 * EY, PZ)], SMALL,
     )(a, raw, lo, hi)
     xs = across(xs, 1)
-    sw = swap(own)
-    raw_beside = from_beside(jnp.concatenate([own[RAW:], sw[RAW:]], 0))
+    sw = swap(sw)
 
     rhs, rhs_lo, rhs_hi, edge0, xedge0, pre0, w0, c0 = call(
         fine_kernel, "level0_pre",
         (shape(H1, PZ), shape(G1, PZ), shape(G1, PZ), shape(EY, PZ), shape(EY, PZ), shape(6, EY, PZ),
          shape(6, 10, EY, PZ), shape(10, EY, PZ)),
-        (VMEM,) * 8, [VMEM] * 3,
-        [scratch(12, EY, PZ), scratch(10, EY, PZ)] + [scratch(10, EY + 2 * PAD, PZ)] * 3 + [scratch(2, EY, PZ)],
+        (VMEM,) * 8, [VMEM] * 3 + [ANY],
+        [scratch(10, EY, PZ), scratch(10, EY, PZ)] + [scratch(10, EY + 2 * PAD, PZ)] * 3 + [scratch(2, EY, PZ)],
         LARGE,
-    )(own, sw, xs)
+    )(own, sw, xs, first_to_arrive(xs))
     rhs_below = shifted(rhs_hi, "narrow", 1)
     rhs_above = shifted(rhs_lo, "narrow", -1)
+    chip = call(
+        chip_coefficients_kernel, "chip_coefficients", shape(3 * R1, PZ), VMEM, [VMEM] * 3,
+        [scratch(4, 5, R1, PZ), scratch(R1 + PAD, PZ)], LARGE,
+    )(own[RAW:], sw[SRAW:], xs)
+    send, send1, send2 = call(
+        extend_kernel, "extend", (shape(5 * R1 + EY, PZ), shape(5 * R1, PZ), shape(2 * R1, PZ)), (VMEM,) * 3,
+        [VMEM] * 6, [], SMALL,
+    )(rhs_below, rhs, rhs_above, xedge0, own[RAW:], chip)
+
+    one = across(send, 1)
+    beside = from_beside(send1)
+    two = across(send2, 2)
+    mine = call(join_kernel, "join", shape(O_END, PZ), VMEM, [VMEM] * 5, [], SMALL)(send, edge0, one, beside, two)
+    its = swap(mine)
     w1_shapes = (shape(*S_SHAPE), shape(6, N1, R1, PZ), shape(N1, R1, PZ), shape(N1, R1, PZ))
-    s1, w1, inv1, d1, coarse = call(
-        near_coefficients_kernel, "near_coefficients", w1_shapes + (shape(R1, PZ),),
-        (VMEM,) * 5, [VMEM] * 3, [], LARGE,
-    )(own[RAW:], sw[RAW:], raw_beside)
-    send, send2 = call(
-        extend_kernel, "extend", (shape(R1 + EY, PZ), shape(2 * R1, PZ)), (VMEM,) * 2, [VMEM] * 7, [], SMALL
-    )(rhs_below, rhs, rhs_above, xedge0, s1, inv1, coarse)
-
-    one = across(send, 1)
-    beside = from_beside(send[:R1])
-    two = across(send2, 2)
-    mine = call(join_kernel, "join", shape(O_END, PZ), VMEM, [VMEM] * 6, [], SMALL)(
-        send, edge0, one, beside, two, raw_beside
-    )
-    its = swap(mine)
+    s1, w1, inv1, d1 = call(
+        near_coefficients_kernel, "near_coefficients", w1_shapes, (VMEM,) * 4, [VMEM] * 4, [], LARGE,
+    )(own[RAW:], sw[SRAW:], one, beside)
 
     edge, c1, pre1, rhs2, s1, w1, _, _ = call(
         middle_kernel, "level1_pre",

time: 74.1 us -> 73 us (0.985)
  starting transfers between devices: 42.6 us -> 38.4 us
  waiting for transfers between devices: 22.6 us -> 26.3 us
    ppermute x4, waiting for transfers between devices: 8.44 us -> 17.3 us  [across(): return lax.ppermute(v, 'wide', pairs + list(ends))]
    ppermute x2 -> x1, waiting for transfers between devices: 4.98 us -> 0.01 us  [from_beside(): return lax.ppermute(v, 'wide', pairs)]
    ppermute x2 -> x1, starting transfers between devices: 4.92 us -> 1.92 us  [from_beside(): return lax.ppermute(v, 'wide', pairs)]
    ppermute x3, starting transfers between devices: 7.27 us -> 5.75 us  [swap(): lax.ppermute(v, 'wide', [(i, i ^ 1) for i in range(lax.axis_size('wide'))])]
  transfers between devices with their start and end apart: 13 -> 12, of which waited for: 8 -> 8; matrix products, arithmetic and copies ran while one was open for 0% -> 0% of each run, Pallas kernels for 3% -> 2%
where the time goes in v4:
time: 73 us; the launch traced here: 72.5 us
  starting transfers between devices  38.4 us (53%)
  waiting for transfers between devices  26.3 us (36%)
  Pallas kernels  7.58 us (10%)
    ppermute x4, starting transfers between devices, across(): return lax.ppermute(v, 'wide', pairs + list(ends))  19.2 us
    ppermute x4, waiting for transfers between devices, across(): return lax.ppermute(v, 'wide', pairs + list(ends))  17.3 us
    ppermute x4, starting transfers between devices, shifted(): lax.ppermute(v, axis, [(i, i + step) for i in range(count) if 0 <= i + st...  11.6 us
    ppermute x4, waiting for transfers between devices, shifted(): lax.ppermute(v, axis, [(i, i + step) for i in range(count) if 0 <= i + st...  6.96 us
    ppermute x3, starting transfers between devices, swap(): lax.ppermute(v, 'wide', [(i, i ^ 1) for i in range(lax.axis_size('wide'))])  5.75 us
    ppermute x3, waiting for transfers between devices, swap(): lax.ppermute(v, 'wide', [(i, i ^ 1) for i in range(lax.axis_size('wide'))])  1.96 us
    ppermute x1, starting transfers between devices, from_beside(): return lax.ppermute(v, 'wide', pairs)  1.92 us
    pallas_call x1, Pallas kernels, shards(): call(last_kernel, 'coarse_and_post', shape(PX, PY, PZ), VMEM, [VMEM] * 14...  1.86 us
  transfers between devices with their start and end apart: 12, of which 8 were waited for; matrix products, arithmetic and copies ran while one was open for 0% of the time, Pallas kernels for 2%

profile of v4, /device:TPU:215, one launch (start us, length us, event | category | flops | bytes accessed | tf_op | source)
XLA Modules:
  0.0 72.5 jit_solution(2197247204537765900)
XLA Ops:
  0.0 1.3 %pack.1 = (f32[5,4,64,128]{3,2,1,0:T(8,128)S(1)}, f32[224,128]{1,0:T(8,128)S(1)}, f32[224,128]{1,0:T(8,128)S(1)}, f32[4,32,128]{2,1,0:T(8,128)S(1)}) custom-call(f32[4,64,128]{2,1,0:T(8,128)} %b.1, f32[4,64,128]{2,1,0:T(8,128)} %al.1, f32[4,64,128]{2,1,0:T(8,128)} %bx.1, f32[4,64,128]{2,1,0:T(8,128)} %by.1, f32[4,64,128]{2,1,0:T(8,128)} %bz.1), custom_call_target="tpu_custom_call" | custom-call | flops 1000 | tf_op jit(solution)/shard_map/pack/pallas_call | solution.py:648
  1.4 3.2 %collective-permute-start = (f32[224,128]{1,0:T(8,128)S(1)}, f32[224,128]{1,0:T(8,128)S(1)}, u32[]{:S(2)}, u32[]{:S(2)}) collective-permute-start(f32[224,128]{1,0:T(8,128)S(1)} %get-tuple-element.38), channel_id=1, source_target_pairs={{0,1},{1,2},{2,3},{3,4},{4,5},{5,6},{6,7},{8,9},{9,10},{10,11},{11... | collective-permute-start | bytes 344072 | tf_op jit(solution)/shard_map/ppermute | solution.py:644
  4.6 2.1 %collective-permute-start.1 = (f32[224,128]{1,0:T(8,128)S(1)}, f32[224,128]{1,0:T(8,128)S(1)}, u32[]{:S(2)}, u32[]{:S(2)}) collective-permute-start(f32[224,128]{1,0:T(8,128)S(1)} %get-tuple-element.39), channel_id=1, source_target_pairs={{1,0},{2,1},{3,2},{4,3},{5,4},{6,5},{7,6},{9,8},{10,9},{11,10},{12... | collective-permute-start | bytes 344072 | tf_op jit(solution)/shard_map/ppermute | solution.py:644
  6.7 0.6 collective-permute-done.lo
  7.3 4.3 %collective-permute-done.1.hi = f32[224,128]{1,0:T(8,128)S(1)} collective-permute-done((f32[224,128]{1,0:T(8,128)S(1)}, f32[224,128]{1,0:T(8,128)S(1)}, u32[]{:S(2)}, u32[]{:S(2)}) %collective-permute-start.1) | collective-permute-done | bytes 114720 | tf_op jit(solution)/shard_map/ppermute | solution.py:644
  11.5 0.3 corners.1
  11.9 6.6 %collective-permute-start.3 = (f32[704,128]{1,0:T(8,128)S(1)}, f32[704,128]{1,0:T(8,128)S(1)}, u32[]{:S(2)}, u32[]{:S(2)}) collective-permute-start(f32[704,128]{1,0:T(8,128)S(1)} %get-tuple-element.42), channel_id=1, source_target_pairs={{8,16},{24,32},{40,48},{56,64},{72,80},{88,96},{104,112},{120,128}... | collective-permute-start | bytes 1081352 | tf_op jit(solution)/shard_map/ppermute | solution.py:633
  18.4 1.9 %collective-permute-start.2 = (f32[896,128]{1,0:T(8,128)S(1)}, f32[896,128]{1,0:T(8,128)S(1)}, u32[]{:S(2)}, u32[]{:S(2)}) collective-permute-start(f32[896,128]{1,0:T(8,128)S(1)} %get-tuple-element.41), channel_id=1, source_target_pairs={{0,8},{8,0},{16,24},{24,16},{32,40},{40,32},{48,56},{56,48},{64,72... | collective-permute-start | bytes 1376264 | tf_op jit(solution)/shard_map/ppermute | solution.py:625
  20.4 3.6 %collective-permute-done.3._.xs = f32[704,128]{1,0:T(8,128)S(1)} collective-permute-done((f32[704,128]{1,0:T(8,128)S(1)}, f32[704,128]{1,0:T(8,128)S(1)}, u32[]{:S(2)}, u32[]{:S(2)}) %collective-permute-start.3) | collective-permute-done | bytes 360480 | tf_op jit(solution)/shard_map/ppermute | solution.py:633
  23.9 0.0 collective-permute-done.2.sw
  23.9 0.9 %level0_pre.1 = (f32[32,128]{1,0:T(8,128)S(1)}, f32[16,128]{1,0:T(8,128)S(1)}, f32[16,128]{1,0:T(8,128)S(1)}, f32[80,128]{1,0:T(8,128)S(1)}, f32[80,128]{1,0:T(8...) custom-call(f32[1856,128]{1,0:T(8,128)S(1)} %get-tuple-element.40.own, ...), custom_call_target="tpu_custom_call" | custom-call | flops 20000000000 | tf_op jit(solution)/shard_map/level0_pre/pallas_call | solution.py:662
  24.8 4.4 %collective-permute-start.4 = (f32[16,128]{1,0:T(8,128)S(1)}, f32[16,128]{1,0:T(8,128)S(1)}, u32[]{:S(2)}, u32[]{:S(2)}) collective-permute-start(f32[16,128]{1,0:T(8,128)S(1)} %get-tuple-element.43), channel_id=1, source_target_pairs={{0,1},{1,2},{2,3},{3,4},{4,5},{5,6},{6,7},{8,9},{9,10},{10,11},{11... | collective-permute-start | bytes 24584 | tf_op jit(solution)/shard_map/ppermute | solution.py:644
  29.2 1.9 %collective-permute-start.5 = (f32[16,128]{1,0:T(8,128)S(1)}, f32[16,128]{1,0:T(8,128)S(1)}, u32[]{:S(2)}, u32[]{:S(2)}) collective-permute-start(f32[16,128]{1,0:T(8,128)S(1)} %get-tuple-element.45), channel_id=1, source_target_pairs={{1,0},{2,1},{3,2},{4,3},{5,4},{6,5},{7,6},{9,8},{10,9},{11,10},{12... | collective-permute-start | bytes 24584 | tf_op jit(solution)/shard_map/ppermute | solution.py:644
  31.1 0.3 chip_coefficients.1.chip
  31.5 0.0 collective-permute-done.4.lo
  31.5 2.1 %collective-permute-done.5.hi = f32[16,128]{1,0:T(8,128)S(1)} collective-permute-done((f32[16,128]{1,0:T(8,128)S(1)}, f32[16,128]{1,0:T(8,128)S(1)}, u32[]{:S(2)}, u32[]{:S(2)}) %collective-permute-start.5) | collective-permute-done | bytes 8224 | tf_op jit(solution)/shard_map/ppermute | solution.py:644
  33.6 0.1 extend.1
  33.7 8.4 %collective-permute-start.6 = (f32[400,128]{1,0:T(8,128)S(1)}, f32[400,128]{1,0:T(8,128)S(1)}, u32[]{:S(2)}, u32[]{:S(2)}) collective-permute-start(f32[400,128]{1,0:T(8,128)S(1)} %get-tuple-element.47.own), channel_id=1, source_target_pairs={{8,16},{24,32},{40,48},{56,64},{72,80},{88,96},{104,112},{120,128}... | collective-permute-start | bytes 614408 | tf_op jit(solution)/shard_map/ppermute | solution.py:633
  42.1 1.9 %collective-permute-start.7 = (f32[320,128]{1,0:T(8,128)S(1)}, f32[320,128]{1,0:T(8,128)S(1)}, u32[]{:S(2)}, u32[]{:S(2)}) collective-permute-start(f32[320,128]{1,0:T(8,128)S(1)} %get-tuple-element.48), channel_id=1, source_target_pairs={{0,16},{16,32},{32,48},{48,64},{64,80},{80,96},{96,112},{112,128},... | collective-permute-start | bytes 491528 | tf_op jit(solution)/shard_map/ppermute | solution.py:639
  44.0 1.9 %collective-permute-start.8 = (f32[128,128]{1,0:T(8,128)S(1)}, f32[128,128]{1,0:T(8,128)S(1)}, u32[]{:S(2)}, u32[]{:S(2)}) collective-permute-start(f32[128,128]{1,0:T(8,128)S(1)} %get-tuple-element.49), channel_id=1, source_target_pairs={{8,32},{24,48},{40,64},{56,80},{72,96},{88,112},{104,128},{120,144... | collective-permute-start | bytes 196616 | tf_op jit(solution)/shard_map/ppermute | solution.py:633
  45.9 7.3 %collective-permute-done.8.two = f32[128,128]{1,0:T(8,128)S(1)} collective-permute-done((f32[128,128]{1,0:T(8,128)S(1)}, f32[128,128]{1,0:T(8,128)S(1)}, u32[]{:S(2)}, u32[]{:S(2)}) %collective-permute-start.8) | collective-permute-done | bytes 65568 | tf_op jit(solution)/shard_map/ppermute | solution.py:633
  53.2 0.0 collective-permute-done.7.beside
  53.2 0.0 collective-permute-done.6.one.xs
  53.3 1.9 %collective-permute-start.9 = (f32[912,128]{1,0:T(8,128)S(1)}, f32[912,128]{1,0:T(8,128)S(1)}, u32[]{:S(2)}, u32[]{:S(2)}) collective-permute-start(f32[912,128]{1,0:T(8,128)S(1)} %join.1), channel_id=1, source_target_pairs={{0,8},{8,0},{16,24},{24,16},{32,40},{40,32},{48,56},{56,48},{64,72... | collective-permute-start | bytes 1400840 | tf_op jit(solution)/shard_map/ppermute | solution.py:625
  55.2 0.5 near_coefficients.1
  55.7 1.2 %collective-permute-done.9.its.sw = f32[912,128]{1,0:T(8,128)S(1)} collective-permute-done((f32[912,128]{1,0:T(8,128)S(1)}, f32[912,128]{1,0:T(8,128)S(1)}, u32[]{:S(2)}, u32[]{:S(2)}) %collective-permute-start.9) | collective-permute-done | bytes 466976 | tf_op jit(solution)/shard_map/ppermute | solution.py:625
  57.0 1.7 %level1_pre.1 = (f32[64,128]{1,0:T(8,128)S(1)}, f32[14,64,128]{2,1,0:T(8,128)S(1)}, f32[10,64,128]{2,1,0:T(8,128)S(1)}, f32[4,32,128]{2,1,0:T(8,128)S(1)}, f32[4...) custom-call(f32[400,128]{1,0:T(8,128)S(1)} %get-tuple-element.47.own, ...), custom_call_target="tpu_custom_call", output_to_operand_aliasing={{4}: (5, {}), {5}: (6, {}), {6}: (7, {}), {7}: (8, {})} | custom-call | flops 20000000000 | tf_op jit(solution)/shard_map/level1_pre/pallas_call | solution.py:691
  58.7 2.3 %collective-permute-start.10 = (f32[64,128]{1,0:T(8,128)S(1)}, f32[64,128]{1,0:T(8,128)S(1)}, u32[]{:S(2)}, u32[]{:S(2)}) collective-permute-start(f32[64,128]{1,0:T(8,128)S(1)} %get-tuple-element.55), channel_id=1, source_target_pairs={{8,32},{24,48},{40,64},{56,80},{72,96},{88,112},{104,128},{120,144... | collective-permute-start | bytes 98312 | tf_op jit(solution)/shard_map/ppermute | solution.py:633
  61.0 6.5 %collective-permute-done.10.two2 = f32[64,128]{1,0:T(8,128)S(1)} collective-permute-done((f32[64,128]{1,0:T(8,128)S(1)}, f32[64,128]{1,0:T(8,128)S(1)}, u32[]{:S(2)}, u32[]{:S(2)}) %collective-permute-start.10) | collective-permute-done | bytes 32800 | tf_op jit(solution)/shard_map/ppermute | solution.py:633
  67.5 1.9 %collective-permute-start.11 = (f32[64,128]{1,0:T(8,128)S(1)}, f32[64,128]{1,0:T(8,128)S(1)}, u32[]{:S(2)}, u32[]{:S(2)}) collective-permute-start(f32[64,128]{1,0:T(8,128)S(1)} %collective-permute-done.10.two2), channel_id=1, source_target_pairs={{0,8},{8,0},{16,24},{24,16},{32,40},{40,32},{48,56},{56,48},{64,72... | collective-permute-start | bytes 98312 | tf_op jit(solution)/shard_map/ppermute | solution.py:625
  69.4 0.5 level2_coefficients.1
  69.9 0.7 collective-permute-done.11.its2
  70.6 1.9 %coarse_and_post.1 = f32[4,64,128]{2,1,0:T(8,128)} custom-call(f32[64,128]{1,0:T(8,128)S(1)} %collective-permute-done.10.two2, f32[64,128]{1,0:T(8,128)S(1)} %collective-permute-done.11.its2, f32[4,32,128]{2,1,0:T(8,128)S(1)} %get-tuple-element.56.rhs, f32[6,12,32,128]{3,2,1,0:T(8,128)S(1)} %get-tuple-element.58.w2, ...), custom_call_target="tpu_custom_call" | custom-call | flops 20000000000 | tf_op jit(solution)/shard_map/coarse_and_post/pallas_call | solution.py:707
  (4 shorter events, 0.1 us)
Async XLA Ops:
  1.4 5.9 %collective-permute-start = (f32[224,128]{1,0:T(8,128)S(1)}, f32[224,128]{1,0:T(8,128)S(1)}, u32[]{:S(2)}, u32[]{:S(2)}) collective-permute-start(f32[224,128]{1,0:T(8,128)S(1)} %get-tuple-element.38), channel_id=1, source_target_pairs={{0,1},{1,2},{2,3},{3,4},{4,5},{5,6},{6,7},{8,9},{9,10},{10,11},{11... | collective-permute-start | bytes 344072 | tf_op jit(solution)/shard_map/ppermute | solution.py:644
  4.6 7.0 %collective-permute-start.1 = (f32[224,128]{1,0:T(8,128)S(1)}, f32[224,128]{1,0:T(8,128)S(1)}, u32[]{:S(2)}, u32[]{:S(2)}) collective-permute-start(f32[224,128]{1,0:T(8,128)S(1)} %get-tuple-element.39), channel_id=1, source_target_pairs={{1,0},{2,1},{3,2},{4,3},{5,4},{6,5},{7,6},{9,8},{10,9},{11,10},{12... | collective-permute-start | bytes 344072 | tf_op jit(solution)/shard_map/ppermute | solution.py:644
  11.9 12.1 %collective-permute-start.3 = (f32[704,128]{1,0:T(8,128)S(1)}, f32[704,128]{1,0:T(8,128)S(1)}, u32[]{:S(2)}, u32[]{:S(2)}) collective-permute-start(f32[704,128]{1,0:T(8,128)S(1)} %get-tuple-element.42), channel_id=1, source_target_pairs={{8,16},{24,32},{40,48},{56,64},{72,80},{88,96},{104,112},{120,128}... | collective-permute-start | bytes 1081352 | tf_op jit(solution)/shard_map/ppermute | solution.py:633
  18.4 5.5 %collective-permute-start.2 = (f32[896,128]{1,0:T(8,128)S(1)}, f32[896,128]{1,0:T(8,128)S(1)}, u32[]{:S(2)}, u32[]{:S(2)}) collective-permute-start(f32[896,128]{1,0:T(8,128)S(1)} %get-tuple-element.41), channel_id=1, source_target_pairs={{0,8},{8,0},{16,24},{24,16},{32,40},{40,32},{48,56},{56,48},{64,72... | collective-permute-start | bytes 1376264 | tf_op jit(solution)/shard_map/ppermute | solution.py:625
  24.8 6.7 %collective-permute-start.4 = (f32[16,128]{1,0:T(8,128)S(1)}, f32[16,128]{1,0:T(8,128)S(1)}, u32[]{:S(2)}, u32[]{:S(2)}) collective-permute-start(f32[16,128]{1,0:T(8,128)S(1)} %get-tuple-element.43), channel_id=1, source_target_pairs={{0,1},{1,2},{2,3},{3,4},{4,5},{5,6},{6,7},{8,9},{9,10},{10,11},{11... | collective-permute-start | bytes 24584 | tf_op jit(solution)/shard_map/ppermute | solution.py:644
  29.2 4.4 %collective-permute-start.5 = (f32[16,128]{1,0:T(8,128)S(1)}, f32[16,128]{1,0:T(8,128)S(1)}, u32[]{:S(2)}, u32[]{:S(2)}) collective-permute-start(f32[16,128]{1,0:T(8,128)S(1)} %get-tuple-element.45), channel_id=1, source_target_pairs={{1,0},{2,1},{3,2},{4,3},{5,4},{6,5},{7,6},{9,8},{10,9},{11,10},{12... | collective-permute-start | bytes 24584 | tf_op jit(solution)/shard_map/ppermute | solution.py:644
  33.7 19.5 %collective-permute-start.6 = (f32[400,128]{1,0:T(8,128)S(1)}, f32[400,128]{1,0:T(8,128)S(1)}, u32[]{:S(2)}, u32[]{:S(2)}) collective-permute-start(f32[400,128]{1,0:T(8,128)S(1)} %get-tuple-element.47.own), channel_id=1, source_target_pairs={{8,16},{24,32},{40,48},{56,64},{72,80},{88,96},{104,112},{120,128}... | collective-permute-start | bytes 614408 | tf_op jit(solution)/shard_map/ppermute | solution.py:633
  42.1 11.1 %collective-permute-start.7 = (f32[320,128]{1,0:T(8,128)S(1)}, f32[320,128]{1,0:T(8,128)S(1)}, u32[]{:S(2)}, u32[]{:S(2)}) collective-permute-start(f32[320,128]{1,0:T(8,128)S(1)} %get-tuple-element.48), channel_id=1, source_target_pairs={{0,16},{16,32},{32,48},{48,64},{64,80},{80,96},{96,112},{112,128},... | collective-permute-start | bytes 491528 | tf_op jit(solution)/shard_map/ppermute | solution.py:639
  44.0 9.2 %collective-permute-start.8 = (f32[128,128]{1,0:T(8,128)S(1)}, f32[128,128]{1,0:T(8,128)S(1)}, u32[]{:S(2)}, u32[]{:S(2)}) collective-permute-start(f32[128,128]{1,0:T(8,128)S(1)} %get-tuple-element.49), channel_id=1, source_target_pairs={{8,32},{24,48},{40,64},{56,80},{72,96},{88,112},{104,128},{120,144... | collective-permute-start | bytes 196616 | tf_op jit(solution)/shard_map/ppermute | solution.py:633
  53.3 3.7 %collective-permute-start.9 = (f32[912,128]{1,0:T(8,128)S(1)}, f32[912,128]{1,0:T(8,128)S(1)}, u32[]{:S(2)}, u32[]{:S(2)}) collective-permute-start(f32[912,128]{1,0:T(8,128)S(1)} %join.1), channel_id=1, source_target_pairs={{0,8},{8,0},{16,24},{24,16},{32,40},{40,32},{48,56},{56,48},{64,72... | collective-permute-start | bytes 1400840 | tf_op jit(solution)/shard_map/ppermute | solution.py:625
  58.7 8.8 %collective-permute-start.10 = (f32[64,128]{1,0:T(8,128)S(1)}, f32[64,128]{1,0:T(8,128)S(1)}, u32[]{:S(2)}, u32[]{:S(2)}) collective-permute-start(f32[64,128]{1,0:T(8,128)S(1)} %get-tuple-element.55), channel_id=1, source_target_pairs={{8,32},{24,48},{40,64},{56,80},{72,96},{88,112},{104,128},{120,144... | collective-permute-start | bytes 98312 | tf_op jit(solution)/shard_map/ppermute | solution.py:633
  67.5 3.1 %collective-permute-start.11 = (f32[64,128]{1,0:T(8,128)S(1)}, f32[64,128]{1,0:T(8,128)S(1)}, u32[]{:S(2)}, u32[]{:S(2)}) collective-permute-start(f32[64,128]{1,0:T(8,128)S(1)} %collective-permute-done.10.two2), channel_id=1, source_target_pairs={{0,8},{8,0},{16,24},{24,16},{32,40},{40,32},{48,56},{56,48},{64,72... | collective-permute-start | bytes 98312 | tf_op jit(solution)/shard_map/ppermute | solution.py:625

commit v5 on v4

--- a/solution.py
+++ b/solution.py
@@ -16,15 +16,14 @@
 GAIN = [1.0 / THETA] + [2.0 * RHO[k] / DELTA for k in range(1, 4)]
 
 PX, PY, PZ = 4, 64, 128
-HY = 8
+HY = 32
 EY = PY + 2 * HY
-H1 = PY // 2
-G1 = 16
-R1 = H1 + 2 * G1
+MID = PY + 16
+MID0 = HY - 8
+R1 = EY // 2
 R2 = R1 // 2
 RAW = 5 * PX * EY
 SRAW = 8 * EY
-SIDE = 5 * PX * HY
 PAD = 8
 SMALL, LARGE = 1000, 2 * 10**10
 B, ALPHA, BX, BY, BZ = range(5)
@@ -192,7 +191,7 @@
     return al, bx, by, bz
 
 
-def pack_kernel(b, al, bx, by, bz, a, lo_out, hi_out, raw, sems):
+def pack_kernel(b, al, bx, by, bz, a, lo_out, hi_out, sems):
     wide, narrow = lax.axis_index("wide"), lax.axis_index("narrow")
     copies = [pltpu.make_async_copy(ref, a.at[i], sems.at[i]) for i, ref in enumerate((b, al, bx, by, bz))]
     for c in copies:
@@ -206,18 +205,6 @@
     for p in range(PX):
         a[BY, p, :PAD] = jnp.where(first_row, 0.0, a[BY, p, :PAD])
         a[BZ, p] = jnp.where(first_z, 0.0, a[BZ, p])
-    got = []
-    for c in range(2):
-
-        def load(i, k, row):
-            return a[i + 1, 2 * c + k, pl.ds(row, H1, 2), :]
-
-        got.append(coarser(load, H1, 1))
-    for i in range(4):
-        v = pack2(got[0][i], got[1][i])
-        raw[i] = v
-        lo_out[pl.ds(SIDE + G1 * i, G1), :] = v[:G1]
-        hi_out[pl.ds(SIDE + G1 * i, G1), :] = v[H1 - G1 :]
     for i in range(5):
         for p in range(PX):
             here = pl.ds((PX * i + p) * HY, HY)
@@ -230,7 +217,7 @@
     return ref[pl.ds(pl.multiple_of(start, 8) if r0 % 8 == 0 else start, n), :]
 
 
-def corner_kernel(a, raw, lo, hi, own, sw, xs, x, v):
+def corner_kernel(a, lo, hi, own, sw, xs, x, v):
     par = parity()
     for i in range(5):
         for p in range(PX):
@@ -238,12 +225,17 @@
             own[pl.ds(k * EY, HY), :] = lo[pl.ds(k * HY, HY), :]
             own[pl.ds(k * EY + HY, PY), :] = a[i, p]
             own[pl.ds(k * EY + HY + PY, HY), :] = hi[pl.ds(k * HY, HY), :]
+    got = []
+    for c in range(2):
+
+        def load(i, k, row):
+            return own[pl.ds((PX * (i + 1) + 2 * c + k) * EY + row, R1, 2), :]
+
+        got.append(coarser(load, R1, 1))
     for i in range(4):
-        here = pl.ds(SIDE + G1 * i, G1)
-        for ref, base in ((own, RAW + R1 * i), (sw, SRAW + R1 * i)):
-            ref[pl.ds(base, G1), :] = lo[here, :]
-            ref[pl.ds(base + G1, H1), :] = raw[i]
-            ref[pl.ds(base + G1 + H1, G1), :] = hi[here, :]
+        t = pack2(got[0][i], got[1][i])
+        own[pl.ds(RAW + R1 * i, R1), :] = t
+        sw[pl.ds(SRAW + R1 * i, R1), :] = t
     xs[pl.ds(SRAW, R1), :] = own[pl.ds(RAW + R1, R1), :]
     for i in range(5):
         here = pl.ds(i * EY, EY)
@@ -280,9 +272,15 @@
 Q0 = 3
 
 
-def fine_kernel(own, sw, xs, _, rhs, rhs_lo, rhs_hi, edge, xedge, pre, w, cc, sx, d, x, y, z, t):
+def fine_kernel(own, sw, xs, _, send, send1, send2, edge, pre, w, cc, sx, d, x, y, z, t, s, u):
     par = parity()
     sides2 = ((xs, par), (sw, 1 - par))
+    for i in range(4):
+        for p, ref, base in ((par, own, RAW), (1 - par, sw, SRAW)):
+            v0, v1 = unpack2(ref[pl.ds(base + R1 * i, R1), :])
+            s[i, 2 * p] = v0
+            s[i, 2 * p + 1] = v1
+    s[1, 4] = unpack2(xs[pl.ds(SRAW, R1), :])[0]
     for p in range(PX):
         sx[Q0 + p] = plane(own, PX * BX + p)
     for ref, above in sides2:
@@ -290,7 +288,7 @@
         sx[9 - above] = plane(ref, 7)
     clear_pads(x, EY)
     clear_pads(y, EY)
-    chunk = 40
+    chunk = 32
 
     def prepare(q, get):
         for r0 in range(0, EY, chunk):
@@ -332,14 +330,26 @@
                 _, zz = defect(z, cc, w, q, r0, chunk, 1, q, 0, q, 0)
                 v = v + d[q, pl.ds(r0, chunk), :] * zz
             t[c, pl.ds(r0, chunk), :] = v
-        got.append(pair_lanes(t[c, pl.ds(HY, H1, 2), :] + t[c, pl.ds(HY + 1, H1, 2), :], 1) * 0.125)
-    v = pack2(got[0], got[1])
-    rhs[...] = v
-    rhs_lo[...] = v[:G1]
-    rhs_hi[...] = v[H1 - G1 :]
-    mid = pl.ds(PAD, EY)
+        got.append(pair_lanes(t[c, pl.ds(0, R1, 2), :] + t[c, pl.ds(1, R1, 2), :], 1) * 0.125)
+    mid = pl.ds(PAD + MID0, MID)
+    rhs = pack2(got[0], got[1])
+    for out in (send, send1):
+        out[:R1] = rhs
+        out[pl.ds(R1, 4 * R1), :] = own[pl.ds(RAW, 4 * R1), :]
     edge[...] = z[Q0 + 2 - par, mid, :]
-    xedge[...] = z[Q0 + 1 + par, mid, :]
+    send[pl.ds(5 * R1, MID), :] = z[Q0 + 1 + par, mid, :]
+    q = 3 * par
+    u[:R1] = s[2, q]
+    u[R1:] = jnp.zeros((PAD, PZ), F32)
+    _, inv, _ = faces(s[0, q], s[1, q], s[1, q + 1], u[:R1], u[pl.ds(1, R1), :], s[3, q], 2, 0.25)
+    x1 = inv * jnp.where(jnp.broadcast_to(par, rhs.shape) == 0, *unpack2(rhs)) * (1.0 / THETA)
+    send2[:R1] = pack2(x1, s[1, q])
+    for c in range(2):
+
+        def load(i, k, row):
+            return s[i, 2 * c + k, pl.ds(row, R2, 2), :]
+
+        send2[pl.ds(R1 + R2 * c, R2), :] = pack4(coarser(load, R2, 2))
     for p in range(6):
         pre[p] = z[Q0 - 1 + p, mid, :]
 
@@ -349,7 +359,7 @@
 M0 = 5
 S_SHAPE = (4, N1, R1 + 2 * PAD, PZ)
 O_EDGE = R1
-O_ONE = O_EDGE + EY
+O_ONE = O_EDGE + MID
 O_BESIDE = O_ONE + R1
 O_TWO = O_BESIDE + R1
 O_RAW = O_TWO + 2 * R1
@@ -401,47 +411,9 @@
         middle_faces(s, w1, inv1, d1, 1 + 4 * par + k)
 
 
-def chip_coefficients_kernel(own, other, xs, out, s, u):
-    par = parity()
-    for i in range(4):
-        rows = pl.ds(R1 * i, R1)
-        for p, ref in ((par, own), (1 - par, other)):
-            v0, v1 = unpack2(ref[rows, :])
-            s[i, 2 * p] = v0
-            s[i, 2 * p + 1] = v1
-    s[1, 4] = unpack2(xs[pl.ds(SRAW, R1), :])[0]
-    q = 3 * par
-    u[:R1] = s[2, q]
-    u[R1:] = jnp.zeros((PAD, PZ), F32)
-    _, inv, _ = faces(s[0, q], s[1, q], s[1, q + 1], u[:R1], u[pl.ds(1, R1), :], s[3, q], 2, 0.25)
-    out[:R1] = inv * (1.0 / THETA)
-    out[pl.ds(R1, R1), :] = s[1, q]
-    for c in range(2):
-
-        def load(i, k, row):
-            return s[i, 2 * c + k, pl.ds(row, R2, 2), :]
-
-        out[pl.ds(2 * R1 + R2 * c, R2), :] = pack4(coarser(load, R2, 2))
-
-
-def extend_kernel(lo, rhs, hi, xedge, raw, chip, send, send1, send2):
-    par = parity()
-    for out in (send, send1):
-        out[:G1] = lo[...]
-        out[pl.ds(G1, H1), :] = rhs[...]
-        out[pl.ds(G1 + H1, G1), :] = hi[...]
-        out[pl.ds(R1, 4 * R1), :] = raw[...]
-    send[pl.ds(5 * R1, EY), :] = xedge[...]
-    v = send[:R1]
-    odd = jnp.broadcast_to(par, v.shape)
-    v0, v1 = unpack2(v)
-    send2[:R1] = pack2(chip[:R1] * jnp.where(odd == 0, v0, v1), chip[pl.ds(R1, R1), :])
-    send2[R1:] = chip[pl.ds(2 * R1, R1), :]
-
-
 def join_kernel(own, edge, one, beside, two, out):
     out[:R1] = own[:R1]
-    out[pl.ds(O_EDGE, EY), :] = edge[...]
+    out[pl.ds(O_EDGE, MID), :] = edge[...]
     out[pl.ds(O_ONE, R1), :] = one[:R1]
     out[pl.ds(O_BESIDE, R1), :] = beside[:R1]
     out[pl.ds(O_TWO, 2 * R1), :] = two[...]
@@ -600,25 +572,25 @@
     sweep(x1, None, c1, w1, 1, 9, rows, 2, 0, into(y1), 32, woff=off, coff=off)
     sweep(y1, x1, c1, w1, 2, 8, rows, 2, 1, into(z1), 32, woff=off, coff=off, unroll=6)
 
-    clear_pads(x0, EY)
-    clear_pads(y0, EY)
+    clear_pads(x0, MID)
+    clear_pads(y0, MID)
     near, far = 7 - 7 * par, 7 * par
-    body = pl.ds(PAD, EY)
+    body = pl.ds(PAD, MID)
     for q in range(8):
-        v = z1[(q - 2) // 2 + 3 + 2 * par, pl.ds(PAD + 12, EY // 2), :]
-        x0[q, pl.ds(PAD, EY // 2, 2), :] = v
-        x0[q, pl.ds(PAD + 1, EY // 2, 2), :] = v
+        v = z1[(q - 2) // 2 + 3 + 2 * par, pl.ds(PAD + 12, MID // 2), :]
+        x0[q, pl.ds(PAD, MID // 2, 2), :] = v
+        x0[q, pl.ds(PAD + 1, MID // 2, 2), :] = v
         if 0 < q < 7:
             x0[q, body, :] += pre0[q - 1]
-    x0[near, body, :] += sw[pl.ds(O_EDGE, EY), :]
-    x0[far, body, :] += xs[pl.ds(5 * R1, EY), :]
+    x0[near, body, :] += sw[pl.ds(O_EDGE, MID), :]
+    x0[far, body, :] += xs[pl.ds(5 * R1, MID), :]
     off = Q0 - 2
-    sweep(x0, None, c0, w0, 1, 7, (0, EY), 1, 0, into(y0), 40, woff=off, coff=off, unroll=6)
+    sweep(x0, None, c0, w0, 1, 7, (0, MID), 1, 0, into(y0), 40, woff=off, coff=off, wr=MID0, cr=MID0, unroll=6)
 
     def finish(q, r0, n, v):
         out[q - 2, pl.ds(r0 - 8, n), :] = v
 
-    sweep(y0, x0, c0, w0, 2, 6, (8, 8 + PY), 1, 1, finish, 32, woff=off, coff=off, unroll=4)
+    sweep(y0, x0, c0, w0, 2, 6, (8, 8 + PY), 1, 1, finish, 32, woff=off, coff=off, wr=MID0, cr=MID0, unroll=4)
 
 
 def swap(v):
@@ -645,38 +617,28 @@
 
 
 def shards(right_side, alpha_coef, beta_x, beta_y, beta_z):
-    a, ylo, yhi, raw = call(
-        pack_kernel, "pack",
-        (shape(5, PX, PY, PZ), shape(SIDE + 4 * G1, PZ), shape(SIDE + 4 * G1, PZ), shape(4, H1, PZ)),
-        (VMEM,) * 4, [ANY] * 5, [pltpu.SemaphoreType.DMA((5,))], SMALL,
+    a, ylo, yhi = call(
+        pack_kernel, "pack", (shape(5, PX, PY, PZ), shape(5 * PX * HY, PZ), shape(5 * PX * HY, PZ)),
+        (VMEM,) * 3, [ANY] * 5, [pltpu.SemaphoreType.DMA((5,))], SMALL,
     )(*[pltpu.with_memory_space_constraint(v, pltpu.HBM) for v in (right_side, alpha_coef, beta_x, beta_y, beta_z)])
     lo = shifted(yhi, "narrow", 1)
     hi = shifted(ylo, "narrow", -1)
     own, sw, xs = call(
         corner_kernel, "corners", (shape(RAW + 4 * R1, PZ), shape(SRAW + 4 * R1, PZ), shape(SRAW + R1, PZ)),
-        (VMEM,) * 3, [VMEM] * 4, [scratch(3, EY + 2 * PAD, PZ), scratch(2, 3 * EY, PZ)], SMALL,
-    )(a, raw, lo, hi)
+        (VMEM,) * 3, [VMEM] * 3, [scratch(3, EY + 2 * PAD, PZ), scratch(2, 3 * EY, PZ)], SMALL,
+    )(a, lo, hi)
     xs = across(xs, 1)
     sw = swap(sw)
 
-    rhs, rhs_lo, rhs_hi, edge0, xedge0, pre0, w0, c0 = call(
+    send, send1, send2, edge0, pre0, w0, c0 = call(
         fine_kernel, "level0_pre",
-        (shape(H1, PZ), shape(G1, PZ), shape(G1, PZ), shape(EY, PZ), shape(EY, PZ), shape(6, EY, PZ),
+        (shape(5 * R1 + MID, PZ), shape(5 * R1, PZ), shape(2 * R1, PZ), shape(MID, PZ), shape(6, MID, PZ),
          shape(6, 10, EY, PZ), shape(10, EY, PZ)),
-        (VMEM,) * 8, [VMEM] * 3 + [ANY],
-        [scratch(10, EY, PZ), scratch(10, EY, PZ)] + [scratch(10, EY + 2 * PAD, PZ)] * 3 + [scratch(2, EY, PZ)],
+        (VMEM,) * 7, [VMEM] * 3 + [ANY],
+        [scratch(10, EY, PZ), scratch(10, EY, PZ)] + [scratch(10, EY + 2 * PAD, PZ)] * 3
+        + [scratch(2, EY, PZ), scratch(4, 5, R1, PZ), scratch(R1 + PAD, PZ)],
         LARGE,
     )(own, sw, xs, first_to_arrive(xs))
-    rhs_below = shifted(rhs_hi, "narrow", 1)
-    rhs_above = shifted(rhs_lo, "narrow", -1)
-    chip = call(
-        chip_coefficients_kernel, "chip_coefficients", shape(3 * R1, PZ), VMEM, [VMEM] * 3,
-        [scratch(4, 5, R1, PZ), scratch(R1 + PAD, PZ)], LARGE,
-    )(own[RAW:], sw[SRAW:], xs)
-    send, send1, send2 = call(
-        extend_kernel, "extend", (shape(5 * R1 + EY, PZ), shape(5 * R1, PZ), shape(2 * R1, PZ)), (VMEM,) * 3,
-        [VMEM] * 6, [], SMALL,
-    )(rhs_below, rhs, rhs_above, xedge0, own[RAW:], chip)
 
     one = across(send, 1)
     beside = from_beside(send1)
@@ -707,7 +669,7 @@
     return call(
         last_kernel, "coarse_and_post", shape(PX, PY, PZ), VMEM, [VMEM] * 14,
         [scratch(6, 1, R2, PZ), scratch(12, R2, PZ)] + [scratch(12, R2 + 2 * PAD, PZ)] * 3
-        + [scratch(10, R1 + 2 * PAD, PZ)] * 3 + [scratch(8, EY + 2 * PAD, PZ)] * 2,
+        + [scratch(10, R1 + 2 * PAD, PZ)] * 3 + [scratch(8, MID + 2 * PAD, PZ)] * 2,
         LARGE,
     )(two2, its2, rhs2, w2, inv2, last2, pre1, w1, c1, pre0, its, one, w0, c0)
 

time: 73 us -> 71.4 us (0.978)
  the two profiles are of different devices: /device:TPU:215 before, /device:TPU:223 now
where the time goes in v5:
time: 71.4 us; the launch traced here: 71 us
  starting transfers between devices  32.1 us (45%)
  waiting for transfers between devices  30.4 us (43%)
  Pallas kernels  8.38 us (12%)
    ppermute x4, waiting for transfers between devices, across(): return lax.ppermute(v, 'wide', pairs + list(ends))  19 us
    ppermute x4, starting transfers between devices, across(): return lax.ppermute(v, 'wide', pairs + list(ends))  18.1 us
    ppermute x2, waiting for transfers between devices, shifted(): lax.ppermute(v, axis, [(i, i + step) for i in range(count) if 0 <= i + st...  9.44 us
    ppermute x2, starting transfers between devices, shifted(): lax.ppermute(v, axis, [(i, i + step) for i in range(count) if 0 <= i + st...  6.34 us
    ppermute x3, starting transfers between devices, swap(): lax.ppermute(v, 'wide', [(i, i ^ 1) for i in range(lax.axis_size('wide'))])  5.75 us
    ppermute x3, waiting for transfers between devices, swap(): lax.ppermute(v, 'wide', [(i, i ^ 1) for i in range(lax.axis_size('wide'))])  1.95 us
    ppermute x1, starting transfers between devices, from_beside(): return lax.ppermute(v, 'wide', pairs)  1.92 us
    pallas_call x1, Pallas kernels, shards(): call(fine_kernel, 'level0_pre', (shape(5 * R1 + MID, PZ), shape(5 * R1, P...  1.84 us
  transfers between devices with their start and end apart: 10, of which 7 were waited for; matrix products, arithmetic and copies ran while one was open for 0% of the time, Pallas kernels for 1%

profile of v5, /device:TPU:223, one launch (start us, length us, event | category | flops | bytes accessed | tf_op | source)
XLA Modules:
  0.0 71.0 jit_solution(16486929748219049127)
XLA Ops:
  0.0 1.3 %pack.1 = (f32[5,4,64,128]{3,2,1,0:T(8,128)S(1)}, f32[640,128]{1,0:T(8,128)S(1)}, f32[640,128]{1,0:T(8,128)S(1)}) custom-call(f32[4,64,128]{2,1,0:T(8,128)} %b.1, f32[4,64,128]{2,1,0:T(8,128)} %al.1, f32[4,64,128]{2,1,0:T(8,128)} %bx.1, f32[4,64,128]{2,1,0:T(8,128)} %by.1, f32[4,64,128]{2,1,0:T(8,128)} %bz.1), custom_call_target="tpu_custom_call" | custom-call | flops 1000 | tf_op jit(solution)/shard_map/pack/pallas_call | solution.py:620
  1.3 4.4 %collective-permute-start = (f32[640,128]{1,0:T(8,128)S(1)}, f32[640,128]{1,0:T(8,128)S(1)}, u32[]{:S(2)}, u32[]{:S(2)}) collective-permute-start(f32[640,128]{1,0:T(8,128)S(1)} %get-tuple-element.32), channel_id=1, source_target_pairs={{0,1},{1,2},{2,3},{3,4},{4,5},{5,6},{6,7},{8,9},{9,10},{10,11},{11... | collective-permute-start | bytes 983048 | tf_op jit(solution)/shard_map/ppermute | solution.py:616
  5.7 1.9 %collective-permute-start.1 = (f32[640,128]{1,0:T(8,128)S(1)}, f32[640,128]{1,0:T(8,128)S(1)}, u32[]{:S(2)}, u32[]{:S(2)}) collective-permute-start(f32[640,128]{1,0:T(8,128)S(1)} %get-tuple-element.33), channel_id=1, source_target_pairs={{1,0},{2,1},{3,2},{4,3},{5,4},{6,5},{7,6},{9,8},{10,9},{11,10},{12... | collective-permute-start | bytes 983048 | tf_op jit(solution)/shard_map/ppermute | solution.py:616
  7.6 4.4 %collective-permute-done.lo = f32[640,128]{1,0:T(8,128)S(1)} collective-permute-done((f32[640,128]{1,0:T(8,128)S(1)}, f32[640,128]{1,0:T(8,128)S(1)}, u32[]{:S(2)}, u32[]{:S(2)}) %collective-permute-start) | collective-permute-done | bytes 327712 | tf_op jit(solution)/shard_map/ppermute | solution.py:616
  12.0 5.0 %collective-permute-done.1.hi = f32[640,128]{1,0:T(8,128)S(1)} collective-permute-done((f32[640,128]{1,0:T(8,128)S(1)}, f32[640,128]{1,0:T(8,128)S(1)}, u32[]{:S(2)}, u32[]{:S(2)}) %collective-permute-start.1) | collective-permute-done | bytes 327712 | tf_op jit(solution)/shard_map/ppermute | solution.py:616
  17.1 0.7 corners.1
  17.8 6.9 %collective-permute-start.3 = (f32[1088,128]{1,0:T(8,128)S(1)}, f32[1088,128]{1,0:T(8,128)S(1)}, u32[]{:S(2)}, u32[]{:S(2)}) collective-permute-start(f32[1088,128]{1,0:T(8,128)S(1)} %get-tuple-element.36), channel_id=1, source_target_pairs={{8,16},{24,32},{40,48},{56,64},{72,80},{88,96},{104,112},{120,128}... | collective-permute-start | bytes 1671176 | tf_op jit(solution)/shard_map/ppermute | solution.py:605
  24.6 1.9 %collective-permute-start.2 = (f32[1280,128]{1,0:T(8,128)S(1)}, f32[1280,128]{1,0:T(8,128)S(1)}, u32[]{:S(2)}, u32[]{:S(2)}) collective-permute-start(f32[1280,128]{1,0:T(8,128)S(1)} %get-tuple-element.35), channel_id=1, source_target_pairs={{0,8},{8,0},{16,24},{24,16},{32,40},{40,32},{48,56},{56,48},{64,72... | collective-permute-start | bytes 1966088 | tf_op jit(solution)/shard_map/ppermute | solution.py:597
  26.6 5.4 %collective-permute-done.3._.xs = f32[1088,128]{1,0:T(8,128)S(1)} collective-permute-done((f32[1088,128]{1,0:T(8,128)S(1)}, f32[1088,128]{1,0:T(8,128)S(1)}, u32[]{:S(2)}, u32[]{:S(2)}) %collective-permute-start.3) | collective-permute-done | bytes 557088 | tf_op jit(solution)/shard_map/ppermute | solution.py:605
  31.9 0.0 collective-permute-done.2.sw
  31.9 1.8 %level0_pre.1 = (f32[400,128]{1,0:T(8,128)S(1)}, f32[320,128]{1,0:T(8,128)S(1)}, f32[128,128]{1,0:T(8,128)S(1)}, f32[80,128]{1,0:T(8,128)S(1)}, f32[6,80,128]{2,...) custom-call(f32[2816,128]{1,0:T(8,128)S(1)} %get-tuple-element.34.own, ...), custom_call_target="tpu_custom_call" | custom-call | flops 20000000000 | tf_op jit(solution)/shard_map/level0_pre/pallas_call | solution.py:633
  33.8 6.9 %collective-permute-start.4 = (f32[400,128]{1,0:T(8,128)S(1)}, f32[400,128]{1,0:T(8,128)S(1)}, u32[]{:S(2)}, u32[]{:S(2)}) collective-permute-start(f32[400,128]{1,0:T(8,128)S(1)} %get-tuple-element.37.own), channel_id=1, source_target_pairs={{8,16},{24,32},{40,48},{56,64},{72,80},{88,96},{104,112},{120,128}... | collective-permute-start | bytes 614408 | tf_op jit(solution)/shard_map/ppermute | solution.py:605
  40.7 1.9 %collective-permute-start.5 = (f32[320,128]{1,0:T(8,128)S(1)}, f32[320,128]{1,0:T(8,128)S(1)}, u32[]{:S(2)}, u32[]{:S(2)}) collective-permute-start(f32[320,128]{1,0:T(8,128)S(1)} %get-tuple-element.38), channel_id=1, source_target_pairs={{0,16},{16,32},{32,48},{48,64},{64,80},{80,96},{96,112},{112,128},... | collective-permute-start | bytes 491528 | tf_op jit(solution)/shard_map/ppermute | solution.py:611
  42.6 1.9 %collective-permute-start.6 = (f32[128,128]{1,0:T(8,128)S(1)}, f32[128,128]{1,0:T(8,128)S(1)}, u32[]{:S(2)}, u32[]{:S(2)}) collective-permute-start(f32[128,128]{1,0:T(8,128)S(1)} %get-tuple-element.39), channel_id=1, source_target_pairs={{8,32},{24,48},{40,64},{56,80},{72,96},{88,112},{104,128},{120,144... | collective-permute-start | bytes 196616 | tf_op jit(solution)/shard_map/ppermute | solution.py:605
  44.6 7.2 %collective-permute-done.6.two = f32[128,128]{1,0:T(8,128)S(1)} collective-permute-done((f32[128,128]{1,0:T(8,128)S(1)}, f32[128,128]{1,0:T(8,128)S(1)}, u32[]{:S(2)}, u32[]{:S(2)}) %collective-permute-start.6) | collective-permute-done | bytes 65568 | tf_op jit(solution)/shard_map/ppermute | solution.py:605
  51.8 0.0 collective-permute-done.5.beside
  51.8 0.0 collective-permute-done.4.one.xs
  51.8 1.9 %collective-permute-start.7 = (f32[912,128]{1,0:T(8,128)S(1)}, f32[912,128]{1,0:T(8,128)S(1)}, u32[]{:S(2)}, u32[]{:S(2)}) collective-permute-start(f32[912,128]{1,0:T(8,128)S(1)} %join.1), channel_id=1, source_target_pairs={{0,8},{8,0},{16,24},{24,16},{32,40},{40,32},{48,56},{56,48},{64,72... | collective-permute-start | bytes 1400840 | tf_op jit(solution)/shard_map/ppermute | solution.py:597
  53.8 0.6 near_coefficients.1
  54.3 1.2 %collective-permute-done.7.its.sw = f32[912,128]{1,0:T(8,128)S(1)} collective-permute-done((f32[912,128]{1,0:T(8,128)S(1)}, f32[912,128]{1,0:T(8,128)S(1)}, u32[]{:S(2)}, u32[]{:S(2)}) %collective-permute-start.7) | collective-permute-done | bytes 466976 | tf_op jit(solution)/shard_map/ppermute | solution.py:597
  55.6 1.8 %level1_pre.1 = (f32[64,128]{1,0:T(8,128)S(1)}, f32[14,64,128]{2,1,0:T(8,128)S(1)}, f32[10,64,128]{2,1,0:T(8,128)S(1)}, f32[4,32,128]{2,1,0:T(8,128)S(1)}, f32[4...) custom-call(f32[400,128]{1,0:T(8,128)S(1)} %get-tuple-element.37.own, ...), custom_call_target="tpu_custom_call", output_to_operand_aliasing={{4}: (5, {}), {5}: (6, {}), {6}: (7, {}), {7}: (8, {})} | custom-call | flops 20000000000 | tf_op jit(solution)/shard_map/level1_pre/pallas_call | solution.py:653
  57.3 2.4 %collective-permute-start.8 = (f32[64,128]{1,0:T(8,128)S(1)}, f32[64,128]{1,0:T(8,128)S(1)}, u32[]{:S(2)}, u32[]{:S(2)}) collective-permute-start(f32[64,128]{1,0:T(8,128)S(1)} %get-tuple-element.45), channel_id=1, source_target_pairs={{8,32},{24,48},{40,64},{56,80},{72,96},{88,112},{104,128},{120,144... | collective-permute-start | bytes 98312 | tf_op jit(solution)/shard_map/ppermute | solution.py:605
  59.7 6.4 %collective-permute-done.8.two2 = f32[64,128]{1,0:T(8,128)S(1)} collective-permute-done((f32[64,128]{1,0:T(8,128)S(1)}, f32[64,128]{1,0:T(8,128)S(1)}, u32[]{:S(2)}, u32[]{:S(2)}) %collective-permute-start.8) | collective-permute-done | bytes 32800 | tf_op jit(solution)/shard_map/ppermute | solution.py:605
  66.2 1.9 %collective-permute-start.9 = (f32[64,128]{1,0:T(8,128)S(1)}, f32[64,128]{1,0:T(8,128)S(1)}, u32[]{:S(2)}, u32[]{:S(2)}) collective-permute-start(f32[64,128]{1,0:T(8,128)S(1)} %collective-permute-done.8.two2), channel_id=1, source_target_pairs={{0,8},{8,0},{16,24},{24,16},{32,40},{40,32},{48,56},{56,48},{64,72... | collective-permute-start | bytes 98312 | tf_op jit(solution)/shard_map/ppermute | solution.py:597
  68.1 0.5 level2_coefficients.1
  68.6 0.7 %collective-permute-done.9.its2 = f32[64,128]{1,0:T(8,128)S(1)} collective-permute-done((f32[64,128]{1,0:T(8,128)S(1)}, f32[64,128]{1,0:T(8,128)S(1)}, u32[]{:S(2)}, u32[]{:S(2)}) %collective-permute-start.9) | collective-permute-done | bytes 32800 | tf_op jit(solution)/shard_map/ppermute | solution.py:597
  69.3 1.8 %coarse_and_post.1 = f32[4,64,128]{2,1,0:T(8,128)} custom-call(f32[64,128]{1,0:T(8,128)S(1)} %collective-permute-done.8.two2, f32[64,128]{1,0:T(8,128)S(1)} %collective-permute-done.9.its2, f32[4,32,128]{2,1,0:T(8,128)S(1)} %get-tuple-element.46.rhs, f32[6,12,32,128]{3,2,1,0:T(8,128)S(1)} %get-tuple-element.48.w2, ...), custom_call_target="tpu_custom_call" | custom-call | flops 20000000000 | tf_op jit(solution)/shard_map/coarse_and_post/pallas_call | solution.py:669
  (4 shorter events, 0.1 us)
Async XLA Ops:
  1.3 10.8 %collective-permute-start = (f32[640,128]{1,0:T(8,128)S(1)}, f32[640,128]{1,0:T(8,128)S(1)}, u32[]{:S(2)}, u32[]{:S(2)}) collective-permute-start(f32[640,128]{1,0:T(8,128)S(1)} %get-tuple-element.32), channel_id=1, source_target_pairs={{0,1},{1,2},{2,3},{3,4},{4,5},{5,6},{6,7},{8,9},{9,10},{10,11},{11... | collective-permute-start | bytes 983048 | tf_op jit(solution)/shard_map/ppermute | solution.py:616
  5.7 11.4 %collective-permute-start.1 = (f32[640,128]{1,0:T(8,128)S(1)}, f32[640,128]{1,0:T(8,128)S(1)}, u32[]{:S(2)}, u32[]{:S(2)}) collective-permute-start(f32[640,128]{1,0:T(8,128)S(1)} %get-tuple-element.33), channel_id=1, source_target_pairs={{1,0},{2,1},{3,2},{4,3},{5,4},{6,5},{7,6},{9,8},{10,9},{11,10},{12... | collective-permute-start | bytes 983048 | tf_op jit(solution)/shard_map/ppermute | solution.py:616
  17.8 14.2 %collective-permute-start.3 = (f32[1088,128]{1,0:T(8,128)S(1)}, f32[1088,128]{1,0:T(8,128)S(1)}, u32[]{:S(2)}, u32[]{:S(2)}) collective-permute-start(f32[1088,128]{1,0:T(8,128)S(1)} %get-tuple-element.36), channel_id=1, source_target_pairs={{8,16},{24,32},{40,48},{56,64},{72,80},{88,96},{104,112},{120,128}... | collective-permute-start | bytes 1671176 | tf_op jit(solution)/shard_map/ppermute | solution.py:605
  24.6 7.3 %collective-permute-start.2 = (f32[1280,128]{1,0:T(8,128)S(1)}, f32[1280,128]{1,0:T(8,128)S(1)}, u32[]{:S(2)}, u32[]{:S(2)}) collective-permute-start(f32[1280,128]{1,0:T(8,128)S(1)} %get-tuple-element.35), channel_id=1, source_target_pairs={{0,8},{8,0},{16,24},{24,16},{32,40},{40,32},{48,56},{56,48},{64,72... | collective-permute-start | bytes 1966088 | tf_op jit(solution)/shard_map/ppermute | solution.py:597
  33.8 18.0 %collective-permute-start.4 = (f32[400,128]{1,0:T(8,128)S(1)}, f32[400,128]{1,0:T(8,128)S(1)}, u32[]{:S(2)}, u32[]{:S(2)}) collective-permute-start(f32[400,128]{1,0:T(8,128)S(1)} %get-tuple-element.37.own), channel_id=1, source_target_pairs={{8,16},{24,32},{40,48},{56,64},{72,80},{88,96},{104,112},{120,128}... | collective-permute-start | bytes 614408 | tf_op jit(solution)/shard_map/ppermute | solution.py:605
  40.7 11.1 %collective-permute-start.5 = (f32[320,128]{1,0:T(8,128)S(1)}, f32[320,128]{1,0:T(8,128)S(1)}, u32[]{:S(2)}, u32[]{:S(2)}) collective-permute-start(f32[320,128]{1,0:T(8,128)S(1)} %get-tuple-element.38), channel_id=1, source_target_pairs={{0,16},{16,32},{32,48},{48,64},{64,80},{80,96},{96,112},{112,128},... | collective-permute-start | bytes 491528 | tf_op jit(solution)/shard_map/ppermute | solution.py:611
  42.6 9.2 %collective-permute-start.6 = (f32[128,128]{1,0:T(8,128)S(1)}, f32[128,128]{1,0:T(8,128)S(1)}, u32[]{:S(2)}, u32[]{:S(2)}) collective-permute-start(f32[128,128]{1,0:T(8,128)S(1)} %get-tuple-element.39), channel_id=1, source_target_pairs={{8,32},{24,48},{40,64},{56,80},{72,96},{88,112},{104,128},{120,144... | collective-permute-start | bytes 196616 | tf_op jit(solution)/shard_map/ppermute | solution.py:605
  51.8 3.7 %collective-permute-start.7 = (f32[912,128]{1,0:T(8,128)S(1)}, f32[912,128]{1,0:T(8,128)S(1)}, u32[]{:S(2)}, u32[]{:S(2)}) collective-permute-start(f32[912,128]{1,0:T(8,128)S(1)} %join.1), channel_id=1, source_target_pairs={{0,8},{8,0},{16,24},{24,16},{32,40},{40,32},{48,56},{56,48},{64,72... | collective-permute-start | bytes 1400840 | tf_op jit(solution)/shard_map/ppermute | solution.py:597
  57.3 8.8 %collective-permute-start.8 = (f32[64,128]{1,0:T(8,128)S(1)}, f32[64,128]{1,0:T(8,128)S(1)}, u32[]{:S(2)}, u32[]{:S(2)}) collective-permute-start(f32[64,128]{1,0:T(8,128)S(1)} %get-tuple-element.45), channel_id=1, source_target_pairs={{8,32},{24,48},{40,64},{56,80},{72,96},{88,112},{104,128},{120,144... | collective-permute-start | bytes 98312 | tf_op jit(solution)/shard_map/ppermute | solution.py:605
  66.2 3.1 %collective-permute-start.9 = (f32[64,128]{1,0:T(8,128)S(1)}, f32[64,128]{1,0:T(8,128)S(1)}, u32[]{:S(2)}, u32[]{:S(2)}) collective-permute-start(f32[64,128]{1,0:T(8,128)S(1)} %collective-permute-done.8.two2), channel_id=1, source_target_pairs={{0,8},{8,0},{16,24},{24,16},{32,40},{40,32},{48,56},{56,48},{64,72... | collective-permute-start | bytes 98312 | tf_op jit(solution)/shard_map/ppermute | solution.py:597

commit v6 on v5

--- a/solution.py
+++ b/solution.py
@@ -24,6 +24,8 @@
 R2 = R1 // 2
 RAW = 5 * PX * EY
 SRAW = 8 * EY
+XP = 5 * 2 * HY
+XB = XP + 3 * EY
 PAD = 8
 SMALL, LARGE = 1000, 2 * 10**10
 B, ALPHA, BX, BY, BZ = range(5)
@@ -191,8 +193,9 @@
     return al, bx, by, bz
 
 
-def pack_kernel(b, al, bx, by, bz, a, lo_out, hi_out, sems):
+def pack_kernel(b, al, bx, by, bz, a, lo_out, hi_out, xs_out, sems):
     wide, narrow = lax.axis_index("wide"), lax.axis_index("narrow")
+    par = lax.rem(wide, 2)
     copies = [pltpu.make_async_copy(ref, a.at[i], sems.at[i]) for i, ref in enumerate((b, al, bx, by, bz))]
     for c in copies:
         c.start()
@@ -210,6 +213,7 @@
             here = pl.ds((PX * i + p) * HY, HY)
             lo_out[here, :] = a[i, p, :HY]
             hi_out[here, :] = a[i, p, PY - HY :]
+        xs_out[pl.ds(i * PY, PY), :] = a[i, 3 * par]
 
 
 def plane(ref, k, r0=0, n=EY):
@@ -217,7 +221,7 @@
     return ref[pl.ds(pl.multiple_of(start, 8) if r0 % 8 == 0 else start, n), :]
 
 
-def corner_kernel(a, lo, hi, own, sw, xs, x, v):
+def corner_kernel(a, lo, hi, _, __, own, sw, xs, x, v):
     par = parity()
     for i in range(5):
         for p in range(PX):
@@ -236,11 +240,11 @@
         t = pack2(got[0][i], got[1][i])
         own[pl.ds(RAW + R1 * i, R1), :] = t
         sw[pl.ds(SRAW + R1 * i, R1), :] = t
-    xs[pl.ds(SRAW, R1), :] = own[pl.ds(RAW + R1, R1), :]
+    xs[pl.ds(XB, R1), :] = own[pl.ds(RAW + R1, R1), :]
     for i in range(5):
-        here = pl.ds(i * EY, EY)
-        xs[here, :] = plane(own, PX * i + 3 * par)
-        sw[here, :] = plane(own, PX * i + 3 - 3 * par)
+        xs[pl.ds(2 * HY * i, HY), :] = plane(own, PX * i + 3 * par, 0, HY)
+        xs[pl.ds(2 * HY * i + HY, HY), :] = plane(own, PX * i + 3 * par, HY + PY, HY)
+        sw[pl.ds(i * EY, EY), :] = plane(own, PX * i + 3 - 3 * par)
     clear_pads(x, EY)
     body = pl.ds(PAD, EY)
     kept = []
@@ -265,27 +269,38 @@
         v[up, pl.ds(0, EY), :] = here
         v[up, pl.ds(EY, EY), :] = here + GAIN[1] * z + MOMENTUM[1] * here
         v[up, pl.ds(2 * EY, EY), :] = w[1] if up else plane(own, PX * BX + second)
-    xs[pl.ds(5 * EY, 3 * EY), :] = v[par]
+    xs[pl.ds(XP, 3 * EY), :] = v[par]
     sw[pl.ds(5 * EY, 3 * EY), :] = v[1 - par]
 
 
 Q0 = 3
 
 
-def fine_kernel(own, sw, xs, _, send, send1, send2, edge, pre, w, cc, sx, d, x, y, z, t, s, u):
+def fine_kernel(own, sw, xs, ex, _, send, send1, send2, edge, pre, w, cc, sx, d, x, y, z, t, s, u, sf):
     par = parity()
-    sides2 = ((xs, par), (sw, 1 - par))
+    for i in range(5):
+        sf[i, :HY] = xs[pl.ds(2 * HY * i, HY), :]
+        sf[i, HY : HY + PY] = ex[pl.ds(PY * i, PY), :]
+        sf[i, HY + PY :] = xs[pl.ds(2 * HY * i + HY, HY), :]
+
+    def far(i, r, n):
+        return sf[i, pl.ds(r, n), :] if i < 5 else xs[pl.ds(XP + (i - 5) * EY + r, n), :]
+
+    def near(i, r, n):
+        return plane(sw, i, r, n)
+
+    sides2 = ((far, par), (near, 1 - par))
     for i in range(4):
         for p, ref, base in ((par, own, RAW), (1 - par, sw, SRAW)):
             v0, v1 = unpack2(ref[pl.ds(base + R1 * i, R1), :])
             s[i, 2 * p] = v0
             s[i, 2 * p + 1] = v1
-    s[1, 4] = unpack2(xs[pl.ds(SRAW, R1), :])[0]
+    s[1, 4] = unpack2(xs[pl.ds(XB, R1), :])[0]
     for p in range(PX):
         sx[Q0 + p] = plane(own, PX * BX + p)
-    for ref, above in sides2:
-        sx[2 + 5 * above] = plane(ref, BX)
-        sx[9 - above] = plane(ref, 7)
+    for get, above in sides2:
+        sx[2 + 5 * above] = get(BX, 0, EY)
+        sx[9 - above] = get(7, 0, EY)
     clear_pads(x, EY)
     clear_pads(y, EY)
     chunk = 32
@@ -311,13 +326,13 @@
     for p in range(PX):
         prepare(Q0 + p, lambda i, r, n: plane(own, PX * i + p, r, n))
     body = pl.ds(PAD, EY)
-    for ref, above in sides2:
+    for get, above in sides2:
         q = 2 + 5 * above
-        prepare(q, lambda i, r, n: plane(ref, i, r, n))
-        x[1 + 7 * above, body, :] = plane(ref, 5)
-        missing = GAIN[1] * plane(ref, 7) * x[q, body, :]
+        prepare(q, get)
+        x[1 + 7 * above, body, :] = get(5, 0, EY)
+        missing = GAIN[1] * get(7, 0, EY) * x[q, body, :]
         below = jnp.broadcast_to(above, missing.shape) == 0
-        y[1 + 7 * above, body, :] = plane(ref, 6) + jnp.where(below, missing, 0.0)
+        y[1 + 7 * above, body, :] = get(6, 0, EY) + jnp.where(below, missing, 0.0)
 
     rows = (0, EY)
     sweep(x, None, cc, w, 2, 8, rows, 1, 1, into(y), chunk)
@@ -421,12 +436,12 @@
     out[pl.ds(O_RAW + 4 * R1, 4 * R1), :] = beside[pl.ds(R1, 4 * R1), :]
 
 
-def tick_kernel(_, out):
-    out[...] = jnp.zeros(out.shape, F32)
-
-
-def first_to_arrive(v):
-    return call(tick_kernel, "tick", shape(PAD, PZ), VMEM, [ANY], [], LARGE)(v)
+def tick_kernel(*refs):
+    refs[-1][...] = jnp.zeros(refs[-1].shape, F32)
+
+
+def first_to_arrive(*values):
+    return call(tick_kernel, "tick", shape(PAD, PZ), VMEM, [ANY] * len(values), [], LARGE)(*values)
 
 
 def both_sides(par, mine, its):
@@ -560,24 +575,22 @@
     sweep(y2, x2, c2, w2, 2, 10, rows, 4, 2, into(z2), R2, unroll=8)
     sweep(z2, y2, c2, w2, 3, 9, rows, 4, 3, into(x2), R2, unroll=6)
 
-    clear_pads(x1, R1)
-    clear_pads(y1, R1)
-    for q in range(10):
-        v = x2[(q - 3) // 2 + M0, body, :]
+    for q in range(8):
+        v = x2[(q - 3) // 2 + M0 + par, body, :]
         z1[q, pl.ds(PAD, R2, 2), :] = v
         z1[q, pl.ds(PAD + 1, R2, 2), :] = v
-        x1[q, pl.ds(PAD, R1), :] = pre1[q] + z1[q, pl.ds(PAD, R1), :]
-    rows = (0, R1)
-    off = C0 - 3
-    sweep(x1, None, c1, w1, 1, 9, rows, 2, 0, into(y1), 32, woff=off, coff=off)
-    sweep(y1, x1, c1, w1, 2, 8, rows, 2, 1, into(z1), 32, woff=off, coff=off, unroll=6)
+        x1[q, pl.ds(PAD, R1), :] = pre1[q + 2 * par] + z1[q, pl.ds(PAD, R1), :]
+    rows = (8, R1 - 8)
+    off = C0 - 3 + 2 * par
+    sweep(x1, None, c1, w1, 1, 7, rows, 2, 0, into(y1), 24, woff=off, coff=off, unroll=6)
+    sweep(y1, x1, c1, w1, 2, 6, rows, 2, 1, into(z1), 24, woff=off, coff=off, unroll=4)
 
     clear_pads(x0, MID)
     clear_pads(y0, MID)
     near, far = 7 - 7 * par, 7 * par
     body = pl.ds(PAD, MID)
     for q in range(8):
-        v = z1[(q - 2) // 2 + 3 + 2 * par, pl.ds(PAD + 12, MID // 2), :]
+        v = z1[(q - 2) // 2 + 3, pl.ds(PAD + 12, MID // 2), :]
         x0[q, pl.ds(PAD, MID // 2, 2), :] = v
         x0[q, pl.ds(PAD + 1, MID // 2, 2), :] = v
         if 0 < q < 7:
@@ -617,16 +630,17 @@
 
 
 def shards(right_side, alpha_coef, beta_x, beta_y, beta_z):
-    a, ylo, yhi = call(
-        pack_kernel, "pack", (shape(5, PX, PY, PZ), shape(5 * PX * HY, PZ), shape(5 * PX * HY, PZ)),
-        (VMEM,) * 3, [ANY] * 5, [pltpu.SemaphoreType.DMA((5,))], SMALL,
+    a, ylo, yhi, ex = call(
+        pack_kernel, "pack", (shape(5, PX, PY, PZ), shape(5 * PX * HY, PZ), shape(5 * PX * HY, PZ), shape(5 * PY, PZ)),
+        (VMEM,) * 4, [ANY] * 5, [pltpu.SemaphoreType.DMA((5,))], SMALL,
     )(*[pltpu.with_memory_space_constraint(v, pltpu.HBM) for v in (right_side, alpha_coef, beta_x, beta_y, beta_z)])
     lo = shifted(yhi, "narrow", 1)
     hi = shifted(ylo, "narrow", -1)
+    ex = across(ex, 1)
     own, sw, xs = call(
-        corner_kernel, "corners", (shape(RAW + 4 * R1, PZ), shape(SRAW + 4 * R1, PZ), shape(SRAW + R1, PZ)),
-        (VMEM,) * 3, [VMEM] * 3, [scratch(3, EY + 2 * PAD, PZ), scratch(2, 3 * EY, PZ)], SMALL,
-    )(a, lo, hi)
+        corner_kernel, "corners", (shape(RAW + 4 * R1, PZ), shape(SRAW + 4 * R1, PZ), shape(XB + R1, PZ)),
+        (VMEM,) * 3, [VMEM] * 3 + [ANY] * 2, [scratch(3, EY + 2 * PAD, PZ), scratch(2, 3 * EY, PZ)], SMALL,
+    )(a, lo, hi, ex, first_to_arrive(lo, hi))
     xs = across(xs, 1)
     sw = swap(sw)
 
@@ -634,11 +648,11 @@
         fine_kernel, "level0_pre",
         (shape(5 * R1 + MID, PZ), shape(5 * R1, PZ), shape(2 * R1, PZ), shape(MID, PZ), shape(6, MID, PZ),
          shape(6, 10, EY, PZ), shape(10, EY, PZ)),
-        (VMEM,) * 7, [VMEM] * 3 + [ANY],
+        (VMEM,) * 7, [VMEM] * 4 + [ANY],
         [scratch(10, EY, PZ), scratch(10, EY, PZ)] + [scratch(10, EY + 2 * PAD, PZ)] * 3
-        + [scratch(2, EY, PZ), scratch(4, 5, R1, PZ), scratch(R1 + PAD, PZ)],
+        + [scratch(2, EY, PZ), scratch(4, 5, R1, PZ), scratch(R1 + PAD, PZ), scratch(5, EY, PZ)],
         LARGE,
-    )(own, sw, xs, first_to_arrive(xs))
+    )(own, sw, xs, ex, first_to_arrive(xs))
 
     one = across(send, 1)
     beside = from_beside(send1)
@@ -669,7 +683,7 @@
     return call(
         last_kernel, "coarse_and_post", shape(PX, PY, PZ), VMEM, [VMEM] * 14,
         [scratch(6, 1, R2, PZ), scratch(12, R2, PZ)] + [scratch(12, R2 + 2 * PAD, PZ)] * 3
-        + [scratch(10, R1 + 2 * PAD, PZ)] * 3 + [scratch(8, MID + 2 * PAD, PZ)] * 2,
+        + [scratch(8, R1 + 2 * PAD, PZ)] * 3 + [scratch(8, MID + 2 * PAD, PZ)] * 2,
         LARGE,
     )(two2, its2, rhs2, w2, inv2, last2, pre1, w1, c1, pre0, its, one, w0, c0)
 

time: 71.4 us -> 69.7 us (0.976)
  waiting for transfers between devices: 30.4 us -> 23.5 us
  starting transfers between devices: 32.1 us -> 37.2 us
    ppermute x2, waiting for transfers between devices: 9.44 us -> 3.45 us  [shifted(): lax.ppermute(v, axis, [(i, i + step) for i in range(count) if 0 <= i + st...]
    ppermute x4 -> x5, starting transfers between devices: 18.1 us -> 23.2 us  [across(): return lax.ppermute(v, 'wide', pairs + list(ends))]
    ppermute x4 -> x5, waiting for transfers between devices: 19 us -> 18.1 us  [across(): return lax.ppermute(v, 'wide', pairs + list(ends))]
  transfers between devices with their start and end apart: 10 -> 11, of which waited for: 7 -> 7; matrix products, arithmetic and copies ran while one was open for 0% -> 0% of each run, Pallas kernels for 1% -> 1%
where the time goes in v6:
time: 69.7 us; the launch traced here: 69.2 us
  starting transfers between devices  37.2 us (53%)
  waiting for transfers between devices  23.5 us (34%)
  Pallas kernels  8.31 us (12%)
    ppermute x5, starting transfers between devices, across(): return lax.ppermute(v, 'wide', pairs + list(ends))  23.2 us
    ppermute x5, waiting for transfers between devices, across(): return lax.ppermute(v, 'wide', pairs + list(ends))  18.1 us
    ppermute x2, starting transfers between devices, shifted(): lax.ppermute(v, axis, [(i, i + step) for i in range(count) if 0 <= i + st...  6.34 us
    ppermute x3, starting transfers between devices, swap(): lax.ppermute(v, 'wide', [(i, i ^ 1) for i in range(lax.axis_size('wide'))])  5.75 us
    ppermute x2, waiting for transfers between devices, shifted(): lax.ppermute(v, axis, [(i, i + step) for i in range(count) if 0 <= i + st...  3.45 us
    ppermute x3, waiting for transfers between devices, swap(): lax.ppermute(v, 'wide', [(i, i ^ 1) for i in range(lax.axis_size('wide'))])  1.95 us
    ppermute x1, starting transfers between devices, from_beside(): return lax.ppermute(v, 'wide', pairs)  1.92 us
    pallas_call x1, Pallas kernels, shards(): call(fine_kernel, 'level0_pre', (shape(5 * R1 + MID, PZ), shape(5 * R1, P...  1.9 us
  transfers between devices with their start and end apart: 11, of which 7 were waited for; matrix products, arithmetic and copies ran while one was open for 0% of the time, Pallas kernels for 1%

profile of v6, /device:TPU:223, one launch (start us, length us, event | category | flops | bytes accessed | tf_op | source)
XLA Modules:
  0.0 69.2 jit_solution(8059751107664729328)
XLA Ops:
  0.0 1.3 %pack.1 = (f32[5,4,64,128]{3,2,1,0:T(8,128)S(1)}, f32[640,128]{1,0:T(8,128)S(1)}, f32[640,128]{1,0:T(8,128)S(1)}, f32[320,128]{1,0:T(8,128)S(1)}) custom-call(f32[4,64,128]{2,1,0:T(8,128)} %b.1, f32[4,64,128]{2,1,0:T(8,128)} %al.1, f32[4,64,128]{2,1,0:T(8,128)} %bx.1, f32[4,64,128]{2,1,0:T(8,128)} %by.1, f32[4,64,128]{2,1,0:T(8,128)} %bz.1), custom_call_target="tpu_custom_call" | custom-call | flops 1000 | tf_op jit(solution)/shard_map/pack/pallas_call | solution.py:633
  1.3 4.4 %collective-permute-start = (f32[640,128]{1,0:T(8,128)S(1)}, f32[640,128]{1,0:T(8,128)S(1)}, u32[]{:S(2)}, u32[]{:S(2)}) collective-permute-start(f32[640,128]{1,0:T(8,128)S(1)} %get-tuple-element.33), channel_id=1, source_target_pairs={{0,1},{1,2},{2,3},{3,4},{4,5},{5,6},{6,7},{8,9},{9,10},{10,11},{11... | collective-permute-start | bytes 983048 | tf_op jit(solution)/shard_map/ppermute | solution.py:629
  5.7 1.9 %collective-permute-start.1 = (f32[640,128]{1,0:T(8,128)S(1)}, f32[640,128]{1,0:T(8,128)S(1)}, u32[]{:S(2)}, u32[]{:S(2)}) collective-permute-start(f32[640,128]{1,0:T(8,128)S(1)} %get-tuple-element.34), channel_id=1, source_target_pairs={{1,0},{2,1},{3,2},{4,3},{5,4},{6,5},{7,6},{9,8},{10,9},{11,10},{12... | collective-permute-start | bytes 983048 | tf_op jit(solution)/shard_map/ppermute | solution.py:629
  7.6 6.0 %collective-permute-start.2 = (f32[320,128]{1,0:T(8,128)S(1)}, f32[320,128]{1,0:T(8,128)S(1)}, u32[]{:S(2)}, u32[]{:S(2)}) collective-permute-start(f32[320,128]{1,0:T(8,128)S(1)} %get-tuple-element.35), channel_id=1, source_target_pairs={{8,16},{24,32},{40,48},{56,64},{72,80},{88,96},{104,112},{120,128}... | collective-permute-start | bytes 491528 | tf_op jit(solution)/shard_map/ppermute | solution.py:618
  13.6 0.0 collective-permute-done.refs_0_.lo
  13.6 3.5 %collective-permute-done.1.refs_1_.hi = f32[640,128]{1,0:T(8,128)S(1)} collective-permute-done((f32[640,128]{1,0:T(8,128)S(1)}, f32[640,128]{1,0:T(8,128)S(1)}, u32[]{:S(2)}, u32[]{:S(2)}) %collective-permute-start.1) | collective-permute-done | bytes 327712 | tf_op jit(solution)/shard_map/ppermute | solution.py:629
  17.1 0.5 collective-permute-done.2._.ex
  17.6 0.7 corners.1
  18.3 6.4 %collective-permute-start.4 = (f32[768,128]{1,0:T(8,128)S(1)}, f32[768,128]{1,0:T(8,128)S(1)}, u32[]{:S(2)}, u32[]{:S(2)}) collective-permute-start(f32[768,128]{1,0:T(8,128)S(1)} %get-tuple-element.38), channel_id=1, source_target_pairs={{8,16},{24,32},{40,48},{56,64},{72,80},{88,96},{104,112},{120,128}... | collective-permute-start | bytes 1179656 | tf_op jit(solution)/shard_map/ppermute | solution.py:618
  24.6 1.9 %collective-permute-start.3 = (f32[1280,128]{1,0:T(8,128)S(1)}, f32[1280,128]{1,0:T(8,128)S(1)}, u32[]{:S(2)}, u32[]{:S(2)}) collective-permute-start(f32[1280,128]{1,0:T(8,128)S(1)} %get-tuple-element.37), channel_id=1, source_target_pairs={{0,8},{8,0},{16,24},{24,16},{32,40},{40,32},{48,56},{56,48},{64,72... | collective-permute-start | bytes 1966088 | tf_op jit(solution)/shard_map/ppermute | solution.py:610
  26.6 4.1 %collective-permute-done.4.refs_0_.xs = f32[768,128]{1,0:T(8,128)S(1)} collective-permute-done((f32[768,128]{1,0:T(8,128)S(1)}, f32[768,128]{1,0:T(8,128)S(1)}, u32[]{:S(2)}, u32[]{:S(2)}) %collective-permute-start.4) | collective-permute-done | bytes 393248 | tf_op jit(solution)/shard_map/ppermute | solution.py:618
  30.7 0.0 collective-permute-done.3.sw
  30.7 1.9 %level0_pre.1 = (f32[400,128]{1,0:T(8,128)S(1)}, f32[320,128]{1,0:T(8,128)S(1)}, f32[128,128]{1,0:T(8,128)S(1)}, f32[80,128]{1,0:T(8,128)S(1)}, f32[6,80,128]{2,...) custom-call(f32[2816,128]{1,0:T(8,128)S(1)} %get-tuple-element.36.own, ...), custom_call_target="tpu_custom_call" | custom-call | flops 20000000000 | tf_op jit(solution)/shard_map/level0_pre/pallas_call | solution.py:647
  32.6 6.4 %collective-permute-start.5 = (f32[400,128]{1,0:T(8,128)S(1)}, f32[400,128]{1,0:T(8,128)S(1)}, u32[]{:S(2)}, u32[]{:S(2)}) collective-permute-start(f32[400,128]{1,0:T(8,128)S(1)} %get-tuple-element.39.own), channel_id=1, source_target_pairs={{8,16},{24,32},{40,48},{56,64},{72,80},{88,96},{104,112},{120,128}... | collective-permute-start | bytes 614408 | tf_op jit(solution)/shard_map/ppermute | solution.py:618
  39.0 1.9 %collective-permute-start.6 = (f32[320,128]{1,0:T(8,128)S(1)}, f32[320,128]{1,0:T(8,128)S(1)}, u32[]{:S(2)}, u32[]{:S(2)}) collective-permute-start(f32[320,128]{1,0:T(8,128)S(1)} %get-tuple-element.40), channel_id=1, source_target_pairs={{0,16},{16,32},{32,48},{48,64},{64,80},{80,96},{96,112},{112,128},... | collective-permute-start | bytes 491528 | tf_op jit(solution)/shard_map/ppermute | solution.py:624
  40.9 1.9 %collective-permute-start.7 = (f32[128,128]{1,0:T(8,128)S(1)}, f32[128,128]{1,0:T(8,128)S(1)}, u32[]{:S(2)}, u32[]{:S(2)}) collective-permute-start(f32[128,128]{1,0:T(8,128)S(1)} %get-tuple-element.41), channel_id=1, source_target_pairs={{8,32},{24,48},{40,64},{56,80},{72,96},{88,112},{104,128},{120,144... | collective-permute-start | bytes 196616 | tf_op jit(solution)/shard_map/ppermute | solution.py:618
  42.9 7.2 %collective-permute-done.7.two = f32[128,128]{1,0:T(8,128)S(1)} collective-permute-done((f32[128,128]{1,0:T(8,128)S(1)}, f32[128,128]{1,0:T(8,128)S(1)}, u32[]{:S(2)}, u32[]{:S(2)}) %collective-permute-start.7) | collective-permute-done | bytes 65568 | tf_op jit(solution)/shard_map/ppermute | solution.py:618
  50.1 0.0 collective-permute-done.6.beside
  50.1 0.0 collective-permute-done.5.one.xs
  50.1 1.9 %collective-permute-start.8 = (f32[912,128]{1,0:T(8,128)S(1)}, f32[912,128]{1,0:T(8,128)S(1)}, u32[]{:S(2)}, u32[]{:S(2)}) collective-permute-start(f32[912,128]{1,0:T(8,128)S(1)} %join.1), channel_id=1, source_target_pairs={{0,8},{8,0},{16,24},{24,16},{32,40},{40,32},{48,56},{56,48},{64,72... | collective-permute-start | bytes 1400840 | tf_op jit(solution)/shard_map/ppermute | solution.py:610
  52.1 0.6 near_coefficients.1
  52.6 1.2 %collective-permute-done.8.its.sw = f32[912,128]{1,0:T(8,128)S(1)} collective-permute-done((f32[912,128]{1,0:T(8,128)S(1)}, f32[912,128]{1,0:T(8,128)S(1)}, u32[]{:S(2)}, u32[]{:S(2)}) %collective-permute-start.8) | collective-permute-done | bytes 466976 | tf_op jit(solution)/shard_map/ppermute | solution.py:610
  53.9 1.8 %level1_pre.1 = (f32[64,128]{1,0:T(8,128)S(1)}, f32[14,64,128]{2,1,0:T(8,128)S(1)}, f32[10,64,128]{2,1,0:T(8,128)S(1)}, f32[4,32,128]{2,1,0:T(8,128)S(1)}, f32[4...) custom-call(f32[400,128]{1,0:T(8,128)S(1)} %get-tuple-element.39.own, ...), custom_call_target="tpu_custom_call", output_to_operand_aliasing={{4}: (5, {}), {5}: (6, {}), {6}: (7, {}), {7}: (8, {})} | custom-call | flops 20000000000 | tf_op jit(solution)/shard_map/level1_pre/pallas_call | solution.py:667
  55.6 2.6 %collective-permute-start.9 = (f32[64,128]{1,0:T(8,128)S(1)}, f32[64,128]{1,0:T(8,128)S(1)}, u32[]{:S(2)}, u32[]{:S(2)}) collective-permute-start(f32[64,128]{1,0:T(8,128)S(1)} %get-tuple-element.47), channel_id=1, source_target_pairs={{8,32},{24,48},{40,64},{56,80},{72,96},{88,112},{104,128},{120,144... | collective-permute-start | bytes 98312 | tf_op jit(solution)/shard_map/ppermute | solution.py:618
  58.2 6.3 %collective-permute-done.9.two2 = f32[64,128]{1,0:T(8,128)S(1)} collective-permute-done((f32[64,128]{1,0:T(8,128)S(1)}, f32[64,128]{1,0:T(8,128)S(1)}, u32[]{:S(2)}, u32[]{:S(2)}) %collective-permute-start.9) | collective-permute-done | bytes 32800 | tf_op jit(solution)/shard_map/ppermute | solution.py:618
  64.5 1.9 %collective-permute-start.10 = (f32[64,128]{1,0:T(8,128)S(1)}, f32[64,128]{1,0:T(8,128)S(1)}, u32[]{:S(2)}, u32[]{:S(2)}) collective-permute-start(f32[64,128]{1,0:T(8,128)S(1)} %collective-permute-done.9.two2), channel_id=1, source_target_pairs={{0,8},{8,0},{16,24},{24,16},{32,40},{40,32},{48,56},{56,48},{64,72... | collective-permute-start | bytes 98312 | tf_op jit(solution)/shard_map/ppermute | solution.py:610
  66.4 0.5 level2_coefficients.1
  66.9 0.7 %collective-permute-done.10.its2 = f32[64,128]{1,0:T(8,128)S(1)} collective-permute-done((f32[64,128]{1,0:T(8,128)S(1)}, f32[64,128]{1,0:T(8,128)S(1)}, u32[]{:S(2)}, u32[]{:S(2)}) %collective-permute-start.10) | collective-permute-done | bytes 32800 | tf_op jit(solution)/shard_map/ppermute | solution.py:610
  67.6 1.7 %coarse_and_post.1 = f32[4,64,128]{2,1,0:T(8,128)} custom-call(f32[64,128]{1,0:T(8,128)S(1)} %collective-permute-done.9.two2, f32[64,128]{1,0:T(8,128)S(1)} %collective-permute-done.10.its2, f32[4,32,128]{2,1,0:T(8,128)S(1)} %get-tuple-element.48.rhs, f32[6,12,32,128]{3,2,1,0:T(8,128)S(1)} %get-tuple-element.50.w2, ...), custom_call_target="tpu_custom_call" | custom-call | flops 20000000000 | tf_op jit(solution)/shard_map/coarse_and_post/pallas_call | solution.py:683
  (5 shorter events, 0.1 us)
Async XLA Ops:
  1.3 12.3 %collective-permute-start = (f32[640,128]{1,0:T(8,128)S(1)}, f32[640,128]{1,0:T(8,128)S(1)}, u32[]{:S(2)}, u32[]{:S(2)}) collective-permute-start(f32[640,128]{1,0:T(8,128)S(1)} %get-tuple-element.33), channel_id=1, source_target_pairs={{0,1},{1,2},{2,3},{3,4},{4,5},{5,6},{6,7},{8,9},{9,10},{10,11},{11... | collective-permute-start | bytes 983048 | tf_op jit(solution)/shard_map/ppermute | solution.py:629
  5.7 11.4 %collective-permute-start.1 = (f32[640,128]{1,0:T(8,128)S(1)}, f32[640,128]{1,0:T(8,128)S(1)}, u32[]{:S(2)}, u32[]{:S(2)}) collective-permute-start(f32[640,128]{1,0:T(8,128)S(1)} %get-tuple-element.34), channel_id=1, source_target_pairs={{1,0},{2,1},{3,2},{4,3},{5,4},{6,5},{7,6},{9,8},{10,9},{11,10},{12... | collective-permute-start | bytes 983048 | tf_op jit(solution)/shard_map/ppermute | solution.py:629
  7.6 10.0 %collective-permute-start.2 = (f32[320,128]{1,0:T(8,128)S(1)}, f32[320,128]{1,0:T(8,128)S(1)}, u32[]{:S(2)}, u32[]{:S(2)}) collective-permute-start(f32[320,128]{1,0:T(8,128)S(1)} %get-tuple-element.35), channel_id=1, source_target_pairs={{8,16},{24,32},{40,48},{56,64},{72,80},{88,96},{104,112},{120,128}... | collective-permute-start | bytes 491528 | tf_op jit(solution)/shard_map/ppermute | solution.py:618
  18.3 12.4 %collective-permute-start.4 = (f32[768,128]{1,0:T(8,128)S(1)}, f32[768,128]{1,0:T(8,128)S(1)}, u32[]{:S(2)}, u32[]{:S(2)}) collective-permute-start(f32[768,128]{1,0:T(8,128)S(1)} %get-tuple-element.38), channel_id=1, source_target_pairs={{8,16},{24,32},{40,48},{56,64},{72,80},{88,96},{104,112},{120,128}... | collective-permute-start | bytes 1179656 | tf_op jit(solution)/shard_map/ppermute | solution.py:618
  24.6 6.1 %collective-permute-start.3 = (f32[1280,128]{1,0:T(8,128)S(1)}, f32[1280,128]{1,0:T(8,128)S(1)}, u32[]{:S(2)}, u32[]{:S(2)}) collective-permute-start(f32[1280,128]{1,0:T(8,128)S(1)} %get-tuple-element.37), channel_id=1, source_target_pairs={{0,8},{8,0},{16,24},{24,16},{32,40},{40,32},{48,56},{56,48},{64,72... | collective-permute-start | bytes 1966088 | tf_op jit(solution)/shard_map/ppermute | solution.py:610
  32.6 17.5 %collective-permute-start.5 = (f32[400,128]{1,0:T(8,128)S(1)}, f32[400,128]{1,0:T(8,128)S(1)}, u32[]{:S(2)}, u32[]{:S(2)}) collective-permute-start(f32[400,128]{1,0:T(8,128)S(1)} %get-tuple-element.39.own), channel_id=1, source_target_pairs={{8,16},{24,32},{40,48},{56,64},{72,80},{88,96},{104,112},{120,128}... | collective-permute-start | bytes 614408 | tf_op jit(solution)/shard_map/ppermute | solution.py:618
  39.0 11.1 %collective-permute-start.6 = (f32[320,128]{1,0:T(8,128)S(1)}, f32[320,128]{1,0:T(8,128)S(1)}, u32[]{:S(2)}, u32[]{:S(2)}) collective-permute-start(f32[320,128]{1,0:T(8,128)S(1)} %get-tuple-element.40), channel_id=1, source_target_pairs={{0,16},{16,32},{32,48},{48,64},{64,80},{80,96},{96,112},{112,128},... | collective-permute-start | bytes 491528 | tf_op jit(solution)/shard_map/ppermute | solution.py:624
  40.9 9.2 %collective-permute-start.7 = (f32[128,128]{1,0:T(8,128)S(1)}, f32[128,128]{1,0:T(8,128)S(1)}, u32[]{:S(2)}, u32[]{:S(2)}) collective-permute-start(f32[128,128]{1,0:T(8,128)S(1)} %get-tuple-element.41), channel_id=1, source_target_pairs={{8,32},{24,48},{40,64},{56,80},{72,96},{88,112},{104,128},{120,144... | collective-permute-start | bytes 196616 | tf_op jit(solution)/shard_map/ppermute | solution.py:618
  50.1 3.7 %collective-permute-start.8 = (f32[912,128]{1,0:T(8,128)S(1)}, f32[912,128]{1,0:T(8,128)S(1)}, u32[]{:S(2)}, u32[]{:S(2)}) collective-permute-start(f32[912,128]{1,0:T(8,128)S(1)} %join.1), channel_id=1, source_target_pairs={{0,8},{8,0},{16,24},{24,16},{32,40},{40,32},{48,56},{56,48},{64,72... | collective-permute-start | bytes 1400840 | tf_op jit(solution)/shard_map/ppermute | solution.py:610
  55.6 8.8 %collective-permute-start.9 = (f32[64,128]{1,0:T(8,128)S(1)}, f32[64,128]{1,0:T(8,128)S(1)}, u32[]{:S(2)}, u32[]{:S(2)}) collective-permute-start(f32[64,128]{1,0:T(8,128)S(1)} %get-tuple-element.47), channel_id=1, source_target_pairs={{8,32},{24,48},{40,64},{56,80},{72,96},{88,112},{104,128},{120,144... | collective-permute-start | bytes 98312 | tf_op jit(solution)/shard_map/ppermute | solution.py:618
  64.5 3.1 %collective-permute-start.10 = (f32[64,128]{1,0:T(8,128)S(1)}, f32[64,128]{1,0:T(8,128)S(1)}, u32[]{:S(2)}, u32[]{:S(2)}) collective-permute-start(f32[64,128]{1,0:T(8,128)S(1)} %collective-permute-done.9.two2), channel_id=1, source_target_pairs={{0,8},{8,0},{16,24},{24,16},{32,40},{40,32},{48,56},{56,48},{64,72... | collective-permute-start | bytes 98312 | tf_op jit(solution)/shard_map/ppermute | solution.py:610

commit v7 on v6

--- a/solution.py
+++ b/solution.py
@@ -193,7 +193,7 @@
     return al, bx, by, bz
 
 
-def pack_kernel(b, al, bx, by, bz, a, lo_out, hi_out, xs_out, sems):
+def pack_kernel(b, al, bx, by, bz, a, one_out, two_out, xs_out, sems):
     wide, narrow = lax.axis_index("wide"), lax.axis_index("narrow")
     par = lax.rem(wide, 2)
     copies = [pltpu.make_async_copy(ref, a.at[i], sems.at[i]) for i, ref in enumerate((b, al, bx, by, bz))]
@@ -211,8 +211,8 @@
     for i in range(5):
         for p in range(PX):
             here = pl.ds((PX * i + p) * HY, HY)
-            lo_out[here, :] = a[i, p, :HY]
-            hi_out[here, :] = a[i, p, PY - HY :]
+            one_out[here, :] = a[i, p, pl.ds(pl.multiple_of((1 - par) * (PY - HY), 8), HY), :]
+            two_out[here, :] = a[i, p, pl.ds(pl.multiple_of(par * (PY - HY), 8), HY), :]
         xs_out[pl.ds(i * PY, PY), :] = a[i, 3 * par]
 
 
@@ -221,14 +221,15 @@
     return ref[pl.ds(pl.multiple_of(start, 8) if r0 % 8 == 0 else start, n), :]
 
 
-def corner_kernel(a, lo, hi, _, __, own, sw, xs, x, v):
+def corner_kernel(a, one, two, _, __, own, sw, xs, x, v):
     par = parity()
     for i in range(5):
         for p in range(PX):
             k = PX * i + p
-            own[pl.ds(k * EY, HY), :] = lo[pl.ds(k * HY, HY), :]
+            here = pl.ds(k * HY, HY)
+            own[pl.ds(pl.multiple_of(k * EY + par * (HY + PY), 8), HY), :] = one[here, :]
             own[pl.ds(k * EY + HY, PY), :] = a[i, p]
-            own[pl.ds(k * EY + HY + PY, HY), :] = hi[pl.ds(k * HY, HY), :]
+            own[pl.ds(pl.multiple_of(k * EY + (1 - par) * (HY + PY), 8), HY), :] = two[here, :]
     got = []
     for c in range(2):
 
@@ -624,23 +625,26 @@
     return lax.ppermute(v, "wide", pairs)
 
 
-def shifted(v, axis, step):
-    count = lax.axis_size(axis)
-    return lax.ppermute(v, axis, [(i, i + step) for i in range(count) if 0 <= i + step < count])
+def along_narrow(v, step):
+    wide, narrow = lax.axis_size("wide"), lax.axis_size("narrow")
+    pairs = []
+    for i in range(wide):
+        to = step if i % 2 == 0 else -step
+        pairs += [(i * narrow + j, i * narrow + j + to) for j in range(narrow) if 0 <= j + to < narrow]
+    return lax.ppermute(v, ("wide", "narrow"), pairs)
 
 
 def shards(right_side, alpha_coef, beta_x, beta_y, beta_z):
-    a, ylo, yhi, ex = call(
+    a, y1, y2, ex = call(
         pack_kernel, "pack", (shape(5, PX, PY, PZ), shape(5 * PX * HY, PZ), shape(5 * PX * HY, PZ), shape(5 * PY, PZ)),
         (VMEM,) * 4, [ANY] * 5, [pltpu.SemaphoreType.DMA((5,))], SMALL,
     )(*[pltpu.with_memory_space_constraint(v, pltpu.HBM) for v in (right_side, alpha_coef, beta_x, beta_y, beta_z)])
-    lo = shifted(yhi, "narrow", 1)
-    hi = shifted(ylo, "narrow", -1)
+    y1, y2 = along_narrow(y1, 1), along_narrow(y2, -1)
     ex = across(ex, 1)
     own, sw, xs = call(
         corner_kernel, "corners", (shape(RAW + 4 * R1, PZ), shape(SRAW + 4 * R1, PZ), shape(XB + R1, PZ)),
         (VMEM,) * 3, [VMEM] * 3 + [ANY] * 2, [scratch(3, EY + 2 * PAD, PZ), scratch(2, 3 * EY, PZ)], SMALL,
-    )(a, lo, hi, ex, first_to_arrive(lo, hi))
+    )(a, y1, y2, ex, first_to_arrive(y1, y2))
     xs = across(xs, 1)
     sw = swap(sw)
 

time: 69.7 us -> 69.7 us (level)
  the two profiles are of different devices: /device:TPU:223 before, /device:TPU:231 now
where the time goes in v7:
time: 69.7 us; the launch traced here: 69.3 us
  starting transfers between devices  38.6 us (55%)
  waiting for transfers between devices  22.2 us (32%)
  Pallas kernels  8.32 us (12%)
    ppermute x5, starting transfers between devices, across(): return lax.ppermute(v, 'wide', pairs + list(ends))  25.6 us
    ppermute x5, waiting for transfers between devices, across(): return lax.ppermute(v, 'wide', pairs + list(ends))  19.4 us
    ppermute x3, starting transfers between devices, swap(): lax.ppermute(v, 'wide', [(i, i ^ 1) for i in range(lax.axis_size('wide'))])  5.75 us
    ppermute x2, starting transfers between devices, along_narrow(): return lax.ppermute(v, ('wide', 'narrow'), pairs)  5.28 us
    ppermute x3, waiting for transfers between devices, swap(): lax.ppermute(v, 'wide', [(i, i ^ 1) for i in range(lax.axis_size('wide'))])  1.95 us
    ppermute x1, starting transfers between devices, from_beside(): return lax.ppermute(v, 'wide', pairs)  1.92 us
    pallas_call x1, Pallas kernels, shards(): call(fine_kernel, 'level0_pre', (shape(5 * R1 + MID, PZ), shape(5 * R1, P...  1.9 us
    pallas_call x1, Pallas kernels, shards(): call(middle_kernel, 'level1_pre', (shape(2 * R2, PZ), shape(N1, R1, PZ),...  1.76 us
  transfers between devices with their start and end apart: 11, of which 7 were waited for; matrix products, arithmetic and copies ran while one was open for 0% of the time, Pallas kernels for 1%

profile of v7, /device:TPU:231, one launch (start us, length us, event | category | flops | bytes accessed | tf_op | source)
XLA Modules:
  0.0 69.3 jit_solution(9599832837985632701)
XLA Ops:
  0.0 1.3 %pack.1 = (f32[5,4,64,128]{3,2,1,0:T(8,128)S(1)}, f32[640,128]{1,0:T(8,128)S(1)}, f32[640,128]{1,0:T(8,128)S(1)}, f32[320,128]{1,0:T(8,128)S(1)}) custom-call(f32[4,64,128]{2,1,0:T(8,128)} %b.1, f32[4,64,128]{2,1,0:T(8,128)} %al.1, f32[4,64,128]{2,1,0:T(8,128)} %bx.1, f32[4,64,128]{2,1,0:T(8,128)} %by.1, f32[4,64,128]{2,1,0:T(8,128)} %bz.1), custom_call_target="tpu_custom_call" | custom-call | flops 1000 | tf_op jit(solution)/shard_map/pack/pallas_call | solution.py:638
  1.3 2.1 %collective-permute-start = (f32[640,128]{1,0:T(8,128)S(1)}, f32[640,128]{1,0:T(8,128)S(1)}, u32[]{:S(2)}, u32[]{:S(2)}) collective-permute-start(f32[640,128]{1,0:T(8,128)S(1)} %get-tuple-element.33), channel_id=1, source_target_pairs={{0,1},{1,2},{2,3},{3,4},{4,5},{5,6},{6,7},{9,8},{10,9},{11,10},{12... | collective-permute-start | bytes 983048 | tf_op jit(solution)/shard_map/ppermute | solution.py:634
  3.4 3.2 %collective-permute-start.1 = (f32[640,128]{1,0:T(8,128)S(1)}, f32[640,128]{1,0:T(8,128)S(1)}, u32[]{:S(2)}, u32[]{:S(2)}) collective-permute-start(f32[640,128]{1,0:T(8,128)S(1)} %get-tuple-element.34), channel_id=1, source_target_pairs={{1,0},{2,1},{3,2},{4,3},{5,4},{6,5},{7,6},{8,9},{9,10},{10,11},{11... | collective-permute-start | bytes 983048 | tf_op jit(solution)/shard_map/ppermute | solution.py:634
  6.6 7.5 %collective-permute-start.2 = (f32[320,128]{1,0:T(8,128)S(1)}, f32[320,128]{1,0:T(8,128)S(1)}, u32[]{:S(2)}, u32[]{:S(2)}) collective-permute-start(f32[320,128]{1,0:T(8,128)S(1)} %get-tuple-element.35), channel_id=1, source_target_pairs={{8,16},{24,32},{40,48},{56,64},{72,80},{88,96},{104,112},{120,128}... | collective-permute-start | bytes 491528 | tf_op jit(solution)/shard_map/ppermute | solution.py:619
  14.0 0.0 collective-permute-done.refs_0_.one
  14.1 0.9 %collective-permute-done.1.refs_1_.two = f32[640,128]{1,0:T(8,128)S(1)} collective-permute-done((f32[640,128]{1,0:T(8,128)S(1)}, f32[640,128]{1,0:T(8,128)S(1)}, u32[]{:S(2)}, u32[]{:S(2)}) %collective-permute-start.1) | collective-permute-done | bytes 327712 | tf_op jit(solution)/shard_map/ppermute | solution.py:634
  15.0 2.1 %collective-permute-done.2._.ex = f32[320,128]{1,0:T(8,128)S(1)} collective-permute-done((f32[320,128]{1,0:T(8,128)S(1)}, f32[320,128]{1,0:T(8,128)S(1)}, u32[]{:S(2)}, u32[]{:S(2)}) %collective-permute-start.2) | collective-permute-done | bytes 163872 | tf_op jit(solution)/shard_map/ppermute | solution.py:619
  17.0 0.7 corners.1
  17.7 7.0 %collective-permute-start.4 = (f32[768,128]{1,0:T(8,128)S(1)}, f32[768,128]{1,0:T(8,128)S(1)}, u32[]{:S(2)}, u32[]{:S(2)}) collective-permute-start(f32[768,128]{1,0:T(8,128)S(1)} %get-tuple-element.38), channel_id=1, source_target_pairs={{8,16},{24,32},{40,48},{56,64},{72,80},{88,96},{104,112},{120,128}... | collective-permute-start | bytes 1179656 | tf_op jit(solution)/shard_map/ppermute | solution.py:619
  24.7 1.9 %collective-permute-start.3 = (f32[1280,128]{1,0:T(8,128)S(1)}, f32[1280,128]{1,0:T(8,128)S(1)}, u32[]{:S(2)}, u32[]{:S(2)}) collective-permute-start(f32[1280,128]{1,0:T(8,128)S(1)} %get-tuple-element.37), channel_id=1, source_target_pairs={{0,8},{8,0},{16,24},{24,16},{32,40},{40,32},{48,56},{56,48},{64,72... | collective-permute-start | bytes 1966088 | tf_op jit(solution)/shard_map/ppermute | solution.py:611
  26.6 3.5 %collective-permute-done.4.refs_0_.xs = f32[768,128]{1,0:T(8,128)S(1)} collective-permute-done((f32[768,128]{1,0:T(8,128)S(1)}, f32[768,128]{1,0:T(8,128)S(1)}, u32[]{:S(2)}, u32[]{:S(2)}) %collective-permute-start.4) | collective-permute-done | bytes 393248 | tf_op jit(solution)/shard_map/ppermute | solution.py:619
  30.1 0.0 collective-permute-done.3.sw
  30.1 1.9 %level0_pre.1 = (f32[400,128]{1,0:T(8,128)S(1)}, f32[320,128]{1,0:T(8,128)S(1)}, f32[128,128]{1,0:T(8,128)S(1)}, f32[80,128]{1,0:T(8,128)S(1)}, f32[6,80,128]{2,...) custom-call(f32[2816,128]{1,0:T(8,128)S(1)} %get-tuple-element.36.own, ...), custom_call_target="tpu_custom_call" | custom-call | flops 20000000000 | tf_op jit(solution)/shard_map/level0_pre/pallas_call | solution.py:651
  32.0 7.0 %collective-permute-start.5 = (f32[400,128]{1,0:T(8,128)S(1)}, f32[400,128]{1,0:T(8,128)S(1)}, u32[]{:S(2)}, u32[]{:S(2)}) collective-permute-start(f32[400,128]{1,0:T(8,128)S(1)} %get-tuple-element.39.own), channel_id=1, source_target_pairs={{8,16},{24,32},{40,48},{56,64},{72,80},{88,96},{104,112},{120,128}... | collective-permute-start | bytes 614408 | tf_op jit(solution)/shard_map/ppermute | solution.py:619
  39.0 1.9 %collective-permute-start.6 = (f32[320,128]{1,0:T(8,128)S(1)}, f32[320,128]{1,0:T(8,128)S(1)}, u32[]{:S(2)}, u32[]{:S(2)}) collective-permute-start(f32[320,128]{1,0:T(8,128)S(1)} %get-tuple-element.40), channel_id=1, source_target_pairs={{0,16},{16,32},{32,48},{48,64},{64,80},{80,96},{96,112},{112,128},... | collective-permute-start | bytes 491528 | tf_op jit(solution)/shard_map/ppermute | solution.py:625
  40.9 1.9 %collective-permute-start.7 = (f32[128,128]{1,0:T(8,128)S(1)}, f32[128,128]{1,0:T(8,128)S(1)}, u32[]{:S(2)}, u32[]{:S(2)}) collective-permute-start(f32[128,128]{1,0:T(8,128)S(1)} %get-tuple-element.41), channel_id=1, source_target_pairs={{8,32},{24,48},{40,64},{56,80},{72,96},{88,112},{104,128},{120,144... | collective-permute-start | bytes 196616 | tf_op jit(solution)/shard_map/ppermute | solution.py:619
  42.9 7.2 %collective-permute-done.7.two = f32[128,128]{1,0:T(8,128)S(1)} collective-permute-done((f32[128,128]{1,0:T(8,128)S(1)}, f32[128,128]{1,0:T(8,128)S(1)}, u32[]{:S(2)}, u32[]{:S(2)}) %collective-permute-start.7) | collective-permute-done | bytes 65568 | tf_op jit(solution)/shard_map/ppermute | solution.py:619
  50.1 0.0 collective-permute-done.6.beside
  50.1 0.0 collective-permute-done.5.one.xs
  50.2 1.9 %collective-permute-start.8 = (f32[912,128]{1,0:T(8,128)S(1)}, f32[912,128]{1,0:T(8,128)S(1)}, u32[]{:S(2)}, u32[]{:S(2)}) collective-permute-start(f32[912,128]{1,0:T(8,128)S(1)} %join.1), channel_id=1, source_target_pairs={{0,8},{8,0},{16,24},{24,16},{32,40},{40,32},{48,56},{56,48},{64,72... | collective-permute-start | bytes 1400840 | tf_op jit(solution)/shard_map/ppermute | solution.py:611
  52.1 0.6 near_coefficients.1
  52.7 1.2 %collective-permute-done.8.its.sw = f32[912,128]{1,0:T(8,128)S(1)} collective-permute-done((f32[912,128]{1,0:T(8,128)S(1)}, f32[912,128]{1,0:T(8,128)S(1)}, u32[]{:S(2)}, u32[]{:S(2)}) %collective-permute-start.8) | collective-permute-done | bytes 466976 | tf_op jit(solution)/shard_map/ppermute | solution.py:611
  53.9 1.8 %level1_pre.1 = (f32[64,128]{1,0:T(8,128)S(1)}, f32[14,64,128]{2,1,0:T(8,128)S(1)}, f32[10,64,128]{2,1,0:T(8,128)S(1)}, f32[4,32,128]{2,1,0:T(8,128)S(1)}, f32[4...) custom-call(f32[400,128]{1,0:T(8,128)S(1)} %get-tuple-element.39.own, ...), custom_call_target="tpu_custom_call", output_to_operand_aliasing={{4}: (5, {}), {5}: (6, {}), {6}: (7, {}), {7}: (8, {})} | custom-call | flops 20000000000 | tf_op jit(solution)/shard_map/level1_pre/pallas_call | solution.py:671
  55.7 2.3 %collective-permute-start.9 = (f32[64,128]{1,0:T(8,128)S(1)}, f32[64,128]{1,0:T(8,128)S(1)}, u32[]{:S(2)}, u32[]{:S(2)}) collective-permute-start(f32[64,128]{1,0:T(8,128)S(1)} %get-tuple-element.47), channel_id=1, source_target_pairs={{8,32},{24,48},{40,64},{56,80},{72,96},{88,112},{104,128},{120,144... | collective-permute-start | bytes 98312 | tf_op jit(solution)/shard_map/ppermute | solution.py:619
  58.0 6.5 %collective-permute-done.9.two2 = f32[64,128]{1,0:T(8,128)S(1)} collective-permute-done((f32[64,128]{1,0:T(8,128)S(1)}, f32[64,128]{1,0:T(8,128)S(1)}, u32[]{:S(2)}, u32[]{:S(2)}) %collective-permute-start.9) | collective-permute-done | bytes 32800 | tf_op jit(solution)/shard_map/ppermute | solution.py:619
  64.5 1.9 %collective-permute-start.10 = (f32[64,128]{1,0:T(8,128)S(1)}, f32[64,128]{1,0:T(8,128)S(1)}, u32[]{:S(2)}, u32[]{:S(2)}) collective-permute-start(f32[64,128]{1,0:T(8,128)S(1)} %collective-permute-done.9.two2), channel_id=1, source_target_pairs={{0,8},{8,0},{16,24},{24,16},{32,40},{40,32},{48,56},{56,48},{64,72... | collective-permute-start | bytes 98312 | tf_op jit(solution)/shard_map/ppermute | solution.py:611
  66.4 0.5 level2_coefficients.1
  66.9 0.7 %collective-permute-done.10.its2 = f32[64,128]{1,0:T(8,128)S(1)} collective-permute-done((f32[64,128]{1,0:T(8,128)S(1)}, f32[64,128]{1,0:T(8,128)S(1)}, u32[]{:S(2)}, u32[]{:S(2)}) %collective-permute-start.10) | collective-permute-done | bytes 32800 | tf_op jit(solution)/shard_map/ppermute | solution.py:611
  67.6 1.7 %coarse_and_post.1 = f32[4,64,128]{2,1,0:T(8,128)} custom-call(f32[64,128]{1,0:T(8,128)S(1)} %collective-permute-done.9.two2, f32[64,128]{1,0:T(8,128)S(1)} %collective-permute-done.10.its2, f32[4,32,128]{2,1,0:T(8,128)S(1)} %get-tuple-element.48.rhs, f32[6,12,32,128]{3,2,1,0:T(8,128)S(1)} %get-tuple-element.50.w2, ...), custom_call_target="tpu_custom_call" | custom-call | flops 20000000000 | tf_op jit(solution)/shard_map/coarse_and_post/pallas_call | solution.py:687
  (5 shorter events, 0.1 us)
Async XLA Ops:
  1.3 12.8 %collective-permute-start = (f32[640,128]{1,0:T(8,128)S(1)}, f32[640,128]{1,0:T(8,128)S(1)}, u32[]{:S(2)}, u32[]{:S(2)}) collective-permute-start(f32[640,128]{1,0:T(8,128)S(1)} %get-tuple-element.33), channel_id=1, source_target_pairs={{0,1},{1,2},{2,3},{3,4},{4,5},{5,6},{6,7},{9,8},{10,9},{11,10},{12... | collective-permute-start | bytes 983048 | tf_op jit(solution)/shard_map/ppermute | solution.py:634
  3.4 11.6 %collective-permute-start.1 = (f32[640,128]{1,0:T(8,128)S(1)}, f32[640,128]{1,0:T(8,128)S(1)}, u32[]{:S(2)}, u32[]{:S(2)}) collective-permute-start(f32[640,128]{1,0:T(8,128)S(1)} %get-tuple-element.34), channel_id=1, source_target_pairs={{1,0},{2,1},{3,2},{4,3},{5,4},{6,5},{7,6},{8,9},{9,10},{10,11},{11... | collective-permute-start | bytes 983048 | tf_op jit(solution)/shard_map/ppermute | solution.py:634
  6.6 10.5 %collective-permute-start.2 = (f32[320,128]{1,0:T(8,128)S(1)}, f32[320,128]{1,0:T(8,128)S(1)}, u32[]{:S(2)}, u32[]{:S(2)}) collective-permute-start(f32[320,128]{1,0:T(8,128)S(1)} %get-tuple-element.35), channel_id=1, source_target_pairs={{8,16},{24,32},{40,48},{56,64},{72,80},{88,96},{104,112},{120,128}... | collective-permute-start | bytes 491528 | tf_op jit(solution)/shard_map/ppermute | solution.py:619
  17.7 12.4 %collective-permute-start.4 = (f32[768,128]{1,0:T(8,128)S(1)}, f32[768,128]{1,0:T(8,128)S(1)}, u32[]{:S(2)}, u32[]{:S(2)}) collective-permute-start(f32[768,128]{1,0:T(8,128)S(1)} %get-tuple-element.38), channel_id=1, source_target_pairs={{8,16},{24,32},{40,48},{56,64},{72,80},{88,96},{104,112},{120,128}... | collective-permute-start | bytes 1179656 | tf_op jit(solution)/shard_map/ppermute | solution.py:619
  24.7 5.5 %collective-permute-start.3 = (f32[1280,128]{1,0:T(8,128)S(1)}, f32[1280,128]{1,0:T(8,128)S(1)}, u32[]{:S(2)}, u32[]{:S(2)}) collective-permute-start(f32[1280,128]{1,0:T(8,128)S(1)} %get-tuple-element.37), channel_id=1, source_target_pairs={{0,8},{8,0},{16,24},{24,16},{32,40},{40,32},{48,56},{56,48},{64,72... | collective-permute-start | bytes 1966088 | tf_op jit(solution)/shard_map/ppermute | solution.py:611
  32.0 18.1 %collective-permute-start.5 = (f32[400,128]{1,0:T(8,128)S(1)}, f32[400,128]{1,0:T(8,128)S(1)}, u32[]{:S(2)}, u32[]{:S(2)}) collective-permute-start(f32[400,128]{1,0:T(8,128)S(1)} %get-tuple-element.39.own), channel_id=1, source_target_pairs={{8,16},{24,32},{40,48},{56,64},{72,80},{88,96},{104,112},{120,128}... | collective-permute-start | bytes 614408 | tf_op jit(solution)/shard_map/ppermute | solution.py:619
  39.0 11.1 %collective-permute-start.6 = (f32[320,128]{1,0:T(8,128)S(1)}, f32[320,128]{1,0:T(8,128)S(1)}, u32[]{:S(2)}, u32[]{:S(2)}) collective-permute-start(f32[320,128]{1,0:T(8,128)S(1)} %get-tuple-element.40), channel_id=1, source_target_pairs={{0,16},{16,32},{32,48},{48,64},{64,80},{80,96},{96,112},{112,128},... | collective-permute-start | bytes 491528 | tf_op jit(solution)/shard_map/ppermute | solution.py:625
  40.9 9.2 %collective-permute-start.7 = (f32[128,128]{1,0:T(8,128)S(1)}, f32[128,128]{1,0:T(8,128)S(1)}, u32[]{:S(2)}, u32[]{:S(2)}) collective-permute-start(f32[128,128]{1,0:T(8,128)S(1)} %get-tuple-element.41), channel_id=1, source_target_pairs={{8,32},{24,48},{40,64},{56,80},{72,96},{88,112},{104,128},{120,144... | collective-permute-start | bytes 196616 | tf_op jit(solution)/shard_map/ppermute | solution.py:619
  50.2 3.7 %collective-permute-start.8 = (f32[912,128]{1,0:T(8,128)S(1)}, f32[912,128]{1,0:T(8,128)S(1)}, u32[]{:S(2)}, u32[]{:S(2)}) collective-permute-start(f32[912,128]{1,0:T(8,128)S(1)} %join.1), channel_id=1, source_target_pairs={{0,8},{8,0},{16,24},{24,16},{32,40},{40,32},{48,56},{56,48},{64,72... | collective-permute-start | bytes 1400840 | tf_op jit(solution)/shard_map/ppermute | solution.py:611
  55.7 8.8 %collective-permute-start.9 = (f32[64,128]{1,0:T(8,128)S(1)}, f32[64,128]{1,0:T(8,128)S(1)}, u32[]{:S(2)}, u32[]{:S(2)}) collective-permute-start(f32[64,128]{1,0:T(8,128)S(1)} %get-tuple-element.47), channel_id=1, source_target_pairs={{8,32},{24,48},{40,64},{56,80},{72,96},{88,112},{104,128},{120,144... | collective-permute-start | bytes 98312 | tf_op jit(solution)/shard_map/ppermute | solution.py:619
  64.5 3.1 %collective-permute-start.10 = (f32[64,128]{1,0:T(8,128)S(1)}, f32[64,128]{1,0:T(8,128)S(1)}, u32[]{:S(2)}, u32[]{:S(2)}) collective-permute-start(f32[64,128]{1,0:T(8,128)S(1)} %collective-permute-done.9.two2), channel_id=1, source_target_pairs={{0,8},{8,0},{16,24},{24,16},{32,40},{40,32},{48,56},{56,48},{64,72... | collective-permute-start | bytes 98312 | tf_op jit(solution)/shard_map/ppermute | solution.py:611

commit v8 on v7

--- a/solution.py
+++ b/solution.py
@@ -25,7 +25,9 @@
 RAW = 5 * PX * EY
 SRAW = 8 * EY
 XP = 5 * 2 * HY
-XB = XP + 3 * EY
+INNER, EDGE = PY - 16, HY + 8
+XB = XP + 3 * 2 * EDGE
+EX_IN = 5 * PY
 PAD = 8
 SMALL, LARGE = 1000, 2 * 10**10
 B, ALPHA, BX, BY, BZ = range(5)
@@ -193,7 +195,7 @@
     return al, bx, by, bz
 
 
-def pack_kernel(b, al, bx, by, bz, a, one_out, two_out, xs_out, sems):
+def pack_kernel(b, al, bx, by, bz, a, one_out, two_out, sems):
     wide, narrow = lax.axis_index("wide"), lax.axis_index("narrow")
     par = lax.rem(wide, 2)
     copies = [pltpu.make_async_copy(ref, a.at[i], sems.at[i]) for i, ref in enumerate((b, al, bx, by, bz))]
@@ -213,7 +215,6 @@
             here = pl.ds((PX * i + p) * HY, HY)
             one_out[here, :] = a[i, p, pl.ds(pl.multiple_of((1 - par) * (PY - HY), 8), HY), :]
             two_out[here, :] = a[i, p, pl.ds(pl.multiple_of(par * (PY - HY), 8), HY), :]
-        xs_out[pl.ds(i * PY, PY), :] = a[i, 3 * par]
 
 
 def plane(ref, k, r0=0, n=EY):
@@ -221,7 +222,45 @@
     return ref[pl.ds(pl.multiple_of(start, 8) if r0 % 8 == 0 else start, n), :]
 
 
-def corner_kernel(a, one, two, _, __, own, sw, xs, x, v):
+def second_planes(get, rows, x, keep):
+    clear_pads(x, rows)
+    body = pl.ds(PAD, rows)
+    kept = []
+    for p in range(3):
+        by = get(BY, p)
+        _, inv, w = faces(
+            get(ALPHA, p), get(BX, p), get(BX, p + 1), by, pltpu.roll(by, rows - 1, 0), get(BZ, p), 1, 1.0
+        )
+        c0 = inv * get(B, p)
+        x[p, body, :] = c0 * (1.0 / THETA)
+        kept.append((w, c0))
+    for up in range(2):
+        second = 1 + up
+        w, c0 = kept[second]
+        here = x[second, body, :]
+        z = c0 - here + w[0] * x[second - 1, body, :]
+        if not up:
+            z += w[1] * x[2, body, :]
+        z += w[2] * x[second, pl.ds(PAD - 1, rows), :] + w[3] * x[second, pl.ds(PAD + 1, rows), :]
+        z += w[4] * moved(here, 1) + w[5] * moved(here, -1)
+        keep(up, 0, here)
+        keep(up, 1, here + GAIN[1] * z + MOMENTUM[1] * here)
+        keep(up, 2, w[1] if up else get(BX, second))
+
+
+def inner_kernel(a, ex, v, x):
+    par = parity()
+
+    def keep(up, k, value):
+        v[up, pl.ds(INNER * k, INNER), :] = value[8 : 8 + INNER]
+
+    second_planes(lambda i, p: a[i, p], PY, x, keep)
+    for i in range(5):
+        ex[pl.ds(i * PY, PY), :] = a[i, 3 * par]
+    ex[pl.ds(EX_IN, 3 * INNER), :] = v[par]
+
+
+def corner_kernel(a, one, two, inner, _, own, sw, xs, x, v):
     par = parity()
     for i in range(5):
         for p in range(PX):
@@ -246,32 +285,19 @@
         xs[pl.ds(2 * HY * i, HY), :] = plane(own, PX * i + 3 * par, 0, HY)
         xs[pl.ds(2 * HY * i + HY, HY), :] = plane(own, PX * i + 3 * par, HY + PY, HY)
         sw[pl.ds(i * EY, EY), :] = plane(own, PX * i + 3 - 3 * par)
-    clear_pads(x, EY)
-    body = pl.ds(PAD, EY)
-    kept = []
-    for p in range(3):
-        by = plane(own, PX * BY + p)
-        _, inv, w = faces(
-            plane(own, PX * ALPHA + p), plane(own, PX * BX + p), plane(own, PX * BX + p + 1), by,
-            pltpu.roll(by, EY - 1, 0), plane(own, PX * BZ + p), 1, 1.0,
-        )
-        c0 = inv * plane(own, PX * B + p)
-        x[p, body, :] = c0 * (1.0 / THETA)
-        kept.append((w, c0))
-    for up in range(2):
-        second = 1 + up
-        w, c0 = kept[second]
-        here = x[second, body, :]
-        z = c0 - here + w[0] * x[second - 1, body, :]
-        if not up:
-            z += w[1] * x[2, body, :]
-        z += w[2] * x[second, pl.ds(PAD - 1, EY), :] + w[3] * x[second, pl.ds(PAD + 1, EY), :]
-        z += w[4] * moved(here, 1) + w[5] * moved(here, -1)
-        v[up, pl.ds(0, EY), :] = here
-        v[up, pl.ds(EY, EY), :] = here + GAIN[1] * z + MOMENTUM[1] * here
-        v[up, pl.ds(2 * EY, EY), :] = w[1] if up else plane(own, PX * BX + second)
-    xs[pl.ds(XP, 3 * EY), :] = v[par]
-    sw[pl.ds(5 * EY, 3 * EY), :] = v[1 - par]
+    span = EDGE + 8
+    for side, r0 in ((0, 0), (1, EY - span)):
+
+        def keep(up, k, value):
+            v[up, pl.ds((2 * k + side) * EDGE, EDGE), :] = value[8 * side : 8 * side + EDGE]
+
+        second_planes(lambda i, p: plane(own, PX * i + p, r0, span), span, x.at[side], keep)
+    xs[pl.ds(XP, 6 * EDGE), :] = v[par]
+    for k in range(3):
+        base = (5 + k) * EY
+        sw[pl.ds(base, EDGE), :] = v[1 - par, pl.ds(2 * k * EDGE, EDGE), :]
+        sw[pl.ds(base + EDGE, INNER), :] = inner[1 - par, pl.ds(k * INNER, INNER), :]
+        sw[pl.ds(base + EDGE + INNER, EDGE), :] = v[1 - par, pl.ds((2 * k + 1) * EDGE, EDGE), :]
 
 
 Q0 = 3
@@ -284,8 +310,13 @@
         sf[i, HY : HY + PY] = ex[pl.ds(PY * i, PY), :]
         sf[i, HY + PY :] = xs[pl.ds(2 * HY * i + HY, HY), :]
 
+    for k in range(3):
+        sf[5 + k, :EDGE] = xs[pl.ds(XP + 2 * k * EDGE, EDGE), :]
+        sf[5 + k, EDGE : EDGE + INNER] = ex[pl.ds(EX_IN + k * INNER, INNER), :]
+        sf[5 + k, EDGE + INNER :] = xs[pl.ds(XP + (2 * k + 1) * EDGE, EDGE), :]
+
     def far(i, r, n):
-        return sf[i, pl.ds(r, n), :] if i < 5 else xs[pl.ds(XP + (i - 5) * EY + r, n), :]
+        return sf[i, pl.ds(r, n), :]
 
     def near(i, r, n):
         return plane(sw, i, r, n)
@@ -635,16 +666,20 @@
 
 
 def shards(right_side, alpha_coef, beta_x, beta_y, beta_z):
-    a, y1, y2, ex = call(
-        pack_kernel, "pack", (shape(5, PX, PY, PZ), shape(5 * PX * HY, PZ), shape(5 * PX * HY, PZ), shape(5 * PY, PZ)),
-        (VMEM,) * 4, [ANY] * 5, [pltpu.SemaphoreType.DMA((5,))], SMALL,
+    a, y1, y2 = call(
+        pack_kernel, "pack", (shape(5, PX, PY, PZ), shape(5 * PX * HY, PZ), shape(5 * PX * HY, PZ)),
+        (VMEM,) * 3, [ANY] * 5, [pltpu.SemaphoreType.DMA((5,))], SMALL,
     )(*[pltpu.with_memory_space_constraint(v, pltpu.HBM) for v in (right_side, alpha_coef, beta_x, beta_y, beta_z)])
     y1, y2 = along_narrow(y1, 1), along_narrow(y2, -1)
+    ex, inner = call(
+        inner_kernel, "inner_rows", (shape(EX_IN + 3 * INNER, PZ), shape(2, 3 * INNER, PZ)), (VMEM,) * 2, [VMEM],
+        [scratch(3, PY + 2 * PAD, PZ)], LARGE,
+    )(a)
     ex = across(ex, 1)
     own, sw, xs = call(
         corner_kernel, "corners", (shape(RAW + 4 * R1, PZ), shape(SRAW + 4 * R1, PZ), shape(XB + R1, PZ)),
-        (VMEM,) * 3, [VMEM] * 3 + [ANY] * 2, [scratch(3, EY + 2 * PAD, PZ), scratch(2, 3 * EY, PZ)], SMALL,
-    )(a, y1, y2, ex, first_to_arrive(y1, y2))
+        (VMEM,) * 3, [VMEM] * 4 + [ANY], [scratch(2, 3, EDGE + 8 + 2 * PAD, PZ), scratch(2, 6 * EDGE, PZ)], SMALL,
+    )(a, y1, y2, inner, first_to_arrive(y1, y2))
     xs = across(xs, 1)
     sw = swap(sw)
 
@@ -654,9 +689,9 @@
          shape(6, 10, EY, PZ), shape(10, EY, PZ)),
         (VMEM,) * 7, [VMEM] * 4 + [ANY],
         [scratch(10, EY, PZ), scratch(10, EY, PZ)] + [scratch(10, EY + 2 * PAD, PZ)] * 3
-        + [scratch(2, EY, PZ), scratch(4, 5, R1, PZ), scratch(R1 + PAD, PZ), scratch(5, EY, PZ)],
+        + [scratch(2, EY, PZ), scratch(4, 5, R1, PZ), scratch(R1 + PAD, PZ), scratch(8, EY, PZ)],
         LARGE,
-    )(own, sw, xs, ex, first_to_arrive(xs))
+    )(own, sw, xs, ex, first_to_arrive(xs, first_to_arrive(ex)))
 
     one = across(send, 1)
     beside = from_beside(send1)

time: 69.7 us -> 66.7 us (0.957)
  the two profiles are of different devices: /device:TPU:231 before, /device:TPU:223 now
where the time goes in v8:
time: 66.7 us; the launch traced here: 66.2 us
  starting transfers between devices  38.7 us (58%)
  waiting for transfers between devices  18.9 us (28%)
  Pallas kernels  8.43 us (13%)
    ppermute x5, starting transfers between devices, across(): return lax.ppermute(v, 'wide', pairs + list(ends))  24.5 us
    ppermute x5, waiting for transfers between devices, across(): return lax.ppermute(v, 'wide', pairs + list(ends))  16.5 us
    ppermute x2, starting transfers between devices, along_narrow(): return lax.ppermute(v, ('wide', 'narrow'), pairs)  6.49 us
    ppermute x3, starting transfers between devices, swap(): lax.ppermute(v, 'wide', [(i, i ^ 1) for i in range(lax.axis_size('wide'))])  5.75 us
    ppermute x3, waiting for transfers between devices, swap(): lax.ppermute(v, 'wide', [(i, i ^ 1) for i in range(lax.axis_size('wide'))])  1.95 us
    pallas_call x1, Pallas kernels, shards(): call(fine_kernel, 'level0_pre', (shape(5 * R1 + MID, PZ), shape(5 * R1, P...  1.93 us
    ppermute x1, starting transfers between devices, from_beside(): return lax.ppermute(v, 'wide', pairs)  1.92 us
    pallas_call x1, Pallas kernels, shards(): call(middle_kernel, 'level1_pre', (shape(2 * R2, PZ), shape(N1, R1, PZ),...  1.77 us
  transfers between devices with their start and end apart: 11, of which 6 were waited for; matrix products, arithmetic and copies ran while one was open for 0% of the time, Pallas kernels for 3%

profile of v8, /device:TPU:223, one launch (start us, length us, event | category | flops | bytes accessed | tf_op | source)
XLA Modules:
  0.0 66.2 jit_solution(10263847410884373828)
XLA Ops:
  0.0 1.3 %pack.1 = (f32[5,4,64,128]{3,2,1,0:T(8,128)S(1)}, f32[640,128]{1,0:T(8,128)S(1)}, f32[640,128]{1,0:T(8,128)S(1)}) custom-call(f32[4,64,128]{2,1,0:T(8,128)} %b.1, f32[4,64,128]{2,1,0:T(8,128)} %al.1, f32[4,64,128]{2,1,0:T(8,128)} %bx.1, f32[4,64,128]{2,1,0:T(8,128)} %by.1, f32[4,64,128]{2,1,0:T(8,128)} %bz.1), custom_call_target="tpu_custom_call" | custom-call | flops 1000 | tf_op jit(solution)/shard_map/pack/pallas_call | solution.py:669
  1.3 2.1 %collective-permute-start = (f32[640,128]{1,0:T(8,128)S(1)}, f32[640,128]{1,0:T(8,128)S(1)}, u32[]{:S(2)}, u32[]{:S(2)}) collective-permute-start(f32[640,128]{1,0:T(8,128)S(1)} %get-tuple-element.34), channel_id=1, source_target_pairs={{0,1},{1,2},{2,3},{3,4},{4,5},{5,6},{6,7},{9,8},{10,9},{11,10},{12... | collective-permute-start | bytes 983048 | tf_op jit(solution)/shard_map/ppermute | solution.py:665
  3.4 4.4 %collective-permute-start.1 = (f32[640,128]{1,0:T(8,128)S(1)}, f32[640,128]{1,0:T(8,128)S(1)}, u32[]{:S(2)}, u32[]{:S(2)}) collective-permute-start(f32[640,128]{1,0:T(8,128)S(1)} %get-tuple-element.35), channel_id=1, source_target_pairs={{1,0},{2,1},{3,2},{4,3},{5,4},{6,5},{7,6},{8,9},{9,10},{10,11},{11... | collective-permute-start | bytes 983048 | tf_op jit(solution)/shard_map/ppermute | solution.py:665
  7.8 0.2 inner_rows.1
  8.0 5.8 %collective-permute-start.4 = (f32[464,128]{1,0:T(8,128)S(1)}, f32[464,128]{1,0:T(8,128)S(1)}, u32[]{:S(2)}, u32[]{:S(2)}) collective-permute-start(f32[464,128]{1,0:T(8,128)S(1)} %get-tuple-element.40), channel_id=1, source_target_pairs={{8,16},{24,32},{40,48},{56,64},{72,80},{88,96},{104,112},{120,128}... | collective-permute-start | bytes 712712 | tf_op jit(solution)/shard_map/ppermute | solution.py:650
  13.8 0.0 collective-permute-done.refs_0_.one
  13.8 0.5 collective-permute-done.1.refs_1_.two
  14.3 0.6 corners.1
  14.9 7.5 %collective-permute-start.3 = (f32[624,128]{1,0:T(8,128)S(1)}, f32[624,128]{1,0:T(8,128)S(1)}, u32[]{:S(2)}, u32[]{:S(2)}) collective-permute-start(f32[624,128]{1,0:T(8,128)S(1)} %get-tuple-element.39), channel_id=1, source_target_pairs={{8,16},{24,32},{40,48},{56,64},{72,80},{88,96},{104,112},{120,128}... | collective-permute-start | bytes 958472 | tf_op jit(solution)/shard_map/ppermute | solution.py:650
  22.4 0.0 collective-permute-done.4.refs_0_.ex
  22.4 1.9 %collective-permute-start.2 = (f32[1280,128]{1,0:T(8,128)S(1)}, f32[1280,128]{1,0:T(8,128)S(1)}, u32[]{:S(2)}, u32[]{:S(2)}) collective-permute-start(f32[1280,128]{1,0:T(8,128)S(1)} %get-tuple-element.38), channel_id=1, source_target_pairs={{0,8},{8,0},{16,24},{24,16},{32,40},{40,32},{48,56},{56,48},{64,72... | collective-permute-start | bytes 1966088 | tf_op jit(solution)/shard_map/ppermute | solution.py:642
  24.4 2.7 %collective-permute-done.3.refs_0_.xs = f32[624,128]{1,0:T(8,128)S(1)} collective-permute-done((f32[624,128]{1,0:T(8,128)S(1)}, f32[624,128]{1,0:T(8,128)S(1)}, u32[]{:S(2)}, u32[]{:S(2)}) %collective-permute-start.3) | collective-permute-done | bytes 319520 | tf_op jit(solution)/shard_map/ppermute | solution.py:650
  27.1 0.0 collective-permute-done.2.sw
  27.1 1.9 %level0_pre.1 = (f32[400,128]{1,0:T(8,128)S(1)}, f32[320,128]{1,0:T(8,128)S(1)}, f32[128,128]{1,0:T(8,128)S(1)}, f32[80,128]{1,0:T(8,128)S(1)}, f32[6,80,128]{2,...) custom-call(f32[2816,128]{1,0:T(8,128)S(1)} %get-tuple-element.37.own, ...), custom_call_target="tpu_custom_call" | custom-call | flops 20000000000 | tf_op jit(solution)/shard_map/level0_pre/pallas_call | solution.py:686
  29.0 7.0 %collective-permute-start.5 = (f32[400,128]{1,0:T(8,128)S(1)}, f32[400,128]{1,0:T(8,128)S(1)}, u32[]{:S(2)}, u32[]{:S(2)}) collective-permute-start(f32[400,128]{1,0:T(8,128)S(1)} %get-tuple-element.41.own), channel_id=1, source_target_pairs={{8,16},{24,32},{40,48},{56,64},{72,80},{88,96},{104,112},{120,128}... | collective-permute-start | bytes 614408 | tf_op jit(solution)/shard_map/ppermute | solution.py:650
  36.0 1.9 %collective-permute-start.6 = (f32[320,128]{1,0:T(8,128)S(1)}, f32[320,128]{1,0:T(8,128)S(1)}, u32[]{:S(2)}, u32[]{:S(2)}) collective-permute-start(f32[320,128]{1,0:T(8,128)S(1)} %get-tuple-element.42), channel_id=1, source_target_pairs={{0,16},{16,32},{32,48},{48,64},{64,80},{80,96},{96,112},{112,128},... | collective-permute-start | bytes 491528 | tf_op jit(solution)/shard_map/ppermute | solution.py:656
  37.9 1.9 %collective-permute-start.7 = (f32[128,128]{1,0:T(8,128)S(1)}, f32[128,128]{1,0:T(8,128)S(1)}, u32[]{:S(2)}, u32[]{:S(2)}) collective-permute-start(f32[128,128]{1,0:T(8,128)S(1)} %get-tuple-element.43), channel_id=1, source_target_pairs={{8,32},{24,48},{40,64},{56,80},{72,96},{88,112},{104,128},{120,144... | collective-permute-start | bytes 196616 | tf_op jit(solution)/shard_map/ppermute | solution.py:650
  39.9 7.2 %collective-permute-done.7.two = f32[128,128]{1,0:T(8,128)S(1)} collective-permute-done((f32[128,128]{1,0:T(8,128)S(1)}, f32[128,128]{1,0:T(8,128)S(1)}, u32[]{:S(2)}, u32[]{:S(2)}) %collective-permute-start.7) | collective-permute-done | bytes 65568 | tf_op jit(solution)/shard_map/ppermute | solution.py:650
  47.1 0.0 collective-permute-done.6.beside
  47.1 0.0 collective-permute-done.5.one.xs
  47.2 1.9 %collective-permute-start.8 = (f32[912,128]{1,0:T(8,128)S(1)}, f32[912,128]{1,0:T(8,128)S(1)}, u32[]{:S(2)}, u32[]{:S(2)}) collective-permute-start(f32[912,128]{1,0:T(8,128)S(1)} %join.1), channel_id=1, source_target_pairs={{0,8},{8,0},{16,24},{24,16},{32,40},{40,32},{48,56},{56,48},{64,72... | collective-permute-start | bytes 1400840 | tf_op jit(solution)/shard_map/ppermute | solution.py:642
  49.1 0.6 near_coefficients.1
  49.6 1.2 %collective-permute-done.8.its.sw = f32[912,128]{1,0:T(8,128)S(1)} collective-permute-done((f32[912,128]{1,0:T(8,128)S(1)}, f32[912,128]{1,0:T(8,128)S(1)}, u32[]{:S(2)}, u32[]{:S(2)}) %collective-permute-start.8) | collective-permute-done | bytes 466976 | tf_op jit(solution)/shard_map/ppermute | solution.py:642
  50.9 1.8 %level1_pre.1 = (f32[64,128]{1,0:T(8,128)S(1)}, f32[14,64,128]{2,1,0:T(8,128)S(1)}, f32[10,64,128]{2,1,0:T(8,128)S(1)}, f32[4,32,128]{2,1,0:T(8,128)S(1)}, f32[4...) custom-call(f32[400,128]{1,0:T(8,128)S(1)} %get-tuple-element.41.own, ...), custom_call_target="tpu_custom_call", output_to_operand_aliasing={{4}: (5, {}), {5}: (6, {}), {6}: (7, {}), {7}: (8, {})} | custom-call | flops 20000000000 | tf_op jit(solution)/shard_map/level1_pre/pallas_call | solution.py:706
  52.7 2.3 %collective-permute-start.9 = (f32[64,128]{1,0:T(8,128)S(1)}, f32[64,128]{1,0:T(8,128)S(1)}, u32[]{:S(2)}, u32[]{:S(2)}) collective-permute-start(f32[64,128]{1,0:T(8,128)S(1)} %get-tuple-element.49), channel_id=1, source_target_pairs={{8,32},{24,48},{40,64},{56,80},{72,96},{88,112},{104,128},{120,144... | collective-permute-start | bytes 98312 | tf_op jit(solution)/shard_map/ppermute | solution.py:650
  55.0 6.5 %collective-permute-done.9.two2 = f32[64,128]{1,0:T(8,128)S(1)} collective-permute-done((f32[64,128]{1,0:T(8,128)S(1)}, f32[64,128]{1,0:T(8,128)S(1)}, u32[]{:S(2)}, u32[]{:S(2)}) %collective-permute-start.9) | collective-permute-done | bytes 32800 | tf_op jit(solution)/shard_map/ppermute | solution.py:650
  61.5 1.9 %collective-permute-start.10 = (f32[64,128]{1,0:T(8,128)S(1)}, f32[64,128]{1,0:T(8,128)S(1)}, u32[]{:S(2)}, u32[]{:S(2)}) collective-permute-start(f32[64,128]{1,0:T(8,128)S(1)} %collective-permute-done.9.two2), channel_id=1, source_target_pairs={{0,8},{8,0},{16,24},{24,16},{32,40},{40,32},{48,56},{56,48},{64,72... | collective-permute-start | bytes 98312 | tf_op jit(solution)/shard_map/ppermute | solution.py:642
  63.4 0.5 level2_coefficients.1
  63.9 0.7 %collective-permute-done.10.its2 = f32[64,128]{1,0:T(8,128)S(1)} collective-permute-done((f32[64,128]{1,0:T(8,128)S(1)}, f32[64,128]{1,0:T(8,128)S(1)}, u32[]{:S(2)}, u32[]{:S(2)}) %collective-permute-start.10) | collective-permute-done | bytes 32800 | tf_op jit(solution)/shard_map/ppermute | solution.py:642
  64.6 1.7 %coarse_and_post.1 = f32[4,64,128]{2,1,0:T(8,128)} custom-call(f32[64,128]{1,0:T(8,128)S(1)} %collective-permute-done.9.two2, f32[64,128]{1,0:T(8,128)S(1)} %collective-permute-done.10.its2, f32[4,32,128]{2,1,0:T(8,128)S(1)} %get-tuple-element.50.rhs, f32[6,12,32,128]{3,2,1,0:T(8,128)S(1)} %get-tuple-element.52.w2, ...), custom_call_target="tpu_custom_call" | custom-call | flops 20000000000 | tf_op jit(solution)/shard_map/coarse_and_post/pallas_call | solution.py:722
  (6 shorter events, 0.1 us)
Async XLA Ops:
  1.3 12.5 %collective-permute-start = (f32[640,128]{1,0:T(8,128)S(1)}, f32[640,128]{1,0:T(8,128)S(1)}, u32[]{:S(2)}, u32[]{:S(2)}) collective-permute-start(f32[640,128]{1,0:T(8,128)S(1)} %get-tuple-element.34), channel_id=1, source_target_pairs={{0,1},{1,2},{2,3},{3,4},{4,5},{5,6},{6,7},{9,8},{10,9},{11,10},{12... | collective-permute-start | bytes 983048 | tf_op jit(solution)/shard_map/ppermute | solution.py:665
  3.4 11.0 %collective-permute-start.1 = (f32[640,128]{1,0:T(8,128)S(1)}, f32[640,128]{1,0:T(8,128)S(1)}, u32[]{:S(2)}, u32[]{:S(2)}) collective-permute-start(f32[640,128]{1,0:T(8,128)S(1)} %get-tuple-element.35), channel_id=1, source_target_pairs={{1,0},{2,1},{3,2},{4,3},{5,4},{6,5},{7,6},{8,9},{9,10},{10,11},{11... | collective-permute-start | bytes 983048 | tf_op jit(solution)/shard_map/ppermute | solution.py:665
  8.0 14.4 %collective-permute-start.4 = (f32[464,128]{1,0:T(8,128)S(1)}, f32[464,128]{1,0:T(8,128)S(1)}, u32[]{:S(2)}, u32[]{:S(2)}) collective-permute-start(f32[464,128]{1,0:T(8,128)S(1)} %get-tuple-element.40), channel_id=1, source_target_pairs={{8,16},{24,32},{40,48},{56,64},{72,80},{88,96},{104,112},{120,128}... | collective-permute-start | bytes 712712 | tf_op jit(solution)/shard_map/ppermute | solution.py:650
  14.9 12.2 %collective-permute-start.3 = (f32[624,128]{1,0:T(8,128)S(1)}, f32[624,128]{1,0:T(8,128)S(1)}, u32[]{:S(2)}, u32[]{:S(2)}) collective-permute-start(f32[624,128]{1,0:T(8,128)S(1)} %get-tuple-element.39), channel_id=1, source_target_pairs={{8,16},{24,32},{40,48},{56,64},{72,80},{88,96},{104,112},{120,128}... | collective-permute-start | bytes 958472 | tf_op jit(solution)/shard_map/ppermute | solution.py:650
  22.4 4.6 %collective-permute-start.2 = (f32[1280,128]{1,0:T(8,128)S(1)}, f32[1280,128]{1,0:T(8,128)S(1)}, u32[]{:S(2)}, u32[]{:S(2)}) collective-permute-start(f32[1280,128]{1,0:T(8,128)S(1)} %get-tuple-element.38), channel_id=1, source_target_pairs={{0,8},{8,0},{16,24},{24,16},{32,40},{40,32},{48,56},{56,48},{64,72... | collective-permute-start | bytes 1966088 | tf_op jit(solution)/shard_map/ppermute | solution.py:642
  29.0 18.1 %collective-permute-start.5 = (f32[400,128]{1,0:T(8,128)S(1)}, f32[400,128]{1,0:T(8,128)S(1)}, u32[]{:S(2)}, u32[]{:S(2)}) collective-permute-start(f32[400,128]{1,0:T(8,128)S(1)} %get-tuple-element.41.own), channel_id=1, source_target_pairs={{8,16},{24,32},{40,48},{56,64},{72,80},{88,96},{104,112},{120,128}... | collective-permute-start | bytes 614408 | tf_op jit(solution)/shard_map/ppermute | solution.py:650
  36.0 11.1 %collective-permute-start.6 = (f32[320,128]{1,0:T(8,128)S(1)}, f32[320,128]{1,0:T(8,128)S(1)}, u32[]{:S(2)}, u32[]{:S(2)}) collective-permute-start(f32[320,128]{1,0:T(8,128)S(1)} %get-tuple-element.42), channel_id=1, source_target_pairs={{0,16},{16,32},{32,48},{48,64},{64,80},{80,96},{96,112},{112,128},... | collective-permute-start | bytes 491528 | tf_op jit(solution)/shard_map/ppermute | solution.py:656
  37.9 9.2 %collective-permute-start.7 = (f32[128,128]{1,0:T(8,128)S(1)}, f32[128,128]{1,0:T(8,128)S(1)}, u32[]{:S(2)}, u32[]{:S(2)}) collective-permute-start(f32[128,128]{1,0:T(8,128)S(1)} %get-tuple-element.43), channel_id=1, source_target_pairs={{8,32},{24,48},{40,64},{56,80},{72,96},{88,112},{104,128},{120,144... | collective-permute-start | bytes 196616 | tf_op jit(solution)/shard_map/ppermute | solution.py:650
  47.2 3.7 %collective-permute-start.8 = (f32[912,128]{1,0:T(8,128)S(1)}, f32[912,128]{1,0:T(8,128)S(1)}, u32[]{:S(2)}, u32[]{:S(2)}) collective-permute-start(f32[912,128]{1,0:T(8,128)S(1)} %join.1), channel_id=1, source_target_pairs={{0,8},{8,0},{16,24},{24,16},{32,40},{40,32},{48,56},{56,48},{64,72... | collective-permute-start | bytes 1400840 | tf_op jit(solution)/shard_map/ppermute | solution.py:642
  52.7 8.8 %collective-permute-start.9 = (f32[64,128]{1,0:T(8,128)S(1)}, f32[64,128]{1,0:T(8,128)S(1)}, u32[]{:S(2)}, u32[]{:S(2)}) collective-permute-start(f32[64,128]{1,0:T(8,128)S(1)} %get-tuple-element.49), channel_id=1, source_target_pairs={{8,32},{24,48},{40,64},{56,80},{72,96},{88,112},{104,128},{120,144... | collective-permute-start | bytes 98312 | tf_op jit(solution)/shard_map/ppermute | solution.py:650
  61.5 3.1 %collective-permute-start.10 = (f32[64,128]{1,0:T(8,128)S(1)}, f32[64,128]{1,0:T(8,128)S(1)}, u32[]{:S(2)}, u32[]{:S(2)}) collective-permute-start(f32[64,128]{1,0:T(8,128)S(1)} %collective-permute-done.9.two2), channel_id=1, source_target_pairs={{0,8},{8,0},{16,24},{24,16},{32,40},{40,32},{48,56},{56,48},{64,72... | collective-permute-start | bytes 98312 | tf_op jit(solution)/shard_map/ppermute | solution.py:642

commit v9 on v8

--- a/solution.py
+++ b/solution.py
@@ -28,6 +28,8 @@
 INNER, EDGE = PY - 16, HY + 8
 XB = XP + 3 * 2 * EDGE
 EX_IN = 5 * PY
+H1 = PY // 2
+G1 = (R1 - H1) // 2
 PAD = 8
 SMALL, LARGE = 1000, 2 * 10**10
 B, ALPHA, BX, BY, BZ = range(5)
@@ -248,7 +250,7 @@
         keep(up, 2, w[1] if up else get(BX, second))
 
 
-def inner_kernel(a, ex, v, x):
+def inner_kernel(a, ex, v, own, x):
     par = parity()
 
     def keep(up, k, value):
@@ -258,28 +260,39 @@
     for i in range(5):
         ex[pl.ds(i * PY, PY), :] = a[i, 3 * par]
     ex[pl.ds(EX_IN, 3 * INNER), :] = v[par]
-
-
-def corner_kernel(a, one, two, inner, _, own, sw, xs, x, v):
+    for i in range(5):
+        for p in range(PX):
+            own[pl.ds((PX * i + p) * EY + HY, PY), :] = a[i, p]
+    got = []
+    for c in range(2):
+
+        def load(i, k, row):
+            return a[i + 1, 2 * c + k, pl.ds(row, H1, 2), :]
+
+        got.append(coarser(load, H1, 1))
+    for i in range(4):
+        own[pl.ds(RAW + R1 * i + G1, H1), :] = pack2(got[0][i], got[1][i])
+
+
+def corner_kernel(own_in, one, two, inner, _, own, sw, xs, x, v):
     par = parity()
     for i in range(5):
         for p in range(PX):
             k = PX * i + p
             here = pl.ds(k * HY, HY)
             own[pl.ds(pl.multiple_of(k * EY + par * (HY + PY), 8), HY), :] = one[here, :]
-            own[pl.ds(k * EY + HY, PY), :] = a[i, p]
             own[pl.ds(pl.multiple_of(k * EY + (1 - par) * (HY + PY), 8), HY), :] = two[here, :]
-    got = []
-    for c in range(2):
-
-        def load(i, k, row):
-            return own[pl.ds((PX * (i + 1) + 2 * c + k) * EY + row, R1, 2), :]
-
-        got.append(coarser(load, R1, 1))
-    for i in range(4):
-        t = pack2(got[0][i], got[1][i])
-        own[pl.ds(RAW + R1 * i, R1), :] = t
-        sw[pl.ds(SRAW + R1 * i, R1), :] = t
+    for r0, r1 in ((0, 0), (HY + PY, G1 + H1)):
+        got = []
+        for c in range(2):
+
+            def load(i, k, row):
+                return own[pl.ds((PX * (i + 1) + 2 * c + k) * EY + r0 + row, G1, 2), :]
+
+            got.append(coarser(load, G1, 1))
+        for i in range(4):
+            own[pl.ds(RAW + R1 * i + r1, G1), :] = pack2(got[0][i], got[1][i])
+    sw[pl.ds(SRAW, 4 * R1), :] = own[pl.ds(RAW, 4 * R1), :]
     xs[pl.ds(XB, R1), :] = own[pl.ds(RAW + R1, R1), :]
     for i in range(5):
         xs[pl.ds(2 * HY * i, HY), :] = plane(own, PX * i + 3 * par, 0, HY)
@@ -671,15 +684,16 @@
         (VMEM,) * 3, [ANY] * 5, [pltpu.SemaphoreType.DMA((5,))], SMALL,
     )(*[pltpu.with_memory_space_constraint(v, pltpu.HBM) for v in (right_side, alpha_coef, beta_x, beta_y, beta_z)])
     y1, y2 = along_narrow(y1, 1), along_narrow(y2, -1)
-    ex, inner = call(
-        inner_kernel, "inner_rows", (shape(EX_IN + 3 * INNER, PZ), shape(2, 3 * INNER, PZ)), (VMEM,) * 2, [VMEM],
+    ex, inner, own = call(
+        inner_kernel, "inner_rows", (shape(EX_IN + 3 * INNER, PZ), shape(2, 3 * INNER, PZ), shape(RAW + 4 * R1, PZ)),
+        (VMEM,) * 3, [VMEM],
         [scratch(3, PY + 2 * PAD, PZ)], LARGE,
     )(a)
     ex = across(ex, 1)
     own, sw, xs = call(
         corner_kernel, "corners", (shape(RAW + 4 * R1, PZ), shape(SRAW + 4 * R1, PZ), shape(XB + R1, PZ)),
-        (VMEM,) * 3, [VMEM] * 4 + [ANY], [scratch(2, 3, EDGE + 8 + 2 * PAD, PZ), scratch(2, 6 * EDGE, PZ)], SMALL,
-    )(a, y1, y2, inner, first_to_arrive(y1, y2))
+        (VMEM,) * 3, [VMEM] * 4 + [ANY], [scratch(2, 3, EDGE + 8 + 2 * PAD, PZ), scratch(2, 6 * EDGE, PZ)], SMALL, aliases={0: 0},
+    )(own, y1, y2, inner, first_to_arrive(y1, y2))
     xs = across(xs, 1)
     sw = swap(sw)
 

time: 66.7 us -> 66.4 us (level)
  no operation moved by 1% of the time
where the time goes in v9:
time: 66.4 us; the launch traced here: 66 us
  starting transfers between devices  38.7 us (58%)
  waiting for transfers between devices  18.9 us (28%)
  Pallas kernels  8.2 us (12%)
    ppermute x5, starting transfers between devices, across(): return lax.ppermute(v, 'wide', pairs + list(ends))  24.5 us
    ppermute x5, waiting for transfers between devices, across(): return lax.ppermute(v, 'wide', pairs + list(ends))  16.5 us
    ppermute x2, starting transfers between devices, along_narrow(): return lax.ppermute(v, ('wide', 'narrow'), pairs)  6.49 us
    ppermute x3, starting transfers between devices, swap(): lax.ppermute(v, 'wide', [(i, i ^ 1) for i in range(lax.axis_size('wide'))])  5.75 us
    ppermute x3, waiting for transfers between devices, swap(): lax.ppermute(v, 'wide', [(i, i ^ 1) for i in range(lax.axis_size('wide'))])  1.96 us
    ppermute x1, starting transfers between devices, from_beside(): return lax.ppermute(v, 'wide', pairs)  1.92 us
    pallas_call x1, Pallas kernels, shards(): call(fine_kernel, 'level0_pre', (shape(5 * R1 + MID, PZ), shape(5 * R1, P...  1.85 us
    pallas_call x1, Pallas kernels, shards(): call(middle_kernel, 'level1_pre', (shape(2 * R2, PZ), shape(N1, R1, PZ),...  1.76 us
  transfers between devices with their start and end apart: 11, of which 6 were waited for; matrix products, arithmetic and copies ran while one was open for 0% of the time, Pallas kernels for 3%

profile of v9, /device:TPU:223, one launch (start us, length us, event | category | flops | bytes accessed | tf_op | source)
XLA Modules:
  0.0 66.0 jit_solution(1781438864086370329)
XLA Ops:
  0.0 1.3 %pack.1 = (f32[5,4,64,128]{3,2,1,0:T(8,128)S(1)}, f32[640,128]{1,0:T(8,128)S(1)}, f32[640,128]{1,0:T(8,128)S(1)}) custom-call(f32[4,64,128]{2,1,0:T(8,128)} %b.1, f32[4,64,128]{2,1,0:T(8,128)} %al.1, f32[4,64,128]{2,1,0:T(8,128)} %bx.1, f32[4,64,128]{2,1,0:T(8,128)} %by.1, f32[4,64,128]{2,1,0:T(8,128)} %bz.1), custom_call_target="tpu_custom_call" | custom-call | flops 1000 | tf_op jit(solution)/shard_map/pack/pallas_call | solution.py:682
  1.3 2.1 %collective-permute-start = (f32[640,128]{1,0:T(8,128)S(1)}, f32[640,128]{1,0:T(8,128)S(1)}, u32[]{:S(2)}, u32[]{:S(2)}) collective-permute-start(f32[640,128]{1,0:T(8,128)S(1)} %get-tuple-element.36), channel_id=1, source_target_pairs={{0,1},{1,2},{2,3},{3,4},{4,5},{5,6},{6,7},{9,8},{10,9},{11,10},{12... | collective-permute-start | bytes 983048 | tf_op jit(solution)/shard_map/ppermute | solution.py:678
  3.4 4.4 %collective-permute-start.1 = (f32[640,128]{1,0:T(8,128)S(1)}, f32[640,128]{1,0:T(8,128)S(1)}, u32[]{:S(2)}, u32[]{:S(2)}) collective-permute-start(f32[640,128]{1,0:T(8,128)S(1)} %get-tuple-element.37), channel_id=1, source_target_pairs={{1,0},{2,1},{3,2},{4,3},{5,4},{6,5},{7,6},{8,9},{9,10},{10,11},{11... | collective-permute-start | bytes 983048 | tf_op jit(solution)/shard_map/ppermute | solution.py:678
  7.8 0.2 inner_rows.1
  8.0 5.8 %collective-permute-start.4 = (f32[464,128]{1,0:T(8,128)S(1)}, f32[464,128]{1,0:T(8,128)S(1)}, u32[]{:S(2)}, u32[]{:S(2)}) collective-permute-start(f32[464,128]{1,0:T(8,128)S(1)} %get-tuple-element.42), channel_id=1, source_target_pairs={{8,16},{24,32},{40,48},{56,64},{72,80},{88,96},{104,112},{120,128}... | collective-permute-start | bytes 712712 | tf_op jit(solution)/shard_map/ppermute | solution.py:663
  13.8 0.0 collective-permute-done.refs_0_.one
  13.9 0.5 collective-permute-done.1.refs_1_.two
  14.3 0.4 corners.1
  14.8 7.5 %collective-permute-start.3 = (f32[624,128]{1,0:T(8,128)S(1)}, f32[624,128]{1,0:T(8,128)S(1)}, u32[]{:S(2)}, u32[]{:S(2)}) collective-permute-start(f32[624,128]{1,0:T(8,128)S(1)} %get-tuple-element.41), channel_id=1, source_target_pairs={{8,16},{24,32},{40,48},{56,64},{72,80},{88,96},{104,112},{120,128}... | collective-permute-start | bytes 958472 | tf_op jit(solution)/shard_map/ppermute | solution.py:663
  22.3 0.0 collective-permute-done.4.refs_0_.ex
  22.3 1.9 %collective-permute-start.2 = (f32[1280,128]{1,0:T(8,128)S(1)}, f32[1280,128]{1,0:T(8,128)S(1)}, u32[]{:S(2)}, u32[]{:S(2)}) collective-permute-start(f32[1280,128]{1,0:T(8,128)S(1)} %get-tuple-element.40), channel_id=1, source_target_pairs={{0,8},{8,0},{16,24},{24,16},{32,40},{40,32},{48,56},{56,48},{64,72... | collective-permute-start | bytes 1966088 | tf_op jit(solution)/shard_map/ppermute | solution.py:655
  24.2 2.7 %collective-permute-done.3.refs_0_.xs = f32[624,128]{1,0:T(8,128)S(1)} collective-permute-done((f32[624,128]{1,0:T(8,128)S(1)}, f32[624,128]{1,0:T(8,128)S(1)}, u32[]{:S(2)}, u32[]{:S(2)}) %collective-permute-start.3) | collective-permute-done | bytes 319520 | tf_op jit(solution)/shard_map/ppermute | solution.py:663
  26.9 0.0 collective-permute-done.2.sw
  26.9 1.8 %level0_pre.1 = (f32[400,128]{1,0:T(8,128)S(1)}, f32[320,128]{1,0:T(8,128)S(1)}, f32[128,128]{1,0:T(8,128)S(1)}, f32[80,128]{1,0:T(8,128)S(1)}, f32[6,80,128]{2,...) custom-call(f32[2816,128]{1,0:T(8,128)S(1)} %get-tuple-element.39.own, ...), custom_call_target="tpu_custom_call" | custom-call | flops 20000000000 | tf_op jit(solution)/shard_map/level0_pre/pallas_call | solution.py:700
  28.8 7.0 %collective-permute-start.5 = (f32[400,128]{1,0:T(8,128)S(1)}, f32[400,128]{1,0:T(8,128)S(1)}, u32[]{:S(2)}, u32[]{:S(2)}) collective-permute-start(f32[400,128]{1,0:T(8,128)S(1)} %get-tuple-element.43.own), channel_id=1, source_target_pairs={{8,16},{24,32},{40,48},{56,64},{72,80},{88,96},{104,112},{120,128}... | collective-permute-start | bytes 614408 | tf_op jit(solution)/shard_map/ppermute | solution.py:663
  35.8 1.9 %collective-permute-start.6 = (f32[320,128]{1,0:T(8,128)S(1)}, f32[320,128]{1,0:T(8,128)S(1)}, u32[]{:S(2)}, u32[]{:S(2)}) collective-permute-start(f32[320,128]{1,0:T(8,128)S(1)} %get-tuple-element.44), channel_id=1, source_target_pairs={{0,16},{16,32},{32,48},{48,64},{64,80},{80,96},{96,112},{112,128},... | collective-permute-start | bytes 491528 | tf_op jit(solution)/shard_map/ppermute | solution.py:669
  37.7 1.9 %collective-permute-start.7 = (f32[128,128]{1,0:T(8,128)S(1)}, f32[128,128]{1,0:T(8,128)S(1)}, u32[]{:S(2)}, u32[]{:S(2)}) collective-permute-start(f32[128,128]{1,0:T(8,128)S(1)} %get-tuple-element.45), channel_id=1, source_target_pairs={{8,32},{24,48},{40,64},{56,80},{72,96},{88,112},{104,128},{120,144... | collective-permute-start | bytes 196616 | tf_op jit(solution)/shard_map/ppermute | solution.py:663
  39.7 7.2 %collective-permute-done.7.two = f32[128,128]{1,0:T(8,128)S(1)} collective-permute-done((f32[128,128]{1,0:T(8,128)S(1)}, f32[128,128]{1,0:T(8,128)S(1)}, u32[]{:S(2)}, u32[]{:S(2)}) %collective-permute-start.7) | collective-permute-done | bytes 65568 | tf_op jit(solution)/shard_map/ppermute | solution.py:663
  46.9 0.0 collective-permute-done.6.beside
  46.9 0.0 collective-permute-done.5.one.xs
  46.9 1.9 %collective-permute-start.8 = (f32[912,128]{1,0:T(8,128)S(1)}, f32[912,128]{1,0:T(8,128)S(1)}, u32[]{:S(2)}, u32[]{:S(2)}) collective-permute-start(f32[912,128]{1,0:T(8,128)S(1)} %join.1), channel_id=1, source_target_pairs={{0,8},{8,0},{16,24},{24,16},{32,40},{40,32},{48,56},{56,48},{64,72... | collective-permute-start | bytes 1400840 | tf_op jit(solution)/shard_map/ppermute | solution.py:655
  48.9 0.5 near_coefficients.1
  49.4 1.2 %collective-permute-done.8.its.sw = f32[912,128]{1,0:T(8,128)S(1)} collective-permute-done((f32[912,128]{1,0:T(8,128)S(1)}, f32[912,128]{1,0:T(8,128)S(1)}, u32[]{:S(2)}, u32[]{:S(2)}) %collective-permute-start.8) | collective-permute-done | bytes 466976 | tf_op jit(solution)/shard_map/ppermute | solution.py:655
  50.7 1.8 %level1_pre.1 = (f32[64,128]{1,0:T(8,128)S(1)}, f32[14,64,128]{2,1,0:T(8,128)S(1)}, f32[10,64,128]{2,1,0:T(8,128)S(1)}, f32[4,32,128]{2,1,0:T(8,128)S(1)}, f32[4...) custom-call(f32[400,128]{1,0:T(8,128)S(1)} %get-tuple-element.43.own, ...), custom_call_target="tpu_custom_call", output_to_operand_aliasing={{4}: (5, {}), {5}: (6, {}), {6}: (7, {}), {7}: (8, {})} | custom-call | flops 20000000000 | tf_op jit(solution)/shard_map/level1_pre/pallas_call | solution.py:720
  52.4 2.3 %collective-permute-start.9 = (f32[64,128]{1,0:T(8,128)S(1)}, f32[64,128]{1,0:T(8,128)S(1)}, u32[]{:S(2)}, u32[]{:S(2)}) collective-permute-start(f32[64,128]{1,0:T(8,128)S(1)} %get-tuple-element.51), channel_id=1, source_target_pairs={{8,32},{24,48},{40,64},{56,80},{72,96},{88,112},{104,128},{120,144... | collective-permute-start | bytes 98312 | tf_op jit(solution)/shard_map/ppermute | solution.py:663
  54.7 6.5 %collective-permute-done.9.two2 = f32[64,128]{1,0:T(8,128)S(1)} collective-permute-done((f32[64,128]{1,0:T(8,128)S(1)}, f32[64,128]{1,0:T(8,128)S(1)}, u32[]{:S(2)}, u32[]{:S(2)}) %collective-permute-start.9) | collective-permute-done | bytes 32800 | tf_op jit(solution)/shard_map/ppermute | solution.py:663
  61.3 1.9 %collective-permute-start.10 = (f32[64,128]{1,0:T(8,128)S(1)}, f32[64,128]{1,0:T(8,128)S(1)}, u32[]{:S(2)}, u32[]{:S(2)}) collective-permute-start(f32[64,128]{1,0:T(8,128)S(1)} %collective-permute-done.9.two2), channel_id=1, source_target_pairs={{0,8},{8,0},{16,24},{24,16},{32,40},{40,32},{48,56},{56,48},{64,72... | collective-permute-start | bytes 98312 | tf_op jit(solution)/shard_map/ppermute | solution.py:655
  63.2 0.5 level2_coefficients.1
  63.6 0.7 %collective-permute-done.10.its2 = f32[64,128]{1,0:T(8,128)S(1)} collective-permute-done((f32[64,128]{1,0:T(8,128)S(1)}, f32[64,128]{1,0:T(8,128)S(1)}, u32[]{:S(2)}, u32[]{:S(2)}) %collective-permute-start.10) | collective-permute-done | bytes 32800 | tf_op jit(solution)/shard_map/ppermute | solution.py:655
  64.4 1.6 %coarse_and_post.1 = f32[4,64,128]{2,1,0:T(8,128)} custom-call(f32[64,128]{1,0:T(8,128)S(1)} %collective-permute-done.9.two2, f32[64,128]{1,0:T(8,128)S(1)} %collective-permute-done.10.its2, f32[4,32,128]{2,1,0:T(8,128)S(1)} %get-tuple-element.52.rhs, f32[6,12,32,128]{3,2,1,0:T(8,128)S(1)} %get-tuple-element.54.w2, ...), custom_call_target="tpu_custom_call" | custom-call | flops 20000000000 | tf_op jit(solution)/shard_map/coarse_and_post/pallas_call | solution.py:736
  (6 shorter events, 0.1 us)
Async XLA Ops:
  1.3 12.6 %collective-permute-start = (f32[640,128]{1,0:T(8,128)S(1)}, f32[640,128]{1,0:T(8,128)S(1)}, u32[]{:S(2)}, u32[]{:S(2)}) collective-permute-start(f32[640,128]{1,0:T(8,128)S(1)} %get-tuple-element.36), channel_id=1, source_target_pairs={{0,1},{1,2},{2,3},{3,4},{4,5},{5,6},{6,7},{9,8},{10,9},{11,10},{12... | collective-permute-start | bytes 983048 | tf_op jit(solution)/shard_map/ppermute | solution.py:678
  3.4 11.0 %collective-permute-start.1 = (f32[640,128]{1,0:T(8,128)S(1)}, f32[640,128]{1,0:T(8,128)S(1)}, u32[]{:S(2)}, u32[]{:S(2)}) collective-permute-start(f32[640,128]{1,0:T(8,128)S(1)} %get-tuple-element.37), channel_id=1, source_target_pairs={{1,0},{2,1},{3,2},{4,3},{5,4},{6,5},{7,6},{8,9},{9,10},{10,11},{11... | collective-permute-start | bytes 983048 | tf_op jit(solution)/shard_map/ppermute | solution.py:678
  8.0 14.2 %collective-permute-start.4 = (f32[464,128]{1,0:T(8,128)S(1)}, f32[464,128]{1,0:T(8,128)S(1)}, u32[]{:S(2)}, u32[]{:S(2)}) collective-permute-start(f32[464,128]{1,0:T(8,128)S(1)} %get-tuple-element.42), channel_id=1, source_target_pairs={{8,16},{24,32},{40,48},{56,64},{72,80},{88,96},{104,112},{120,128}... | collective-permute-start | bytes 712712 | tf_op jit(solution)/shard_map/ppermute | solution.py:663
  14.8 12.2 %collective-permute-start.3 = (f32[624,128]{1,0:T(8,128)S(1)}, f32[624,128]{1,0:T(8,128)S(1)}, u32[]{:S(2)}, u32[]{:S(2)}) collective-permute-start(f32[624,128]{1,0:T(8,128)S(1)} %get-tuple-element.41), channel_id=1, source_target_pairs={{8,16},{24,32},{40,48},{56,64},{72,80},{88,96},{104,112},{120,128}... | collective-permute-start | bytes 958472 | tf_op jit(solution)/shard_map/ppermute | solution.py:663
  22.3 4.6 %collective-permute-start.2 = (f32[1280,128]{1,0:T(8,128)S(1)}, f32[1280,128]{1,0:T(8,128)S(1)}, u32[]{:S(2)}, u32[]{:S(2)}) collective-permute-start(f32[1280,128]{1,0:T(8,128)S(1)} %get-tuple-element.40), channel_id=1, source_target_pairs={{0,8},{8,0},{16,24},{24,16},{32,40},{40,32},{48,56},{56,48},{64,72... | collective-permute-start | bytes 1966088 | tf_op jit(solution)/shard_map/ppermute | solution.py:655
  28.8 18.1 %collective-permute-start.5 = (f32[400,128]{1,0:T(8,128)S(1)}, f32[400,128]{1,0:T(8,128)S(1)}, u32[]{:S(2)}, u32[]{:S(2)}) collective-permute-start(f32[400,128]{1,0:T(8,128)S(1)} %get-tuple-element.43.own), channel_id=1, source_target_pairs={{8,16},{24,32},{40,48},{56,64},{72,80},{88,96},{104,112},{120,128}... | collective-permute-start | bytes 614408 | tf_op jit(solution)/shard_map/ppermute | solution.py:663
  35.8 11.1 %collective-permute-start.6 = (f32[320,128]{1,0:T(8,128)S(1)}, f32[320,128]{1,0:T(8,128)S(1)}, u32[]{:S(2)}, u32[]{:S(2)}) collective-permute-start(f32[320,128]{1,0:T(8,128)S(1)} %get-tuple-element.44), channel_id=1, source_target_pairs={{0,16},{16,32},{32,48},{48,64},{64,80},{80,96},{96,112},{112,128},... | collective-permute-start | bytes 491528 | tf_op jit(solution)/shard_map/ppermute | solution.py:669
  37.7 9.2 %collective-permute-start.7 = (f32[128,128]{1,0:T(8,128)S(1)}, f32[128,128]{1,0:T(8,128)S(1)}, u32[]{:S(2)}, u32[]{:S(2)}) collective-permute-start(f32[128,128]{1,0:T(8,128)S(1)} %get-tuple-element.45), channel_id=1, source_target_pairs={{8,32},{24,48},{40,64},{56,80},{72,96},{88,112},{104,128},{120,144... | collective-permute-start | bytes 196616 | tf_op jit(solution)/shard_map/ppermute | solution.py:663
  46.9 3.7 %collective-permute-start.8 = (f32[912,128]{1,0:T(8,128)S(1)}, f32[912,128]{1,0:T(8,128)S(1)}, u32[]{:S(2)}, u32[]{:S(2)}) collective-permute-start(f32[912,128]{1,0:T(8,128)S(1)} %join.1), channel_id=1, source_target_pairs={{0,8},{8,0},{16,24},{24,16},{32,40},{40,32},{48,56},{56,48},{64,72... | collective-permute-start | bytes 1400840 | tf_op jit(solution)/shard_map/ppermute | solution.py:655
  52.4 8.8 %collective-permute-start.9 = (f32[64,128]{1,0:T(8,128)S(1)}, f32[64,128]{1,0:T(8,128)S(1)}, u32[]{:S(2)}, u32[]{:S(2)}) collective-permute-start(f32[64,128]{1,0:T(8,128)S(1)} %get-tuple-element.51), channel_id=1, source_target_pairs={{8,32},{24,48},{40,64},{56,80},{72,96},{88,112},{104,128},{120,144... | collective-permute-start | bytes 98312 | tf_op jit(solution)/shard_map/ppermute | solution.py:663
  61.3 3.1 %collective-permute-start.10 = (f32[64,128]{1,0:T(8,128)S(1)}, f32[64,128]{1,0:T(8,128)S(1)}, u32[]{:S(2)}, u32[]{:S(2)}) collective-permute-start(f32[64,128]{1,0:T(8,128)S(1)} %collective-permute-done.9.two2), channel_id=1, source_target_pairs={{0,8},{8,0},{16,24},{24,16},{32,40},{40,32},{48,56},{56,48},{64,72... | collective-permute-start | bytes 98312 | tf_op jit(solution)/shard_map/ppermute | solution.py:655

commit v10 on v9

--- a/solution.py
+++ b/solution.py
@@ -30,6 +30,8 @@
 EX_IN = 5 * PY
 H1 = PY // 2
 G1 = (R1 - H1) // 2
+EX_RAW = EX_IN + 3 * INNER
+A_EDGE = R1 + 8 * G1
 PAD = 8
 SMALL, LARGE = 1000, 2 * 10**10
 B, ALPHA, BX, BY, BZ = range(5)
@@ -271,7 +273,9 @@
 
         got.append(coarser(load, H1, 1))
     for i in range(4):
-        own[pl.ds(RAW + R1 * i + G1, H1), :] = pack2(got[0][i], got[1][i])
+        t = pack2(got[0][i], got[1][i])
+        own[pl.ds(RAW + R1 * i + G1, H1), :] = t
+        ex[pl.ds(EX_RAW + H1 * i, H1), :] = t
 
 
 def corner_kernel(own_in, one, two, inner, _, own, sw, xs, x, v):
@@ -393,11 +397,14 @@
         got.append(pair_lanes(t[c, pl.ds(0, R1, 2), :] + t[c, pl.ds(1, R1, 2), :], 1) * 0.125)
     mid = pl.ds(PAD + MID0, MID)
     rhs = pack2(got[0], got[1])
-    for out in (send, send1):
-        out[:R1] = rhs
-        out[pl.ds(R1, 4 * R1), :] = own[pl.ds(RAW, 4 * R1), :]
+    send[:R1] = rhs
+    send1[:R1] = rhs
+    send1[pl.ds(R1, 4 * R1), :] = own[pl.ds(RAW, 4 * R1), :]
+    for i in range(4):
+        send[pl.ds(R1 + 2 * G1 * i, G1), :] = own[pl.ds(RAW + R1 * i, G1), :]
+        send[pl.ds(R1 + 2 * G1 * i + G1, G1), :] = own[pl.ds(RAW + R1 * i + G1 + H1, G1), :]
     edge[...] = z[Q0 + 2 - par, mid, :]
-    send[pl.ds(5 * R1, MID), :] = z[Q0 + 1 + par, mid, :]
+    send[pl.ds(A_EDGE, MID), :] = z[Q0 + 1 + par, mid, :]
     q = 3 * par
     u[:R1] = s[2, q]
     u[R1:] = jnp.zeros((PAD, PZ), F32)
@@ -457,7 +464,12 @@
     return load
 
 
-def near_coefficients_kernel(own, other, one, beside, s, w1, inv1, d1):
+def across_coefficients(one, ex, i):
+    base = R1 + 2 * G1 * i
+    return jnp.concatenate([one[pl.ds(base, G1), :], ex[pl.ds(EX_RAW + H1 * i, H1), :], one[pl.ds(base + G1, G1), :]], 0)
+
+
+def near_coefficients_kernel(own, other, one, ex, beside, s, w1, inv1, d1):
     par = parity()
     for i in range(4):
         s[i, :, PAD + R1 :, :] = jnp.zeros((N1, PAD, PZ), F32)
@@ -465,19 +477,20 @@
         sent = pl.ds(R1 * (1 + i), R1)
         place_coefficients(s, i, 2 + par, own[rows, :])
         place_coefficients(s, i, 3 - par, other[rows, :])
-        place_coefficients(s, i, sides(par, 0)[0], one[sent, :])
+        place_coefficients(s, i, sides(par, 0)[0], across_coefficients(one, ex, i))
         place_coefficients(s, i, sides(par, 1)[0], beside[sent, :])
     for k in range(7):
         middle_faces(s, w1, inv1, d1, 1 + 4 * par + k)
 
 
-def join_kernel(own, edge, one, beside, two, out):
+def join_kernel(own, edge, one, ex, beside, two, out):
     out[:R1] = own[:R1]
     out[pl.ds(O_EDGE, MID), :] = edge[...]
     out[pl.ds(O_ONE, R1), :] = one[:R1]
     out[pl.ds(O_BESIDE, R1), :] = beside[:R1]
     out[pl.ds(O_TWO, 2 * R1), :] = two[...]
-    out[pl.ds(O_RAW, 4 * R1), :] = one[pl.ds(R1, 4 * R1), :]
+    for i in range(4):
+        out[pl.ds(O_RAW + R1 * i, R1), :] = across_coefficients(one, ex, i)
     out[pl.ds(O_RAW + 4 * R1, 4 * R1), :] = beside[pl.ds(R1, 4 * R1), :]
 
 
@@ -641,7 +654,7 @@
         if 0 < q < 7:
             x0[q, body, :] += pre0[q - 1]
     x0[near, body, :] += sw[pl.ds(O_EDGE, MID), :]
-    x0[far, body, :] += xs[pl.ds(5 * R1, MID), :]
+    x0[far, body, :] += xs[pl.ds(A_EDGE, MID), :]
     off = Q0 - 2
     sweep(x0, None, c0, w0, 1, 7, (0, MID), 1, 0, into(y0), 40, woff=off, coff=off, wr=MID0, cr=MID0, unroll=6)
 
@@ -685,7 +698,7 @@
     )(*[pltpu.with_memory_space_constraint(v, pltpu.HBM) for v in (right_side, alpha_coef, beta_x, beta_y, beta_z)])
     y1, y2 = along_narrow(y1, 1), along_narrow(y2, -1)
     ex, inner, own = call(
-        inner_kernel, "inner_rows", (shape(EX_IN + 3 * INNER, PZ), shape(2, 3 * INNER, PZ), shape(RAW + 4 * R1, PZ)),
+        inner_kernel, "inner_rows", (shape(EX_RAW + 4 * H1, PZ), shape(2, 3 * INNER, PZ), shape(RAW + 4 * R1, PZ)),
         (VMEM,) * 3, [VMEM],
         [scratch(3, PY + 2 * PAD, PZ)], LARGE,
     )(a)
@@ -699,7 +712,7 @@
 
     send, send1, send2, edge0, pre0, w0, c0 = call(
         fine_kernel, "level0_pre",
-        (shape(5 * R1 + MID, PZ), shape(5 * R1, PZ), shape(2 * R1, PZ), shape(MID, PZ), shape(6, MID, PZ),
+        (shape(A_EDGE + MID, PZ), shape(5 * R1, PZ), shape(2 * R1, PZ), shape(MID, PZ), shape(6, MID, PZ),
          shape(6, 10, EY, PZ), shape(10, EY, PZ)),
         (VMEM,) * 7, [VMEM] * 4 + [ANY],
         [scratch(10, EY, PZ), scratch(10, EY, PZ)] + [scratch(10, EY + 2 * PAD, PZ)] * 3
@@ -710,12 +723,14 @@
     one = across(send, 1)
     beside = from_beside(send1)
     two = across(send2, 2)
-    mine = call(join_kernel, "join", shape(O_END, PZ), VMEM, [VMEM] * 5, [], SMALL)(send, edge0, one, beside, two)
+    mine = call(join_kernel, "join", shape(O_END, PZ), VMEM, [VMEM] * 6, [], SMALL)(
+        send, edge0, one, ex, beside, two
+    )
     its = swap(mine)
     w1_shapes = (shape(*S_SHAPE), shape(6, N1, R1, PZ), shape(N1, R1, PZ), shape(N1, R1, PZ))
     s1, w1, inv1, d1 = call(
-        near_coefficients_kernel, "near_coefficients", w1_shapes, (VMEM,) * 4, [VMEM] * 4, [], LARGE,
-    )(own[RAW:], sw[SRAW:], one, beside)
+        near_coefficients_kernel, "near_coefficients", w1_shapes, (VMEM,) * 4, [VMEM] * 5, [], LARGE,
+    )(own[RAW:], sw[SRAW:], one, ex, beside)
 
     edge, c1, pre1, rhs2, s1, w1, _, _ = call(
         middle_kernel, "level1_pre",

time: 66.4 us -> 67.7 us (1.020)
  the two profiles are of different devices: /device:TPU:223 before, /device:TPU:221 now
where the time goes in v10:
time: 67.7 us; the launch traced here: 67.3 us
  starting transfers between devices  36.9 us (55%)
  waiting for transfers between devices  21.9 us (32%)
  Pallas kernels  8.29 us (12%)
    ppermute x5, starting transfers between devices, across(): return lax.ppermute(v, 'wide', pairs + list(ends))  22.2 us
    ppermute x5, waiting for transfers between devices, across(): return lax.ppermute(v, 'wide', pairs + list(ends))  17.2 us
    ppermute x2, starting transfers between devices, along_narrow(): return lax.ppermute(v, ('wide', 'narrow'), pairs)  6.49 us
    ppermute x3, starting transfers between devices, swap(): lax.ppermute(v, 'wide', [(i, i ^ 1) for i in range(lax.axis_size('wide'))])  5.75 us
    ppermute x2, waiting for transfers between devices, along_narrow(): return lax.ppermute(v, ('wide', 'narrow'), pairs)  2.79 us
    ppermute x1, starting transfers between devices, from_beside(): return lax.ppermute(v, 'wide', pairs)  2.41 us
    ppermute x3, waiting for transfers between devices, swap(): lax.ppermute(v, 'wide', [(i, i ^ 1) for i in range(lax.axis_size('wide'))])  1.96 us
    pallas_call x1, Pallas kernels, shards(): call(fine_kernel, 'level0_pre', (shape(A_EDGE + MID, PZ), shape(5 * R1, P...  1.9 us
  transfers between devices with their start and end apart: 11, of which 6 were waited for; matrix products, arithmetic and copies ran while one was open for 0% of the time, Pallas kernels for 2%

profile of v10, /device:TPU:221, one launch (start us, length us, event | category | flops | bytes accessed | tf_op | source)
XLA Modules:
  0.0 67.3 jit_solution(11739871184140058872)
XLA Ops:
  0.0 1.3 %pack.1 = (f32[5,4,64,128]{3,2,1,0:T(8,128)S(1)}, f32[640,128]{1,0:T(8,128)S(1)}, f32[640,128]{1,0:T(8,128)S(1)}) custom-call(f32[4,64,128]{2,1,0:T(8,128)} %b.1, f32[4,64,128]{2,1,0:T(8,128)} %al.1, f32[4,64,128]{2,1,0:T(8,128)} %bx.1, f32[4,64,128]{2,1,0:T(8,128)} %by.1, f32[4,64,128]{2,1,0:T(8,128)} %bz.1), custom_call_target="tpu_custom_call" | custom-call | flops 1000 | tf_op jit(solution)/shard_map/pack/pallas_call | solution.py:695
  1.3 2.1 %collective-permute-start = (f32[640,128]{1,0:T(8,128)S(1)}, f32[640,128]{1,0:T(8,128)S(1)}, u32[]{:S(2)}, u32[]{:S(2)}) collective-permute-start(f32[640,128]{1,0:T(8,128)S(1)} %get-tuple-element.36), channel_id=1, source_target_pairs={{0,1},{1,2},{2,3},{3,4},{4,5},{5,6},{6,7},{9,8},{10,9},{11,10},{12... | collective-permute-start | bytes 983048 | tf_op jit(solution)/shard_map/ppermute | solution.py:691
  3.4 4.4 %collective-permute-start.1 = (f32[640,128]{1,0:T(8,128)S(1)}, f32[640,128]{1,0:T(8,128)S(1)}, u32[]{:S(2)}, u32[]{:S(2)}) collective-permute-start(f32[640,128]{1,0:T(8,128)S(1)} %get-tuple-element.37), channel_id=1, source_target_pairs={{1,0},{2,1},{3,2},{4,3},{5,4},{6,5},{7,6},{8,9},{9,10},{10,11},{11... | collective-permute-start | bytes 983048 | tf_op jit(solution)/shard_map/ppermute | solution.py:691
  7.8 0.2 inner_rows.1
  8.0 3.5 %collective-permute-start.4 = (f32[592,128]{1,0:T(8,128)S(1)}, f32[592,128]{1,0:T(8,128)S(1)}, u32[]{:S(2)}, u32[]{:S(2)}) collective-permute-start(f32[592,128]{1,0:T(8,128)S(1)} %get-tuple-element.42), channel_id=1, source_target_pairs={{8,16},{24,32},{40,48},{56,64},{72,80},{88,96},{104,112},{120,128}... | collective-permute-start | bytes 909320 | tf_op jit(solution)/shard_map/ppermute | solution.py:676
  11.5 0.0 collective-permute-done.refs_0_.one
  11.6 2.8 %collective-permute-done.1.refs_1_.two = f32[640,128]{1,0:T(8,128)S(1)} collective-permute-done((f32[640,128]{1,0:T(8,128)S(1)}, f32[640,128]{1,0:T(8,128)S(1)}, u32[]{:S(2)}, u32[]{:S(2)}) %collective-permute-start.1) | collective-permute-done | bytes 327712 | tf_op jit(solution)/shard_map/ppermute | solution.py:691
  14.3 0.4 corners.1
  14.8 5.2 %collective-permute-start.3 = (f32[624,128]{1,0:T(8,128)S(1)}, f32[624,128]{1,0:T(8,128)S(1)}, u32[]{:S(2)}, u32[]{:S(2)}) collective-permute-start(f32[624,128]{1,0:T(8,128)S(1)} %get-tuple-element.41), channel_id=1, source_target_pairs={{8,16},{24,32},{40,48},{56,64},{72,80},{88,96},{104,112},{120,128}... | collective-permute-start | bytes 958472 | tf_op jit(solution)/shard_map/ppermute | solution.py:676
  20.0 0.0 collective-permute-done.4.refs_0_.ex
  20.0 1.9 %collective-permute-start.2 = (f32[1280,128]{1,0:T(8,128)S(1)}, f32[1280,128]{1,0:T(8,128)S(1)}, u32[]{:S(2)}, u32[]{:S(2)}) collective-permute-start(f32[1280,128]{1,0:T(8,128)S(1)} %get-tuple-element.40), channel_id=1, source_target_pairs={{0,8},{8,0},{16,24},{24,16},{32,40},{40,32},{48,56},{56,48},{64,72... | collective-permute-start | bytes 1966088 | tf_op jit(solution)/shard_map/ppermute | solution.py:668
  21.9 3.0 %collective-permute-done.3.refs_0_.xs = f32[624,128]{1,0:T(8,128)S(1)} collective-permute-done((f32[624,128]{1,0:T(8,128)S(1)}, f32[624,128]{1,0:T(8,128)S(1)}, u32[]{:S(2)}, u32[]{:S(2)}) %collective-permute-start.3) | collective-permute-done | bytes 319520 | tf_op jit(solution)/shard_map/ppermute | solution.py:676
  24.9 0.0 collective-permute-done.2.sw
  24.9 1.9 %level0_pre.1 = (f32[272,128]{1,0:T(8,128)S(1)}, f32[320,128]{1,0:T(8,128)S(1)}, f32[128,128]{1,0:T(8,128)S(1)}, f32[80,128]{1,0:T(8,128)S(1)}, f32[6,80,128]{2,...) custom-call(f32[2816,128]{1,0:T(8,128)S(1)} %get-tuple-element.39.own, ...), custom_call_target="tpu_custom_call" | custom-call | flops 20000000000 | tf_op jit(solution)/shard_map/level0_pre/pallas_call | solution.py:713
  26.8 2.4 %collective-permute-start.6 = (f32[320,128]{1,0:T(8,128)S(1)}, f32[320,128]{1,0:T(8,128)S(1)}, u32[]{:S(2)}, u32[]{:S(2)}) collective-permute-start(f32[320,128]{1,0:T(8,128)S(1)} %get-tuple-element.44), channel_id=1, source_target_pairs={{0,16},{16,32},{32,48},{48,64},{64,80},{80,96},{96,112},{112,128},... | collective-permute-start | bytes 491528 | tf_op jit(solution)/shard_map/ppermute | solution.py:682
  29.2 9.7 %collective-permute-start.5 = (f32[272,128]{1,0:T(8,128)S(1)}, f32[272,128]{1,0:T(8,128)S(1)}, u32[]{:S(2)}, u32[]{:S(2)}) collective-permute-start(f32[272,128]{1,0:T(8,128)S(1)} %get-tuple-element.43.own), channel_id=1, source_target_pairs={{8,16},{24,32},{40,48},{56,64},{72,80},{88,96},{104,112},{120,128}... | collective-permute-start | bytes 417800 | tf_op jit(solution)/shard_map/ppermute | solution.py:676
  38.9 1.9 %collective-permute-start.7 = (f32[128,128]{1,0:T(8,128)S(1)}, f32[128,128]{1,0:T(8,128)S(1)}, u32[]{:S(2)}, u32[]{:S(2)}) collective-permute-start(f32[128,128]{1,0:T(8,128)S(1)} %get-tuple-element.45), channel_id=1, source_target_pairs={{8,32},{24,48},{40,64},{56,80},{72,96},{88,112},{104,128},{120,144... | collective-permute-start | bytes 196616 | tf_op jit(solution)/shard_map/ppermute | solution.py:676
  40.9 7.2 %collective-permute-done.7.two = f32[128,128]{1,0:T(8,128)S(1)} collective-permute-done((f32[128,128]{1,0:T(8,128)S(1)}, f32[128,128]{1,0:T(8,128)S(1)}, u32[]{:S(2)}, u32[]{:S(2)}) %collective-permute-start.7) | collective-permute-done | bytes 65568 | tf_op jit(solution)/shard_map/ppermute | solution.py:676
  48.1 0.0 collective-permute-done.5.one.xs
  48.1 0.0 collective-permute-done.6.beside
  48.2 1.9 %collective-permute-start.8 = (f32[912,128]{1,0:T(8,128)S(1)}, f32[912,128]{1,0:T(8,128)S(1)}, u32[]{:S(2)}, u32[]{:S(2)}) collective-permute-start(f32[912,128]{1,0:T(8,128)S(1)} %join.1), channel_id=1, source_target_pairs={{0,8},{8,0},{16,24},{24,16},{32,40},{40,32},{48,56},{56,48},{64,72... | collective-permute-start | bytes 1400840 | tf_op jit(solution)/shard_map/ppermute | solution.py:668
  50.1 0.5 near_coefficients.1
  50.6 1.2 %collective-permute-done.8.its.sw = f32[912,128]{1,0:T(8,128)S(1)} collective-permute-done((f32[912,128]{1,0:T(8,128)S(1)}, f32[912,128]{1,0:T(8,128)S(1)}, u32[]{:S(2)}, u32[]{:S(2)}) %collective-permute-start.8) | collective-permute-done | bytes 466976 | tf_op jit(solution)/shard_map/ppermute | solution.py:668
  51.9 1.8 %level1_pre.1 = (f32[64,128]{1,0:T(8,128)S(1)}, f32[14,64,128]{2,1,0:T(8,128)S(1)}, f32[10,64,128]{2,1,0:T(8,128)S(1)}, f32[4,32,128]{2,1,0:T(8,128)S(1)}, f32[4...) custom-call(f32[272,128]{1,0:T(8,128)S(1)} %get-tuple-element.43.own, ...), custom_call_target="tpu_custom_call", output_to_operand_aliasing={{4}: (5, {}), {5}: (6, {}), {6}: (7, {}), {7}: (8, {})} | custom-call | flops 20000000000 | tf_op jit(solution)/shard_map/level1_pre/pallas_call | solution.py:735
  53.7 1.9 %collective-permute-start.9 = (f32[64,128]{1,0:T(8,128)S(1)}, f32[64,128]{1,0:T(8,128)S(1)}, u32[]{:S(2)}, u32[]{:S(2)}) collective-permute-start(f32[64,128]{1,0:T(8,128)S(1)} %get-tuple-element.51), channel_id=1, source_target_pairs={{8,32},{24,48},{40,64},{56,80},{72,96},{88,112},{104,128},{120,144... | collective-permute-start | bytes 98312 | tf_op jit(solution)/shard_map/ppermute | solution.py:676
  55.6 6.9 %collective-permute-done.9.two2 = f32[64,128]{1,0:T(8,128)S(1)} collective-permute-done((f32[64,128]{1,0:T(8,128)S(1)}, f32[64,128]{1,0:T(8,128)S(1)}, u32[]{:S(2)}, u32[]{:S(2)}) %collective-permute-start.9) | collective-permute-done | bytes 32800 | tf_op jit(solution)/shard_map/ppermute | solution.py:676
  62.5 1.9 %collective-permute-start.10 = (f32[64,128]{1,0:T(8,128)S(1)}, f32[64,128]{1,0:T(8,128)S(1)}, u32[]{:S(2)}, u32[]{:S(2)}) collective-permute-start(f32[64,128]{1,0:T(8,128)S(1)} %collective-permute-done.9.two2), channel_id=1, source_target_pairs={{0,8},{8,0},{16,24},{24,16},{32,40},{40,32},{48,56},{56,48},{64,72... | collective-permute-start | bytes 98312 | tf_op jit(solution)/shard_map/ppermute | solution.py:668
  64.4 0.5 level2_coefficients.1
  64.9 0.7 %collective-permute-done.10.its2 = f32[64,128]{1,0:T(8,128)S(1)} collective-permute-done((f32[64,128]{1,0:T(8,128)S(1)}, f32[64,128]{1,0:T(8,128)S(1)}, u32[]{:S(2)}, u32[]{:S(2)}) %collective-permute-start.10) | collective-permute-done | bytes 32800 | tf_op jit(solution)/shard_map/ppermute | solution.py:668
  65.6 1.7 %coarse_and_post.1 = f32[4,64,128]{2,1,0:T(8,128)} custom-call(f32[64,128]{1,0:T(8,128)S(1)} %collective-permute-done.9.two2, f32[64,128]{1,0:T(8,128)S(1)} %collective-permute-done.10.its2, f32[4,32,128]{2,1,0:T(8,128)S(1)} %get-tuple-element.52.rhs, f32[6,12,32,128]{3,2,1,0:T(8,128)S(1)} %get-tuple-element.54.w2, ...), custom_call_target="tpu_custom_call" | custom-call | flops 20000000000 | tf_op jit(solution)/shard_map/coarse_and_post/pallas_call | solution.py:751
  (6 shorter events, 0.1 us)
Async XLA Ops:
  1.3 10.3 %collective-permute-start = (f32[640,128]{1,0:T(8,128)S(1)}, f32[640,128]{1,0:T(8,128)S(1)}, u32[]{:S(2)}, u32[]{:S(2)}) collective-permute-start(f32[640,128]{1,0:T(8,128)S(1)} %get-tuple-element.36), channel_id=1, source_target_pairs={{0,1},{1,2},{2,3},{3,4},{4,5},{5,6},{6,7},{9,8},{10,9},{11,10},{12... | collective-permute-start | bytes 983048 | tf_op jit(solution)/shard_map/ppermute | solution.py:691
  3.4 11.0 %collective-permute-start.1 = (f32[640,128]{1,0:T(8,128)S(1)}, f32[640,128]{1,0:T(8,128)S(1)}, u32[]{:S(2)}, u32[]{:S(2)}) collective-permute-start(f32[640,128]{1,0:T(8,128)S(1)} %get-tuple-element.37), channel_id=1, source_target_pairs={{1,0},{2,1},{3,2},{4,3},{5,4},{6,5},{7,6},{8,9},{9,10},{10,11},{11... | collective-permute-start | bytes 983048 | tf_op jit(solution)/shard_map/ppermute | solution.py:691
  8.0 11.9 %collective-permute-start.4 = (f32[592,128]{1,0:T(8,128)S(1)}, f32[592,128]{1,0:T(8,128)S(1)}, u32[]{:S(2)}, u32[]{:S(2)}) collective-permute-start(f32[592,128]{1,0:T(8,128)S(1)} %get-tuple-element.42), channel_id=1, source_target_pairs={{8,16},{24,32},{40,48},{56,64},{72,80},{88,96},{104,112},{120,128}... | collective-permute-start | bytes 909320 | tf_op jit(solution)/shard_map/ppermute | solution.py:676
  14.8 10.2 %collective-permute-start.3 = (f32[624,128]{1,0:T(8,128)S(1)}, f32[624,128]{1,0:T(8,128)S(1)}, u32[]{:S(2)}, u32[]{:S(2)}) collective-permute-start(f32[624,128]{1,0:T(8,128)S(1)} %get-tuple-element.41), channel_id=1, source_target_pairs={{8,16},{24,32},{40,48},{56,64},{72,80},{88,96},{104,112},{120,128}... | collective-permute-start | bytes 958472 | tf_op jit(solution)/shard_map/ppermute | solution.py:676
  20.0 4.9 %collective-permute-start.2 = (f32[1280,128]{1,0:T(8,128)S(1)}, f32[1280,128]{1,0:T(8,128)S(1)}, u32[]{:S(2)}, u32[]{:S(2)}) collective-permute-start(f32[1280,128]{1,0:T(8,128)S(1)} %get-tuple-element.40), channel_id=1, source_target_pairs={{0,8},{8,0},{16,24},{24,16},{32,40},{40,32},{48,56},{56,48},{64,72... | collective-permute-start | bytes 1966088 | tf_op jit(solution)/shard_map/ppermute | solution.py:668
  26.8 21.3 %collective-permute-start.6 = (f32[320,128]{1,0:T(8,128)S(1)}, f32[320,128]{1,0:T(8,128)S(1)}, u32[]{:S(2)}, u32[]{:S(2)}) collective-permute-start(f32[320,128]{1,0:T(8,128)S(1)} %get-tuple-element.44), channel_id=1, source_target_pairs={{0,16},{16,32},{32,48},{48,64},{64,80},{80,96},{96,112},{112,128},... | collective-permute-start | bytes 491528 | tf_op jit(solution)/shard_map/ppermute | solution.py:682
  29.2 18.9 %collective-permute-start.5 = (f32[272,128]{1,0:T(8,128)S(1)}, f32[272,128]{1,0:T(8,128)S(1)}, u32[]{:S(2)}, u32[]{:S(2)}) collective-permute-start(f32[272,128]{1,0:T(8,128)S(1)} %get-tuple-element.43.own), channel_id=1, source_target_pairs={{8,16},{24,32},{40,48},{56,64},{72,80},{88,96},{104,112},{120,128}... | collective-permute-start | bytes 417800 | tf_op jit(solution)/shard_map/ppermute | solution.py:676
  38.9 9.2 %collective-permute-start.7 = (f32[128,128]{1,0:T(8,128)S(1)}, f32[128,128]{1,0:T(8,128)S(1)}, u32[]{:S(2)}, u32[]{:S(2)}) collective-permute-start(f32[128,128]{1,0:T(8,128)S(1)} %get-tuple-element.45), channel_id=1, source_target_pairs={{8,32},{24,48},{40,64},{56,80},{72,96},{88,112},{104,128},{120,144... | collective-permute-start | bytes 196616 | tf_op jit(solution)/shard_map/ppermute | solution.py:676
  48.2 3.7 %collective-permute-start.8 = (f32[912,128]{1,0:T(8,128)S(1)}, f32[912,128]{1,0:T(8,128)S(1)}, u32[]{:S(2)}, u32[]{:S(2)}) collective-permute-start(f32[912,128]{1,0:T(8,128)S(1)} %join.1), channel_id=1, source_target_pairs={{0,8},{8,0},{16,24},{24,16},{32,40},{40,32},{48,56},{56,48},{64,72... | collective-permute-start | bytes 1400840 | tf_op jit(solution)/shard_map/ppermute | solution.py:668
  53.7 8.8 %collective-permute-start.9 = (f32[64,128]{1,0:T(8,128)S(1)}, f32[64,128]{1,0:T(8,128)S(1)}, u32[]{:S(2)}, u32[]{:S(2)}) collective-permute-start(f32[64,128]{1,0:T(8,128)S(1)} %get-tuple-element.51), channel_id=1, source_target_pairs={{8,32},{24,48},{40,64},{56,80},{72,96},{88,112},{104,128},{120,144... | collective-permute-start | bytes 98312 | tf_op jit(solution)/shard_map/ppermute | solution.py:676
  62.5 3.1 %collective-permute-start.10 = (f32[64,128]{1,0:T(8,128)S(1)}, f32[64,128]{1,0:T(8,128)S(1)}, u32[]{:S(2)}, u32[]{:S(2)}) collective-permute-start(f32[64,128]{1,0:T(8,128)S(1)} %collective-permute-done.9.two2), channel_id=1, source_target_pairs={{0,8},{8,0},{16,24},{24,16},{32,40},{40,32},{48,56},{56,48},{64,72... | collective-permute-start | bytes 98312 | tf_op jit(solution)/shard_map/ppermute | solution.py:668
